TPU v7x, 32 devices: a whole 2x2x4 slice. The times are simulated.
32 devices in a mesh: obs: 4 (over x, core), flux: 8 (over z, y).
Axes of the slice: x: 2, y: 2, z: 4, core: 2. Of those that a mesh axis runs over, the one named last changes fastest.
Arguments:
- probes: bfloat16 [384, 32, 128], P('flux'), may hold values from -6 to 6
- prior_tiles: bfloat16 [384, 8, 128, 128], P('flux'), may hold values from -0.1875 to 0.1875
- neighbours: int32 [384, 8], P('flux'), may hold values from 0 to 383, as said below
- jac: bfloat16 [4, 8, 384, 128, 128], P('obs', 'flux'), may hold values from -0.0546875 to 0.0546875
- jac_obs: int32 [4, 8, 384], P('obs', 'flux'), may hold values from 0 to 31
- jac_flux: int32 [4, 8, 384], P('obs', 'flux'), may hold values from 0 to 47
- counts: int32 [4, 8], P('obs', 'flux'), may hold values from 96 to 384
- rinv: float32 [128, 128], P('obs'), may hold values from 0.25 to 2.5
Outputs:
- power: bfloat16 [384, 32, 128], P('flux')
Inputs may be any that keep to these rules, and one draw needn't show every extreme that they name: `neighbours`: every entry lies within 12 tiles of its own tile t, and entry 0 is t itself.
All inputs are finite; a program needn't handle non-finite values.
Results may differ from a plain program's by a relative error of at most 0.024.
Values may be sent and summed in bfloat16 or wider, within the bound.
No kernel may reach another device: no remote copies, remote signals or barrier semaphores. Data moves between devices by JAX's collectives and lax.ppermute only.
A program may use at most 128 MiB of HBM per device.

v0:
```python
import jax
import jax.numpy as jnp
from jax import lax
from jax.sharding import PartitionSpec as P

STEPS = 4


def with_halo(value, sides, width):
    for axis, dim in sides:
        count, length = (lax.axis_size(axis), value.shape[dim])
        up = [(i, (i + 1) % count) for i in range(count - 1)]
        down = [(j, i) for i, j in up]
        last = lax.slice_in_dim(value, length - width, length, axis=dim)
        first = lax.slice_in_dim(value, 0, width, axis=dim)
        before = lax.ppermute(last, axis, up)
        after = lax.ppermute(first, axis, down)
        value = jnp.concatenate([before, value, after], axis=dim)
    return value


def shifted(block, axis, distance):
    devices = range(lax.axis_size(axis))
    route = [(i - distance, i) for i in devices if i - distance in devices]
    return lax.ppermute(block, axis, route)


def spread_tiles(field, prior_tiles, local_nbr, reach_tiles):
    padded = with_halo(field, (("flux", 0),), reach_tiles)
    gathered = jnp.take(padded, local_nbr, axis=0)
    return jnp.einsum(
        "tkpc,tkcd->tpd", gathered, prior_tiles, preferred_element_type=jnp.float32
    ).astype(jnp.bfloat16)


def gather_tiles(adjoint, prior_tiles, local_nbr, reach_tiles):
    tile_count = adjoint.shape[0]
    probe_count = adjoint.shape[1]
    width = adjoint.shape[2]
    contrib = jnp.einsum("tpd,tkcd->tkpc", adjoint, prior_tiles, preferred_element_type=jnp.float32)
    contrib = contrib.reshape(-1, probe_count, width)
    extended = jax.ops.segment_sum(
        contrib, local_nbr.reshape(-1), num_segments=tile_count + 2 * reach_tiles
    )
    lower_rim = extended[:reach_tiles]
    upper_rim = extended[reach_tiles + tile_count :]
    from_below = shifted(upper_rim.astype(jnp.bfloat16), "flux", 1).astype(upper_rim.dtype)
    from_above = shifted(lower_rim.astype(jnp.bfloat16), "flux", -1).astype(lower_rim.dtype)
    inner = extended[reach_tiles : reach_tiles + tile_count]
    inner = inner.at[:reach_tiles].add(from_below)
    inner = inner.at[tile_count - reach_tiles :].add(from_above)
    return inner.astype(jnp.bfloat16)


def shards(probes, prior_tiles, neighbours, jac, jac_obs, jac_flux, counts, rinv):
    f32 = jnp.float32
    half = jnp.bfloat16
    tile_count = probes.shape[0]
    reach_tiles = tile_count // 4
    obs_rows = rinv.shape[0]
    blocks = jac[0, 0]
    block_obs = jac_obs[0, 0]
    block_flux = jac_flux[0, 0]
    block_count = blocks.shape[0]
    first_tile = lax.axis_index("flux") * tile_count
    local_nbr = neighbours - first_tile + reach_tiles
    live = (jnp.arange(block_count, dtype=jnp.int32) < counts[0, 0]).astype(f32)
    probe_count = probes.shape[1]
    share_probes = probe_count // lax.axis_size("obs")
    field = lax.dynamic_slice_in_dim(probes, lax.axis_index("obs") * share_probes, share_probes, 1)
    for step in range(STEPS):
        spread_share = spread_tiles(field, prior_tiles, local_nbr, reach_tiles)
        spread = lax.all_gather(spread_share, "obs", axis=1, tiled=True)
        picked = jnp.take(spread, block_flux, axis=0)
        product = jnp.einsum("npc,nco->npo", picked, blocks, preferred_element_type=f32)
        product = product * live[:, None, None]
        partial_obs = jax.ops.segment_sum(product, block_obs, num_segments=obs_rows)
        total = lax.psum(partial_obs.astype(jnp.bfloat16), "flux").astype(jnp.float32)
        weighted = (total * rinv[:, None, :]).astype(half)
        picked_obs = jnp.take(weighted, block_obs, axis=0)
        backward = jnp.einsum("npo,nco->npc", picked_obs, blocks, preferred_element_type=f32)
        backward = backward * live[:, None, None]
        partial_cells = jax.ops.segment_sum(backward, block_flux, num_segments=tile_count)
        adjoint = (
            lax.psum_scatter(
                partial_cells.astype(jnp.bfloat16), "obs", scatter_dimension=1, tiled=True
            )
            .astype(jnp.float32)
            .astype(half)
        )
        field = gather_tiles(adjoint, prior_tiles, local_nbr, reach_tiles)
    field = lax.all_gather(field, "obs", axis=1, tiled=True)
    return field


def solution(mesh):
    placed = (
        P("flux", None, None),
        P("flux", None, None, None),
        P("flux", None),
        P("obs", "flux", None, None, None),
        P("obs", "flux", None),
        P("obs", "flux", None),
        P("obs", "flux"),
        P("obs", None),
    )
    return jax.shard_map(
        shards, mesh=mesh, in_specs=placed, out_specs=P("flux", None, None), check_vma=False
    )
```

profile of v0, /device:TPU:0, one launch (start us, length us, event | category | flops | bytes accessed | tf_op | source)
XLA Modules:
  0.0 997.7 jit_solution(12309472608433845383)
XLA Ops:
  7.3 4.9 collective-permute-start
  21.0 5.6 fusion.72
  26.6 6.5 all_gather.15
  33.1 2.6 gather_fusion.1
  35.7 8.6 broadcast_multiply_fusion.7
  44.3 34.7 %scatter_fusion = f32[32,32,128]{2,1,0:T(8,128)S(1)} fusion(f32[32,32,128]{2,1,0:T(8,128)S(1)} %broadcast.129.clone.2, s32[384]{0:T(512)} %copy-done.10, f32[384,32,128]{2,1,0:T(8,128)} %broadcast_multiply_fusion.7), kind=kCustom, calls=%fused_computation.12 | custom fusion | flops 1572864 | bytes 18875904 | tf_op jit(solution)/shard_map/scatter-add | solution.py:77
  79.9 72.6 %all-reduce.5.cloned.1.call-done = bf16[32,32,128]{2,1,0:T(8,128)(2,1)} async-done(((bf16[32,32,128]{2,1,0:T(8,128)(2,1)}), bf16[32,32,128]{2,1,0:T(8,128)(2,1)}) %all-reduce.5.cloned.1.call-update) | async-done | bytes 262160 | tf_op jit(solution)/shard_map/psum | solution.py:78
  153.5 2.4 gather_fusion.2
  156.0 12.2 %broadcast_multiply_fusion.6 = f32[384,32,128]{2,1,0:T(8,128)} fusion(f32[384]{0:T(512)S(1)} %fusion.108, bf16[1,1,384,128,128]{4,3,2,1,0:T(8,128)(2,1)} %param.33, bf16[384,32,128]{2,1,0:T(8,128)(2,1)S(1)} %gather_fusion.2, pred[384]{0:T(512)(128)(4,1)S(1)} %compare_and_fusion.1), kind=kOutput, calls=%fused_computation.54 | convolution fusion | flops 405798912 | bytes 22022016 | tf_op jit(solution)/shard_map/npo,nco->npc/dot_general | solution.py:81
  168.3 34.4 %scatter_fusion.1 = f32[48,32,128]{2,1,0:T(8,128)S(1)} fusion(f32[48,32,128]{2,1,0:T(8,128)S(1)} %broadcast.128.clone.2, s32[384]{0:T(512)S(1)} %copy-done.6, f32[384,32,128]{2,1,0:T(8,128)} %broadcast_multiply_fusion.6), kind=kCustom, calls=%fused_computation.13 | custom fusion | flops 1572864 | bytes 18875904 | tf_op jit(solution)/shard_map/scatter-add | solution.py:83
  204.5 19.5 %reduce-scatter.13.cloned.1.call-done = bf16[8,6144]{1,0:T(8,128)(2,1)} async-done(((bf16[32,6144]{1,0:T(8,128)(2,1)}), bf16[8,6144]{1,0:T(8,128)(2,1)}) %reduce-scatter.13.cloned.1.call-update) | async-done | bytes 98320
  225.0 6.3 fusion.94
  231.4 14.4 %scatter_fusion.2 = f32[72,8,128]{2,1,0:T(8,128)S(1)} fusion(f32[72,8,128]{2,1,0:T(8,128)S(1)} %broadcast.127.clone.2, s32[384]{0:T(512)S(1)} %reshape.451, f32[384,8,128]{2,1,0:T(8,128)S(1)} %bitcast.148), kind=kCustom, calls=%fused_computation.14 | custom fusion | flops 393216 | bytes 4720128 | tf_op jit(solution)/shard_map/scatter-add | solution.py:42
  245.8 3.3 collective-permute-start.2
  250.7 4.2 collective-permute-done.3
  254.9 4.3 collective-permute-start.4
  260.7 4.2 collective-permute-done.5
  266.7 5.6 fusion.73
  272.4 6.2 all_gather.16
  278.5 2.6 gather_fusion.4
  281.1 8.6 broadcast_multiply_fusion.5
  289.7 34.5 %scatter_fusion.3 = f32[32,32,128]{2,1,0:T(8,128)S(1)} fusion(f32[32,32,128]{2,1,0:T(8,128)S(1)} %broadcast.129.clone.1, s32[384]{0:T(512)} %copy-done.10, f32[384,32,128]{2,1,0:T(8,128)} %broadcast_multiply_fusion.5), kind=kCustom, calls=%fused_computation.15 | custom fusion | flops 1572864 | bytes 18875904 | tf_op jit(solution)/shard_map/scatter-add | solution.py:77
  325.1 70.1 %all-reduce.7.cloned.1.call-done = bf16[32,32,128]{2,1,0:T(8,128)(2,1)} async-done(((bf16[32,32,128]{2,1,0:T(8,128)(2,1)}), bf16[32,32,128]{2,1,0:T(8,128)(2,1)}) %all-reduce.7.cloned.1.call-update) | async-done | bytes 262160 | tf_op jit(solution)/shard_map/psum | solution.py:78
  396.3 2.4 gather_fusion.5
  398.7 12.2 %broadcast_multiply_fusion.4 = f32[384,32,128]{2,1,0:T(8,128)} fusion(f32[384]{0:T(512)S(1)} %fusion.108, bf16[1,1,384,128,128]{4,3,2,1,0:T(8,128)(2,1)} %param.33, bf16[384,32,128]{2,1,0:T(8,128)(2,1)S(1)} %gather_fusion.5, pred[384]{0:T(512)(128)(4,1)S(1)} %copy-done.23), kind=kOutput, calls=%fused_computation.52 | convolution fusion | flops 405798912 | bytes 22022016 | tf_op jit(solution)/shard_map/npo,nco->npc/dot_general | solution.py:81
  411.1 34.4 %scatter_fusion.4 = f32[48,32,128]{2,1,0:T(8,128)S(1)} fusion(f32[48,32,128]{2,1,0:T(8,128)S(1)} %broadcast.128.clone.1, s32[384]{0:T(512)S(1)} %copy-done.7, f32[384,32,128]{2,1,0:T(8,128)} %broadcast_multiply_fusion.4), kind=kCustom, calls=%fused_computation.16 | custom fusion | flops 1572864 | bytes 18875904 | tf_op jit(solution)/shard_map/scatter-add | solution.py:83
  446.7 20.0 %reduce-scatter.15.cloned.1.call-done = bf16[8,6144]{1,0:T(8,128)(2,1)} async-done(((bf16[32,6144]{1,0:T(8,128)(2,1)}), bf16[8,6144]{1,0:T(8,128)(2,1)}) %reduce-scatter.15.cloned.1.call-update) | async-done | bytes 98320
  467.7 6.3 fusion.92
  474.1 14.4 %scatter_fusion.5 = f32[72,8,128]{2,1,0:T(8,128)S(1)} fusion(f32[72,8,128]{2,1,0:T(8,128)S(1)} %broadcast.127.clone.1, s32[384]{0:T(512)S(1)} %copy-done.14, f32[384,8,128]{2,1,0:T(8,128)S(1)} %bitcast.149), kind=kCustom, calls=%fused_computation.17 | custom fusion | flops 393216 | bytes 4720128 | tf_op jit(solution)/shard_map/scatter-add | solution.py:42
  488.5 3.3 collective-permute-start.6
  493.4 4.2 collective-permute-done.7
  497.7 4.3 collective-permute-start.8
  503.4 4.2 collective-permute-done.9
  509.4 5.6 fusion.74
  515.1 6.2 all_gather.17
  521.3 2.6 gather_fusion.7
  523.8 8.6 broadcast_multiply_fusion.3
  532.5 34.5 %scatter_fusion.6 = f32[32,32,128]{2,1,0:T(8,128)S(1)} fusion(f32[32,32,128]{2,1,0:T(8,128)S(1)} %broadcast.129.clone, s32[384]{0:T(512)} %copy-done.10, f32[384,32,128]{2,1,0:T(8,128)} %broadcast_multiply_fusion.3), kind=kCustom, calls=%fused_computation.18 | custom fusion | flops 1572864 | bytes 18875904 | tf_op jit(solution)/shard_map/scatter-add | solution.py:77
  567.8 70.2 %all-reduce.9.cloned.1.call-done = bf16[32,32,128]{2,1,0:T(8,128)(2,1)} async-done(((bf16[32,32,128]{2,1,0:T(8,128)(2,1)}), bf16[32,32,128]{2,1,0:T(8,128)(2,1)}) %all-reduce.9.cloned.1.call-update) | async-done | bytes 262160 | tf_op jit(solution)/shard_map/psum | solution.py:78
  639.0 2.4 gather_fusion.8
  641.5 12.2 %broadcast_multiply_fusion.2 = f32[384,32,128]{2,1,0:T(8,128)} fusion(f32[384]{0:T(512)S(1)} %fusion.108, bf16[1,1,384,128,128]{4,3,2,1,0:T(8,128)(2,1)} %param.33, bf16[384,32,128]{2,1,0:T(8,128)(2,1)S(1)} %gather_fusion.8, pred[384]{0:T(512)(128)(4,1)S(1)} %copy-done.24), kind=kOutput, calls=%fused_computation.50 | convolution fusion | flops 405798912 | bytes 22022016 | tf_op jit(solution)/shard_map/npo,nco->npc/dot_general | solution.py:81
  653.8 34.4 %scatter_fusion.7 = f32[48,32,128]{2,1,0:T(8,128)S(1)} fusion(f32[48,32,128]{2,1,0:T(8,128)S(1)} %broadcast.128.clone, s32[384]{0:T(512)S(1)} %copy-done.8, f32[384,32,128]{2,1,0:T(8,128)} %broadcast_multiply_fusion.2), kind=kCustom, calls=%fused_computation.19 | custom fusion | flops 1572864 | bytes 18875904 | tf_op jit(solution)/shard_map/scatter-add | solution.py:83
  689.5 20.0 %reduce-scatter.17.cloned.1.call-done = bf16[8,6144]{1,0:T(8,128)(2,1)} async-done(((bf16[32,6144]{1,0:T(8,128)(2,1)}), bf16[8,6144]{1,0:T(8,128)(2,1)}) %reduce-scatter.17.cloned.1.call-update) | async-done | bytes 98320
  710.5 6.3 fusion.90
  716.9 14.4 %scatter_fusion.8 = f32[72,8,128]{2,1,0:T(8,128)S(1)} fusion(f32[72,8,128]{2,1,0:T(8,128)S(1)} %broadcast.127.clone, s32[384]{0:T(512)S(1)} %copy-done.15, f32[384,8,128]{2,1,0:T(8,128)S(1)} %bitcast.150), kind=kCustom, calls=%fused_computation.20 | custom fusion | flops 393216 | bytes 4720128 | tf_op jit(solution)/shard_map/scatter-add | solution.py:42
  731.3 3.3 collective-permute-start.10
  736.2 4.2 collective-permute-done.11
  740.4 4.3 collective-permute-start.12
  746.2 4.2 collective-permute-done.13
  752.2 5.6 fusion.75
  757.9 6.2 all_gather.18
  764.0 2.6 gather_fusion.10
  766.6 9.1 broadcast_multiply_fusion.1
  775.8 34.4 %scatter_fusion.9 = f32[32,32,128]{2,1,0:T(8,128)S(1)} fusion(f32[32,32,128]{2,1,0:T(8,128)S(1)} %broadcast.129, s32[384]{0:T(512)S(1)} %copy-done.12, f32[384,32,128]{2,1,0:T(8,128)} %broadcast_multiply_fusion.1), kind=kCustom, calls=%fused_computation.21 | custom fusion | flops 1572864 | bytes 18875904 | tf_op jit(solution)/shard_map/scatter-add | solution.py:77
  811.2 69.9 %all-reduce.11.cloned.1.call-done = bf16[32,32,128]{2,1,0:T(8,128)(2,1)} async-done(((bf16[32,32,128]{2,1,0:T(8,128)(2,1)}), bf16[32,32,128]{2,1,0:T(8,128)(2,1)}) %all-reduce.11.cloned.1.call-update) | async-done | bytes 262160 | tf_op jit(solution)/shard_map/psum | solution.py:78
  882.1 2.4 gather_fusion.11
  884.6 12.2 %broadcast_multiply_fusion = f32[384,32,128]{2,1,0:T(8,128)} fusion(f32[384]{0:T(512)S(1)} %fusion.108, bf16[1,1,384,128,128]{4,3,2,1,0:T(8,128)(2,1)} %param.33, bf16[384,32,128]{2,1,0:T(8,128)(2,1)S(1)} %gather_fusion.11, pred[384]{0:T(512)(128)(4,1)S(1)} %copy-done.25), kind=kOutput, calls=%fused_computation.48 | convolution fusion | flops 405798912 | bytes 22022016 | tf_op jit(solution)/shard_map/npo,nco->npc/dot_general | solution.py:81
  896.9 34.4 %scatter_fusion.10 = f32[48,32,128]{2,1,0:T(8,128)S(1)} fusion(f32[48,32,128]{2,1,0:T(8,128)S(1)} %broadcast.128, s32[384]{0:T(512)S(1)} %copy-done.9, f32[384,32,128]{2,1,0:T(8,128)} %broadcast_multiply_fusion), kind=kCustom, calls=%fused_computation.22 | custom fusion | flops 1572864 | bytes 18875904 | tf_op jit(solution)/shard_map/scatter-add | solution.py:83
  932.4 20.3 %reduce-scatter.19.cloned.1.call-done = bf16[8,6144]{1,0:T(8,128)(2,1)} async-done(((bf16[32,6144]{1,0:T(8,128)(2,1)}), bf16[8,6144]{1,0:T(8,128)(2,1)}) %reduce-scatter.19.cloned.1.call-update) | async-done | bytes 98320
  953.6 6.3 fusion.88
  960.0 14.4 %scatter_fusion.11 = f32[72,8,128]{2,1,0:T(8,128)S(1)} fusion(f32[72,8,128]{2,1,0:T(8,128)S(1)} %broadcast.127, s32[384]{0:T(512)S(1)} %copy-done.16, f32[384,8,128]{2,1,0:T(8,128)S(1)} %bitcast.147), kind=kCustom, calls=%fused_computation.23 | custom fusion | flops 393216 | bytes 4720128 | tf_op jit(solution)/shard_map/scatter-add | solution.py:42
  974.4 3.3 collective-permute-start.14
  979.3 4.2 collective-permute-done.15
  983.5 6.2 all_gather.19
  (178 shorter events, 42.9 us)
Async XLA Ops:
  6.5 146.0 %all-reduce.5.cloned.1.call-start = ((), (), s32[]{:S(2)}) async-start(), calls=%async_computation.4 | async-start | bytes 524288 | tf_op jit(solution)/shard_map/psum | solution.py:78
  7.3 11.9 %collective-permute-start = (bf16[12,8,128]{2,1,0:T(8,128)(2,1)S(1)}, bf16[12,8,128]{2,1,0:T(8,128)(2,1)S(1)}, u32[]{:S(2)}, u32[]{:S(2)}) collective-permute-start(bf16[12,8,128]{2,1,0:T(8,128)(2,1)S(1)} %get-tuple-element.106), channel_id=1, source_target_pairs={{0,1},{1,2},{2,3},{3,4},{4,5},{5,6},{6,7},{8,9},{9,10},{10,11},{11... | collective-permute-start | bytes 73736 | tf_op jit(solution)/shard_map/ppermute | solution.py:16
  12.2 7.0 collective-permute-start.1
  15.1 4.1 copy-start.5
  18.5 0.7 copy-start.10
  44.3 35.5 %copy-start.26 = (s32[384]{0:T(512)S(1)}, s32[384]{0:T(512)}, u32[]{:S(2)}) copy-start(s32[384]{0:T(512)} %compare_select_fusion.1) | copy-start | bytes 4612
  44.3 35.5 %copy-start.11 = (s32[384]{0:T(512)S(1)}, s32[384]{0:T(512)}, u32[]{:S(2)}) copy-start(s32[384]{0:T(512)} %copy-done.10) | copy-start | bytes 4612
  44.3 108.2 %copy-start = (f32[32,128]{1,0:T(8,128)S(1)}, f32[32,128]{1,0:T(8,128)}, u32[]{:S(2)}) copy-start(f32[32,128]{1,0:T(8,128)} %param.37) | copy-start | bytes 49156
  79.8 144.3 %reduce-scatter.13.cloned.1.call-start = ((), (), s32[]{:S(2)}) async-start(), calls=%async_computation.8 | async-start | bytes 491520
  79.8 73.7 %copy-start.17 = (s32[1024]{0:T(1024)}, s32[1024]{0:T(1024)S(1)}, u32[]{:S(2)}) copy-start(s32[1024]{0:T(1024)S(1)} %pad_clamp_fusion) | copy-start | bytes 12292
  79.9 88.4 %copy-start.22 = (pred[384]{0:T(512)(128)(4,1)}, pred[384]{0:T(512)(128)(4,1)S(1)}, u32[]{:S(2)}) copy-start(pred[384]{0:T(512)(128)(4,1)S(1)} %compare_and_fusion.1) | copy-start | bytes 1156
  156.0 12.3 %copy-start.6 = (s32[384]{0:T(512)S(1)}, s32[384]{0:T(512)}, u32[]{:S(2)}) copy-start(s32[384]{0:T(512)} %copy-done.5) | copy-start | bytes 4612
  168.3 36.0 %copy-start.21 = (s32[48,8]{0,1:T(8,128)S(1)}, s32[48,8]{0,1:T(8,128)}, u32[]{:S(2)}) copy-start(s32[48,8]{0,1:T(8,128)} %param.32) | copy-start | bytes 4612
  203.8 191.4 %all-reduce.7.cloned.1.call-start = ((), (), s32[]{:S(2)}) async-start(), calls=%async_computation.5 | async-start | bytes 524288 | tf_op jit(solution)/shard_map/psum | solution.py:78
  204.5 26.8 %copy-start.13 = (s32[384]{0:T(512)}, s32[384]{0:T(512)S(1)}, u32[]{:S(2)}) copy-start(s32[384]{0:T(512)S(1)} %reshape.451) | copy-start | bytes 4612
  245.8 4.9 collective-permute-start.2
  249.2 5.7 collective-permute-start.3
  254.9 5.8 collective-permute-start.4
  259.2 5.7 collective-permute-start.5
  289.7 105.5 %copy-start.1 = (f32[32,128]{1,0:T(8,128)S(1)}, f32[32,128]{1,0:T(8,128)}, u32[]{:S(2)}) copy-start(f32[32,128]{1,0:T(8,128)} %param.37) | copy-start | bytes 49156
  289.7 106.5 %copy-start.18 = (s32[1024]{0:T(1024)S(1)}, s32[1024]{0:T(1024)}, u32[]{:S(2)}) copy-start(s32[1024]{0:T(1024)} %copy-done.17) | copy-start | bytes 12292
  324.3 74.4 %copy-start.23 = (pred[384]{0:T(512)(128)(4,1)S(1)}, pred[384]{0:T(512)(128)(4,1)}, u32[]{:S(2)}) copy-start(pred[384]{0:T(512)(128)(4,1)} %copy-done.22) | copy-start | bytes 1156
  325.1 141.7 %reduce-scatter.15.cloned.1.call-start = ((), (), s32[]{:S(2)}) async-start(), calls=%async_computation.9 | async-start | bytes 491520
  398.7 12.3 %copy-start.7 = (s32[384]{0:T(512)S(1)}, s32[384]{0:T(512)}, u32[]{:S(2)}) copy-start(s32[384]{0:T(512)} %copy-done.5) | copy-start | bytes 4612
  446.5 191.5 %all-reduce.9.cloned.1.call-start = ((), (), s32[]{:S(2)}) async-start(), calls=%async_computation.6 | async-start | bytes 524288 | tf_op jit(solution)/shard_map/psum | solution.py:78
  467.7 6.4 copy-start.14
  488.5 4.9 collective-permute-start.6
  491.9 5.7 collective-permute-start.7
  497.7 5.8 collective-permute-start.8
  501.9 5.7 collective-permute-start.9
  532.4 105.5 %copy-start.2 = (f32[32,128]{1,0:T(8,128)S(1)}, f32[32,128]{1,0:T(8,128)}, u32[]{:S(2)}) copy-start(f32[32,128]{1,0:T(8,128)} %param.37) | copy-start | bytes 49156
  532.5 106.5 %copy-start.19 = (s32[1024]{0:T(1024)S(1)}, s32[1024]{0:T(1024)}, u32[]{:S(2)}) copy-start(s32[1024]{0:T(1024)} %copy-done.17) | copy-start | bytes 12292
  567.0 74.5 %copy-start.24 = (pred[384]{0:T(512)(128)(4,1)S(1)}, pred[384]{0:T(512)(128)(4,1)}, u32[]{:S(2)}) copy-start(pred[384]{0:T(512)(128)(4,1)} %copy-done.22) | copy-start | bytes 1156
  567.8 141.8 %reduce-scatter.17.cloned.1.call-start = ((), (), s32[]{:S(2)}) async-start(), calls=%async_computation.10 | async-start | bytes 491520
  641.5 12.3 %copy-start.8 = (s32[384]{0:T(512)S(1)}, s32[384]{0:T(512)}, u32[]{:S(2)}) copy-start(s32[384]{0:T(512)} %copy-done.5) | copy-start | bytes 4612
  689.3 191.8 %all-reduce.11.cloned.1.call-start = ((), (), s32[]{:S(2)}) async-start(), calls=%async_computation.7 | async-start | bytes 524288 | tf_op jit(solution)/shard_map/psum | solution.py:78
  710.5 6.4 copy-start.15
  731.3 4.9 collective-permute-start.10
  734.7 5.7 collective-permute-start.11
  740.4 5.8 collective-permute-start.12
  744.7 5.7 collective-permute-start.13
  757.8 8.8 copy-start.4
  766.6 9.1 copy-start.12
  775.7 105.4 %copy-start.3 = (f32[32,128]{1,0:T(8,128)S(1)}, f32[32,128]{1,0:T(8,128)}, u32[]{:S(2)}) copy-start(f32[32,128]{1,0:T(8,128)} %param.37) | copy-start | bytes 49156
  775.8 106.4 %copy-start.20 = (s32[1024]{0:T(1024)S(1)}, s32[1024]{0:T(1024)}, u32[]{:S(2)}) copy-start(s32[1024]{0:T(1024)} %copy-done.17) | copy-start | bytes 12292
  810.2 74.4 %copy-start.25 = (pred[384]{0:T(512)(128)(4,1)S(1)}, pred[384]{0:T(512)(128)(4,1)}, u32[]{:S(2)}) copy-start(pred[384]{0:T(512)(128)(4,1)} %copy-done.22) | copy-start | bytes 1156
  810.9 141.7 %reduce-scatter.19.cloned.1.call-start = ((), (), s32[]{:S(2)}) async-start(), calls=%async_computation.11 | async-start | bytes 491520
  884.6 12.3 %copy-start.9 = (s32[384]{0:T(512)S(1)}, s32[384]{0:T(512)}, u32[]{:S(2)}) copy-start(s32[384]{0:T(512)} %copy-done.5) | copy-start | bytes 4612
  953.6 6.4 copy-start.16
  974.4 4.9 collective-permute-start.14
  977.8 5.7 collective-permute-start.15
Sparse Core Ops, SparseCore 0:
  79.9 72.5 all-reduce.4
  203.9 20.1 reduce-scatter.12
  325.2 70.0 all-reduce.6
  446.6 20.0 reduce-scatter.14
  567.9 70.0 all-reduce.8
  689.4 20.1 reduce-scatter.16
  811.1 70.0 all-reduce.10
  932.5 20.0 reduce-scatter.18
where the time goes:
time: 1010 us; the launch traced here: 998 us
  waiting for transfers between devices  394 us (39%)
  other arithmetic  344 us (34%)
  matrix products  132 us (13%)
  starting transfers between devices  42.8 us (4%)
  local copies, waits for them, and re-layouts  38.4 us (4%)
  blocking collectives  31.2 us (3%)
  between operations  15.7 us (2%)
    psum x4, waiting for transfers between devices, shards(): lax.psum(partial_obs.astype(jnp.bfloat16), 'flux').astype(jnp.float32)  283 us
    scatter-add x4, other arithmetic, shards(): partial_obs = jax.ops.segment_sum(product, block_obs, num_segments=obs_rows)  138 us
    scatter-add x4, other arithmetic, shards(): jax.ops.segment_sum(backward, block_flux, num_segments=tile_count)  137 us
    unnamed x12, waiting for transfers between devices  80 us
    scatter-add x4, other arithmetic, gather_tiles(): jax.ops.segment_sum(contrib, local_nbr.reshape(-1), num_segments=tile_cou...  57.6 us
    dot_general x4, matrix products, shards(): jnp.einsum('npo,nco->npc', picked_obs, blocks, preferred_element_type=f32)  48.9 us
    dot_general x4, matrix products, shards(): jnp.einsum('npc,nco->npo', picked, blocks, preferred_element_type=f32)  34.7 us
    dot_general x4, matrix products, gather_tiles(): jnp.einsum('tpd,tkcd->tkpc', adjoint, prior_tiles, preferred_element_type...  25.3 us
  transfers between devices with their start and end apart: 24, of which 22 were waited for; matrix products, arithmetic and copies ran while one was open for 1% of the time, Pallas kernels for 0%

commit v1 on v0

v1 whole, which is shorter than its diff:
```python
import functools

import jax
import jax.numpy as jnp
from jax import lax
from jax.experimental import pallas as pl
from jax.experimental.pallas import tpu as pltpu
from jax.sharding import PartitionSpec as P

STEPS = 4
F32 = jnp.float32
HALF = jnp.bfloat16
VMEM_LIMIT = 48 * 2**20


def matmul(a, b):
    return lax.dot_general(a, b, (((1,), (0,)), ((), ())), preferred_element_type=F32)


def matmul_t(a, b):
    return lax.dot_general(a, b, (((1,), (1,)), ((), ())), preferred_element_type=F32)


def chunk_of(count, most):
    return max(c for c in range(1, most + 1) if count % c == 0)


def exchange(value, partner):
    n_obs, n_flux = lax.axis_size("obs"), lax.axis_size("flux")
    route = []
    for i in range(n_obs):
        for j in range(n_flux):
            to = partner(i, j)
            if to is not None:
                route.append((i * n_flux + j, to[0] * n_flux + to[1]))
    return lax.ppermute(value, ("obs", "flux"), route)


def start_copies(source, first, buffer, sems, chunk):
    def one(c, _):
        at = pl.ds(c * chunk, chunk)
        pltpu.make_async_copy(source.at[pl.ds(first + c * chunk, chunk)], buffer.at[at], sems.at[c]).start()
        return 0

    lax.fori_loop(0, buffer.shape[0] // chunk, one, 0)


def wait_copy(source, buffer, sems, chunk, c):
    at = pl.ds(c * chunk, chunk)
    pltpu.make_async_copy(source.at[pl.ds(0, chunk)], buffer.at[at], sems.at[c]).wait()


def jac_kernel(dot, chunk, n_parts, n_outs, src, dst, *refs):
    parts = refs[:n_parts]
    jac = refs[n_parts]
    outs = refs[n_parts + 1 : n_parts + 1 + n_outs]
    x, total, buffer, sems = refs[n_parts + 1 + n_outs :]
    start_copies(jac, 0, buffer, sems, chunk)
    rows = x.shape[0] // n_parts
    for k, part in enumerate(parts):
        x[k * rows : (k + 1) * rows] = part[...]
    total[...] = jnp.zeros_like(total)

    def one(c, _):
        wait_copy(jac, buffer, sems, chunk, c)
        first = c * chunk
        products = [dot(x[src[first + u]], buffer[first + u]) for u in range(chunk)]
        for u in range(chunk):
            total[dst[first + u]] += products[u]
        return 0

    lax.fori_loop(0, buffer.shape[0] // chunk, one, 0)
    rows = (total.shape[0] - 1) // n_outs
    for k, out in enumerate(outs):
        out[...] = total[k * rows : (k + 1) * rows].astype(out.dtype)


def jac_pass(dot, src, dst, parts, jac, out_rows, n_outs, name):
    probes, width = parts[0].shape[1:]
    count = jac.shape[0]
    chunk = chunk_of(count, 48)
    in_rows = len(parts) * parts[0].shape[0]
    smem = pl.BlockSpec(memory_space=pltpu.SMEM)
    vmem = pl.BlockSpec(memory_space=pltpu.VMEM)
    out = (out_rows // n_outs, probes, width)
    return pl.pallas_call(
        functools.partial(jac_kernel, dot, chunk, len(parts), n_outs),
        in_specs=[smem, smem] + [vmem] * len(parts) + [pl.BlockSpec(memory_space=pl.ANY)],
        out_specs=[vmem] * n_outs,
        out_shape=[jax.ShapeDtypeStruct(out, F32 if k == 0 else HALF) for k in range(n_outs)],
        scratch_shapes=[
            pltpu.VMEM((in_rows, probes, width), HALF),
            pltpu.VMEM((out_rows + 1, probes, width), F32),
            pltpu.VMEM(jac.shape, HALF),
            pltpu.SemaphoreType.DMA((count // chunk,)),
        ],
        compiler_params=pltpu.CompilerParams(vmem_limit_bytes=VMEM_LIMIT),
        name=name,
    )(src, dst, *parts, jac)


def gather_kernel(chunk, core, nbr, mine, other, prior, ext, to_core, to_far, buffer, sems):
    tiles, fan = buffer.shape[:2]
    half = tiles
    side = core[0]
    start_copies(prior, side * tiles, buffer, sems, chunk)
    ext[...] = jnp.zeros_like(ext)

    def one(c, _):
        wait_copy(prior, buffer, sems, chunk, c)
        first = c * chunk
        products = []
        for u in range(chunk):
            adjoint = (mine[first + u].astype(F32) + other[first + u].astype(F32)).astype(HALF)
            for k in range(fan):
                products.append(matmul_t(adjoint, buffer[first + u, k]))
        for u in range(chunk):
            for k in range(fan):
                ext[nbr[(first + u) * fan + k]] += products[u * fan + k]
        return 0

    lax.fori_loop(0, tiles // chunk, one, 0)
    to_core[...] = ext[pl.ds(half * (1 - side), half)].astype(HALF)
    to_far[...] = ext[pl.ds(half * side, half)].astype(HALF)


def gather_tiles(core, nbr, mine, other, prior):
    tiles, probes, width = mine.shape
    chunk = chunk_of(tiles, 6)
    smem = pl.BlockSpec(memory_space=pltpu.SMEM)
    vmem = pl.BlockSpec(memory_space=pltpu.VMEM)
    return pl.pallas_call(
        functools.partial(gather_kernel, chunk),
        in_specs=[smem, smem, vmem, vmem, pl.BlockSpec(memory_space=pl.ANY)],
        out_specs=[vmem] * 3,
        out_shape=[
            jax.ShapeDtypeStruct((2 * tiles, probes, width), F32),
            jax.ShapeDtypeStruct((tiles, probes, width), HALF),
            jax.ShapeDtypeStruct((tiles, probes, width), HALF),
        ],
        scratch_shapes=[
            pltpu.VMEM((tiles,) + prior.shape[1:], HALF),
            pltpu.SemaphoreType.DMA((tiles // chunk,)),
        ],
        compiler_params=pltpu.CompilerParams(vmem_limit_bytes=VMEM_LIMIT),
        name="prior_adjoint",
    )(core, nbr, mine, other, prior)


def spread_kernel(chunk, summed, core, nbr, *refs):
    if summed:
        ext, from_core, from_far, prior, out, field, buffer, sems = refs
    else:
        field, prior, out, buffer, sems = refs
    tiles, fan = buffer.shape[:2]
    side = core[0]
    start_copies(prior, side * tiles, buffer, sems, chunk)
    if summed:
        for begin, update in ((tiles * (1 - side), from_core), (tiles * side, from_far)):
            at = pl.ds(begin, tiles)
            field[at] = (ext[at] + update[...].astype(F32)).astype(HALF)

    def one(c, _):
        wait_copy(prior, buffer, sems, chunk, c)
        first = c * chunk
        for u in range(chunk):
            row = [field[nbr[(first + u) * fan + k]] for k in range(fan)]
            tile = buffer[first + u].reshape(fan * buffer.shape[2], buffer.shape[3])
            out[first + u] = matmul(jnp.concatenate(row, axis=1), tile).astype(HALF)
        return 0

    lax.fori_loop(0, tiles // chunk, one, 0)


def spread_tiles(core, nbr, fields, prior):
    summed = len(fields) > 1
    ext_tiles, probes, width = fields[0].shape
    tiles = ext_tiles // 2
    chunk = chunk_of(tiles, 6)
    smem = pl.BlockSpec(memory_space=pltpu.SMEM)
    vmem = pl.BlockSpec(memory_space=pltpu.VMEM)
    scratch = [pltpu.VMEM(fields[0].shape, HALF)] if summed else []
    return pl.pallas_call(
        functools.partial(spread_kernel, chunk, summed),
        in_specs=[smem, smem] + [vmem] * len(fields) + [pl.BlockSpec(memory_space=pl.ANY)],
        out_specs=vmem,
        out_shape=jax.ShapeDtypeStruct((tiles, probes, width), HALF),
        scratch_shapes=scratch
        + [
            pltpu.VMEM((tiles,) + prior.shape[1:], HALF),
            pltpu.SemaphoreType.DMA((tiles // chunk,)),
        ],
        compiler_params=pltpu.CompilerParams(vmem_limit_bytes=VMEM_LIMIT),
        name="prior_spread",
    )(core, nbr, *fields, prior)


def shards(probes, prior_tiles, neighbours, jac, jac_obs, jac_flux, counts, rinv):
    n_obs, n_flux = lax.axis_size("obs"), lax.axis_size("flux")
    tile_count = probes.shape[0]
    half = tile_count // 2
    reach = tile_count // 4
    obs_rows = rinv.shape[0]
    quarter = obs_rows // 4
    blocks = jac[0, 0]
    flux_at = lax.axis_index("flux")
    side = lax.rem(lax.axis_index("obs"), 2)
    corner = lax.rem(flux_at, 4)
    core = side.reshape(1)

    live = jnp.arange(blocks.shape[0], dtype=jnp.int32) < counts[0, 0]
    obs_all, flux_all = jac_obs[0, 0], jac_flux[0, 0]
    obs_at = ((obs_all // quarter) ^ corner) * quarter + obs_all % quarter
    tile_at = ((flux_all // half) ^ side) * half + flux_all % half
    obs_to = jnp.where(live, obs_at, obs_rows)
    tile_to = jnp.where(live, tile_at, tile_count)
    own_rinv = lax.dynamic_slice_in_dim(rinv, corner * quarter, quarter, 0)[:, None, :]
    first_tile = flux_at * tile_count + side * half
    own_nbr = lax.dynamic_slice_in_dim(neighbours, side * half, half, 0)
    nbr = (own_nbr - first_tile + reach).reshape(-1)

    def swap_core(value):
        return exchange(value, lambda i, j: (i ^ 1, j))

    def swap_far(value):
        def partner(i, j):
            to = j - 1 if i % 2 == 0 else j + 1
            return (i ^ 1, to) if 0 <= to < n_flux else None

        return exchange(value, partner)

    def swap_flux(value, bits):
        return exchange(value, lambda i, j: (i, j ^ bits))

    edge = jnp.where(side == 0, probes[:reach], probes[tile_count - reach :])
    beyond = swap_far(edge)
    around = jnp.concatenate([beyond, probes, beyond], axis=0)
    fields = (lax.dynamic_slice_in_dim(around, side * half, 2 * half, 0),)
    for step in range(STEPS):
        spread = spread_tiles(core, nbr, fields, prior_tiles)
        parts = (spread, swap_core(spread))
        pieces = jac_pass(matmul, tile_at, obs_to, parts, blocks, obs_rows, 4, "jac_forward")
        total = pieces[0]
        for bits in range(1, 4):
            total = total + swap_flux(pieces[bits], bits).astype(F32)
        bits = 4
        while bits < n_flux:
            sent = total.astype(HALF)
            total = sent.astype(F32) + swap_flux(sent, bits).astype(F32)
            bits *= 2
        weighted = (total * own_rinv).astype(HALF)
        parts = (weighted,) + tuple(swap_flux(weighted, bits) for bits in range(1, 4))
        mine, theirs = jac_pass(matmul_t, obs_at, tile_to, parts, blocks, tile_count, 2, "jac_adjoint")
        mine = (mine + swap_core(theirs).astype(F32)).astype(HALF)
        bits = 2
        while bits < n_obs:
            other = exchange(mine, lambda i, j, bits=bits: (i ^ bits, j))
            bits *= 2
            if bits < n_obs:
                mine = (mine.astype(F32) + other.astype(F32)).astype(HALF)
        ext, to_core, to_far = gather_tiles(core, nbr, mine, other, prior_tiles)
        fields = (ext, swap_core(to_core), swap_far(to_far))
    ext, from_core, from_far = fields
    low = jnp.where(side == 0, from_far, from_core).astype(F32)
    high = jnp.where(side == 0, from_core, from_far).astype(F32)
    own = (ext + jnp.concatenate([low, high], axis=0))[reach : reach + half].astype(HALF)
    other = swap_core(own)
    first = jnp.where(side == 0, own, other)
    second = jnp.where(side == 0, other, own)
    return jnp.concatenate([first, second], axis=0)


def solution(mesh):
    placed = (
        P("flux", None, None),
        P("flux", None, None, None),
        P("flux", None),
        P("obs", "flux", None, None, None),
        P("obs", "flux", None),
        P("obs", "flux", None),
        P("obs", "flux"),
        P("obs", None),
    )
    return jax.shard_map(
        shards, mesh=mesh, in_specs=placed, out_specs=P("flux", None, None), check_vma=False
    )
```

time: 1010 us -> 271 us (0.27); the launches traced: 998 us -> 270 us
  other arithmetic: 344 us -> 6.4 us
  waiting for transfers between devices: 394 us -> 80.3 us
  matrix products: 132 us -> 0 us
  Pallas kernels: 0 us -> 104 us
  local copies, waits for them, and re-layouts: 38.4 us -> 0.17 us
  starting transfers between devices: 42.8 us -> 78.7 us
  blocking collectives: 31.2 us -> 0 us
  between operations: 15.7 us -> 1.01 us
    scatter-add x20 -> x0, other arithmetic: 333 us -> none  [the longest x4 138 us: shards(): partial_obs = jax.ops.segment_sum(product, block_obs, num_segments=obs_rows)]
    psum x4 -> x0, waiting for transfers between devices: 283 us -> none  [shards(): lax.psum(partial_obs.astype(jnp.bfloat16), 'flux').astype(jnp.float32)]
    dot_general x16 -> x0, matrix products: 132 us -> none  [the longest x4 48.9 us: shards(): jnp.einsum('npo,nco->npc', picked_obs, blocks, preferred_element_type=f32)]
    pallas_call x0 -> x16, Pallas kernels: none -> 104 us  [the longest x8 65.3 us: jac_pass(): pl.pallas_call(functools.partial(jac_kernel, dot, chunk, len(parts), n_ou...]
    unnamed x12 -> x0, waiting for transfers between devices: 80 us -> none
    ppermute x16 -> x50, waiting for transfers between devices: 30.9 us -> 80.3 us  [exchange(): return lax.ppermute(value, ('obs', 'flux'), route)]
    ppermute x16 -> x50, starting transfers between devices: 41.4 us -> 78.7 us  [exchange(): return lax.ppermute(value, ('obs', 'flux'), route)]
    all_gather x5 -> x0, blocking collectives: 31.2 us -> none  [the longest x4 25 us: shards(): spread = lax.all_gather(spread_share, 'obs', axis=1, tiled=True)]
  transfers between devices with their start and end apart: 24 -> 50, of which waited for: 22 -> 43; matrix products, arithmetic and copies ran while one was open for 1% -> 1% of each run, Pallas kernels for 0% -> 0%
where the time goes in v1:
time: 271 us; the launch traced here: 270 us
  Pallas kernels  104 us (38%)
  waiting for transfers between devices  80.3 us (30%)
  starting transfers between devices  78.7 us (29%)
  other arithmetic  6.4 us (2%)
    ppermute x50, waiting for transfers between devices, exchange(): return lax.ppermute(value, ('obs', 'flux'), route)  80.3 us
    ppermute x50, starting transfers between devices, exchange(): return lax.ppermute(value, ('obs', 'flux'), route)  78.7 us
    pallas_call x8, Pallas kernels, jac_pass(): pl.pallas_call(functools.partial(jac_kernel, dot, chunk, len(parts), n_ou...  65.3 us
    pallas_call x4, Pallas kernels, gather_tiles(): pl.pallas_call(functools.partial(gather_kernel, chunk), in_specs=[smem, s...  23.2 us
    pallas_call x4, Pallas kernels, spread_tiles(): pl.pallas_call(functools.partial(spread_kernel, chunk, summed), in_specs=...  15.2 us
  transfers between devices with their start and end apart: 50, of which 43 were waited for; matrix products, arithmetic and copies ran while one was open for 1% of the time, Pallas kernels for 0%

profile of v1, /device:TPU:0, one launch (start us, length us, event | category | flops | bytes accessed | tf_op | source)
XLA Modules:
  0.0 270.3 jit_solution(15483686776959363110)
XLA Ops:
  6.6 3.8 %prior_spread.4.refs_0_ = bf16[24,32,128]{2,1,0:T(8,128)(2,1)S(1)} custom-call(s32[1]{0:T(128)} %bitcast.core, s32[192]{0:T(256)S(1)} %reshape.15.nbr, bf16[48,32,128]{2,1,0:T(8,128)(2,1)S(1)} %fusion.1.refs_0_, bf16[48,8,128,128]{3,2,1,0:T(8,128)(2,1)} %prior.7), custom_call_target="tpu_custom_call" | custom-call | tf_op jit(solution)/shard_map/prior_spread/pallas_call | solution.py:183
  10.4 4.4 %collective-permute-start.1 = (bf16[24,32,128]{2,1,0:T(8,128)(2,1)S(1)}, bf16[24,32,128]{2,1,0:T(8,128)(2,1)S(1)}, u32[]{:S(2)}, u32[]{:S(2)}) collective-permute-start(bf16[24,32,128]{2,1,0:T(8,128)(2,1)S(1)} %prior_spread.4.refs_0_), channel_id=1, source_target_pairs={{0,8},{1,9},{2,10},{3,11},{4,12},{5,13},{6,14},{7,15},{8,0},{9,1},... | collective-permute-start | bytes 589832 | tf_op jit(solution)/shard_map/ppermute | solution.py:36
  15.9 6.6 %jac_forward.4 = (f32[8,32,128]{2,1,0:T(8,128)S(1)}, bf16[8,32,128]{2,1,0:T(8,128)(2,1)S(1)}, bf16[8,32,128]{2,1,0:T(8,128)(2,1)S(1)}, bf16[8,32,128]{2,1,0:T(8,128)(2,1)S(1)}) custom-call(s32[384]{0:T(512)S(1)} %get-tuple-element.88.src, s32[384]{0:T(512)S(1)} %get-tuple-element.79.dst, bf16[24,32,128]{2,1,0:T(8,128)(2,1)S(1)} %prior_spread.4.refs_0_, ...), custom_call_target="tpu_custom_call" | custom-call | tf_op jit(solution)/shard_map/jac_forward/pallas_call | solution.py:86
  22.4 1.6 collective-permute-start.2
  24.0 1.4 collective-permute-start.3
  26.9 1.9 collective-permute-done.3
  28.7 1.9 collective-permute-done.4
  30.7 1.6 collective-permute-start.5
  32.3 4.3 %collective-permute-done.5 = bf16[8,32,128]{2,1,0:T(8,128)(2,1)S(1)} collective-permute-done((bf16[8,32,128]{2,1,0:T(8,128)(2,1)S(1)}, bf16[8,32,128]{2,1,0:T(8,128)(2,1)S(1)}, u32[]{:S(2)}, u32[]{:S(2)}) %collective-permute-start.5) | collective-permute-done | bytes 65568 | tf_op jit(solution)/shard_map/ppermute | solution.py:36
  38.1 2.1 collective-permute-start.6
  40.2 1.7 collective-permute-done.8.refs_3_
  42.6 9.7 %jac_adjoint.4 = (f32[24,32,128]{2,1,0:T(8,128)S(1)}, bf16[24,32,128]{2,1,0:T(8,128)(2,1)S(1)}) custom-call(s32[384]{0:T(512)S(1)} %get-tuple-element.80.src, s32[384]{0:T(512)S(1)} %get-tuple-element.87.dst, bf16[8,32,128]{2,1,0:T(8,128)(2,1)S(1)} %multiply_convert_fusion.3.refs_0_, bf16[8,32,128]{2,1,0:T(8,128)(2,1)S(1)} %collective-permute-done.6.refs_1_, ...), custom_call_target="tpu_custom_call" | custom-call | tf_op jit(solution)/shard_map/jac_adjoint/pallas_call | solution.py:86
  52.4 1.4 collective-permute-done.9
  53.9 1.6 collective-permute-start.10
  55.4 5.4 %collective-permute-done.10.other = bf16[24,32,128]{2,1,0:T(8,128)(2,1)S(1)} collective-permute-done((bf16[24,32,128]{2,1,0:T(8,128)(2,1)S(1)}, bf16[24,32,128]{2,1,0:T(8,128)(2,1)S(1)}, u32[]{:S(2)}, u32[]{:S(2)}) %collective-permute-start.10) | collective-permute-done | bytes 196640 | tf_op jit(solution)/shard_map/ppermute | solution.py:36
  60.9 5.8 %prior_adjoint.4 = (f32[48,32,128]{2,1,0:T(8,128)S(1)}, bf16[24,32,128]{2,1,0:T(8,128)(2,1)S(1)}, bf16[24,32,128]{2,1,0:T(8,128)(2,1)S(1)}) custom-call(s32[1]{0:T(128)} %bitcast.core, s32[192]{0:T(256)S(1)} %reshape.15.nbr, bf16[24,32,128]{2,1,0:T(8,128)(2,1)S(1)} %add_convert_fusion.3.mine, bf16[24,32,128]{2,1,0:T(8,128)(2,1)S(1)} %collective-permute-done.10.other, ...), custom_call_target="tpu_custom_call" | custom-call | tf_op jit(solution)/shard_map/prior_adjoint/pallas_call | solution.py:132
  68.2 3.8 %prior_spread.5.refs_0_ = bf16[24,32,128]{2,1,0:T(8,128)(2,1)S(1)} custom-call(s32[1]{0:T(128)} %bitcast.core, s32[192]{0:T(256)S(1)} %reshape.15.nbr, f32[48,32,128]{2,1,0:T(8,128)S(1)} %get-tuple-element.47.refs_0_, bf16[24,32,128]{2,1,0:T(8,128)(2,1)S(1)} %collective-permute-done.11.refs_1_, bf16[24,32,128]{2,1,0:T(8,128)(2,1)S(1)} %collective-permute-done.12.refs_2_, ...), custom_call_target="tpu_custom_call" | custom-call | tf_op jit(solution)/shard_map/prior_spread/pallas_call | solution.py:183
  72.0 7.2 %collective-permute-start.13 = (bf16[24,32,128]{2,1,0:T(8,128)(2,1)S(1)}, bf16[24,32,128]{2,1,0:T(8,128)(2,1)S(1)}, u32[]{:S(2)}, u32[]{:S(2)}) collective-permute-start(bf16[24,32,128]{2,1,0:T(8,128)(2,1)S(1)} %prior_spread.5.refs_0_), channel_id=1, source_target_pairs={{0,8},{1,9},{2,10},{3,11},{4,12},{5,13},{6,14},{7,15},{8,0},{9,1},... | collective-permute-start | bytes 589832 | tf_op jit(solution)/shard_map/ppermute | solution.py:36
  80.3 6.6 %jac_forward.5 = (f32[8,32,128]{2,1,0:T(8,128)S(1)}, bf16[8,32,128]{2,1,0:T(8,128)(2,1)S(1)}, bf16[8,32,128]{2,1,0:T(8,128)(2,1)S(1)}, bf16[8,32,128]{2,1,0:T(8,128)(2,1)S(1)}) custom-call(s32[384]{0:T(512)S(1)} %get-tuple-element.88.src, s32[384]{0:T(512)S(1)} %get-tuple-element.79.dst, bf16[24,32,128]{2,1,0:T(8,128)(2,1)S(1)} %prior_spread.5.refs_0_, ...), custom_call_target="tpu_custom_call" | custom-call | tf_op jit(solution)/shard_map/jac_forward/pallas_call | solution.py:86
  86.9 2.7 collective-permute-start.14
  89.6 1.5 collective-permute-start.16
  91.9 2.2 collective-permute-done.15
  94.8 2.3 collective-permute-start.17
  97.1 2.9 %collective-permute-done.17 = bf16[8,32,128]{2,1,0:T(8,128)(2,1)S(1)} collective-permute-done((bf16[8,32,128]{2,1,0:T(8,128)(2,1)S(1)}, bf16[8,32,128]{2,1,0:T(8,128)(2,1)S(1)}, u32[]{:S(2)}, u32[]{:S(2)}) %collective-permute-start.17) | collective-permute-done | bytes 65568 | tf_op jit(solution)/shard_map/ppermute | solution.py:36
  100.0 1.7 collective-permute-start.20
  101.7 2.0 collective-permute-start.19
  103.8 1.5 collective-permute-done.20.refs_3_
  105.3 1.4 collective-permute-done.19.refs_2_
  108.0 9.7 %jac_adjoint.5 = (f32[24,32,128]{2,1,0:T(8,128)S(1)}, bf16[24,32,128]{2,1,0:T(8,128)(2,1)S(1)}) custom-call(s32[384]{0:T(512)S(1)} %get-tuple-element.80.src, s32[384]{0:T(512)S(1)} %get-tuple-element.87.dst, bf16[8,32,128]{2,1,0:T(8,128)(2,1)S(1)} %multiply_convert_fusion.2.refs_0_, bf16[8,32,128]{2,1,0:T(8,128)(2,1)S(1)} %collective-permute-done.18.refs_1_, ...), custom_call_target="tpu_custom_call" | custom-call | tf_op jit(solution)/shard_map/jac_adjoint/pallas_call | solution.py:86
  117.8 1.4 collective-permute-done.21
  119.3 1.6 collective-permute-start.22
  120.9 5.5 %collective-permute-done.22.other = bf16[24,32,128]{2,1,0:T(8,128)(2,1)S(1)} collective-permute-done((bf16[24,32,128]{2,1,0:T(8,128)(2,1)S(1)}, bf16[24,32,128]{2,1,0:T(8,128)(2,1)S(1)}, u32[]{:S(2)}, u32[]{:S(2)}) %collective-permute-start.22) | collective-permute-done | bytes 196640 | tf_op jit(solution)/shard_map/ppermute | solution.py:36
  126.3 5.8 %prior_adjoint.5 = (f32[48,32,128]{2,1,0:T(8,128)S(1)}, bf16[24,32,128]{2,1,0:T(8,128)(2,1)S(1)}, bf16[24,32,128]{2,1,0:T(8,128)(2,1)S(1)}) custom-call(s32[1]{0:T(128)} %bitcast.core, s32[192]{0:T(256)S(1)} %reshape.15.nbr, bf16[24,32,128]{2,1,0:T(8,128)(2,1)S(1)} %add_convert_fusion.2.mine, bf16[24,32,128]{2,1,0:T(8,128)(2,1)S(1)} %collective-permute-done.22.other, ...), custom_call_target="tpu_custom_call" | custom-call | tf_op jit(solution)/shard_map/prior_adjoint/pallas_call | solution.py:132
  133.6 3.8 %prior_spread.6.refs_0_ = bf16[24,32,128]{2,1,0:T(8,128)(2,1)S(1)} custom-call(s32[1]{0:T(128)} %bitcast.core, s32[192]{0:T(256)S(1)} %reshape.15.nbr, f32[48,32,128]{2,1,0:T(8,128)S(1)} %get-tuple-element.56.refs_0_, bf16[24,32,128]{2,1,0:T(8,128)(2,1)S(1)} %collective-permute-done.23.refs_1_, bf16[24,32,128]{2,1,0:T(8,128)(2,1)S(1)} %collective-permute-done.24.refs_2_, ...), custom_call_target="tpu_custom_call" | custom-call | tf_op jit(solution)/shard_map/prior_spread/pallas_call | solution.py:183
  137.4 6.1 %collective-permute-start.25 = (bf16[24,32,128]{2,1,0:T(8,128)(2,1)S(1)}, bf16[24,32,128]{2,1,0:T(8,128)(2,1)S(1)}, u32[]{:S(2)}, u32[]{:S(2)}) collective-permute-start(bf16[24,32,128]{2,1,0:T(8,128)(2,1)S(1)} %prior_spread.6.refs_0_), channel_id=1, source_target_pairs={{0,8},{1,9},{2,10},{3,11},{4,12},{5,13},{6,14},{7,15},{8,0},{9,1},... | collective-permute-start | bytes 589832 | tf_op jit(solution)/shard_map/ppermute | solution.py:36
  144.6 6.6 %jac_forward.6 = (f32[8,32,128]{2,1,0:T(8,128)S(1)}, bf16[8,32,128]{2,1,0:T(8,128)(2,1)S(1)}, bf16[8,32,128]{2,1,0:T(8,128)(2,1)S(1)}, bf16[8,32,128]{2,1,0:T(8,128)(2,1)S(1)}) custom-call(s32[384]{0:T(512)S(1)} %get-tuple-element.88.src, s32[384]{0:T(512)S(1)} %get-tuple-element.79.dst, bf16[24,32,128]{2,1,0:T(8,128)(2,1)S(1)} %prior_spread.6.refs_0_, ...), custom_call_target="tpu_custom_call" | custom-call | tf_op jit(solution)/shard_map/jac_forward/pallas_call | solution.py:86
  151.2 2.3 collective-permute-start.26
  155.9 2.6 collective-permute-done.27
  158.5 1.5 collective-permute-done.28
  160.0 1.7 collective-permute-start.29
  161.7 4.2 %collective-permute-done.29 = bf16[8,32,128]{2,1,0:T(8,128)(2,1)S(1)} collective-permute-done((bf16[8,32,128]{2,1,0:T(8,128)(2,1)S(1)}, bf16[8,32,128]{2,1,0:T(8,128)(2,1)S(1)}, u32[]{:S(2)}, u32[]{:S(2)}) %collective-permute-start.29) | collective-permute-done | bytes 65568 | tf_op jit(solution)/shard_map/ppermute | solution.py:36
  166.6 1.6 collective-permute-start.31
  169.5 1.7 collective-permute-done.32.refs_3_
  172.4 9.7 %jac_adjoint.6 = (f32[24,32,128]{2,1,0:T(8,128)S(1)}, bf16[24,32,128]{2,1,0:T(8,128)(2,1)S(1)}) custom-call(s32[384]{0:T(512)S(1)} %get-tuple-element.80.src, s32[384]{0:T(512)S(1)} %get-tuple-element.87.dst, bf16[8,32,128]{2,1,0:T(8,128)(2,1)S(1)} %multiply_convert_fusion.1.refs_0_, bf16[8,32,128]{2,1,0:T(8,128)(2,1)S(1)} %collective-permute-done.30.refs_1_, ...), custom_call_target="tpu_custom_call" | custom-call | tf_op jit(solution)/shard_map/jac_adjoint/pallas_call | solution.py:86
  183.7 1.5 collective-permute-start.34
  185.3 5.5 %collective-permute-done.34.other = bf16[24,32,128]{2,1,0:T(8,128)(2,1)S(1)} collective-permute-done((bf16[24,32,128]{2,1,0:T(8,128)(2,1)S(1)}, bf16[24,32,128]{2,1,0:T(8,128)(2,1)S(1)}, u32[]{:S(2)}, u32[]{:S(2)}) %collective-permute-start.34) | collective-permute-done | bytes 196640 | tf_op jit(solution)/shard_map/ppermute | solution.py:36
  190.7 5.8 %prior_adjoint.6 = (f32[48,32,128]{2,1,0:T(8,128)S(1)}, bf16[24,32,128]{2,1,0:T(8,128)(2,1)S(1)}, bf16[24,32,128]{2,1,0:T(8,128)(2,1)S(1)}) custom-call(s32[1]{0:T(128)} %bitcast.core, s32[192]{0:T(256)S(1)} %reshape.15.nbr, bf16[24,32,128]{2,1,0:T(8,128)(2,1)S(1)} %add_convert_fusion.1.mine, bf16[24,32,128]{2,1,0:T(8,128)(2,1)S(1)} %collective-permute-done.34.other, ...), custom_call_target="tpu_custom_call" | custom-call | tf_op jit(solution)/shard_map/prior_adjoint/pallas_call | solution.py:132
  198.1 3.8 %prior_spread.7.refs_0_ = bf16[24,32,128]{2,1,0:T(8,128)(2,1)S(1)} custom-call(s32[1]{0:T(128)} %bitcast.core, s32[192]{0:T(256)S(1)} %reshape.15.nbr, f32[48,32,128]{2,1,0:T(8,128)S(1)} %get-tuple-element.65.refs_0_, bf16[24,32,128]{2,1,0:T(8,128)(2,1)S(1)} %collective-permute-done.35.refs_1_, bf16[24,32,128]{2,1,0:T(8,128)(2,1)S(1)} %collective-permute-done.36.refs_2_, ...), custom_call_target="tpu_custom_call" | custom-call | tf_op jit(solution)/shard_map/prior_spread/pallas_call | solution.py:183
  201.9 6.6 %collective-permute-start.37 = (bf16[24,32,128]{2,1,0:T(8,128)(2,1)S(1)}, bf16[24,32,128]{2,1,0:T(8,128)(2,1)S(1)}, u32[]{:S(2)}, u32[]{:S(2)}) collective-permute-start(bf16[24,32,128]{2,1,0:T(8,128)(2,1)S(1)} %prior_spread.7.refs_0_), channel_id=1, source_target_pairs={{0,8},{1,9},{2,10},{3,11},{4,12},{5,13},{6,14},{7,15},{8,0},{9,1},... | collective-permute-start | bytes 589832 | tf_op jit(solution)/shard_map/ppermute | solution.py:36
  209.6 6.6 %jac_forward.7 = (f32[8,32,128]{2,1,0:T(8,128)S(1)}, bf16[8,32,128]{2,1,0:T(8,128)(2,1)S(1)}, bf16[8,32,128]{2,1,0:T(8,128)(2,1)S(1)}, bf16[8,32,128]{2,1,0:T(8,128)(2,1)S(1)}) custom-call(s32[384]{0:T(512)S(1)} %get-tuple-element.88.src, s32[384]{0:T(512)S(1)} %get-tuple-element.79.dst, bf16[24,32,128]{2,1,0:T(8,128)(2,1)S(1)} %prior_spread.7.refs_0_, ...), custom_call_target="tpu_custom_call" | custom-call | tf_op jit(solution)/shard_map/jac_forward/pallas_call | solution.py:86
  216.2 2.7 collective-permute-start.38
  218.9 1.5 collective-permute-start.40
  221.2 2.2 collective-permute-done.39
  224.1 2.8 %collective-permute-start.41 = (bf16[8,32,128]{2,1,0:T(8,128)(2,1)S(1)}, bf16[8,32,128]{2,1,0:T(8,128)(2,1)S(1)}, u32[]{:S(2)}, u32[]{:S(2)}) collective-permute-start(bf16[8,32,128]{2,1,0:T(8,128)(2,1)S(1)} %add_convert_fusion.4), channel_id=1, source_target_pairs={{0,4},{1,5},{2,6},{3,7},{4,0},{5,1},{6,2},{7,3},{8,12},{9,13},{10,... | collective-permute-start | bytes 196616 | tf_op jit(solution)/shard_map/ppermute | solution.py:36
  226.8 2.5 collective-permute-done.41
  229.3 1.8 collective-permute-start.44
  231.1 2.0 collective-permute-start.43
  233.1 1.5 collective-permute-done.44.refs_3_
  237.3 9.7 %jac_adjoint.7 = (f32[24,32,128]{2,1,0:T(8,128)S(1)}, bf16[24,32,128]{2,1,0:T(8,128)(2,1)S(1)}) custom-call(s32[384]{0:T(512)S(1)} %get-tuple-element.80.src, s32[384]{0:T(512)S(1)} %get-tuple-element.87.dst, bf16[8,32,128]{2,1,0:T(8,128)(2,1)S(1)} %multiply_convert_fusion.refs_0_, bf16[8,32,128]{2,1,0:T(8,128)(2,1)S(1)} %collective-permute-done.42.refs_1_, ...), custom_call_target="tpu_custom_call" | custom-call | tf_op jit(solution)/shard_map/jac_adjoint/pallas_call | solution.py:86
  248.6 1.7 collective-permute-start.46
  250.3 5.3 %collective-permute-done.46.other = bf16[24,32,128]{2,1,0:T(8,128)(2,1)S(1)} collective-permute-done((bf16[24,32,128]{2,1,0:T(8,128)(2,1)S(1)}, bf16[24,32,128]{2,1,0:T(8,128)(2,1)S(1)}, u32[]{:S(2)}, u32[]{:S(2)}) %collective-permute-start.46) | collective-permute-done | bytes 196640 | tf_op jit(solution)/shard_map/ppermute | solution.py:36
  255.6 5.8 %prior_adjoint.7 = (f32[48,32,128]{2,1,0:T(8,128)S(1)}, bf16[24,32,128]{2,1,0:T(8,128)(2,1)S(1)}, bf16[24,32,128]{2,1,0:T(8,128)(2,1)S(1)}) custom-call(s32[1]{0:T(128)} %bitcast.core, s32[192]{0:T(256)S(1)} %reshape.15.nbr, bf16[24,32,128]{2,1,0:T(8,128)(2,1)S(1)} %add_convert_fusion.mine, bf16[24,32,128]{2,1,0:T(8,128)(2,1)S(1)} %collective-permute-done.46.other, ...), custom_call_target="tpu_custom_call" | custom-call | tf_op jit(solution)/shard_map/prior_adjoint/pallas_call | solution.py:132
  262.1 1.5 collective-permute-start.48
  264.8 3.6 %collective-permute-start.49 = (bf16[24,32,128]{2,1,0:T(8,128)(2,1)S(1)}, bf16[24,32,128]{2,1,0:T(8,128)(2,1)S(1)}, u32[]{:S(2)}, u32[]{:S(2)}) collective-permute-start(bf16[24,32,128]{2,1,0:T(8,128)(2,1)S(1)} %fusion.2), channel_id=1, source_target_pairs={{0,8},{1,9},{2,10},{3,11},{4,12},{5,13},{6,14},{7,15},{8,0},{9,1},... | collective-permute-start | bytes 589832 | tf_op jit(solution)/shard_map/ppermute | solution.py:36
  (80 shorter events, 38.1 us)
Async XLA Ops:
  0.0 32.3 %copy-start = (f32[32,128]{1,0:T(8,128)S(1)}, f32[32,128]{1,0:T(8,128)}, u32[]{:S(2)}) copy-start(f32[32,128]{1,0:T(8,128)} %param.15) | copy-start | bytes 49156
  1.0 4.4 %collective-permute-start = (bf16[12,32,128]{2,1,0:T(8,128)(2,1)S(1)}, bf16[12,32,128]{2,1,0:T(8,128)(2,1)S(1)}, u32[]{:S(2)}, u32[]{:S(2)}) collective-permute-start(bf16[12,32,128]{2,1,0:T(8,128)(2,1)S(1)} %slice_select_fusion), channel_id=1, source_target_pairs={{1,8},{2,9},{3,10},{4,11},{5,12},{6,13},{7,14},{8,1},{9,2},{10,3},... | collective-permute-start | bytes 294920 | tf_op jit(solution)/shard_map/ppermute | solution.py:36
  10.4 5.5 %collective-permute-start.1 = (bf16[24,32,128]{2,1,0:T(8,128)(2,1)S(1)}, bf16[24,32,128]{2,1,0:T(8,128)(2,1)S(1)}, u32[]{:S(2)}, u32[]{:S(2)}) collective-permute-start(bf16[24,32,128]{2,1,0:T(8,128)(2,1)S(1)} %prior_spread.4.refs_0_), channel_id=1, source_target_pairs={{0,8},{1,9},{2,10},{3,11},{4,12},{5,13},{6,14},{7,15},{8,0},{9,1},... | collective-permute-start | bytes 589832 | tf_op jit(solution)/shard_map/ppermute | solution.py:36
  22.4 4.4 %collective-permute-start.2 = (bf16[8,32,128]{2,1,0:T(8,128)(2,1)S(1)}, bf16[8,32,128]{2,1,0:T(8,128)(2,1)S(1)}, u32[]{:S(2)}, u32[]{:S(2)}) collective-permute-start(bf16[8,32,128]{2,1,0:T(8,128)(2,1)S(1)} %get-tuple-element.42), channel_id=1, source_target_pairs={{0,1},{1,0},{2,3},{3,2},{4,5},{5,4},{6,7},{7,6},{8,9},{9,8},{10,11... | collective-permute-start | bytes 196616 | tf_op jit(solution)/shard_map/ppermute | solution.py:36
  24.0 4.7 %collective-permute-start.3 = (bf16[8,32,128]{2,1,0:T(8,128)(2,1)S(1)}, bf16[8,32,128]{2,1,0:T(8,128)(2,1)S(1)}, u32[]{:S(2)}, u32[]{:S(2)}) collective-permute-start(bf16[8,32,128]{2,1,0:T(8,128)(2,1)S(1)} %get-tuple-element.43), channel_id=1, source_target_pairs={{0,2},{1,3},{2,0},{3,1},{4,6},{5,7},{6,4},{7,5},{8,10},{9,11},{10,... | collective-permute-start | bytes 196616 | tf_op jit(solution)/shard_map/ppermute | solution.py:36
  25.4 5.2 %collective-permute-start.4 = (bf16[8,32,128]{2,1,0:T(8,128)(2,1)S(1)}, bf16[8,32,128]{2,1,0:T(8,128)(2,1)S(1)}, u32[]{:S(2)}, u32[]{:S(2)}) collective-permute-start(bf16[8,32,128]{2,1,0:T(8,128)(2,1)S(1)} %get-tuple-element.44), channel_id=1, source_target_pairs={{0,3},{1,2},{2,1},{3,0},{4,7},{5,6},{6,5},{7,4},{8,11},{9,10},{10,... | collective-permute-start | bytes 196616 | tf_op jit(solution)/shard_map/ppermute | solution.py:36
  30.7 5.9 %collective-permute-start.5 = (bf16[8,32,128]{2,1,0:T(8,128)(2,1)S(1)}, bf16[8,32,128]{2,1,0:T(8,128)(2,1)S(1)}, u32[]{:S(2)}, u32[]{:S(2)}) collective-permute-start(bf16[8,32,128]{2,1,0:T(8,128)(2,1)S(1)} %add_convert_fusion.7), channel_id=1, source_target_pairs={{0,4},{1,5},{2,6},{3,7},{4,0},{5,1},{6,2},{7,3},{8,12},{9,13},{10,... | collective-permute-start | bytes 196616 | tf_op jit(solution)/shard_map/ppermute | solution.py:36
  36.6 5.2 %collective-permute-start.8 = (bf16[8,32,128]{2,1,0:T(8,128)(2,1)S(1)}, bf16[8,32,128]{2,1,0:T(8,128)(2,1)S(1)}, u32[]{:S(2)}, u32[]{:S(2)}) collective-permute-start(bf16[8,32,128]{2,1,0:T(8,128)(2,1)S(1)} %multiply_convert_fusion.3.refs_0_), channel_id=1, source_target_pairs={{0,3},{1,2},{2,1},{3,0},{4,7},{5,6},{6,5},{7,4},{8,11},{9,10},{10,... | collective-permute-start | bytes 196616 | tf_op jit(solution)/shard_map/ppermute | solution.py:36
  37.3 4.6 %collective-permute-start.7 = (bf16[8,32,128]{2,1,0:T(8,128)(2,1)S(1)}, bf16[8,32,128]{2,1,0:T(8,128)(2,1)S(1)}, u32[]{:S(2)}, u32[]{:S(2)}) collective-permute-start(bf16[8,32,128]{2,1,0:T(8,128)(2,1)S(1)} %multiply_convert_fusion.3.refs_0_), channel_id=1, source_target_pairs={{0,2},{1,3},{2,0},{3,1},{4,6},{5,7},{6,4},{7,5},{8,10},{9,11},{10,... | collective-permute-start | bytes 196616 | tf_op jit(solution)/shard_map/ppermute | solution.py:36
  38.1 4.5 %collective-permute-start.6 = (bf16[8,32,128]{2,1,0:T(8,128)(2,1)S(1)}, bf16[8,32,128]{2,1,0:T(8,128)(2,1)S(1)}, u32[]{:S(2)}, u32[]{:S(2)}) collective-permute-start(bf16[8,32,128]{2,1,0:T(8,128)(2,1)S(1)} %multiply_convert_fusion.3.refs_0_), channel_id=1, source_target_pairs={{0,1},{1,0},{2,3},{3,2},{4,5},{5,4},{6,7},{7,6},{8,9},{9,8},{10,11... | collective-permute-start | bytes 196616 | tf_op jit(solution)/shard_map/ppermute | solution.py:36
  52.3 1.5 collective-permute-start.9
  53.9 7.0 %collective-permute-start.10 = (bf16[24,32,128]{2,1,0:T(8,128)(2,1)S(1)}, bf16[24,32,128]{2,1,0:T(8,128)(2,1)S(1)}, u32[]{:S(2)}, u32[]{:S(2)}) collective-permute-start(bf16[24,32,128]{2,1,0:T(8,128)(2,1)S(1)} %add_convert_fusion.3.mine), channel_id=1, source_target_pairs={{0,16},{1,17},{2,18},{3,19},{4,20},{5,21},{6,22},{7,23},{8,24},{9,... | collective-permute-start | bytes 589832 | tf_op jit(solution)/shard_map/ppermute | solution.py:36
  66.7 1.5 collective-permute-start.11
  66.8 1.4 collective-permute-start.12
  72.0 8.3 %collective-permute-start.13 = (bf16[24,32,128]{2,1,0:T(8,128)(2,1)S(1)}, bf16[24,32,128]{2,1,0:T(8,128)(2,1)S(1)}, u32[]{:S(2)}, u32[]{:S(2)}) collective-permute-start(bf16[24,32,128]{2,1,0:T(8,128)(2,1)S(1)} %prior_spread.5.refs_0_), channel_id=1, source_target_pairs={{0,8},{1,9},{2,10},{3,11},{4,12},{5,13},{6,14},{7,15},{8,0},{9,1},... | collective-permute-start | bytes 589832 | tf_op jit(solution)/shard_map/ppermute | solution.py:36
  86.9 5.0 %collective-permute-start.14 = (bf16[8,32,128]{2,1,0:T(8,128)(2,1)S(1)}, bf16[8,32,128]{2,1,0:T(8,128)(2,1)S(1)}, u32[]{:S(2)}, u32[]{:S(2)}) collective-permute-start(bf16[8,32,128]{2,1,0:T(8,128)(2,1)S(1)} %get-tuple-element.51), channel_id=1, source_target_pairs={{0,1},{1,0},{2,3},{3,2},{4,5},{5,4},{6,7},{7,6},{8,9},{9,8},{10,11... | collective-permute-start | bytes 196616 | tf_op jit(solution)/shard_map/ppermute | solution.py:36
  89.6 4.5 %collective-permute-start.15 = (bf16[8,32,128]{2,1,0:T(8,128)(2,1)S(1)}, bf16[8,32,128]{2,1,0:T(8,128)(2,1)S(1)}, u32[]{:S(2)}, u32[]{:S(2)}) collective-permute-start(bf16[8,32,128]{2,1,0:T(8,128)(2,1)S(1)} %get-tuple-element.52), channel_id=1, source_target_pairs={{0,2},{1,3},{2,0},{3,1},{4,6},{5,7},{6,4},{7,5},{8,10},{9,11},{10,... | collective-permute-start | bytes 196616 | tf_op jit(solution)/shard_map/ppermute | solution.py:36
  89.6 5.2 %collective-permute-start.16 = (bf16[8,32,128]{2,1,0:T(8,128)(2,1)S(1)}, bf16[8,32,128]{2,1,0:T(8,128)(2,1)S(1)}, u32[]{:S(2)}, u32[]{:S(2)}) collective-permute-start(bf16[8,32,128]{2,1,0:T(8,128)(2,1)S(1)} %get-tuple-element.53), channel_id=1, source_target_pairs={{0,3},{1,2},{2,1},{3,0},{4,7},{5,6},{6,5},{7,4},{8,11},{9,10},{10,... | collective-permute-start | bytes 196616 | tf_op jit(solution)/shard_map/ppermute | solution.py:36
  94.8 5.2 %collective-permute-start.17 = (bf16[8,32,128]{2,1,0:T(8,128)(2,1)S(1)}, bf16[8,32,128]{2,1,0:T(8,128)(2,1)S(1)}, u32[]{:S(2)}, u32[]{:S(2)}) collective-permute-start(bf16[8,32,128]{2,1,0:T(8,128)(2,1)S(1)} %add_convert_fusion.6), channel_id=1, source_target_pairs={{0,4},{1,5},{2,6},{3,7},{4,0},{5,1},{6,2},{7,3},{8,12},{9,13},{10,... | collective-permute-start | bytes 196616 | tf_op jit(solution)/shard_map/ppermute | solution.py:36
  100.0 5.2 %collective-permute-start.20 = (bf16[8,32,128]{2,1,0:T(8,128)(2,1)S(1)}, bf16[8,32,128]{2,1,0:T(8,128)(2,1)S(1)}, u32[]{:S(2)}, u32[]{:S(2)}) collective-permute-start(bf16[8,32,128]{2,1,0:T(8,128)(2,1)S(1)} %multiply_convert_fusion.2.refs_0_), channel_id=1, source_target_pairs={{0,3},{1,2},{2,1},{3,0},{4,7},{5,6},{6,5},{7,4},{8,11},{9,10},{10,... | collective-permute-start | bytes 196616 | tf_op jit(solution)/shard_map/ppermute | solution.py:36
  101.7 5.0 %collective-permute-start.19 = (bf16[8,32,128]{2,1,0:T(8,128)(2,1)S(1)}, bf16[8,32,128]{2,1,0:T(8,128)(2,1)S(1)}, u32[]{:S(2)}, u32[]{:S(2)}) collective-permute-start(bf16[8,32,128]{2,1,0:T(8,128)(2,1)S(1)} %multiply_convert_fusion.2.refs_0_), channel_id=1, source_target_pairs={{0,2},{1,3},{2,0},{3,1},{4,6},{5,7},{6,4},{7,5},{8,10},{9,11},{10,... | collective-permute-start | bytes 196616 | tf_op jit(solution)/shard_map/ppermute | solution.py:36
  103.8 4.3 %collective-permute-start.18 = (bf16[8,32,128]{2,1,0:T(8,128)(2,1)S(1)}, bf16[8,32,128]{2,1,0:T(8,128)(2,1)S(1)}, u32[]{:S(2)}, u32[]{:S(2)}) collective-permute-start(bf16[8,32,128]{2,1,0:T(8,128)(2,1)S(1)} %multiply_convert_fusion.2.refs_0_), channel_id=1, source_target_pairs={{0,1},{1,0},{2,3},{3,2},{4,5},{5,4},{6,7},{7,6},{8,9},{9,8},{10,11... | collective-permute-start | bytes 196616 | tf_op jit(solution)/shard_map/ppermute | solution.py:36
  117.8 1.5 collective-permute-start.21
  119.3 7.0 %collective-permute-start.22 = (bf16[24,32,128]{2,1,0:T(8,128)(2,1)S(1)}, bf16[24,32,128]{2,1,0:T(8,128)(2,1)S(1)}, u32[]{:S(2)}, u32[]{:S(2)}) collective-permute-start(bf16[24,32,128]{2,1,0:T(8,128)(2,1)S(1)} %add_convert_fusion.2.mine), channel_id=1, source_target_pairs={{0,16},{1,17},{2,18},{3,19},{4,20},{5,21},{6,22},{7,23},{8,24},{9,... | collective-permute-start | bytes 589832 | tf_op jit(solution)/shard_map/ppermute | solution.py:36
  132.1 1.5 collective-permute-start.23
  132.2 1.4 collective-permute-start.24
  137.4 7.2 %collective-permute-start.25 = (bf16[24,32,128]{2,1,0:T(8,128)(2,1)S(1)}, bf16[24,32,128]{2,1,0:T(8,128)(2,1)S(1)}, u32[]{:S(2)}, u32[]{:S(2)}) collective-permute-start(bf16[24,32,128]{2,1,0:T(8,128)(2,1)S(1)} %prior_spread.6.refs_0_), channel_id=1, source_target_pairs={{0,8},{1,9},{2,10},{3,11},{4,12},{5,13},{6,14},{7,15},{8,0},{9,1},... | collective-permute-start | bytes 589832 | tf_op jit(solution)/shard_map/ppermute | solution.py:36
  151.2 4.7 %collective-permute-start.26 = (bf16[8,32,128]{2,1,0:T(8,128)(2,1)S(1)}, bf16[8,32,128]{2,1,0:T(8,128)(2,1)S(1)}, u32[]{:S(2)}, u32[]{:S(2)}) collective-permute-start(bf16[8,32,128]{2,1,0:T(8,128)(2,1)S(1)} %get-tuple-element.60), channel_id=1, source_target_pairs={{0,1},{1,0},{2,3},{3,2},{4,5},{5,4},{6,7},{7,6},{8,9},{9,8},{10,11... | collective-permute-start | bytes 196616 | tf_op jit(solution)/shard_map/ppermute | solution.py:36
  153.6 4.9 %collective-permute-start.27 = (bf16[8,32,128]{2,1,0:T(8,128)(2,1)S(1)}, bf16[8,32,128]{2,1,0:T(8,128)(2,1)S(1)}, u32[]{:S(2)}, u32[]{:S(2)}) collective-permute-start(bf16[8,32,128]{2,1,0:T(8,128)(2,1)S(1)} %get-tuple-element.61), channel_id=1, source_target_pairs={{0,2},{1,3},{2,0},{3,1},{4,6},{5,7},{6,4},{7,5},{8,10},{9,11},{10,... | collective-permute-start | bytes 196616 | tf_op jit(solution)/shard_map/ppermute | solution.py:36
  154.8 5.2 %collective-permute-start.28 = (bf16[8,32,128]{2,1,0:T(8,128)(2,1)S(1)}, bf16[8,32,128]{2,1,0:T(8,128)(2,1)S(1)}, u32[]{:S(2)}, u32[]{:S(2)}) collective-permute-start(bf16[8,32,128]{2,1,0:T(8,128)(2,1)S(1)} %get-tuple-element.62), channel_id=1, source_target_pairs={{0,3},{1,2},{2,1},{3,0},{4,7},{5,6},{6,5},{7,4},{8,11},{9,10},{10,... | collective-permute-start | bytes 196616 | tf_op jit(solution)/shard_map/ppermute | solution.py:36
  160.0 5.9 %collective-permute-start.29 = (bf16[8,32,128]{2,1,0:T(8,128)(2,1)S(1)}, bf16[8,32,128]{2,1,0:T(8,128)(2,1)S(1)}, u32[]{:S(2)}, u32[]{:S(2)}) collective-permute-start(bf16[8,32,128]{2,1,0:T(8,128)(2,1)S(1)} %add_convert_fusion.5), channel_id=1, source_target_pairs={{0,4},{1,5},{2,6},{3,7},{4,0},{5,1},{6,2},{7,3},{8,12},{9,13},{10,... | collective-permute-start | bytes 196616 | tf_op jit(solution)/shard_map/ppermute | solution.py:36
  165.9 5.2 %collective-permute-start.32 = (bf16[8,32,128]{2,1,0:T(8,128)(2,1)S(1)}, bf16[8,32,128]{2,1,0:T(8,128)(2,1)S(1)}, u32[]{:S(2)}, u32[]{:S(2)}) collective-permute-start(bf16[8,32,128]{2,1,0:T(8,128)(2,1)S(1)} %multiply_convert_fusion.1.refs_0_), channel_id=1, source_target_pairs={{0,3},{1,2},{2,1},{3,0},{4,7},{5,6},{6,5},{7,4},{8,11},{9,10},{10,... | collective-permute-start | bytes 196616 | tf_op jit(solution)/shard_map/ppermute | solution.py:36
  166.6 4.6 %collective-permute-start.31 = (bf16[8,32,128]{2,1,0:T(8,128)(2,1)S(1)}, bf16[8,32,128]{2,1,0:T(8,128)(2,1)S(1)}, u32[]{:S(2)}, u32[]{:S(2)}) collective-permute-start(bf16[8,32,128]{2,1,0:T(8,128)(2,1)S(1)} %multiply_convert_fusion.1.refs_0_), channel_id=1, source_target_pairs={{0,2},{1,3},{2,0},{3,1},{4,6},{5,7},{6,4},{7,5},{8,10},{9,11},{10,... | collective-permute-start | bytes 196616 | tf_op jit(solution)/shard_map/ppermute | solution.py:36
  168.2 4.3 %collective-permute-start.30 = (bf16[8,32,128]{2,1,0:T(8,128)(2,1)S(1)}, bf16[8,32,128]{2,1,0:T(8,128)(2,1)S(1)}, u32[]{:S(2)}, u32[]{:S(2)}) collective-permute-start(bf16[8,32,128]{2,1,0:T(8,128)(2,1)S(1)} %multiply_convert_fusion.1.refs_0_), channel_id=1, source_target_pairs={{0,1},{1,0},{2,3},{3,2},{4,5},{5,4},{6,7},{7,6},{8,9},{9,8},{10,11... | collective-permute-start | bytes 196616 | tf_op jit(solution)/shard_map/ppermute | solution.py:36
  182.2 1.5 collective-permute-start.33
  183.7 7.0 %collective-permute-start.34 = (bf16[24,32,128]{2,1,0:T(8,128)(2,1)S(1)}, bf16[24,32,128]{2,1,0:T(8,128)(2,1)S(1)}, u32[]{:S(2)}, u32[]{:S(2)}) collective-permute-start(bf16[24,32,128]{2,1,0:T(8,128)(2,1)S(1)} %add_convert_fusion.1.mine), channel_id=1, source_target_pairs={{0,16},{1,17},{2,18},{3,19},{4,20},{5,21},{6,22},{7,23},{8,24},{9,... | collective-permute-start | bytes 589832 | tf_op jit(solution)/shard_map/ppermute | solution.py:36
  196.6 1.5 collective-permute-start.35
  196.6 1.4 collective-permute-start.36
  201.9 7.7 %collective-permute-start.37 = (bf16[24,32,128]{2,1,0:T(8,128)(2,1)S(1)}, bf16[24,32,128]{2,1,0:T(8,128)(2,1)S(1)}, u32[]{:S(2)}, u32[]{:S(2)}) collective-permute-start(bf16[24,32,128]{2,1,0:T(8,128)(2,1)S(1)} %prior_spread.7.refs_0_), channel_id=1, source_target_pairs={{0,8},{1,9},{2,10},{3,11},{4,12},{5,13},{6,14},{7,15},{8,0},{9,1},... | collective-permute-start | bytes 589832 | tf_op jit(solution)/shard_map/ppermute | solution.py:36
  216.2 5.0 %collective-permute-start.38 = (bf16[8,32,128]{2,1,0:T(8,128)(2,1)S(1)}, bf16[8,32,128]{2,1,0:T(8,128)(2,1)S(1)}, u32[]{:S(2)}, u32[]{:S(2)}) collective-permute-start(bf16[8,32,128]{2,1,0:T(8,128)(2,1)S(1)} %get-tuple-element.69), channel_id=1, source_target_pairs={{0,1},{1,0},{2,3},{3,2},{4,5},{5,4},{6,7},{7,6},{8,9},{9,8},{10,11... | collective-permute-start | bytes 196616 | tf_op jit(solution)/shard_map/ppermute | solution.py:36
  218.9 4.5 %collective-permute-start.39 = (bf16[8,32,128]{2,1,0:T(8,128)(2,1)S(1)}, bf16[8,32,128]{2,1,0:T(8,128)(2,1)S(1)}, u32[]{:S(2)}, u32[]{:S(2)}) collective-permute-start(bf16[8,32,128]{2,1,0:T(8,128)(2,1)S(1)} %get-tuple-element.70), channel_id=1, source_target_pairs={{0,2},{1,3},{2,0},{3,1},{4,6},{5,7},{6,4},{7,5},{8,10},{9,11},{10,... | collective-permute-start | bytes 196616 | tf_op jit(solution)/shard_map/ppermute | solution.py:36
  218.9 5.2 %collective-permute-start.40 = (bf16[8,32,128]{2,1,0:T(8,128)(2,1)S(1)}, bf16[8,32,128]{2,1,0:T(8,128)(2,1)S(1)}, u32[]{:S(2)}, u32[]{:S(2)}) collective-permute-start(bf16[8,32,128]{2,1,0:T(8,128)(2,1)S(1)} %get-tuple-element.71), channel_id=1, source_target_pairs={{0,3},{1,2},{2,1},{3,0},{4,7},{5,6},{6,5},{7,4},{8,11},{9,10},{10,... | collective-permute-start | bytes 196616 | tf_op jit(solution)/shard_map/ppermute | solution.py:36
  224.1 5.2 %collective-permute-start.41 = (bf16[8,32,128]{2,1,0:T(8,128)(2,1)S(1)}, bf16[8,32,128]{2,1,0:T(8,128)(2,1)S(1)}, u32[]{:S(2)}, u32[]{:S(2)}) collective-permute-start(bf16[8,32,128]{2,1,0:T(8,128)(2,1)S(1)} %add_convert_fusion.4), channel_id=1, source_target_pairs={{0,4},{1,5},{2,6},{3,7},{4,0},{5,1},{6,2},{7,3},{8,12},{9,13},{10,... | collective-permute-start | bytes 196616 | tf_op jit(solution)/shard_map/ppermute | solution.py:36
  229.3 5.2 %collective-permute-start.44 = (bf16[8,32,128]{2,1,0:T(8,128)(2,1)S(1)}, bf16[8,32,128]{2,1,0:T(8,128)(2,1)S(1)}, u32[]{:S(2)}, u32[]{:S(2)}) collective-permute-start(bf16[8,32,128]{2,1,0:T(8,128)(2,1)S(1)} %multiply_convert_fusion.refs_0_), channel_id=1, source_target_pairs={{0,3},{1,2},{2,1},{3,0},{4,7},{5,6},{6,5},{7,4},{8,11},{9,10},{10,... | collective-permute-start | bytes 196616 | tf_op jit(solution)/shard_map/ppermute | solution.py:36
  231.1 4.9 %collective-permute-start.43 = (bf16[8,32,128]{2,1,0:T(8,128)(2,1)S(1)}, bf16[8,32,128]{2,1,0:T(8,128)(2,1)S(1)}, u32[]{:S(2)}, u32[]{:S(2)}) collective-permute-start(bf16[8,32,128]{2,1,0:T(8,128)(2,1)S(1)} %multiply_convert_fusion.refs_0_), channel_id=1, source_target_pairs={{0,2},{1,3},{2,0},{3,1},{4,6},{5,7},{6,4},{7,5},{8,10},{9,11},{10,... | collective-permute-start | bytes 196616 | tf_op jit(solution)/shard_map/ppermute | solution.py:36
  233.1 4.3 %collective-permute-start.42 = (bf16[8,32,128]{2,1,0:T(8,128)(2,1)S(1)}, bf16[8,32,128]{2,1,0:T(8,128)(2,1)S(1)}, u32[]{:S(2)}, u32[]{:S(2)}) collective-permute-start(bf16[8,32,128]{2,1,0:T(8,128)(2,1)S(1)} %multiply_convert_fusion.refs_0_), channel_id=1, source_target_pairs={{0,1},{1,0},{2,3},{3,2},{4,5},{5,4},{6,7},{7,6},{8,9},{9,8},{10,11... | collective-permute-start | bytes 196616 | tf_op jit(solution)/shard_map/ppermute | solution.py:36
  247.1 1.5 collective-permute-start.45
  248.6 7.0 %collective-permute-start.46 = (bf16[24,32,128]{2,1,0:T(8,128)(2,1)S(1)}, bf16[24,32,128]{2,1,0:T(8,128)(2,1)S(1)}, u32[]{:S(2)}, u32[]{:S(2)}) collective-permute-start(bf16[24,32,128]{2,1,0:T(8,128)(2,1)S(1)} %add_convert_fusion.mine), channel_id=1, source_target_pairs={{0,16},{1,17},{2,18},{3,19},{4,20},{5,21},{6,22},{7,23},{8,24},{9,... | collective-permute-start | bytes 589832 | tf_op jit(solution)/shard_map/ppermute | solution.py:36
  261.4 2.2 collective-permute-start.47
  262.1 2.6 collective-permute-start.48
  264.8 4.7 %collective-permute-start.49 = (bf16[24,32,128]{2,1,0:T(8,128)(2,1)S(1)}, bf16[24,32,128]{2,1,0:T(8,128)(2,1)S(1)}, u32[]{:S(2)}, u32[]{:S(2)}) collective-permute-start(bf16[24,32,128]{2,1,0:T(8,128)(2,1)S(1)} %fusion.2), channel_id=1, source_target_pairs={{0,8},{1,9},{2,10},{3,11},{4,12},{5,13},{6,14},{7,15},{8,0},{9,1},... | collective-permute-start | bytes 589832 | tf_op jit(solution)/shard_map/ppermute | solution.py:36

commit v2 on v1

v2 whole, which is shorter than its diff:
```python
import functools

import jax
import jax.numpy as jnp
from jax import lax
from jax.experimental import pallas as pl
from jax.experimental.pallas import tpu as pltpu
from jax.sharding import PartitionSpec as P

STEPS = 4
F32 = jnp.float32
HALF = jnp.bfloat16
VMEM_LIMIT = 8 * 2**20
GROUP = 4
ROUND = 24


def matmul(a, b):
    return lax.dot_general(a, b, (((1,), (0,)), ((), ())), preferred_element_type=F32)


def matmul_t(a, b):
    return lax.dot_general(a, b, (((1,), (1,)), ((), ())), preferred_element_type=F32)


def chunk_of(count, most):
    return max(c for c in range(1, most + 1) if count % c == 0)


def exchange(value, partner):
    n_obs, n_flux = lax.axis_size("obs"), lax.axis_size("flux")
    route = []
    for i in range(n_obs):
        for j in range(n_flux):
            to = partner(i, j)
            if to is not None:
                route.append((i * n_flux + j, to[0] * n_flux + to[1]))
    return lax.ppermute(value, ("obs", "flux"), route)


def plan_groups(src, dst, src_rows, dst_rows):
    passes, blocks = dst.shape
    groups = blocks // GROUP + dst_rows
    groups += -groups % ROUND
    slots = groups * GROUP
    i32 = jnp.int32
    at = jnp.arange(blocks, dtype=i32)
    rows = jnp.arange(dst_rows, dtype=i32)
    same = (dst[:, :, None] == dst[:, None, :]) & (at[None, :] < at[:, None])
    rank = jnp.sum(same.astype(i32), axis=2)
    member = (dst[:, None, :] == rows[:, None]).astype(i32)
    fills = (jnp.sum(member, axis=2) + GROUP - 1) // GROUP
    begin = jnp.sum(jnp.where(rows[None, :] < rows[:, None], fills[:, None, :], 0), axis=2)
    place = jnp.sum(member * begin[:, :, None], axis=1) * GROUP + rank
    place = jnp.where(dst < dst_rows, place, slots)
    hit = place[:, None, :] == jnp.arange(slots, dtype=i32)[:, None]
    src_of = jnp.sum(jnp.where(hit, (src - src_rows)[:, None, :], 0), axis=2) + src_rows
    block_of = jnp.sum(jnp.where(hit, at, 0), axis=2)
    lead = place[:, None, :] == jnp.arange(groups, dtype=i32)[:, None] * GROUP
    dst_of = jnp.sum(jnp.where(lead, (dst - dst_rows)[:, None, :], 0), axis=2) + dst_rows
    rounds = (jnp.sum(fills, axis=1, keepdims=True) + ROUND - 1) // ROUND
    return jnp.concatenate([src_of, block_of, dst_of, rounds], axis=1)


def grouped_products(transposed, plan, x, blocks, total):
    slots = (plan.shape[0] - 1) // (2 * GROUP + 1) * GROUP
    total[...] = jnp.zeros_like(total)

    def one(c, _):
        products = []
        for u in range(ROUND):
            first = (c * ROUND + u) * GROUP
            rows = [x[plan[first + g]] for g in range(GROUP)]
            tiles = [blocks[plan[slots + first + g]] for g in range(GROUP)]
            left = jnp.concatenate(rows, axis=1)
            if transposed:
                products.append(matmul_t(left, jnp.concatenate(tiles, axis=1)))
            else:
                products.append(matmul(left, jnp.concatenate(tiles, axis=0)))
        for u in range(ROUND):
            total[plan[2 * slots + c * ROUND + u]] += products[u]
        return 0

    lax.fori_loop(0, plan[plan.shape[0] - 1], one, 0)


def jac_kernel(transposed, n_parts, n_outs, plan, *refs):
    parts = refs[:n_parts]
    jac = refs[n_parts]
    outs = refs[n_parts + 1 : n_parts + 1 + n_outs]
    x, total = refs[n_parts + 1 + n_outs :]
    rows = parts[0].shape[0]
    for k, part in enumerate(parts):
        x[k * rows : (k + 1) * rows] = part[...]
    for r in range(n_parts * rows, x.shape[0]):
        x[r] = jnp.zeros(x.shape[1:], HALF)
    grouped_products(transposed, plan, x, jac, total)
    rows = outs[0].shape[0]
    for k, out in enumerate(outs):
        out[...] = total[k * rows : (k + 1) * rows].astype(out.dtype)


def jac_pass(transposed, plan, parts, jac, src_rows, dst_rows, out_rows, n_outs, name):
    probes, width = parts[0].shape[1:]
    smem = pl.BlockSpec(memory_space=pltpu.SMEM)
    vmem = pl.BlockSpec(memory_space=pltpu.VMEM)
    out = (out_rows // n_outs, probes, width)
    return pl.pallas_call(
        functools.partial(jac_kernel, transposed, len(parts), n_outs),
        in_specs=[smem] + [vmem] * len(parts) + [vmem],
        out_specs=[vmem] * n_outs,
        out_shape=[jax.ShapeDtypeStruct(out, F32 if k == 0 else HALF) for k in range(n_outs)],
        scratch_shapes=[
            pltpu.VMEM((src_rows + 1, probes, width), HALF),
            pltpu.VMEM((dst_rows + 1, probes, width), F32),
        ],
        compiler_params=pltpu.CompilerParams(vmem_limit_bytes=VMEM_LIMIT),
        name=name,
    )(plan, *parts, jac)


def gather_kernel(src_rows, core, plan, mine, other, prior, ext, to_core, to_far, x, total):
    half = mine.shape[0]
    side = core[0]
    x[:half] = (mine[...].astype(F32) + other[...].astype(F32)).astype(HALF)
    x[src_rows] = jnp.zeros(x.shape[1:], HALF)
    grouped_products(True, plan, x, prior, total)
    ext[...] = total[: 2 * half]
    to_core[...] = total[pl.ds(half * (1 - side), half)].astype(HALF)
    to_far[...] = total[pl.ds(half * side, half)].astype(HALF)


def gather_tiles(core, plan, mine, other, prior, src_rows, dst_rows):
    tiles, probes, width = mine.shape
    smem = pl.BlockSpec(memory_space=pltpu.SMEM)
    vmem = pl.BlockSpec(memory_space=pltpu.VMEM)
    return pl.pallas_call(
        functools.partial(gather_kernel, src_rows),
        in_specs=[smem, smem, vmem, vmem, vmem],
        out_specs=[vmem] * 3,
        out_shape=[
            jax.ShapeDtypeStruct((2 * tiles, probes, width), F32),
            jax.ShapeDtypeStruct((tiles, probes, width), HALF),
            jax.ShapeDtypeStruct((tiles, probes, width), HALF),
        ],
        scratch_shapes=[
            pltpu.VMEM((src_rows + 1, probes, width), HALF),
            pltpu.VMEM((dst_rows + 1, probes, width), F32),
        ],
        compiler_params=pltpu.CompilerParams(vmem_limit_bytes=VMEM_LIMIT),
        name="prior_adjoint",
    )(core, plan, mine, other, prior)


def spread_kernel(summed, fan, core, nbr, *refs):
    if summed:
        ext, from_core, from_far, prior, out, field = refs
    else:
        field, prior, out = refs
    tiles = out.shape[0]
    chunk = chunk_of(tiles, 12)
    side = core[0]
    if summed:
        for begin, update in ((tiles * (1 - side), from_core), (tiles * side, from_far)):
            at = pl.ds(begin, tiles)
            field[at] = (ext[at] + update[...].astype(F32)).astype(HALF)

    def one(c, _):
        first = c * chunk
        for u in range(chunk):
            row = [field[nbr[(first + u) * fan + k]] for k in range(fan)]
            tile = prior[pl.ds((side * tiles + first + u) * fan, fan)]
            tile = tile.reshape(fan * tile.shape[1], tile.shape[2])
            out[first + u] = matmul(jnp.concatenate(row, axis=1), tile).astype(HALF)
        return 0

    lax.fori_loop(0, tiles // chunk, one, 0)


def spread_tiles(core, nbr, fields, prior):
    summed = len(fields) > 1
    ext_tiles, probes, width = fields[0].shape
    tiles = ext_tiles // 2
    smem = pl.BlockSpec(memory_space=pltpu.SMEM)
    vmem = pl.BlockSpec(memory_space=pltpu.VMEM)
    return pl.pallas_call(
        functools.partial(spread_kernel, summed, nbr.shape[0] // tiles),
        in_specs=[smem, smem] + [vmem] * len(fields) + [vmem],
        out_specs=vmem,
        out_shape=jax.ShapeDtypeStruct((tiles, probes, width), HALF),
        scratch_shapes=[pltpu.VMEM(fields[0].shape, HALF)] if summed else [],
        compiler_params=pltpu.CompilerParams(vmem_limit_bytes=VMEM_LIMIT),
        name="prior_spread",
    )(core, nbr, *fields, prior)


def shards(probes, prior_tiles, neighbours, jac, jac_obs, jac_flux, counts, rinv):
    n_obs, n_flux = lax.axis_size("obs"), lax.axis_size("flux")
    tile_count = probes.shape[0]
    half = tile_count // 2
    reach = tile_count // 4
    obs_rows = rinv.shape[0]
    quarter = obs_rows // 4
    blocks = jac[0, 0]
    flux_at = lax.axis_index("flux")
    side = lax.rem(lax.axis_index("obs"), 2)
    corner = lax.rem(flux_at, 4)
    core = side.reshape(1)

    live = jnp.arange(blocks.shape[0], dtype=jnp.int32) < counts[0, 0]
    obs_all, flux_all = jac_obs[0, 0], jac_flux[0, 0]
    obs_at = ((obs_all // quarter) ^ corner) * quarter + obs_all % quarter
    tile_at = ((flux_all // half) ^ side) * half + flux_all % half
    own_rinv = lax.dynamic_slice_in_dim(rinv, corner * quarter, quarter, 0)[:, None, :]
    first_tile = flux_at * tile_count + side * half
    own_nbr = lax.dynamic_slice_in_dim(neighbours, side * half, half, 0)
    nbr = (own_nbr - first_tile + reach).reshape(-1)
    fan = neighbours.shape[1]
    prior = prior_tiles.reshape((tile_count * fan,) + prior_tiles.shape[2:])

    rows = max(obs_rows, tile_count, 2 * half)
    count = max(blocks.shape[0], prior.shape[0])
    fill = lambda value, more: jnp.pad(value, (0, count - value.shape[0]), constant_values=more)
    prior_at = jnp.arange(prior.shape[0], dtype=jnp.int32)
    own = prior_at // (half * fan) == side
    prior_src = prior_at // fan - side * half
    prior_dst = jnp.where(own, jnp.tile(nbr, 2), rows)
    plans = plan_groups(
        jnp.stack([fill(tile_at, 0), fill(obs_at, 0), fill(prior_src, 0)]),
        jnp.stack(
            [
                fill(jnp.where(live, obs_at, rows), rows),
                fill(jnp.where(live, tile_at, rows), rows),
                fill(prior_dst, rows),
            ]
        ),
        rows,
        rows,
    )
    obs_plan, tile_plan, prior_plan = plans[0], plans[1], plans[2]

    def swap_core(value):
        return exchange(value, lambda i, j: (i ^ 1, j))

    def swap_far(value):
        def partner(i, j):
            to = j - 1 if i % 2 == 0 else j + 1
            return (i ^ 1, to) if 0 <= to < n_flux else None

        return exchange(value, partner)

    def swap_flux(value, bits):
        return exchange(value, lambda i, j: (i, j ^ bits))

    edge = jnp.where(side == 0, probes[:reach], probes[tile_count - reach :])
    beyond = swap_far(edge)
    around = jnp.concatenate([beyond, probes, beyond], axis=0)
    fields = (lax.dynamic_slice_in_dim(around, side * half, 2 * half, 0),)
    for step in range(STEPS):
        spread = spread_tiles(core, nbr, fields, prior)
        parts = (spread, swap_core(spread))
        pieces = jac_pass(False, obs_plan, parts, blocks, rows, rows, obs_rows, 4, "jac_forward")
        total = pieces[0]
        for bits in range(1, 4):
            total = total + swap_flux(pieces[bits], bits).astype(F32)
        bits = 4
        while bits < n_flux:
            sent = total.astype(HALF)
            total = sent.astype(F32) + swap_flux(sent, bits).astype(F32)
            bits *= 2
        weighted = (total * own_rinv).astype(HALF)
        parts = (weighted,) + tuple(swap_flux(weighted, bits) for bits in range(1, 4))
        mine, theirs = jac_pass(True, tile_plan, parts, blocks, rows, rows, tile_count, 2, "jac_adjoint")
        mine = (mine + swap_core(theirs).astype(F32)).astype(HALF)
        bits = 2
        while bits < n_obs:
            other = exchange(mine, lambda i, j, bits=bits: (i ^ bits, j))
            bits *= 2
            if bits < n_obs:
                mine = (mine.astype(F32) + other.astype(F32)).astype(HALF)
        ext, to_core, to_far = gather_tiles(core, prior_plan, mine, other, prior, rows, rows)
        fields = (ext, swap_core(to_core), swap_far(to_far))
    ext, from_core, from_far = fields
    low = jnp.where(side == 0, from_far, from_core).astype(F32)
    high = jnp.where(side == 0, from_core, from_far).astype(F32)
    own = (ext + jnp.concatenate([low, high], axis=0))[reach : reach + half].astype(HALF)
    other = swap_core(own)
    first = jnp.where(side == 0, own, other)
    second = jnp.where(side == 0, other, own)
    return jnp.concatenate([first, second], axis=0)


def solution(mesh):
    placed = (
        P("flux", None, None),
        P("flux", None, None, None),
        P("flux", None),
        P("obs", "flux", None, None, None),
        P("obs", "flux", None),
        P("obs", "flux", None),
        P("obs", "flux"),
        P("obs", None),
    )
    return jax.shard_map(
        shards, mesh=mesh, in_specs=placed, out_specs=P("flux", None, None), check_vma=False
    )
```

time: 271 us -> 261 us (0.963)
  Pallas kernels: 104 us -> 67.1 us
  local copies, waits for them, and re-layouts: 0.17 us -> 23.5 us
  waiting for transfers between devices: 80.3 us -> 91.3 us
  starting transfers between devices: 78.7 us -> 68.5 us
  other arithmetic: 6.4 us -> 9.75 us
    pallas_call x16, Pallas kernels: 104 us -> 67.1 us  [the longest x8 42.2 us: jac_pass(): pl.pallas_call(functools.partial(jac_kernel, transposed, len(parts), n_ou...]
    unnamed x2 -> x24, local copies, waits for them, and re-layouts: 0.01 us -> 22.9 us
    ppermute x50, waiting for transfers between devices: 80.3 us -> 91.3 us  [exchange(): return lax.ppermute(value, ('obs', 'flux'), route)]
    ppermute x50, starting transfers between devices: 78.7 us -> 68.5 us  [exchange(): return lax.ppermute(value, ('obs', 'flux'), route)]
  transfers between devices with their start and end apart: 50 -> 50, of which waited for: 43 -> 44; matrix products, arithmetic and copies ran while one was open for 1% -> 3% of each run, Pallas kernels for 0% -> 0%
where the time goes in v2:
time: 261 us
  waiting for transfers between devices  91.3 us (35%)
  starting transfers between devices  68.5 us (26%)
  Pallas kernels  67.1 us (26%)
  local copies, waits for them, and re-layouts  23.5 us (9%)
  other arithmetic  9.75 us (4%)
    ppermute x50, waiting for transfers between devices, exchange(): return lax.ppermute(value, ('obs', 'flux'), route)  91.3 us
    ppermute x50, starting transfers between devices, exchange(): return lax.ppermute(value, ('obs', 'flux'), route)  68.5 us
    pallas_call x8, Pallas kernels, jac_pass(): pl.pallas_call(functools.partial(jac_kernel, transposed, len(parts), n_ou...  42.2 us
    unnamed x24, local copies, waits for them, and re-layouts  22.9 us
    pallas_call x4, Pallas kernels, gather_tiles(): pl.pallas_call(functools.partial(gather_kernel, src_rows), in_specs=[smem...  17.5 us
    pallas_call x4, Pallas kernels, spread_tiles(): pl.pallas_call(functools.partial(spread_kernel, summed, nbr.shape[0] // t...  7.46 us
  transfers between devices with their start and end apart: 50, of which 44 were waited for; matrix products, arithmetic and copies ran while one was open for 3% of the time, Pallas kernels for 0%

profile of v2, /device:TPU:0, one launch (start us, length us, event | category | flops | bytes accessed | tf_op | source)
XLA Modules:
  0.0 261.4 jit_solution(9680723328955952350)
XLA Ops:
  10.3 4.6 %copy-done.3 = bf16[48,8,128,128]{3,2,1,0:T(8,128)(2,1)S(1)} copy-done((bf16[48,8,128,128]{3,2,1,0:T(8,128)(2,1)S(1)}, bf16[48,8,128,128]{3,2,1,0:T(8,128)(2,1)}, u32[]{:S(2)}) %copy-start.3) | copy-done | bytes 12582936
  14.9 1.8 prior_spread.4.refs_0_
  16.7 4.4 %collective-permute-start.1 = (bf16[24,32,128]{2,1,0:T(8,128)(2,1)S(1)}, bf16[24,32,128]{2,1,0:T(8,128)(2,1)S(1)}, u32[]{:S(2)}, u32[]{:S(2)}) collective-permute-start(bf16[24,32,128]{2,1,0:T(8,128)(2,1)S(1)} %prior_spread.4.refs_0_), channel_id=1, source_target_pairs={{0,8},{1,9},{2,10},{3,11},{4,12},{5,13},{6,14},{7,15},{8,0},{9,1},... | collective-permute-start | bytes 589832 | tf_op jit(solution)/shard_map/ppermute | solution.py:38
  22.1 4.6 %copy-done.1 = bf16[1,1,384,128,128]{4,3,2,1,0:T(8,128)(2,1)S(1)} copy-done((bf16[1,1,384,128,128]{4,3,2,1,0:T(8,128)(2,1)S(1)}, bf16[1,1,384,128,128]{4,3,2,1,0:T(8,128)(2,1)}, u32[]{:S(2)}) %copy-start.1) | copy-done | bytes 12582936
  26.7 3.7 %jac_forward.4 = (f32[8,32,128]{2,1,0:T(8,128)S(1)}, bf16[8,32,128]{2,1,0:T(8,128)(2,1)S(1)}, bf16[8,32,128]{2,1,0:T(8,128)(2,1)S(1)}, bf16[8,32,128]{2,1,0:T(8,128)(2,1)S(1)}) custom-call(s32[1297]{0:T(1024)S(1)} %get-tuple-element.77.plan, bf16[24,32,128]{2,1,0:T(8,128)(2,1)S(1)} %prior_spread.4.refs_0_, ...), custom_call_target="tpu_custom_call" | custom-call | tf_op jit(solution)/shard_map/jac_forward/pallas_call | solution.py:108
  30.5 1.9 collective-permute-start.3
  32.4 1.6 collective-permute-start.4
  35.6 2.0 collective-permute-done.4
  37.6 2.4 collective-permute-start.5
  40.0 2.8 %collective-permute-done.5 = bf16[8,32,128]{2,1,0:T(8,128)(2,1)S(1)} collective-permute-done((bf16[8,32,128]{2,1,0:T(8,128)(2,1)S(1)}, bf16[8,32,128]{2,1,0:T(8,128)(2,1)S(1)}, u32[]{:S(2)}, u32[]{:S(2)}) %collective-permute-start.5) | collective-permute-done | bytes 65568 | tf_op jit(solution)/shard_map/ppermute | solution.py:38
  42.9 1.7 collective-permute-start.8
  44.6 2.1 collective-permute-start.7
  46.7 1.4 collective-permute-done.8.refs_3_
  48.1 1.5 collective-permute-done.7.refs_2_
  51.0 4.6 %copy-done.2 = bf16[1,1,384,128,128]{4,3,2,1,0:T(8,128)(2,1)S(1)} copy-done((bf16[1,1,384,128,128]{4,3,2,1,0:T(8,128)(2,1)S(1)}, bf16[1,1,384,128,128]{4,3,2,1,0:T(8,128)(2,1)}, u32[]{:S(2)}) %copy-start.2) | copy-done | bytes 12582936
  55.5 6.7 %jac_adjoint.4 = (f32[24,32,128]{2,1,0:T(8,128)S(1)}, bf16[24,32,128]{2,1,0:T(8,128)(2,1)S(1)}) custom-call(s32[1297]{0:T(1024)S(1)} %get-tuple-element.78.plan, bf16[8,32,128]{2,1,0:T(8,128)(2,1)S(1)} %multiply_convert_fusion.3.refs_0_, bf16[8,32,128]{2,1,0:T(8,128)(2,1)S(1)} %collective-permute-done.6.refs_1_, ...), custom_call_target="tpu_custom_call" | custom-call | tf_op jit(solution)/shard_map/jac_adjoint/pallas_call | solution.py:108
  62.3 1.4 collective-permute-done.9
  63.9 6.9 %collective-permute-done.10.other = bf16[24,32,128]{2,1,0:T(8,128)(2,1)S(1)} collective-permute-done((bf16[24,32,128]{2,1,0:T(8,128)(2,1)S(1)}, bf16[24,32,128]{2,1,0:T(8,128)(2,1)S(1)}, u32[]{:S(2)}, u32[]{:S(2)}) %collective-permute-start.10) | collective-permute-done | bytes 196640 | tf_op jit(solution)/shard_map/ppermute | solution.py:38
  70.8 4.6 %copy-done.4 = bf16[48,8,128,128]{3,2,1,0:T(8,128)(2,1)S(1)} copy-done((bf16[48,8,128,128]{3,2,1,0:T(8,128)(2,1)S(1)}, bf16[48,8,128,128]{3,2,1,0:T(8,128)(2,1)}, u32[]{:S(2)}) %copy-start.4) | copy-done | bytes 12582936
  75.4 4.4 %prior_adjoint.4 = (f32[48,32,128]{2,1,0:T(8,128)S(1)}, bf16[24,32,128]{2,1,0:T(8,128)(2,1)S(1)}, bf16[24,32,128]{2,1,0:T(8,128)(2,1)S(1)}) custom-call(s32[1]{0:T(128)} %bitcast.core, s32[1297]{0:T(1024)S(1)} %get-tuple-element.79.plan, bf16[24,32,128]{2,1,0:T(8,128)(2,1)S(1)} %add_convert_fusion.3.mine, ...), custom_call_target="tpu_custom_call" | custom-call | tf_op jit(solution)/shard_map/prior_adjoint/pallas_call | solution.py:137
  81.3 4.6 %copy-done.5 = bf16[48,8,128,128]{3,2,1,0:T(8,128)(2,1)S(1)} copy-done((bf16[48,8,128,128]{3,2,1,0:T(8,128)(2,1)S(1)}, bf16[48,8,128,128]{3,2,1,0:T(8,128)(2,1)}, u32[]{:S(2)}) %copy-start.5) | copy-done | bytes 12582936
  85.9 1.9 prior_spread.5.refs_0_
  87.8 6.6 %collective-permute-start.13 = (bf16[24,32,128]{2,1,0:T(8,128)(2,1)S(1)}, bf16[24,32,128]{2,1,0:T(8,128)(2,1)S(1)}, u32[]{:S(2)}, u32[]{:S(2)}) collective-permute-start(bf16[24,32,128]{2,1,0:T(8,128)(2,1)S(1)} %prior_spread.5.refs_0_), channel_id=1, source_target_pairs={{0,8},{1,9},{2,10},{3,11},{4,12},{5,13},{6,14},{7,15},{8,0},{9,1},... | collective-permute-start | bytes 589832 | tf_op jit(solution)/shard_map/ppermute | solution.py:38
  95.5 3.9 %jac_forward.5 = (f32[8,32,128]{2,1,0:T(8,128)S(1)}, bf16[8,32,128]{2,1,0:T(8,128)(2,1)S(1)}, bf16[8,32,128]{2,1,0:T(8,128)(2,1)S(1)}, bf16[8,32,128]{2,1,0:T(8,128)(2,1)S(1)}) custom-call(s32[1297]{0:T(1024)S(1)} %get-tuple-element.77.plan, bf16[24,32,128]{2,1,0:T(8,128)(2,1)S(1)} %prior_spread.5.refs_0_, ...), custom_call_target="tpu_custom_call" | custom-call | tf_op jit(solution)/shard_map/jac_forward/pallas_call | solution.py:108
  101.1 1.8 collective-permute-start.16
  105.1 1.5 collective-permute-done.16
  106.7 1.7 collective-permute-start.17
  108.4 4.9 %collective-permute-done.17 = bf16[8,32,128]{2,1,0:T(8,128)(2,1)S(1)} collective-permute-done((bf16[8,32,128]{2,1,0:T(8,128)(2,1)S(1)}, bf16[8,32,128]{2,1,0:T(8,128)(2,1)S(1)}, u32[]{:S(2)}, u32[]{:S(2)}) %collective-permute-start.17) | collective-permute-done | bytes 65568 | tf_op jit(solution)/shard_map/ppermute | solution.py:38
  113.5 2.1 collective-permute-start.19
  116.8 1.7 collective-permute-done.20.refs_3_
  118.6 1.3 collective-permute-done.18.refs_1_
  119.9 6.7 %jac_adjoint.5 = (f32[24,32,128]{2,1,0:T(8,128)S(1)}, bf16[24,32,128]{2,1,0:T(8,128)(2,1)S(1)}) custom-call(s32[1297]{0:T(1024)S(1)} %get-tuple-element.78.plan, bf16[8,32,128]{2,1,0:T(8,128)(2,1)S(1)} %multiply_convert_fusion.2.refs_0_, bf16[8,32,128]{2,1,0:T(8,128)(2,1)S(1)} %collective-permute-done.18.refs_1_, ...), custom_call_target="tpu_custom_call" | custom-call | tf_op jit(solution)/shard_map/jac_adjoint/pallas_call | solution.py:108
  126.7 1.4 collective-permute-done.21
  128.2 6.9 %collective-permute-done.22.other = bf16[24,32,128]{2,1,0:T(8,128)(2,1)S(1)} collective-permute-done((bf16[24,32,128]{2,1,0:T(8,128)(2,1)S(1)}, bf16[24,32,128]{2,1,0:T(8,128)(2,1)S(1)}, u32[]{:S(2)}, u32[]{:S(2)}) %collective-permute-start.22) | collective-permute-done | bytes 196640 | tf_op jit(solution)/shard_map/ppermute | solution.py:38
  135.2 4.4 %prior_adjoint.5 = (f32[48,32,128]{2,1,0:T(8,128)S(1)}, bf16[24,32,128]{2,1,0:T(8,128)(2,1)S(1)}, bf16[24,32,128]{2,1,0:T(8,128)(2,1)S(1)}) custom-call(s32[1]{0:T(128)} %bitcast.core, s32[1297]{0:T(1024)S(1)} %get-tuple-element.79.plan, bf16[24,32,128]{2,1,0:T(8,128)(2,1)S(1)} %add_convert_fusion.2.mine, ...), custom_call_target="tpu_custom_call" | custom-call | tf_op jit(solution)/shard_map/prior_adjoint/pallas_call | solution.py:137
  141.1 1.9 prior_spread.6.refs_0_
  143.0 6.6 %collective-permute-start.25 = (bf16[24,32,128]{2,1,0:T(8,128)(2,1)S(1)}, bf16[24,32,128]{2,1,0:T(8,128)(2,1)S(1)}, u32[]{:S(2)}, u32[]{:S(2)}) collective-permute-start(bf16[24,32,128]{2,1,0:T(8,128)(2,1)S(1)} %prior_spread.6.refs_0_), channel_id=1, source_target_pairs={{0,8},{1,9},{2,10},{3,11},{4,12},{5,13},{6,14},{7,15},{8,0},{9,1},... | collective-permute-start | bytes 589832 | tf_op jit(solution)/shard_map/ppermute | solution.py:38
  150.7 4.0 %jac_forward.6 = (f32[8,32,128]{2,1,0:T(8,128)S(1)}, bf16[8,32,128]{2,1,0:T(8,128)(2,1)S(1)}, bf16[8,32,128]{2,1,0:T(8,128)(2,1)S(1)}, bf16[8,32,128]{2,1,0:T(8,128)(2,1)S(1)}) custom-call(s32[1297]{0:T(1024)S(1)} %get-tuple-element.77.plan, bf16[24,32,128]{2,1,0:T(8,128)(2,1)S(1)} %prior_spread.6.refs_0_, ...), custom_call_target="tpu_custom_call" | custom-call | tf_op jit(solution)/shard_map/jac_forward/pallas_call | solution.py:108
  155.6 2.7 %collective-permute-start.27 = (bf16[8,32,128]{2,1,0:T(8,128)(2,1)S(1)}, bf16[8,32,128]{2,1,0:T(8,128)(2,1)S(1)}, u32[]{:S(2)}, u32[]{:S(2)}) collective-permute-start(bf16[8,32,128]{2,1,0:T(8,128)(2,1)S(1)} %get-tuple-element.61), channel_id=1, source_target_pairs={{0,2},{1,3},{2,0},{3,1},{4,6},{5,7},{6,4},{7,5},{8,10},{9,11},{10,... | collective-permute-start | bytes 196616 | tf_op jit(solution)/shard_map/ppermute | solution.py:38
  159.3 1.9 collective-permute-done.27
  161.2 2.3 collective-permute-done.28
  163.6 5.8 %collective-permute-done.29 = bf16[8,32,128]{2,1,0:T(8,128)(2,1)S(1)} collective-permute-done((bf16[8,32,128]{2,1,0:T(8,128)(2,1)S(1)}, bf16[8,32,128]{2,1,0:T(8,128)(2,1)S(1)}, u32[]{:S(2)}, u32[]{:S(2)}) %collective-permute-start.29) | collective-permute-done | bytes 65568 | tf_op jit(solution)/shard_map/ppermute | solution.py:38
  169.6 1.9 collective-permute-start.31
  171.6 1.4 collective-permute-start.30
  172.9 1.7 collective-permute-done.32.refs_3_
  175.9 6.7 %jac_adjoint.6 = (f32[24,32,128]{2,1,0:T(8,128)S(1)}, bf16[24,32,128]{2,1,0:T(8,128)(2,1)S(1)}) custom-call(s32[1297]{0:T(1024)S(1)} %get-tuple-element.78.plan, bf16[8,32,128]{2,1,0:T(8,128)(2,1)S(1)} %multiply_convert_fusion.1.refs_0_, bf16[8,32,128]{2,1,0:T(8,128)(2,1)S(1)} %collective-permute-done.30.refs_1_, ...), custom_call_target="tpu_custom_call" | custom-call | tf_op jit(solution)/shard_map/jac_adjoint/pallas_call | solution.py:108
  182.6 1.4 collective-permute-done.33
  184.2 6.9 %collective-permute-done.34.other = bf16[24,32,128]{2,1,0:T(8,128)(2,1)S(1)} collective-permute-done((bf16[24,32,128]{2,1,0:T(8,128)(2,1)S(1)}, bf16[24,32,128]{2,1,0:T(8,128)(2,1)S(1)}, u32[]{:S(2)}, u32[]{:S(2)}) %collective-permute-start.34) | collective-permute-done | bytes 196640 | tf_op jit(solution)/shard_map/ppermute | solution.py:38
  191.1 4.4 %prior_adjoint.6 = (f32[48,32,128]{2,1,0:T(8,128)S(1)}, bf16[24,32,128]{2,1,0:T(8,128)(2,1)S(1)}, bf16[24,32,128]{2,1,0:T(8,128)(2,1)S(1)}) custom-call(s32[1]{0:T(128)} %bitcast.core, s32[1297]{0:T(1024)S(1)} %get-tuple-element.79.plan, bf16[24,32,128]{2,1,0:T(8,128)(2,1)S(1)} %add_convert_fusion.1.mine, ...), custom_call_target="tpu_custom_call" | custom-call | tf_op jit(solution)/shard_map/prior_adjoint/pallas_call | solution.py:137
  197.0 1.9 prior_spread.7.refs_0_
  198.9 7.9 %collective-permute-start.37 = (bf16[24,32,128]{2,1,0:T(8,128)(2,1)S(1)}, bf16[24,32,128]{2,1,0:T(8,128)(2,1)S(1)}, u32[]{:S(2)}, u32[]{:S(2)}) collective-permute-start(bf16[24,32,128]{2,1,0:T(8,128)(2,1)S(1)} %prior_spread.7.refs_0_), channel_id=1, source_target_pairs={{0,8},{1,9},{2,10},{3,11},{4,12},{5,13},{6,14},{7,15},{8,0},{9,1},... | collective-permute-start | bytes 589832 | tf_op jit(solution)/shard_map/ppermute | solution.py:38
  207.8 3.9 %jac_forward.7 = (f32[8,32,128]{2,1,0:T(8,128)S(1)}, bf16[8,32,128]{2,1,0:T(8,128)(2,1)S(1)}, bf16[8,32,128]{2,1,0:T(8,128)(2,1)S(1)}, bf16[8,32,128]{2,1,0:T(8,128)(2,1)S(1)}) custom-call(s32[1297]{0:T(1024)S(1)} %get-tuple-element.77.plan, bf16[24,32,128]{2,1,0:T(8,128)(2,1)S(1)} %prior_spread.7.refs_0_, ...), custom_call_target="tpu_custom_call" | custom-call | tf_op jit(solution)/shard_map/jac_forward/pallas_call | solution.py:108
  213.4 1.8 collective-permute-start.40
  217.4 1.5 collective-permute-done.40
  219.1 6.5 %collective-permute-done.41 = bf16[8,32,128]{2,1,0:T(8,128)(2,1)S(1)} collective-permute-done((bf16[8,32,128]{2,1,0:T(8,128)(2,1)S(1)}, bf16[8,32,128]{2,1,0:T(8,128)(2,1)S(1)}, u32[]{:S(2)}, u32[]{:S(2)}) %collective-permute-start.41) | collective-permute-done | bytes 65568 | tf_op jit(solution)/shard_map/ppermute | solution.py:38
  225.9 2.1 collective-permute-start.43
  229.1 1.7 collective-permute-done.44.refs_3_
  230.9 1.3 collective-permute-done.42.refs_1_
  232.2 6.7 %jac_adjoint.7 = (f32[24,32,128]{2,1,0:T(8,128)S(1)}, bf16[24,32,128]{2,1,0:T(8,128)(2,1)S(1)}) custom-call(s32[1297]{0:T(1024)S(1)} %get-tuple-element.78.plan, bf16[8,32,128]{2,1,0:T(8,128)(2,1)S(1)} %multiply_convert_fusion.refs_0_, bf16[8,32,128]{2,1,0:T(8,128)(2,1)S(1)} %collective-permute-done.42.refs_1_, ...), custom_call_target="tpu_custom_call" | custom-call | tf_op jit(solution)/shard_map/jac_adjoint/pallas_call | solution.py:108
  239.0 1.4 collective-permute-done.45
  240.5 6.9 %collective-permute-done.46.other = bf16[24,32,128]{2,1,0:T(8,128)(2,1)S(1)} collective-permute-done((bf16[24,32,128]{2,1,0:T(8,128)(2,1)S(1)}, bf16[24,32,128]{2,1,0:T(8,128)(2,1)S(1)}, u32[]{:S(2)}, u32[]{:S(2)}) %collective-permute-start.46) | collective-permute-done | bytes 196640 | tf_op jit(solution)/shard_map/ppermute | solution.py:38
  247.5 4.4 %prior_adjoint.7 = (f32[48,32,128]{2,1,0:T(8,128)S(1)}, bf16[24,32,128]{2,1,0:T(8,128)(2,1)S(1)}, bf16[24,32,128]{2,1,0:T(8,128)(2,1)S(1)}) custom-call(s32[1]{0:T(128)} %bitcast.core, s32[1297]{0:T(1024)S(1)} %get-tuple-element.79.plan, bf16[24,32,128]{2,1,0:T(8,128)(2,1)S(1)} %add_convert_fusion.mine, ...), custom_call_target="tpu_custom_call" | custom-call | tf_op jit(solution)/shard_map/prior_adjoint/pallas_call | solution.py:137
  252.5 2.2 collective-permute-start.48
  255.9 3.6 %collective-permute-start.49 = (bf16[24,32,128]{2,1,0:T(8,128)(2,1)S(1)}, bf16[24,32,128]{2,1,0:T(8,128)(2,1)S(1)}, u32[]{:S(2)}, u32[]{:S(2)}) collective-permute-start(bf16[24,32,128]{2,1,0:T(8,128)(2,1)S(1)} %fusion.2), channel_id=1, source_target_pairs={{0,8},{1,9},{2,10},{3,11},{4,12},{5,13},{6,14},{7,15},{8,0},{9,1},... | collective-permute-start | bytes 589832 | tf_op jit(solution)/shard_map/ppermute | solution.py:38
  (129 shorter events, 40.4 us)
Async XLA Ops:
  0.0 40.0 %copy-start = (f32[32,128]{1,0:T(8,128)S(1)}, f32[32,128]{1,0:T(8,128)}, u32[]{:S(2)}) copy-start(f32[32,128]{1,0:T(8,128)} %param.15) | copy-start | bytes 49156
  1.0 8.1 %collective-permute-start = (bf16[12,32,128]{2,1,0:T(8,128)(2,1)S(1)}, bf16[12,32,128]{2,1,0:T(8,128)(2,1)S(1)}, u32[]{:S(2)}, u32[]{:S(2)}) collective-permute-start(bf16[12,32,128]{2,1,0:T(8,128)(2,1)S(1)} %slice_select_fusion), channel_id=1, source_target_pairs={{1,8},{2,9},{3,10},{4,11},{5,12},{6,13},{7,14},{8,1},{9,2},{10,3},... | collective-permute-start | bytes 294920 | tf_op jit(solution)/shard_map/ppermute | solution.py:38
  10.3 4.6 %copy-start.3 = (bf16[48,8,128,128]{3,2,1,0:T(8,128)(2,1)S(1)}, bf16[48,8,128,128]{3,2,1,0:T(8,128)(2,1)}, u32[]{:S(2)}) copy-start(bf16[48,8,128,128]{3,2,1,0:T(8,128)(2,1)} %param.9) | copy-start | bytes 37748740
  16.7 5.5 %collective-permute-start.1 = (bf16[24,32,128]{2,1,0:T(8,128)(2,1)S(1)}, bf16[24,32,128]{2,1,0:T(8,128)(2,1)S(1)}, u32[]{:S(2)}, u32[]{:S(2)}) collective-permute-start(bf16[24,32,128]{2,1,0:T(8,128)(2,1)S(1)} %prior_spread.4.refs_0_), channel_id=1, source_target_pairs={{0,8},{1,9},{2,10},{3,11},{4,12},{5,13},{6,14},{7,15},{8,0},{9,1},... | collective-permute-start | bytes 589832 | tf_op jit(solution)/shard_map/ppermute | solution.py:38
  22.1 4.6 %copy-start.1 = (bf16[1,1,384,128,128]{4,3,2,1,0:T(8,128)(2,1)S(1)}, bf16[1,1,384,128,128]{4,3,2,1,0:T(8,128)(2,1)}, u32[]{:S(2)}) copy-start(bf16[1,1,384,128,128]{4,3,2,1,0:T(8,128)(2,1)} %param.11) | copy-start | bytes 37748740
  30.4 4.3 %collective-permute-start.2 = (bf16[8,32,128]{2,1,0:T(8,128)(2,1)S(1)}, bf16[8,32,128]{2,1,0:T(8,128)(2,1)S(1)}, u32[]{:S(2)}, u32[]{:S(2)}) collective-permute-start(bf16[8,32,128]{2,1,0:T(8,128)(2,1)S(1)} %get-tuple-element.42), channel_id=1, source_target_pairs={{0,1},{1,0},{2,3},{3,2},{4,5},{5,4},{6,7},{7,6},{8,9},{9,8},{10,11... | collective-permute-start | bytes 196616 | tf_op jit(solution)/shard_map/ppermute | solution.py:38
  30.5 5.0 %collective-permute-start.3 = (bf16[8,32,128]{2,1,0:T(8,128)(2,1)S(1)}, bf16[8,32,128]{2,1,0:T(8,128)(2,1)S(1)}, u32[]{:S(2)}, u32[]{:S(2)}) collective-permute-start(bf16[8,32,128]{2,1,0:T(8,128)(2,1)S(1)} %get-tuple-element.43), channel_id=1, source_target_pairs={{0,2},{1,3},{2,0},{3,1},{4,6},{5,7},{6,4},{7,5},{8,10},{9,11},{10,... | collective-permute-start | bytes 196616 | tf_op jit(solution)/shard_map/ppermute | solution.py:38
  32.4 5.2 %collective-permute-start.4 = (bf16[8,32,128]{2,1,0:T(8,128)(2,1)S(1)}, bf16[8,32,128]{2,1,0:T(8,128)(2,1)S(1)}, u32[]{:S(2)}, u32[]{:S(2)}) collective-permute-start(bf16[8,32,128]{2,1,0:T(8,128)(2,1)S(1)} %get-tuple-element.44), channel_id=1, source_target_pairs={{0,3},{1,2},{2,1},{3,0},{4,7},{5,6},{6,5},{7,4},{8,11},{9,10},{10,... | collective-permute-start | bytes 196616 | tf_op jit(solution)/shard_map/ppermute | solution.py:38
  37.6 5.2 %collective-permute-start.5 = (bf16[8,32,128]{2,1,0:T(8,128)(2,1)S(1)}, bf16[8,32,128]{2,1,0:T(8,128)(2,1)S(1)}, u32[]{:S(2)}, u32[]{:S(2)}) collective-permute-start(bf16[8,32,128]{2,1,0:T(8,128)(2,1)S(1)} %add_convert_fusion.7), channel_id=1, source_target_pairs={{0,4},{1,5},{2,6},{3,7},{4,0},{5,1},{6,2},{7,3},{8,12},{9,13},{10,... | collective-permute-start | bytes 196616 | tf_op jit(solution)/shard_map/ppermute | solution.py:38
  42.9 5.3 %collective-permute-start.8 = (bf16[8,32,128]{2,1,0:T(8,128)(2,1)S(1)}, bf16[8,32,128]{2,1,0:T(8,128)(2,1)S(1)}, u32[]{:S(2)}, u32[]{:S(2)}) collective-permute-start(bf16[8,32,128]{2,1,0:T(8,128)(2,1)S(1)} %multiply_convert_fusion.3.refs_0_), channel_id=1, source_target_pairs={{0,3},{1,2},{2,1},{3,0},{4,7},{5,6},{6,5},{7,4},{8,11},{9,10},{10,... | collective-permute-start | bytes 196616 | tf_op jit(solution)/shard_map/ppermute | solution.py:38
  44.6 5.0 %collective-permute-start.7 = (bf16[8,32,128]{2,1,0:T(8,128)(2,1)S(1)}, bf16[8,32,128]{2,1,0:T(8,128)(2,1)S(1)}, u32[]{:S(2)}, u32[]{:S(2)}) collective-permute-start(bf16[8,32,128]{2,1,0:T(8,128)(2,1)S(1)} %multiply_convert_fusion.3.refs_0_), channel_id=1, source_target_pairs={{0,2},{1,3},{2,0},{3,1},{4,6},{5,7},{6,4},{7,5},{8,10},{9,11},{10,... | collective-permute-start | bytes 196616 | tf_op jit(solution)/shard_map/ppermute | solution.py:38
  46.7 4.3 %collective-permute-start.6 = (bf16[8,32,128]{2,1,0:T(8,128)(2,1)S(1)}, bf16[8,32,128]{2,1,0:T(8,128)(2,1)S(1)}, u32[]{:S(2)}, u32[]{:S(2)}) collective-permute-start(bf16[8,32,128]{2,1,0:T(8,128)(2,1)S(1)} %multiply_convert_fusion.3.refs_0_), channel_id=1, source_target_pairs={{0,1},{1,0},{2,3},{3,2},{4,5},{5,4},{6,7},{7,6},{8,9},{9,8},{10,11... | collective-permute-start | bytes 196616 | tf_op jit(solution)/shard_map/ppermute | solution.py:38
  51.0 4.6 %copy-start.2 = (bf16[1,1,384,128,128]{4,3,2,1,0:T(8,128)(2,1)S(1)}, bf16[1,1,384,128,128]{4,3,2,1,0:T(8,128)(2,1)}, u32[]{:S(2)}) copy-start(bf16[1,1,384,128,128]{4,3,2,1,0:T(8,128)(2,1)} %param.11) | copy-start | bytes 37748740
  62.2 1.5 collective-permute-start.9
  63.8 7.0 %collective-permute-start.10 = (bf16[24,32,128]{2,1,0:T(8,128)(2,1)S(1)}, bf16[24,32,128]{2,1,0:T(8,128)(2,1)S(1)}, u32[]{:S(2)}, u32[]{:S(2)}) collective-permute-start(bf16[24,32,128]{2,1,0:T(8,128)(2,1)S(1)} %add_convert_fusion.3.mine), channel_id=1, source_target_pairs={{0,16},{1,17},{2,18},{3,19},{4,20},{5,21},{6,22},{7,23},{8,24},{9,... | collective-permute-start | bytes 589832 | tf_op jit(solution)/shard_map/ppermute | solution.py:38
  70.8 4.6 %copy-start.4 = (bf16[48,8,128,128]{3,2,1,0:T(8,128)(2,1)S(1)}, bf16[48,8,128,128]{3,2,1,0:T(8,128)(2,1)}, u32[]{:S(2)}) copy-start(bf16[48,8,128,128]{3,2,1,0:T(8,128)(2,1)} %param.9) | copy-start | bytes 37748740
  75.4 20.1 %slice-start = ((s8[12582912]{0:T(1024)(128)(4,1)}), s8[4194304]{0:T(1024)(128)(4,1)S(1)}, s32[]{:S(2)}) async-start(s8[12582912]{0:T(1024)(128)(4,1)} %bitcast.52), calls=%async_computation | async-start | bytes 8388608
  75.4 20.1 %slice-start.1 = ((s8[12582912]{0:T(1024)(128)(4,1)}), s8[4194304]{0:T(1024)(128)(4,1)S(1)}, s32[]{:S(2)}) async-start(s8[12582912]{0:T(1024)(128)(4,1)} %bitcast.52), calls=%async_computation.1 | async-start | bytes 8388608
  79.8 1.5 collective-permute-start.11
  79.9 1.4 collective-permute-start.12
  81.3 4.6 %copy-start.5 = (bf16[48,8,128,128]{3,2,1,0:T(8,128)(2,1)S(1)}, bf16[48,8,128,128]{3,2,1,0:T(8,128)(2,1)}, u32[]{:S(2)}) copy-start(bf16[48,8,128,128]{3,2,1,0:T(8,128)(2,1)} %param.9) | copy-start | bytes 37748740
  85.9 9.6 %slice-start.2 = ((s8[12582912]{0:T(1024)(128)(4,1)}), s8[4194304]{0:T(1024)(128)(4,1)S(1)}, s32[]{:S(2)}) async-start(s8[12582912]{0:T(1024)(128)(4,1)} %bitcast.52), calls=%async_computation.2 | async-start | bytes 8388608
  87.8 7.7 %collective-permute-start.13 = (bf16[24,32,128]{2,1,0:T(8,128)(2,1)S(1)}, bf16[24,32,128]{2,1,0:T(8,128)(2,1)S(1)}, u32[]{:S(2)}, u32[]{:S(2)}) collective-permute-start(bf16[24,32,128]{2,1,0:T(8,128)(2,1)S(1)} %prior_spread.5.refs_0_), channel_id=1, source_target_pairs={{0,8},{1,9},{2,10},{3,11},{4,12},{5,13},{6,14},{7,15},{8,0},{9,1},... | collective-permute-start | bytes 589832 | tf_op jit(solution)/shard_map/ppermute | solution.py:38
  95.5 39.7 %slice-start.3 = ((s8[12582912]{0:T(1024)(128)(4,1)}), s8[4194304]{0:T(1024)(128)(4,1)S(1)}, s32[]{:S(2)}) async-start(s8[12582912]{0:T(1024)(128)(4,1)} %bitcast.63), calls=%async_computation.3 | async-start | bytes 8388608
  95.5 39.7 %slice-start.4 = ((s8[12582912]{0:T(1024)(128)(4,1)}), s8[4194304]{0:T(1024)(128)(4,1)S(1)}, s32[]{:S(2)}) async-start(s8[12582912]{0:T(1024)(128)(4,1)} %bitcast.63), calls=%async_computation.4 | async-start | bytes 8388608
  99.4 4.6 %collective-permute-start.14 = (bf16[8,32,128]{2,1,0:T(8,128)(2,1)S(1)}, bf16[8,32,128]{2,1,0:T(8,128)(2,1)S(1)}, u32[]{:S(2)}, u32[]{:S(2)}) collective-permute-start(bf16[8,32,128]{2,1,0:T(8,128)(2,1)S(1)} %get-tuple-element.51), channel_id=1, source_target_pairs={{0,1},{1,0},{2,3},{3,2},{4,5},{5,4},{6,7},{7,6},{8,9},{9,8},{10,11... | collective-permute-start | bytes 196616 | tf_op jit(solution)/shard_map/ppermute | solution.py:38
  100.3 4.8 %collective-permute-start.15 = (bf16[8,32,128]{2,1,0:T(8,128)(2,1)S(1)}, bf16[8,32,128]{2,1,0:T(8,128)(2,1)S(1)}, u32[]{:S(2)}, u32[]{:S(2)}) collective-permute-start(bf16[8,32,128]{2,1,0:T(8,128)(2,1)S(1)} %get-tuple-element.52), channel_id=1, source_target_pairs={{0,2},{1,3},{2,0},{3,1},{4,6},{5,7},{6,4},{7,5},{8,10},{9,11},{10,... | collective-permute-start | bytes 196616 | tf_op jit(solution)/shard_map/ppermute | solution.py:38
  101.1 5.5 %collective-permute-start.16 = (bf16[8,32,128]{2,1,0:T(8,128)(2,1)S(1)}, bf16[8,32,128]{2,1,0:T(8,128)(2,1)S(1)}, u32[]{:S(2)}, u32[]{:S(2)}) collective-permute-start(bf16[8,32,128]{2,1,0:T(8,128)(2,1)S(1)} %get-tuple-element.53), channel_id=1, source_target_pairs={{0,3},{1,2},{2,1},{3,0},{4,7},{5,6},{6,5},{7,4},{8,11},{9,10},{10,... | collective-permute-start | bytes 196616 | tf_op jit(solution)/shard_map/ppermute | solution.py:38
  106.7 6.6 %collective-permute-start.17 = (bf16[8,32,128]{2,1,0:T(8,128)(2,1)S(1)}, bf16[8,32,128]{2,1,0:T(8,128)(2,1)S(1)}, u32[]{:S(2)}, u32[]{:S(2)}) collective-permute-start(bf16[8,32,128]{2,1,0:T(8,128)(2,1)S(1)} %add_convert_fusion.6), channel_id=1, source_target_pairs={{0,4},{1,5},{2,6},{3,7},{4,0},{5,1},{6,2},{7,3},{8,12},{9,13},{10,... | collective-permute-start | bytes 196616 | tf_op jit(solution)/shard_map/ppermute | solution.py:38
  113.3 21.9 %slice-start.5 = ((s8[12582912]{0:T(1024)(128)(4,1)}), s8[4194304]{0:T(1024)(128)(4,1)S(1)}, s32[]{:S(2)}) async-start(s8[12582912]{0:T(1024)(128)(4,1)} %bitcast.63), calls=%async_computation.5 | async-start | bytes 8388608
  113.3 5.2 %collective-permute-start.20 = (bf16[8,32,128]{2,1,0:T(8,128)(2,1)S(1)}, bf16[8,32,128]{2,1,0:T(8,128)(2,1)S(1)}, u32[]{:S(2)}, u32[]{:S(2)}) collective-permute-start(bf16[8,32,128]{2,1,0:T(8,128)(2,1)S(1)} %multiply_convert_fusion.2.refs_0_), channel_id=1, source_target_pairs={{0,3},{1,2},{2,1},{3,0},{4,7},{5,6},{6,5},{7,4},{8,11},{9,10},{10,... | collective-permute-start | bytes 196616 | tf_op jit(solution)/shard_map/ppermute | solution.py:38
  113.5 5.0 %collective-permute-start.19 = (bf16[8,32,128]{2,1,0:T(8,128)(2,1)S(1)}, bf16[8,32,128]{2,1,0:T(8,128)(2,1)S(1)}, u32[]{:S(2)}, u32[]{:S(2)}) collective-permute-start(bf16[8,32,128]{2,1,0:T(8,128)(2,1)S(1)} %multiply_convert_fusion.2.refs_0_), channel_id=1, source_target_pairs={{0,2},{1,3},{2,0},{3,1},{4,6},{5,7},{6,4},{7,5},{8,10},{9,11},{10,... | collective-permute-start | bytes 196616 | tf_op jit(solution)/shard_map/ppermute | solution.py:38
  115.6 4.3 %collective-permute-start.18 = (bf16[8,32,128]{2,1,0:T(8,128)(2,1)S(1)}, bf16[8,32,128]{2,1,0:T(8,128)(2,1)S(1)}, u32[]{:S(2)}, u32[]{:S(2)}) collective-permute-start(bf16[8,32,128]{2,1,0:T(8,128)(2,1)S(1)} %multiply_convert_fusion.2.refs_0_), channel_id=1, source_target_pairs={{0,1},{1,0},{2,3},{3,2},{4,5},{5,4},{6,7},{7,6},{8,9},{9,8},{10,11... | collective-permute-start | bytes 196616 | tf_op jit(solution)/shard_map/ppermute | solution.py:38
  126.6 1.5 collective-permute-start.21
  128.2 7.0 %collective-permute-start.22 = (bf16[24,32,128]{2,1,0:T(8,128)(2,1)S(1)}, bf16[24,32,128]{2,1,0:T(8,128)(2,1)S(1)}, u32[]{:S(2)}, u32[]{:S(2)}) collective-permute-start(bf16[24,32,128]{2,1,0:T(8,128)(2,1)S(1)} %add_convert_fusion.2.mine), channel_id=1, source_target_pairs={{0,16},{1,17},{2,18},{3,19},{4,20},{5,21},{6,22},{7,23},{8,24},{9,... | collective-permute-start | bytes 589832 | tf_op jit(solution)/shard_map/ppermute | solution.py:38
  139.6 1.5 collective-permute-start.23
  139.6 1.4 collective-permute-start.24
  143.0 7.7 %collective-permute-start.25 = (bf16[24,32,128]{2,1,0:T(8,128)(2,1)S(1)}, bf16[24,32,128]{2,1,0:T(8,128)(2,1)S(1)}, u32[]{:S(2)}, u32[]{:S(2)}) collective-permute-start(bf16[24,32,128]{2,1,0:T(8,128)(2,1)S(1)} %prior_spread.6.refs_0_), channel_id=1, source_target_pairs={{0,8},{1,9},{2,10},{3,11},{4,12},{5,13},{6,14},{7,15},{8,0},{9,1},... | collective-permute-start | bytes 589832 | tf_op jit(solution)/shard_map/ppermute | solution.py:38
  154.7 4.6 %collective-permute-start.26 = (bf16[8,32,128]{2,1,0:T(8,128)(2,1)S(1)}, bf16[8,32,128]{2,1,0:T(8,128)(2,1)S(1)}, u32[]{:S(2)}, u32[]{:S(2)}) collective-permute-start(bf16[8,32,128]{2,1,0:T(8,128)(2,1)S(1)} %get-tuple-element.60), channel_id=1, source_target_pairs={{0,1},{1,0},{2,3},{3,2},{4,5},{5,4},{6,7},{7,6},{8,9},{9,8},{10,11... | collective-permute-start | bytes 196616 | tf_op jit(solution)/shard_map/ppermute | solution.py:38
  155.6 5.5 %collective-permute-start.27 = (bf16[8,32,128]{2,1,0:T(8,128)(2,1)S(1)}, bf16[8,32,128]{2,1,0:T(8,128)(2,1)S(1)}, u32[]{:S(2)}, u32[]{:S(2)}) collective-permute-start(bf16[8,32,128]{2,1,0:T(8,128)(2,1)S(1)} %get-tuple-element.61), channel_id=1, source_target_pairs={{0,2},{1,3},{2,0},{3,1},{4,6},{5,7},{6,4},{7,5},{8,10},{9,11},{10,... | collective-permute-start | bytes 196616 | tf_op jit(solution)/shard_map/ppermute | solution.py:38
  158.3 5.2 %collective-permute-start.28 = (bf16[8,32,128]{2,1,0:T(8,128)(2,1)S(1)}, bf16[8,32,128]{2,1,0:T(8,128)(2,1)S(1)}, u32[]{:S(2)}, u32[]{:S(2)}) collective-permute-start(bf16[8,32,128]{2,1,0:T(8,128)(2,1)S(1)} %get-tuple-element.62), channel_id=1, source_target_pairs={{0,3},{1,2},{2,1},{3,0},{4,7},{5,6},{6,5},{7,4},{8,11},{9,10},{10,... | collective-permute-start | bytes 196616 | tf_op jit(solution)/shard_map/ppermute | solution.py:38
  163.5 5.9 %collective-permute-start.29 = (bf16[8,32,128]{2,1,0:T(8,128)(2,1)S(1)}, bf16[8,32,128]{2,1,0:T(8,128)(2,1)S(1)}, u32[]{:S(2)}, u32[]{:S(2)}) collective-permute-start(bf16[8,32,128]{2,1,0:T(8,128)(2,1)S(1)} %add_convert_fusion.5), channel_id=1, source_target_pairs={{0,4},{1,5},{2,6},{3,7},{4,0},{5,1},{6,2},{7,3},{8,12},{9,13},{10,... | collective-permute-start | bytes 196616 | tf_op jit(solution)/shard_map/ppermute | solution.py:38
  169.4 5.2 %collective-permute-start.32 = (bf16[8,32,128]{2,1,0:T(8,128)(2,1)S(1)}, bf16[8,32,128]{2,1,0:T(8,128)(2,1)S(1)}, u32[]{:S(2)}, u32[]{:S(2)}) collective-permute-start(bf16[8,32,128]{2,1,0:T(8,128)(2,1)S(1)} %multiply_convert_fusion.1.refs_0_), channel_id=1, source_target_pairs={{0,3},{1,2},{2,1},{3,0},{4,7},{5,6},{6,5},{7,4},{8,11},{9,10},{10,... | collective-permute-start | bytes 196616 | tf_op jit(solution)/shard_map/ppermute | solution.py:38
  169.6 5.0 %collective-permute-start.31 = (bf16[8,32,128]{2,1,0:T(8,128)(2,1)S(1)}, bf16[8,32,128]{2,1,0:T(8,128)(2,1)S(1)}, u32[]{:S(2)}, u32[]{:S(2)}) collective-permute-start(bf16[8,32,128]{2,1,0:T(8,128)(2,1)S(1)} %multiply_convert_fusion.1.refs_0_), channel_id=1, source_target_pairs={{0,2},{1,3},{2,0},{3,1},{4,6},{5,7},{6,4},{7,5},{8,10},{9,11},{10,... | collective-permute-start | bytes 196616 | tf_op jit(solution)/shard_map/ppermute | solution.py:38
  171.6 4.3 %collective-permute-start.30 = (bf16[8,32,128]{2,1,0:T(8,128)(2,1)S(1)}, bf16[8,32,128]{2,1,0:T(8,128)(2,1)S(1)}, u32[]{:S(2)}, u32[]{:S(2)}) collective-permute-start(bf16[8,32,128]{2,1,0:T(8,128)(2,1)S(1)} %multiply_convert_fusion.1.refs_0_), channel_id=1, source_target_pairs={{0,1},{1,0},{2,3},{3,2},{4,5},{5,4},{6,7},{7,6},{8,9},{9,8},{10,11... | collective-permute-start | bytes 196616 | tf_op jit(solution)/shard_map/ppermute | solution.py:38
  182.5 1.5 collective-permute-start.33
  184.1 7.0 %collective-permute-start.34 = (bf16[24,32,128]{2,1,0:T(8,128)(2,1)S(1)}, bf16[24,32,128]{2,1,0:T(8,128)(2,1)S(1)}, u32[]{:S(2)}, u32[]{:S(2)}) collective-permute-start(bf16[24,32,128]{2,1,0:T(8,128)(2,1)S(1)} %add_convert_fusion.1.mine), channel_id=1, source_target_pairs={{0,16},{1,17},{2,18},{3,19},{4,20},{5,21},{6,22},{7,23},{8,24},{9,... | collective-permute-start | bytes 589832 | tf_op jit(solution)/shard_map/ppermute | solution.py:38
  195.5 1.5 collective-permute-start.35
  195.6 1.4 collective-permute-start.36
  198.9 8.9 %collective-permute-start.37 = (bf16[24,32,128]{2,1,0:T(8,128)(2,1)S(1)}, bf16[24,32,128]{2,1,0:T(8,128)(2,1)S(1)}, u32[]{:S(2)}, u32[]{:S(2)}) collective-permute-start(bf16[24,32,128]{2,1,0:T(8,128)(2,1)S(1)} %prior_spread.7.refs_0_), channel_id=1, source_target_pairs={{0,8},{1,9},{2,10},{3,11},{4,12},{5,13},{6,14},{7,15},{8,0},{9,1},... | collective-permute-start | bytes 589832 | tf_op jit(solution)/shard_map/ppermute | solution.py:38
  211.7 4.6 %collective-permute-start.38 = (bf16[8,32,128]{2,1,0:T(8,128)(2,1)S(1)}, bf16[8,32,128]{2,1,0:T(8,128)(2,1)S(1)}, u32[]{:S(2)}, u32[]{:S(2)}) collective-permute-start(bf16[8,32,128]{2,1,0:T(8,128)(2,1)S(1)} %get-tuple-element.69), channel_id=1, source_target_pairs={{0,1},{1,0},{2,3},{3,2},{4,5},{5,4},{6,7},{7,6},{8,9},{9,8},{10,11... | collective-permute-start | bytes 196616 | tf_op jit(solution)/shard_map/ppermute | solution.py:38
  212.6 4.8 %collective-permute-start.39 = (bf16[8,32,128]{2,1,0:T(8,128)(2,1)S(1)}, bf16[8,32,128]{2,1,0:T(8,128)(2,1)S(1)}, u32[]{:S(2)}, u32[]{:S(2)}) collective-permute-start(bf16[8,32,128]{2,1,0:T(8,128)(2,1)S(1)} %get-tuple-element.70), channel_id=1, source_target_pairs={{0,2},{1,3},{2,0},{3,1},{4,6},{5,7},{6,4},{7,5},{8,10},{9,11},{10,... | collective-permute-start | bytes 196616 | tf_op jit(solution)/shard_map/ppermute | solution.py:38
  213.4 5.5 %collective-permute-start.40 = (bf16[8,32,128]{2,1,0:T(8,128)(2,1)S(1)}, bf16[8,32,128]{2,1,0:T(8,128)(2,1)S(1)}, u32[]{:S(2)}, u32[]{:S(2)}) collective-permute-start(bf16[8,32,128]{2,1,0:T(8,128)(2,1)S(1)} %get-tuple-element.71), channel_id=1, source_target_pairs={{0,3},{1,2},{2,1},{3,0},{4,7},{5,6},{6,5},{7,4},{8,11},{9,10},{10,... | collective-permute-start | bytes 196616 | tf_op jit(solution)/shard_map/ppermute | solution.py:38
  219.0 6.5 %collective-permute-start.41 = (bf16[8,32,128]{2,1,0:T(8,128)(2,1)S(1)}, bf16[8,32,128]{2,1,0:T(8,128)(2,1)S(1)}, u32[]{:S(2)}, u32[]{:S(2)}) collective-permute-start(bf16[8,32,128]{2,1,0:T(8,128)(2,1)S(1)} %add_convert_fusion.4), channel_id=1, source_target_pairs={{0,4},{1,5},{2,6},{3,7},{4,0},{5,1},{6,2},{7,3},{8,12},{9,13},{10,... | collective-permute-start | bytes 196616 | tf_op jit(solution)/shard_map/ppermute | solution.py:38
  225.5 5.2 %collective-permute-start.44 = (bf16[8,32,128]{2,1,0:T(8,128)(2,1)S(1)}, bf16[8,32,128]{2,1,0:T(8,128)(2,1)S(1)}, u32[]{:S(2)}, u32[]{:S(2)}) collective-permute-start(bf16[8,32,128]{2,1,0:T(8,128)(2,1)S(1)} %multiply_convert_fusion.refs_0_), channel_id=1, source_target_pairs={{0,3},{1,2},{2,1},{3,0},{4,7},{5,6},{6,5},{7,4},{8,11},{9,10},{10,... | collective-permute-start | bytes 196616 | tf_op jit(solution)/shard_map/ppermute | solution.py:38
  225.9 5.0 %collective-permute-start.43 = (bf16[8,32,128]{2,1,0:T(8,128)(2,1)S(1)}, bf16[8,32,128]{2,1,0:T(8,128)(2,1)S(1)}, u32[]{:S(2)}, u32[]{:S(2)}) collective-permute-start(bf16[8,32,128]{2,1,0:T(8,128)(2,1)S(1)} %multiply_convert_fusion.refs_0_), channel_id=1, source_target_pairs={{0,2},{1,3},{2,0},{3,1},{4,6},{5,7},{6,4},{7,5},{8,10},{9,11},{10,... | collective-permute-start | bytes 196616 | tf_op jit(solution)/shard_map/ppermute | solution.py:38
  228.0 4.3 %collective-permute-start.42 = (bf16[8,32,128]{2,1,0:T(8,128)(2,1)S(1)}, bf16[8,32,128]{2,1,0:T(8,128)(2,1)S(1)}, u32[]{:S(2)}, u32[]{:S(2)}) collective-permute-start(bf16[8,32,128]{2,1,0:T(8,128)(2,1)S(1)} %multiply_convert_fusion.refs_0_), channel_id=1, source_target_pairs={{0,1},{1,0},{2,3},{3,2},{4,5},{5,4},{6,7},{7,6},{8,9},{9,8},{10,11... | collective-permute-start | bytes 196616 | tf_op jit(solution)/shard_map/ppermute | solution.py:38
  238.9 1.5 collective-permute-start.45
  240.5 7.0 %collective-permute-start.46 = (bf16[24,32,128]{2,1,0:T(8,128)(2,1)S(1)}, bf16[24,32,128]{2,1,0:T(8,128)(2,1)S(1)}, u32[]{:S(2)}, u32[]{:S(2)}) collective-permute-start(bf16[24,32,128]{2,1,0:T(8,128)(2,1)S(1)} %add_convert_fusion.mine), channel_id=1, source_target_pairs={{0,16},{1,17},{2,18},{3,19},{4,20},{5,21},{6,22},{7,23},{8,24},{9,... | collective-permute-start | bytes 589832 | tf_op jit(solution)/shard_map/ppermute | solution.py:38
  251.8 2.9 %collective-permute-start.47 = (bf16[24,32,128]{2,1,0:T(8,128)(2,1)S(1)}, bf16[24,32,128]{2,1,0:T(8,128)(2,1)S(1)}, u32[]{:S(2)}, u32[]{:S(2)}) collective-permute-start(bf16[24,32,128]{2,1,0:T(8,128)(2,1)S(1)} %get-tuple-element.75), channel_id=1, source_target_pairs={{1,8},{2,9},{3,10},{4,11},{5,12},{6,13},{7,14},{8,1},{9,2},{10,3},... | collective-permute-start | bytes 589832 | tf_op jit(solution)/shard_map/ppermute | solution.py:38
  252.5 3.3 %collective-permute-start.48 = (bf16[24,32,128]{2,1,0:T(8,128)(2,1)S(1)}, bf16[24,32,128]{2,1,0:T(8,128)(2,1)S(1)}, u32[]{:S(2)}, u32[]{:S(2)}) collective-permute-start(bf16[24,32,128]{2,1,0:T(8,128)(2,1)S(1)} %get-tuple-element.76), channel_id=1, source_target_pairs={{0,8},{1,9},{2,10},{3,11},{4,12},{5,13},{6,14},{7,15},{8,0},{9,1},... | collective-permute-start | bytes 589832 | tf_op jit(solution)/shard_map/ppermute | solution.py:38
  255.9 4.7 %collective-permute-start.49 = (bf16[24,32,128]{2,1,0:T(8,128)(2,1)S(1)}, bf16[24,32,128]{2,1,0:T(8,128)(2,1)S(1)}, u32[]{:S(2)}, u32[]{:S(2)}) collective-permute-start(bf16[24,32,128]{2,1,0:T(8,128)(2,1)S(1)} %fusion.2), channel_id=1, source_target_pairs={{0,8},{1,9},{2,10},{3,11},{4,12},{5,13},{6,14},{7,15},{8,0},{9,1},... | collective-permute-start | bytes 589832 | tf_op jit(solution)/shard_map/ppermute | solution.py:38

commit v3 on v2

--- a/solution.py
+++ b/solution.py
@@ -17,10 +17,6 @@
 
 def matmul(a, b):
     return lax.dot_general(a, b, (((1,), (0,)), ((), ())), preferred_element_type=F32)
-
-
-def matmul_t(a, b):
-    return lax.dot_general(a, b, (((1,), (1,)), ((), ())), preferred_element_type=F32)
 
 
 def chunk_of(count, most):
@@ -62,7 +58,44 @@
     return jnp.concatenate([src_of, block_of, dst_of, rounds], axis=1)
 
 
-def grouped_products(transposed, plan, x, blocks, total):
+def setup_kernel(chunk, first, source, plain, turned, sems):
+    begin = first[0]
+
+    def copy(c):
+        at = pl.ds(c * chunk, chunk)
+        rows = pl.ds(begin + c * chunk, chunk)
+        return pltpu.make_async_copy(source.at[rows], plain.at[at], sems.at[c])
+
+    def start(c, _):
+        copy(c).start()
+        return 0
+
+    def turn(c, _):
+        copy(c).wait()
+        for u in range(chunk):
+            turned[c * chunk + u] = plain[c * chunk + u].T
+        return 0
+
+    lax.fori_loop(0, plain.shape[0] // chunk, start, 0)
+    lax.fori_loop(0, plain.shape[0] // chunk, turn, 0)
+
+
+def setup_blocks(first, count, source, name):
+    shape = (count,) + source.shape[1:]
+    chunk = chunk_of(count, 24)
+    vmem = pl.BlockSpec(memory_space=pltpu.VMEM)
+    return pl.pallas_call(
+        functools.partial(setup_kernel, chunk),
+        in_specs=[pl.BlockSpec(memory_space=pltpu.SMEM), pl.BlockSpec(memory_space=pl.ANY)],
+        out_specs=[vmem, vmem],
+        out_shape=[pltpu.VMEM(shape, HALF), pltpu.VMEM(shape, HALF)],
+        scratch_shapes=[pltpu.SemaphoreType.DMA((count // chunk,))],
+        compiler_params=pltpu.CompilerParams(vmem_limit_bytes=VMEM_LIMIT),
+        name=name,
+    )(first, pltpu.with_memory_space_constraint(source, pltpu.HBM))
+
+
+def grouped_products(plan, x, blocks, total):
     slots = (plan.shape[0] - 1) // (2 * GROUP + 1) * GROUP
     total[...] = jnp.zeros_like(total)
 
@@ -73,10 +106,7 @@
             rows = [x[plan[first + g]] for g in range(GROUP)]
             tiles = [blocks[plan[slots + first + g]] for g in range(GROUP)]
             left = jnp.concatenate(rows, axis=1)
-            if transposed:
-                products.append(matmul_t(left, jnp.concatenate(tiles, axis=1)))
-            else:
-                products.append(matmul(left, jnp.concatenate(tiles, axis=0)))
+            products.append(matmul(left, jnp.concatenate(tiles, axis=0)))
         for u in range(ROUND):
             total[plan[2 * slots + c * ROUND + u]] += products[u]
         return 0
@@ -84,7 +114,7 @@
     lax.fori_loop(0, plan[plan.shape[0] - 1], one, 0)
 
 
-def jac_kernel(transposed, n_parts, n_outs, plan, *refs):
+def jac_kernel(n_parts, n_outs, plan, *refs):
     parts = refs[:n_parts]
     jac = refs[n_parts]
     outs = refs[n_parts + 1 : n_parts + 1 + n_outs]
@@ -94,19 +124,19 @@
         x[k * rows : (k + 1) * rows] = part[...]
     for r in range(n_parts * rows, x.shape[0]):
         x[r] = jnp.zeros(x.shape[1:], HALF)
-    grouped_products(transposed, plan, x, jac, total)
+    grouped_products(plan, x, jac, total)
     rows = outs[0].shape[0]
     for k, out in enumerate(outs):
         out[...] = total[k * rows : (k + 1) * rows].astype(out.dtype)
 
 
-def jac_pass(transposed, plan, parts, jac, src_rows, dst_rows, out_rows, n_outs, name):
+def jac_pass(plan, parts, jac, src_rows, dst_rows, out_rows, n_outs, name):
     probes, width = parts[0].shape[1:]
     smem = pl.BlockSpec(memory_space=pltpu.SMEM)
     vmem = pl.BlockSpec(memory_space=pltpu.VMEM)
     out = (out_rows // n_outs, probes, width)
     return pl.pallas_call(
-        functools.partial(jac_kernel, transposed, len(parts), n_outs),
+        functools.partial(jac_kernel, len(parts), n_outs),
         in_specs=[smem] + [vmem] * len(parts) + [vmem],
         out_specs=[vmem] * n_outs,
         out_shape=[jax.ShapeDtypeStruct(out, F32 if k == 0 else HALF) for k in range(n_outs)],
@@ -124,7 +154,7 @@
     side = core[0]
     x[:half] = (mine[...].astype(F32) + other[...].astype(F32)).astype(HALF)
     x[src_rows] = jnp.zeros(x.shape[1:], HALF)
-    grouped_products(True, plan, x, prior, total)
+    grouped_products(plan, x, prior, total)
     ext[...] = total[: 2 * half]
     to_core[...] = total[pl.ds(half * (1 - side), half)].astype(HALF)
     to_far[...] = total[pl.ds(half * side, half)].astype(HALF)
@@ -169,7 +199,7 @@
         first = c * chunk
         for u in range(chunk):
             row = [field[nbr[(first + u) * fan + k]] for k in range(fan)]
-            tile = prior[pl.ds((side * tiles + first + u) * fan, fan)]
+            tile = prior[pl.ds((first + u) * fan, fan)]
             tile = tile.reshape(fan * tile.shape[1], tile.shape[2])
             out[first + u] = matmul(jnp.concatenate(row, axis=1), tile).astype(HALF)
         return 0
@@ -218,20 +248,23 @@
     fan = neighbours.shape[1]
     prior = prior_tiles.reshape((tile_count * fan,) + prior_tiles.shape[2:])
 
-    rows = max(obs_rows, tile_count, 2 * half)
-    count = max(blocks.shape[0], prior.shape[0])
-    fill = lambda value, more: jnp.pad(value, (0, count - value.shape[0]), constant_values=more)
-    prior_at = jnp.arange(prior.shape[0], dtype=jnp.int32)
-    own = prior_at // (half * fan) == side
-    prior_src = prior_at // fan - side * half
-    prior_dst = jnp.where(own, jnp.tile(nbr, 2), rows)
+    prior_plain, prior_turned = setup_blocks(core * (half * fan), half * fan, prior, "prior_setup")
+    jac_plain, jac_turned = setup_blocks(jnp.zeros((1,), jnp.int32), blocks.shape[0], blocks, "jac_setup")
+
+    rows = max(obs_rows, tile_count)
+    count = max(blocks.shape[0], half * fan)
+
+    def fill(value, more):
+        return jnp.pad(value, (0, count - value.shape[0]), constant_values=more)
+
+    prior_src = jnp.arange(half * fan, dtype=jnp.int32) // fan
     plans = plan_groups(
         jnp.stack([fill(tile_at, 0), fill(obs_at, 0), fill(prior_src, 0)]),
         jnp.stack(
             [
                 fill(jnp.where(live, obs_at, rows), rows),
                 fill(jnp.where(live, tile_at, rows), rows),
-                fill(prior_dst, rows),
+                fill(nbr, rows),
             ]
         ),
         rows,
@@ -257,9 +290,9 @@
     around = jnp.concatenate([beyond, probes, beyond], axis=0)
     fields = (lax.dynamic_slice_in_dim(around, side * half, 2 * half, 0),)
     for step in range(STEPS):
-        spread = spread_tiles(core, nbr, fields, prior)
+        spread = spread_tiles(core, nbr, fields, prior_plain)
         parts = (spread, swap_core(spread))
-        pieces = jac_pass(False, obs_plan, parts, blocks, rows, rows, obs_rows, 4, "jac_forward")
+        pieces = jac_pass(obs_plan, parts, jac_plain, rows, rows, obs_rows, 4, "jac_forward")
         total = pieces[0]
         for bits in range(1, 4):
             total = total + swap_flux(pieces[bits], bits).astype(F32)
@@ -270,7 +303,7 @@
             bits *= 2
         weighted = (total * own_rinv).astype(HALF)
         parts = (weighted,) + tuple(swap_flux(weighted, bits) for bits in range(1, 4))
-        mine, theirs = jac_pass(True, tile_plan, parts, blocks, rows, rows, tile_count, 2, "jac_adjoint")
+        mine, theirs = jac_pass(tile_plan, parts, jac_turned, rows, rows, tile_count, 2, "jac_adjoint")
         mine = (mine + swap_core(theirs).astype(F32)).astype(HALF)
         bits = 2
         while bits < n_obs:
@@ -278,7 +311,7 @@
             bits *= 2
             if bits < n_obs:
                 mine = (mine.astype(F32) + other.astype(F32)).astype(HALF)
-        ext, to_core, to_far = gather_tiles(core, prior_plan, mine, other, prior, rows, rows)
+        ext, to_core, to_far = gather_tiles(core, prior_plan, mine, other, prior_turned, rows, rows)
         fields = (ext, swap_core(to_core), swap_far(to_far))
     ext, from_core, from_far = fields
     low = jnp.where(side == 0, from_far, from_core).astype(F32)

time: 261 us -> 253 us (0.969)
  Pallas kernels: 67.1 us -> 52 us
  starting transfers between devices: 68.5 us -> 76.1 us
  waiting for transfers between devices: 91.3 us -> 86 us
  local copies, waits for them, and re-layouts: 23.5 us -> 27.6 us
    pallas_call x8 -> x10, Pallas kernels: 42.2 us -> 34.1 us  [the longest x8 25.3 us: jac_pass(): pl.pallas_call(functools.partial(jac_kernel, len(parts), n_outs), in_spec...]
    ppermute x50, starting transfers between devices: 68.5 us -> 76.1 us  [exchange(): return lax.ppermute(value, ('obs', 'flux'), route)]
    pallas_call x4, Pallas kernels: 17.5 us -> 10.4 us  [gather_tiles(): pl.pallas_call(functools.partial(gather_kernel, src_rows), in_specs=[smem...]
    ppermute x50, waiting for transfers between devices: 91.3 us -> 86 us  [exchange(): return lax.ppermute(value, ('obs', 'flux'), route)]
    unnamed x24 -> x42, local copies, waits for them, and re-layouts: 22.9 us -> 27.1 us
  transfers between devices with their start and end apart: 50 -> 50, of which waited for: 44 -> 44; matrix products, arithmetic and copies ran while one was open for 3% -> 3% of each run, Pallas kernels for 0% -> 3%
where the time goes in v3:
time: 253 us; the launch traced here: 252 us
  waiting for transfers between devices  86 us (34%)
  starting transfers between devices  76.1 us (30%)
  Pallas kernels  52 us (21%)
  local copies, waits for them, and re-layouts  27.6 us (11%)
  other arithmetic  8.82 us (3%)
    ppermute x50, waiting for transfers between devices, exchange(): return lax.ppermute(value, ('obs', 'flux'), route)  86 us
    ppermute x50, starting transfers between devices, exchange(): return lax.ppermute(value, ('obs', 'flux'), route)  76.1 us
    unnamed x42, local copies, waits for them, and re-layouts  27.1 us
    pallas_call x8, Pallas kernels, jac_pass(): pl.pallas_call(functools.partial(jac_kernel, len(parts), n_outs), in_spec...  25.3 us
    pallas_call x4, Pallas kernels, gather_tiles(): pl.pallas_call(functools.partial(gather_kernel, src_rows), in_specs=[smem...  10.4 us
    pallas_call x2, Pallas kernels, setup_blocks(): pl.pallas_call(functools.partial(setup_kernel, chunk), in_specs=[pl.Block...  8.73 us
    pallas_call x4, Pallas kernels, spread_tiles(): pl.pallas_call(functools.partial(spread_kernel, summed, nbr.shape[0] // t...  7.48 us
  transfers between devices with their start and end apart: 50, of which 44 were waited for; matrix products, arithmetic and copies ran while one was open for 3% of the time, Pallas kernels for 3%

profile of v3, /device:TPU:0, one launch (start us, length us, event | category | flops | bytes accessed | tf_op | source)
XLA Modules:
  0.0 251.8 jit_solution(11900082162439057553)
XLA Ops:
  9.0 3.3 %prior_setup.1 = (bf16[192,128,128]{2,1,0:T(8,128)(2,1)S(1)}, bf16[192,128,128]{2,1,0:T(8,128)(2,1)S(1)}) custom-call(s32[1]{0:T(128)S(6)} %mul.116.first, bf16[384,128,128]{2,1,0:T(8,128)(2,1)} %bitcast.58), custom_call_target="tpu_custom_call" | custom-call | tf_op jit(solution)/shard_map/prior_setup/pallas_call | solution.py:87
  12.3 2.7 %copy-done.6 = bf16[192,128,128]{2,1,0:T(8,128)(2,1)} copy-done((bf16[192,128,128]{2,1,0:T(8,128)(2,1)}, bf16[192,128,128]{2,1,0:T(8,128)(2,1)S(1)}, u32[]{:S(2)}) %copy-start.6) | copy-done | bytes 6291480
  15.3 1.8 prior_spread.4.refs_0_
  17.7 4.3 %collective-permute-start.1 = (bf16[24,32,128]{2,1,0:T(8,128)(2,1)S(1)}, bf16[24,32,128]{2,1,0:T(8,128)(2,1)S(1)}, u32[]{:S(2)}, u32[]{:S(2)}) collective-permute-start(bf16[24,32,128]{2,1,0:T(8,128)(2,1)S(1)} %prior_spread.4.refs_0_), channel_id=1, source_target_pairs={{0,8},{1,9},{2,10},{3,11},{4,12},{5,13},{6,14},{7,15},{8,0},{9,1},... | collective-permute-start | bytes 589832 | tf_op jit(solution)/shard_map/ppermute | solution.py:34
  22.1 5.4 %jac_setup.1 = (bf16[384,128,128]{2,1,0:T(8,128)(2,1)S(1)}, bf16[384,128,128]{2,1,0:T(8,128)(2,1)S(1)}) custom-call(s32[1]{0:T(128)} %constant.116.clone.1.first, bf16[384,128,128]{2,1,0:T(8,128)(2,1)} %bitcast.59), custom_call_target="tpu_custom_call" | custom-call | tf_op jit(solution)/shard_map/jac_setup/pallas_call | solution.py:87
  27.5 4.5 %copy-done.2 = bf16[384,128,128]{2,1,0:T(8,128)(2,1)} copy-done((bf16[384,128,128]{2,1,0:T(8,128)(2,1)}, bf16[384,128,128]{2,1,0:T(8,128)(2,1)S(1)}, u32[]{:S(2)}) %copy-start.2) | copy-done | bytes 12582936
  32.0 4.6 %copy-done.4 = bf16[384,128,128]{2,1,0:T(8,128)(2,1)} copy-done((bf16[384,128,128]{2,1,0:T(8,128)(2,1)}, bf16[384,128,128]{2,1,0:T(8,128)(2,1)S(1)}, u32[]{:S(2)}) %copy-start.4) | copy-done | bytes 12582936
  36.8 4.6 %copy-done.5 = bf16[384,128,128]{2,1,0:T(8,128)(2,1)S(1)} copy-done((bf16[384,128,128]{2,1,0:T(8,128)(2,1)S(1)}, bf16[384,128,128]{2,1,0:T(8,128)(2,1)}, u32[]{:S(2)}) %copy-start.5) | copy-done | bytes 12582936
  41.3 3.1 %jac_forward.4 = (f32[8,32,128]{2,1,0:T(8,128)S(1)}, bf16[8,32,128]{2,1,0:T(8,128)(2,1)S(1)}, bf16[8,32,128]{2,1,0:T(8,128)(2,1)S(1)}, bf16[8,32,128]{2,1,0:T(8,128)(2,1)S(1)}) custom-call(s32[1297]{0:T(1024)S(1)} %get-tuple-element.85.plan, bf16[24,32,128]{2,1,0:T(8,128)(2,1)S(1)} %prior_spread.4.refs_0_, ...), custom_call_target="tpu_custom_call" | custom-call | tf_op jit(solution)/shard_map/jac_forward/pallas_call | solution.py:138
  45.5 2.8 %collective-permute-start.3 = (bf16[8,32,128]{2,1,0:T(8,128)(2,1)S(1)}, bf16[8,32,128]{2,1,0:T(8,128)(2,1)S(1)}, u32[]{:S(2)}, u32[]{:S(2)}) collective-permute-start(bf16[8,32,128]{2,1,0:T(8,128)(2,1)S(1)} %get-tuple-element.49), channel_id=1, source_target_pairs={{0,2},{1,3},{2,0},{3,1},{4,6},{5,7},{6,4},{7,5},{8,10},{9,11},{10,... | collective-permute-start | bytes 196616 | tf_op jit(solution)/shard_map/ppermute | solution.py:34
  48.8 2.0 collective-permute-done.3
  50.8 2.6 %collective-permute-done.4 = bf16[8,32,128]{2,1,0:T(8,128)(2,1)S(1)} collective-permute-done((bf16[8,32,128]{2,1,0:T(8,128)(2,1)S(1)}, bf16[8,32,128]{2,1,0:T(8,128)(2,1)S(1)}, u32[]{:S(2)}, u32[]{:S(2)}) %collective-permute-start.4) | collective-permute-done | bytes 65568 | tf_op jit(solution)/shard_map/ppermute | solution.py:34
  54.7 4.2 %collective-permute-done.5 = bf16[8,32,128]{2,1,0:T(8,128)(2,1)S(1)} collective-permute-done((bf16[8,32,128]{2,1,0:T(8,128)(2,1)S(1)}, bf16[8,32,128]{2,1,0:T(8,128)(2,1)S(1)}, u32[]{:S(2)}, u32[]{:S(2)}) %collective-permute-start.5) | collective-permute-done | bytes 65568 | tf_op jit(solution)/shard_map/ppermute | solution.py:34
  59.6 1.6 collective-permute-start.7
  62.4 1.7 collective-permute-done.8.refs_3_
  65.5 4.6 %copy-done.3 = bf16[384,128,128]{2,1,0:T(8,128)(2,1)S(1)} copy-done((bf16[384,128,128]{2,1,0:T(8,128)(2,1)S(1)}, bf16[384,128,128]{2,1,0:T(8,128)(2,1)}, u32[]{:S(2)}) %copy-start.3) | copy-done | bytes 12582936
  70.1 3.2 %jac_adjoint.4 = (f32[24,32,128]{2,1,0:T(8,128)S(1)}, bf16[24,32,128]{2,1,0:T(8,128)(2,1)S(1)}) custom-call(s32[1297]{0:T(1024)S(1)} %get-tuple-element.86.plan, bf16[8,32,128]{2,1,0:T(8,128)(2,1)S(1)} %multiply_convert_fusion.3.refs_0_, bf16[8,32,128]{2,1,0:T(8,128)(2,1)S(1)} %collective-permute-done.6.refs_1_, ...), custom_call_target="tpu_custom_call" | custom-call | tf_op jit(solution)/shard_map/jac_adjoint/pallas_call | solution.py:138
  75.0 6.8 %collective-permute-done.10.other = bf16[24,32,128]{2,1,0:T(8,128)(2,1)S(1)} collective-permute-done((bf16[24,32,128]{2,1,0:T(8,128)(2,1)S(1)}, bf16[24,32,128]{2,1,0:T(8,128)(2,1)S(1)}, u32[]{:S(2)}, u32[]{:S(2)}) %collective-permute-start.10) | collective-permute-done | bytes 196640 | tf_op jit(solution)/shard_map/ppermute | solution.py:34
  81.8 2.8 %copy-done.7 = bf16[192,128,128]{2,1,0:T(8,128)(2,1)S(1)} copy-done((bf16[192,128,128]{2,1,0:T(8,128)(2,1)S(1)}, bf16[192,128,128]{2,1,0:T(8,128)(2,1)}, u32[]{:S(2)}) %copy-start.7) | copy-done | bytes 6291480
  84.6 2.6 %prior_adjoint.4 = (f32[48,32,128]{2,1,0:T(8,128)S(1)}, bf16[24,32,128]{2,1,0:T(8,128)(2,1)S(1)}, bf16[24,32,128]{2,1,0:T(8,128)(2,1)S(1)}) custom-call(s32[1]{0:T(128)} %bitcast.core, s32[1297]{0:T(1024)S(1)} %get-tuple-element.87.plan, bf16[24,32,128]{2,1,0:T(8,128)(2,1)S(1)} %add_convert_fusion.3.mine, ...), custom_call_target="tpu_custom_call" | custom-call | tf_op jit(solution)/shard_map/prior_adjoint/pallas_call | solution.py:167
  88.7 2.8 %copy-done.9 = bf16[192,128,128]{2,1,0:T(8,128)(2,1)S(1)} copy-done((bf16[192,128,128]{2,1,0:T(8,128)(2,1)S(1)}, bf16[192,128,128]{2,1,0:T(8,128)(2,1)}, u32[]{:S(2)}) %copy-start.9) | copy-done | bytes 6291480
  91.5 1.9 prior_spread.5.refs_0_
  93.4 6.1 %collective-permute-start.13 = (bf16[24,32,128]{2,1,0:T(8,128)(2,1)S(1)}, bf16[24,32,128]{2,1,0:T(8,128)(2,1)S(1)}, u32[]{:S(2)}, u32[]{:S(2)}) collective-permute-start(bf16[24,32,128]{2,1,0:T(8,128)(2,1)S(1)} %prior_spread.5.refs_0_), channel_id=1, source_target_pairs={{0,8},{1,9},{2,10},{3,11},{4,12},{5,13},{6,14},{7,15},{8,0},{9,1},... | collective-permute-start | bytes 589832 | tf_op jit(solution)/shard_map/ppermute | solution.py:34
  100.6 3.1 %jac_forward.5 = (f32[8,32,128]{2,1,0:T(8,128)S(1)}, bf16[8,32,128]{2,1,0:T(8,128)(2,1)S(1)}, bf16[8,32,128]{2,1,0:T(8,128)(2,1)S(1)}, bf16[8,32,128]{2,1,0:T(8,128)(2,1)S(1)}) custom-call(s32[1297]{0:T(1024)S(1)} %get-tuple-element.85.plan, bf16[24,32,128]{2,1,0:T(8,128)(2,1)S(1)} %prior_spread.5.refs_0_, ...), custom_call_target="tpu_custom_call" | custom-call | tf_op jit(solution)/shard_map/jac_forward/pallas_call | solution.py:138
  103.7 2.0 collective-permute-start.14
  105.8 2.4 collective-permute-start.15
  108.8 1.7 collective-permute-done.15
  110.4 2.9 %collective-permute-done.16 = bf16[8,32,128]{2,1,0:T(8,128)(2,1)S(1)} collective-permute-done((bf16[8,32,128]{2,1,0:T(8,128)(2,1)S(1)}, bf16[8,32,128]{2,1,0:T(8,128)(2,1)S(1)}, u32[]{:S(2)}, u32[]{:S(2)}) %collective-permute-start.16) | collective-permute-done | bytes 65568 | tf_op jit(solution)/shard_map/ppermute | solution.py:34
  113.4 2.7 %collective-permute-start.17 = (bf16[8,32,128]{2,1,0:T(8,128)(2,1)S(1)}, bf16[8,32,128]{2,1,0:T(8,128)(2,1)S(1)}, u32[]{:S(2)}, u32[]{:S(2)}) collective-permute-start(bf16[8,32,128]{2,1,0:T(8,128)(2,1)S(1)} %add_convert_fusion.6), channel_id=1, source_target_pairs={{0,4},{1,5},{2,6},{3,7},{4,0},{5,1},{6,2},{7,3},{8,12},{9,13},{10,... | collective-permute-start | bytes 196616 | tf_op jit(solution)/shard_map/ppermute | solution.py:34
  116.1 3.2 %collective-permute-done.17 = bf16[8,32,128]{2,1,0:T(8,128)(2,1)S(1)} collective-permute-done((bf16[8,32,128]{2,1,0:T(8,128)(2,1)S(1)}, bf16[8,32,128]{2,1,0:T(8,128)(2,1)S(1)}, u32[]{:S(2)}, u32[]{:S(2)}) %collective-permute-start.17) | collective-permute-done | bytes 65568 | tf_op jit(solution)/shard_map/ppermute | solution.py:34
  120.8 2.1 collective-permute-start.18
  122.9 1.7 collective-permute-done.20.refs_3_
  125.3 3.2 %jac_adjoint.5 = (f32[24,32,128]{2,1,0:T(8,128)S(1)}, bf16[24,32,128]{2,1,0:T(8,128)(2,1)S(1)}) custom-call(s32[1297]{0:T(1024)S(1)} %get-tuple-element.86.plan, bf16[8,32,128]{2,1,0:T(8,128)(2,1)S(1)} %multiply_convert_fusion.2.refs_0_, bf16[8,32,128]{2,1,0:T(8,128)(2,1)S(1)} %collective-permute-done.18.refs_1_, ...), custom_call_target="tpu_custom_call" | custom-call | tf_op jit(solution)/shard_map/jac_adjoint/pallas_call | solution.py:138
  130.1 6.9 %collective-permute-done.22.other = bf16[24,32,128]{2,1,0:T(8,128)(2,1)S(1)} collective-permute-done((bf16[24,32,128]{2,1,0:T(8,128)(2,1)S(1)}, bf16[24,32,128]{2,1,0:T(8,128)(2,1)S(1)}, u32[]{:S(2)}, u32[]{:S(2)}) %collective-permute-start.22) | collective-permute-done | bytes 196640 | tf_op jit(solution)/shard_map/ppermute | solution.py:34
  137.0 2.6 %prior_adjoint.5 = (f32[48,32,128]{2,1,0:T(8,128)S(1)}, bf16[24,32,128]{2,1,0:T(8,128)(2,1)S(1)}, bf16[24,32,128]{2,1,0:T(8,128)(2,1)S(1)}) custom-call(s32[1]{0:T(128)} %bitcast.core, s32[1297]{0:T(1024)S(1)} %get-tuple-element.87.plan, bf16[24,32,128]{2,1,0:T(8,128)(2,1)S(1)} %add_convert_fusion.2.mine, ...), custom_call_target="tpu_custom_call" | custom-call | tf_op jit(solution)/shard_map/prior_adjoint/pallas_call | solution.py:167
  141.2 1.9 prior_spread.6.refs_0_
  143.1 6.6 %collective-permute-start.25 = (bf16[24,32,128]{2,1,0:T(8,128)(2,1)S(1)}, bf16[24,32,128]{2,1,0:T(8,128)(2,1)S(1)}, u32[]{:S(2)}, u32[]{:S(2)}) collective-permute-start(bf16[24,32,128]{2,1,0:T(8,128)(2,1)S(1)} %prior_spread.6.refs_0_), channel_id=1, source_target_pairs={{0,8},{1,9},{2,10},{3,11},{4,12},{5,13},{6,14},{7,15},{8,0},{9,1},... | collective-permute-start | bytes 589832 | tf_op jit(solution)/shard_map/ppermute | solution.py:34
  150.8 3.3 %jac_forward.6 = (f32[8,32,128]{2,1,0:T(8,128)S(1)}, bf16[8,32,128]{2,1,0:T(8,128)(2,1)S(1)}, bf16[8,32,128]{2,1,0:T(8,128)(2,1)S(1)}, bf16[8,32,128]{2,1,0:T(8,128)(2,1)S(1)}) custom-call(s32[1297]{0:T(1024)S(1)} %get-tuple-element.85.plan, bf16[24,32,128]{2,1,0:T(8,128)(2,1)S(1)} %prior_spread.6.refs_0_, ...), custom_call_target="tpu_custom_call" | custom-call | tf_op jit(solution)/shard_map/jac_forward/pallas_call | solution.py:138
  154.1 2.2 collective-permute-start.26
  156.3 2.4 collective-permute-start.27
  159.2 1.9 collective-permute-done.27
  161.1 2.8 %collective-permute-done.28 = bf16[8,32,128]{2,1,0:T(8,128)(2,1)S(1)} collective-permute-done((bf16[8,32,128]{2,1,0:T(8,128)(2,1)S(1)}, bf16[8,32,128]{2,1,0:T(8,128)(2,1)S(1)}, u32[]{:S(2)}, u32[]{:S(2)}) %collective-permute-start.28) | collective-permute-done | bytes 65568 | tf_op jit(solution)/shard_map/ppermute | solution.py:34
  163.9 3.2 %collective-permute-start.29 = (bf16[8,32,128]{2,1,0:T(8,128)(2,1)S(1)}, bf16[8,32,128]{2,1,0:T(8,128)(2,1)S(1)}, u32[]{:S(2)}, u32[]{:S(2)}) collective-permute-start(bf16[8,32,128]{2,1,0:T(8,128)(2,1)S(1)} %add_convert_fusion.5), channel_id=1, source_target_pairs={{0,4},{1,5},{2,6},{3,7},{4,0},{5,1},{6,2},{7,3},{8,12},{9,13},{10,... | collective-permute-start | bytes 196616 | tf_op jit(solution)/shard_map/ppermute | solution.py:34
  167.2 2.3 collective-permute-done.29
  170.9 2.2 collective-permute-start.31
  177.4 3.2 %jac_adjoint.6 = (f32[24,32,128]{2,1,0:T(8,128)S(1)}, bf16[24,32,128]{2,1,0:T(8,128)(2,1)S(1)}) custom-call(s32[1297]{0:T(1024)S(1)} %get-tuple-element.86.plan, bf16[8,32,128]{2,1,0:T(8,128)(2,1)S(1)} %multiply_convert_fusion.1.refs_0_, bf16[8,32,128]{2,1,0:T(8,128)(2,1)S(1)} %collective-permute-done.30.refs_1_, ...), custom_call_target="tpu_custom_call" | custom-call | tf_op jit(solution)/shard_map/jac_adjoint/pallas_call | solution.py:138
  182.2 6.9 %collective-permute-done.34.other = bf16[24,32,128]{2,1,0:T(8,128)(2,1)S(1)} collective-permute-done((bf16[24,32,128]{2,1,0:T(8,128)(2,1)S(1)}, bf16[24,32,128]{2,1,0:T(8,128)(2,1)S(1)}, u32[]{:S(2)}, u32[]{:S(2)}) %collective-permute-start.34) | collective-permute-done | bytes 196640 | tf_op jit(solution)/shard_map/ppermute | solution.py:34
  189.1 2.6 %prior_adjoint.6 = (f32[48,32,128]{2,1,0:T(8,128)S(1)}, bf16[24,32,128]{2,1,0:T(8,128)(2,1)S(1)}, bf16[24,32,128]{2,1,0:T(8,128)(2,1)S(1)}) custom-call(s32[1]{0:T(128)} %bitcast.core, s32[1297]{0:T(1024)S(1)} %get-tuple-element.87.plan, bf16[24,32,128]{2,1,0:T(8,128)(2,1)S(1)} %add_convert_fusion.1.mine, ...), custom_call_target="tpu_custom_call" | custom-call | tf_op jit(solution)/shard_map/prior_adjoint/pallas_call | solution.py:167
  193.3 1.9 prior_spread.7.refs_0_
  195.2 6.1 %collective-permute-start.37 = (bf16[24,32,128]{2,1,0:T(8,128)(2,1)S(1)}, bf16[24,32,128]{2,1,0:T(8,128)(2,1)S(1)}, u32[]{:S(2)}, u32[]{:S(2)}) collective-permute-start(bf16[24,32,128]{2,1,0:T(8,128)(2,1)S(1)} %prior_spread.7.refs_0_), channel_id=1, source_target_pairs={{0,8},{1,9},{2,10},{3,11},{4,12},{5,13},{6,14},{7,15},{8,0},{9,1},... | collective-permute-start | bytes 589832 | tf_op jit(solution)/shard_map/ppermute | solution.py:34
  202.4 3.1 %jac_forward.7 = (f32[8,32,128]{2,1,0:T(8,128)S(1)}, bf16[8,32,128]{2,1,0:T(8,128)(2,1)S(1)}, bf16[8,32,128]{2,1,0:T(8,128)(2,1)S(1)}, bf16[8,32,128]{2,1,0:T(8,128)(2,1)S(1)}) custom-call(s32[1297]{0:T(1024)S(1)} %get-tuple-element.85.plan, bf16[24,32,128]{2,1,0:T(8,128)(2,1)S(1)} %prior_spread.7.refs_0_, ...), custom_call_target="tpu_custom_call" | custom-call | tf_op jit(solution)/shard_map/jac_forward/pallas_call | solution.py:138
  205.5 1.8 collective-permute-start.38
  207.3 2.4 collective-permute-start.39
  210.3 1.7 collective-permute-done.39
  212.0 2.9 %collective-permute-done.40 = bf16[8,32,128]{2,1,0:T(8,128)(2,1)S(1)} collective-permute-done((bf16[8,32,128]{2,1,0:T(8,128)(2,1)S(1)}, bf16[8,32,128]{2,1,0:T(8,128)(2,1)S(1)}, u32[]{:S(2)}, u32[]{:S(2)}) %collective-permute-start.40) | collective-permute-done | bytes 65568 | tf_op jit(solution)/shard_map/ppermute | solution.py:34
  215.0 3.5 %collective-permute-start.41 = (bf16[8,32,128]{2,1,0:T(8,128)(2,1)S(1)}, bf16[8,32,128]{2,1,0:T(8,128)(2,1)S(1)}, u32[]{:S(2)}, u32[]{:S(2)}) collective-permute-start(bf16[8,32,128]{2,1,0:T(8,128)(2,1)S(1)} %add_convert_fusion.4), channel_id=1, source_target_pairs={{0,4},{1,5},{2,6},{3,7},{4,0},{5,1},{6,2},{7,3},{8,12},{9,13},{10,... | collective-permute-start | bytes 196616 | tf_op jit(solution)/shard_map/ppermute | solution.py:34
  218.5 2.9 %collective-permute-done.41 = bf16[8,32,128]{2,1,0:T(8,128)(2,1)S(1)} collective-permute-done((bf16[8,32,128]{2,1,0:T(8,128)(2,1)S(1)}, bf16[8,32,128]{2,1,0:T(8,128)(2,1)S(1)}, u32[]{:S(2)}, u32[]{:S(2)}) %collective-permute-start.41) | collective-permute-done | bytes 65568 | tf_op jit(solution)/shard_map/ppermute | solution.py:34
  223.1 2.0 collective-permute-start.42
  225.0 1.7 collective-permute-done.44.refs_3_
  227.4 3.2 %jac_adjoint.7 = (f32[24,32,128]{2,1,0:T(8,128)S(1)}, bf16[24,32,128]{2,1,0:T(8,128)(2,1)S(1)}) custom-call(s32[1297]{0:T(1024)S(1)} %get-tuple-element.86.plan, bf16[8,32,128]{2,1,0:T(8,128)(2,1)S(1)} %multiply_convert_fusion.refs_0_, bf16[8,32,128]{2,1,0:T(8,128)(2,1)S(1)} %collective-permute-done.42.refs_1_, ...), custom_call_target="tpu_custom_call" | custom-call | tf_op jit(solution)/shard_map/jac_adjoint/pallas_call | solution.py:138
  232.2 6.9 %collective-permute-done.46.other = bf16[24,32,128]{2,1,0:T(8,128)(2,1)S(1)} collective-permute-done((bf16[24,32,128]{2,1,0:T(8,128)(2,1)S(1)}, bf16[24,32,128]{2,1,0:T(8,128)(2,1)S(1)}, u32[]{:S(2)}, u32[]{:S(2)}) %collective-permute-start.46) | collective-permute-done | bytes 196640 | tf_op jit(solution)/shard_map/ppermute | solution.py:34
  239.1 2.6 %prior_adjoint.7 = (f32[48,32,128]{2,1,0:T(8,128)S(1)}, bf16[24,32,128]{2,1,0:T(8,128)(2,1)S(1)}, bf16[24,32,128]{2,1,0:T(8,128)(2,1)S(1)}) custom-call(s32[1]{0:T(128)} %bitcast.core, s32[1297]{0:T(1024)S(1)} %get-tuple-element.87.plan, bf16[24,32,128]{2,1,0:T(8,128)(2,1)S(1)} %add_convert_fusion.mine, ...), custom_call_target="tpu_custom_call" | custom-call | tf_op jit(solution)/shard_map/prior_adjoint/pallas_call | solution.py:167
  242.4 2.7 %collective-permute-start.48 = (bf16[24,32,128]{2,1,0:T(8,128)(2,1)S(1)}, bf16[24,32,128]{2,1,0:T(8,128)(2,1)S(1)}, u32[]{:S(2)}, u32[]{:S(2)}) collective-permute-start(bf16[24,32,128]{2,1,0:T(8,128)(2,1)S(1)} %get-tuple-element.84), channel_id=1, source_target_pairs={{0,8},{1,9},{2,10},{3,11},{4,12},{5,13},{6,14},{7,15},{8,0},{9,1},... | collective-permute-start | bytes 589832 | tf_op jit(solution)/shard_map/ppermute | solution.py:34
  246.3 3.6 %collective-permute-start.49 = (bf16[24,32,128]{2,1,0:T(8,128)(2,1)S(1)}, bf16[24,32,128]{2,1,0:T(8,128)(2,1)S(1)}, u32[]{:S(2)}, u32[]{:S(2)}) collective-permute-start(bf16[24,32,128]{2,1,0:T(8,128)(2,1)S(1)} %fusion.2), channel_id=1, source_target_pairs={{0,8},{1,9},{2,10},{3,11},{4,12},{5,13},{6,14},{7,15},{8,0},{9,1},... | collective-permute-start | bytes 589832 | tf_op jit(solution)/shard_map/ppermute | solution.py:34
  (152 shorter events, 45.5 us)
Async XLA Ops:
  0.0 54.7 %copy-start = (f32[32,128]{1,0:T(8,128)S(1)}, f32[32,128]{1,0:T(8,128)}, u32[]{:S(2)}) copy-start(f32[32,128]{1,0:T(8,128)} %param.15) | copy-start | bytes 49156
  1.0 14.0 %collective-permute-start = (bf16[12,32,128]{2,1,0:T(8,128)(2,1)S(1)}, bf16[12,32,128]{2,1,0:T(8,128)(2,1)S(1)}, u32[]{:S(2)}, u32[]{:S(2)}) collective-permute-start(bf16[12,32,128]{2,1,0:T(8,128)(2,1)S(1)} %slice_select_fusion), channel_id=1, source_target_pairs={{1,8},{2,9},{3,10},{4,11},{5,12},{6,13},{7,14},{8,1},{9,2},{10,3},... | collective-permute-start | bytes 294920 | tf_op jit(solution)/shard_map/ppermute | solution.py:34
  9.0 6.0 %copy-start.10 = (bf16[48,32,128]{2,1,0:T(8,128)(2,1)S(1)}, bf16[48,32,128]{2,1,0:T(8,128)(2,1)}, u32[]{:S(2)}) copy-start(bf16[48,32,128]{2,1,0:T(8,128)(2,1)} %param.8) | copy-start | bytes 1179652
  17.7 19.0 %collective-permute-start.1 = (bf16[24,32,128]{2,1,0:T(8,128)(2,1)S(1)}, bf16[24,32,128]{2,1,0:T(8,128)(2,1)S(1)}, u32[]{:S(2)}, u32[]{:S(2)}) collective-permute-start(bf16[24,32,128]{2,1,0:T(8,128)(2,1)S(1)} %prior_spread.4.refs_0_), channel_id=1, source_target_pairs={{0,8},{1,9},{2,10},{3,11},{4,12},{5,13},{6,14},{7,15},{8,0},{9,1},... | collective-permute-start | bytes 589832 | tf_op jit(solution)/shard_map/ppermute | solution.py:34
  36.8 4.6 %copy-start.5 = (bf16[384,128,128]{2,1,0:T(8,128)(2,1)S(1)}, bf16[384,128,128]{2,1,0:T(8,128)(2,1)}, u32[]{:S(2)}) copy-start(bf16[384,128,128]{2,1,0:T(8,128)(2,1)} %copy-done.4) | copy-start | bytes 37748740
  44.5 4.3 %collective-permute-start.2 = (bf16[8,32,128]{2,1,0:T(8,128)(2,1)S(1)}, bf16[8,32,128]{2,1,0:T(8,128)(2,1)S(1)}, u32[]{:S(2)}, u32[]{:S(2)}) collective-permute-start(bf16[8,32,128]{2,1,0:T(8,128)(2,1)S(1)} %get-tuple-element.48), channel_id=1, source_target_pairs={{0,1},{1,0},{2,3},{3,2},{4,5},{5,4},{6,7},{7,6},{8,9},{9,8},{10,11... | collective-permute-start | bytes 196616 | tf_op jit(solution)/shard_map/ppermute | solution.py:34
  45.5 5.4 %collective-permute-start.3 = (bf16[8,32,128]{2,1,0:T(8,128)(2,1)S(1)}, bf16[8,32,128]{2,1,0:T(8,128)(2,1)S(1)}, u32[]{:S(2)}, u32[]{:S(2)}) collective-permute-start(bf16[8,32,128]{2,1,0:T(8,128)(2,1)S(1)} %get-tuple-element.49), channel_id=1, source_target_pairs={{0,2},{1,3},{2,0},{3,1},{4,6},{5,7},{6,4},{7,5},{8,10},{9,11},{10,... | collective-permute-start | bytes 196616 | tf_op jit(solution)/shard_map/ppermute | solution.py:34
  48.2 5.2 %collective-permute-start.4 = (bf16[8,32,128]{2,1,0:T(8,128)(2,1)S(1)}, bf16[8,32,128]{2,1,0:T(8,128)(2,1)S(1)}, u32[]{:S(2)}, u32[]{:S(2)}) collective-permute-start(bf16[8,32,128]{2,1,0:T(8,128)(2,1)S(1)} %get-tuple-element.50), channel_id=1, source_target_pairs={{0,3},{1,2},{2,1},{3,0},{4,7},{5,6},{6,5},{7,4},{8,11},{9,10},{10,... | collective-permute-start | bytes 196616 | tf_op jit(solution)/shard_map/ppermute | solution.py:34
  53.4 5.4 %collective-permute-start.5 = (bf16[8,32,128]{2,1,0:T(8,128)(2,1)S(1)}, bf16[8,32,128]{2,1,0:T(8,128)(2,1)S(1)}, u32[]{:S(2)}, u32[]{:S(2)}) collective-permute-start(bf16[8,32,128]{2,1,0:T(8,128)(2,1)S(1)} %add_convert_fusion.7), channel_id=1, source_target_pairs={{0,4},{1,5},{2,6},{3,7},{4,0},{5,1},{6,2},{7,3},{8,12},{9,13},{10,... | collective-permute-start | bytes 196616 | tf_op jit(solution)/shard_map/ppermute | solution.py:34
  58.8 5.2 %collective-permute-start.8 = (bf16[8,32,128]{2,1,0:T(8,128)(2,1)S(1)}, bf16[8,32,128]{2,1,0:T(8,128)(2,1)S(1)}, u32[]{:S(2)}, u32[]{:S(2)}) collective-permute-start(bf16[8,32,128]{2,1,0:T(8,128)(2,1)S(1)} %multiply_convert_fusion.3.refs_0_), channel_id=1, source_target_pairs={{0,3},{1,2},{2,1},{3,0},{4,7},{5,6},{6,5},{7,4},{8,11},{9,10},{10,... | collective-permute-start | bytes 196616 | tf_op jit(solution)/shard_map/ppermute | solution.py:34
  59.6 4.6 %collective-permute-start.7 = (bf16[8,32,128]{2,1,0:T(8,128)(2,1)S(1)}, bf16[8,32,128]{2,1,0:T(8,128)(2,1)S(1)}, u32[]{:S(2)}, u32[]{:S(2)}) collective-permute-start(bf16[8,32,128]{2,1,0:T(8,128)(2,1)S(1)} %multiply_convert_fusion.3.refs_0_), channel_id=1, source_target_pairs={{0,2},{1,3},{2,0},{3,1},{4,6},{5,7},{6,4},{7,5},{8,10},{9,11},{10,... | collective-permute-start | bytes 196616 | tf_op jit(solution)/shard_map/ppermute | solution.py:34
  61.2 4.3 %collective-permute-start.6 = (bf16[8,32,128]{2,1,0:T(8,128)(2,1)S(1)}, bf16[8,32,128]{2,1,0:T(8,128)(2,1)S(1)}, u32[]{:S(2)}, u32[]{:S(2)}) collective-permute-start(bf16[8,32,128]{2,1,0:T(8,128)(2,1)S(1)} %multiply_convert_fusion.3.refs_0_), channel_id=1, source_target_pairs={{0,1},{1,0},{2,3},{3,2},{4,5},{5,4},{6,7},{7,6},{8,9},{9,8},{10,11... | collective-permute-start | bytes 196616 | tf_op jit(solution)/shard_map/ppermute | solution.py:34
  70.1 30.5 %slice-start.3 = ((s8[12582912]{0:T(1024)(128)(4,1)}), s8[4194304]{0:T(1024)(128)(4,1)S(1)}, s32[]{:S(2)}) async-start(s8[12582912]{0:T(1024)(128)(4,1)} %bitcast.52), calls=%async_computation.3 | async-start | bytes 8388608
  70.1 30.5 %slice-start.4 = ((s8[12582912]{0:T(1024)(128)(4,1)}), s8[4194304]{0:T(1024)(128)(4,1)S(1)}, s32[]{:S(2)}) async-start(s8[12582912]{0:T(1024)(128)(4,1)} %bitcast.52), calls=%async_computation.4 | async-start | bytes 8388608
  73.2 1.5 collective-permute-start.9
  74.8 7.0 %collective-permute-start.10 = (bf16[24,32,128]{2,1,0:T(8,128)(2,1)S(1)}, bf16[24,32,128]{2,1,0:T(8,128)(2,1)S(1)}, u32[]{:S(2)}, u32[]{:S(2)}) collective-permute-start(bf16[24,32,128]{2,1,0:T(8,128)(2,1)S(1)} %add_convert_fusion.3.mine), channel_id=1, source_target_pairs={{0,16},{1,17},{2,18},{3,19},{4,20},{5,21},{6,22},{7,23},{8,24},{9,... | collective-permute-start | bytes 589832 | tf_op jit(solution)/shard_map/ppermute | solution.py:34
  84.6 16.0 %slice-start.5 = ((s8[12582912]{0:T(1024)(128)(4,1)}), s8[4194304]{0:T(1024)(128)(4,1)S(1)}, s32[]{:S(2)}) async-start(s8[12582912]{0:T(1024)(128)(4,1)} %bitcast.52), calls=%async_computation.5 | async-start | bytes 8388608
  84.6 40.7 %slice-start = ((s8[12582912]{0:T(1024)(128)(4,1)}), s8[4194304]{0:T(1024)(128)(4,1)S(1)}, s32[]{:S(2)}) async-start(s8[12582912]{0:T(1024)(128)(4,1)} %bitcast.50), calls=%async_computation | async-start | bytes 8388608
  87.2 1.5 collective-permute-start.11
  87.3 1.4 collective-permute-start.12
  91.5 33.8 %slice-start.1 = ((s8[12582912]{0:T(1024)(128)(4,1)}), s8[4194304]{0:T(1024)(128)(4,1)S(1)}, s32[]{:S(2)}) async-start(s8[12582912]{0:T(1024)(128)(4,1)} %bitcast.50), calls=%async_computation.1 | async-start | bytes 8388608
  93.4 31.9 %slice-start.2 = ((s8[12582912]{0:T(1024)(128)(4,1)}), s8[4194304]{0:T(1024)(128)(4,1)S(1)}, s32[]{:S(2)}) async-start(s8[12582912]{0:T(1024)(128)(4,1)} %bitcast.50), calls=%async_computation.2 | async-start | bytes 8388608
  93.4 7.2 %collective-permute-start.13 = (bf16[24,32,128]{2,1,0:T(8,128)(2,1)S(1)}, bf16[24,32,128]{2,1,0:T(8,128)(2,1)S(1)}, u32[]{:S(2)}, u32[]{:S(2)}) collective-permute-start(bf16[24,32,128]{2,1,0:T(8,128)(2,1)S(1)} %prior_spread.5.refs_0_), channel_id=1, source_target_pairs={{0,8},{1,9},{2,10},{3,11},{4,12},{5,13},{6,14},{7,15},{8,0},{9,1},... | collective-permute-start | bytes 589832 | tf_op jit(solution)/shard_map/ppermute | solution.py:34
  100.6 36.5 %slice-start.6 = ((s8[6291456]{0:T(1024)(128)(4,1)}), s8[4194304]{0:T(1024)(128)(4,1)S(1)}, s32[]{:S(2)}) async-start(s8[6291456]{0:T(1024)(128)(4,1)} %bitcast.54), calls=%async_computation.6 | async-start | bytes 8388608
  100.6 40.6 %slice-start.8 = ((s8[6291456]{0:T(1024)(128)(4,1)}), s8[4194304]{0:T(1024)(128)(4,1)S(1)}, s32[]{:S(2)}) async-start(s8[6291456]{0:T(1024)(128)(4,1)} %bitcast.56), calls=%async_computation.8 | async-start | bytes 8388608
  103.7 5.0 %collective-permute-start.14 = (bf16[8,32,128]{2,1,0:T(8,128)(2,1)S(1)}, bf16[8,32,128]{2,1,0:T(8,128)(2,1)S(1)}, u32[]{:S(2)}, u32[]{:S(2)}) collective-permute-start(bf16[8,32,128]{2,1,0:T(8,128)(2,1)S(1)} %get-tuple-element.59), channel_id=1, source_target_pairs={{0,1},{1,0},{2,3},{3,2},{4,5},{5,4},{6,7},{7,6},{8,9},{9,8},{10,11... | collective-permute-start | bytes 196616 | tf_op jit(solution)/shard_map/ppermute | solution.py:34
  105.8 4.6 %collective-permute-start.15 = (bf16[8,32,128]{2,1,0:T(8,128)(2,1)S(1)}, bf16[8,32,128]{2,1,0:T(8,128)(2,1)S(1)}, u32[]{:S(2)}, u32[]{:S(2)}) collective-permute-start(bf16[8,32,128]{2,1,0:T(8,128)(2,1)S(1)} %get-tuple-element.60), channel_id=1, source_target_pairs={{0,2},{1,3},{2,0},{3,1},{4,6},{5,7},{6,4},{7,5},{8,10},{9,11},{10,... | collective-permute-start | bytes 196616 | tf_op jit(solution)/shard_map/ppermute | solution.py:34
  108.2 5.2 %collective-permute-start.16 = (bf16[8,32,128]{2,1,0:T(8,128)(2,1)S(1)}, bf16[8,32,128]{2,1,0:T(8,128)(2,1)S(1)}, u32[]{:S(2)}, u32[]{:S(2)}) collective-permute-start(bf16[8,32,128]{2,1,0:T(8,128)(2,1)S(1)} %get-tuple-element.61), channel_id=1, source_target_pairs={{0,3},{1,2},{2,1},{3,0},{4,7},{5,6},{6,5},{7,4},{8,11},{9,10},{10,... | collective-permute-start | bytes 196616 | tf_op jit(solution)/shard_map/ppermute | solution.py:34
  113.4 5.9 %collective-permute-start.17 = (bf16[8,32,128]{2,1,0:T(8,128)(2,1)S(1)}, bf16[8,32,128]{2,1,0:T(8,128)(2,1)S(1)}, u32[]{:S(2)}, u32[]{:S(2)}) collective-permute-start(bf16[8,32,128]{2,1,0:T(8,128)(2,1)S(1)} %add_convert_fusion.6), channel_id=1, source_target_pairs={{0,4},{1,5},{2,6},{3,7},{4,0},{5,1},{6,2},{7,3},{8,12},{9,13},{10,... | collective-permute-start | bytes 196616 | tf_op jit(solution)/shard_map/ppermute | solution.py:34
  119.3 17.7 %slice-start.7 = ((s8[6291456]{0:T(1024)(128)(4,1)}), s8[2097152]{0:T(1024)(128)(4,1)S(1)}, s32[]{:S(2)}) async-start(s8[6291456]{0:T(1024)(128)(4,1)} %bitcast.54), calls=%async_computation.7 | async-start | bytes 4194304
  119.3 21.8 %slice-start.9 = ((s8[6291456]{0:T(1024)(128)(4,1)}), s8[2097152]{0:T(1024)(128)(4,1)S(1)}, s32[]{:S(2)}) async-start(s8[6291456]{0:T(1024)(128)(4,1)} %bitcast.56), calls=%async_computation.9 | async-start | bytes 4194304
  119.3 5.2 %collective-permute-start.20 = (bf16[8,32,128]{2,1,0:T(8,128)(2,1)S(1)}, bf16[8,32,128]{2,1,0:T(8,128)(2,1)S(1)}, u32[]{:S(2)}, u32[]{:S(2)}) collective-permute-start(bf16[8,32,128]{2,1,0:T(8,128)(2,1)S(1)} %multiply_convert_fusion.2.refs_0_), channel_id=1, source_target_pairs={{0,3},{1,2},{2,1},{3,0},{4,7},{5,6},{6,5},{7,4},{8,11},{9,10},{10,... | collective-permute-start | bytes 196616 | tf_op jit(solution)/shard_map/ppermute | solution.py:34
  120.6 4.3 %collective-permute-start.19 = (bf16[8,32,128]{2,1,0:T(8,128)(2,1)S(1)}, bf16[8,32,128]{2,1,0:T(8,128)(2,1)S(1)}, u32[]{:S(2)}, u32[]{:S(2)}) collective-permute-start(bf16[8,32,128]{2,1,0:T(8,128)(2,1)S(1)} %multiply_convert_fusion.2.refs_0_), channel_id=1, source_target_pairs={{0,2},{1,3},{2,0},{3,1},{4,6},{5,7},{6,4},{7,5},{8,10},{9,11},{10,... | collective-permute-start | bytes 196616 | tf_op jit(solution)/shard_map/ppermute | solution.py:34
  120.8 4.5 %collective-permute-start.18 = (bf16[8,32,128]{2,1,0:T(8,128)(2,1)S(1)}, bf16[8,32,128]{2,1,0:T(8,128)(2,1)S(1)}, u32[]{:S(2)}, u32[]{:S(2)}) collective-permute-start(bf16[8,32,128]{2,1,0:T(8,128)(2,1)S(1)} %multiply_convert_fusion.2.refs_0_), channel_id=1, source_target_pairs={{0,1},{1,0},{2,3},{3,2},{4,5},{5,4},{6,7},{7,6},{8,9},{9,8},{10,11... | collective-permute-start | bytes 196616 | tf_op jit(solution)/shard_map/ppermute | solution.py:34
  128.5 1.5 collective-permute-start.21
  130.0 7.0 %collective-permute-start.22 = (bf16[24,32,128]{2,1,0:T(8,128)(2,1)S(1)}, bf16[24,32,128]{2,1,0:T(8,128)(2,1)S(1)}, u32[]{:S(2)}, u32[]{:S(2)}) collective-permute-start(bf16[24,32,128]{2,1,0:T(8,128)(2,1)S(1)} %add_convert_fusion.2.mine), channel_id=1, source_target_pairs={{0,16},{1,17},{2,18},{3,19},{4,20},{5,21},{6,22},{7,23},{8,24},{9,... | collective-permute-start | bytes 589832 | tf_op jit(solution)/shard_map/ppermute | solution.py:34
  139.6 1.5 collective-permute-start.23
  139.7 1.4 collective-permute-start.24
  143.1 7.7 %collective-permute-start.25 = (bf16[24,32,128]{2,1,0:T(8,128)(2,1)S(1)}, bf16[24,32,128]{2,1,0:T(8,128)(2,1)S(1)}, u32[]{:S(2)}, u32[]{:S(2)}) collective-permute-start(bf16[24,32,128]{2,1,0:T(8,128)(2,1)S(1)} %prior_spread.6.refs_0_), channel_id=1, source_target_pairs={{0,8},{1,9},{2,10},{3,11},{4,12},{5,13},{6,14},{7,15},{8,0},{9,1},... | collective-permute-start | bytes 589832 | tf_op jit(solution)/shard_map/ppermute | solution.py:34
  154.1 5.1 %collective-permute-start.26 = (bf16[8,32,128]{2,1,0:T(8,128)(2,1)S(1)}, bf16[8,32,128]{2,1,0:T(8,128)(2,1)S(1)}, u32[]{:S(2)}, u32[]{:S(2)}) collective-permute-start(bf16[8,32,128]{2,1,0:T(8,128)(2,1)S(1)} %get-tuple-element.68), channel_id=1, source_target_pairs={{0,1},{1,0},{2,3},{3,2},{4,5},{5,4},{6,7},{7,6},{8,9},{9,8},{10,11... | collective-permute-start | bytes 196616 | tf_op jit(solution)/shard_map/ppermute | solution.py:34
  156.3 4.8 %collective-permute-start.27 = (bf16[8,32,128]{2,1,0:T(8,128)(2,1)S(1)}, bf16[8,32,128]{2,1,0:T(8,128)(2,1)S(1)}, u32[]{:S(2)}, u32[]{:S(2)}) collective-permute-start(bf16[8,32,128]{2,1,0:T(8,128)(2,1)S(1)} %get-tuple-element.69), channel_id=1, source_target_pairs={{0,2},{1,3},{2,0},{3,1},{4,6},{5,7},{6,4},{7,5},{8,10},{9,11},{10,... | collective-permute-start | bytes 196616 | tf_op jit(solution)/shard_map/ppermute | solution.py:34
  158.7 5.2 %collective-permute-start.28 = (bf16[8,32,128]{2,1,0:T(8,128)(2,1)S(1)}, bf16[8,32,128]{2,1,0:T(8,128)(2,1)S(1)}, u32[]{:S(2)}, u32[]{:S(2)}) collective-permute-start(bf16[8,32,128]{2,1,0:T(8,128)(2,1)S(1)} %get-tuple-element.70), channel_id=1, source_target_pairs={{0,3},{1,2},{2,1},{3,0},{4,7},{5,6},{6,5},{7,4},{8,11},{9,10},{10,... | collective-permute-start | bytes 196616 | tf_op jit(solution)/shard_map/ppermute | solution.py:34
  163.9 5.5 %collective-permute-start.29 = (bf16[8,32,128]{2,1,0:T(8,128)(2,1)S(1)}, bf16[8,32,128]{2,1,0:T(8,128)(2,1)S(1)}, u32[]{:S(2)}, u32[]{:S(2)}) collective-permute-start(bf16[8,32,128]{2,1,0:T(8,128)(2,1)S(1)} %add_convert_fusion.5), channel_id=1, source_target_pairs={{0,4},{1,5},{2,6},{3,7},{4,0},{5,1},{6,2},{7,3},{8,12},{9,13},{10,... | collective-permute-start | bytes 196616 | tf_op jit(solution)/shard_map/ppermute | solution.py:34
  169.5 5.2 %collective-permute-start.32 = (bf16[8,32,128]{2,1,0:T(8,128)(2,1)S(1)}, bf16[8,32,128]{2,1,0:T(8,128)(2,1)S(1)}, u32[]{:S(2)}, u32[]{:S(2)}) collective-permute-start(bf16[8,32,128]{2,1,0:T(8,128)(2,1)S(1)} %multiply_convert_fusion.1.refs_0_), channel_id=1, source_target_pairs={{0,3},{1,2},{2,1},{3,0},{4,7},{5,6},{6,5},{7,4},{8,11},{9,10},{10,... | collective-permute-start | bytes 196616 | tf_op jit(solution)/shard_map/ppermute | solution.py:34
  170.9 5.2 %collective-permute-start.31 = (bf16[8,32,128]{2,1,0:T(8,128)(2,1)S(1)}, bf16[8,32,128]{2,1,0:T(8,128)(2,1)S(1)}, u32[]{:S(2)}, u32[]{:S(2)}) collective-permute-start(bf16[8,32,128]{2,1,0:T(8,128)(2,1)S(1)} %multiply_convert_fusion.1.refs_0_), channel_id=1, source_target_pairs={{0,2},{1,3},{2,0},{3,1},{4,6},{5,7},{6,4},{7,5},{8,10},{9,11},{10,... | collective-permute-start | bytes 196616 | tf_op jit(solution)/shard_map/ppermute | solution.py:34
  173.1 4.3 %collective-permute-start.30 = (bf16[8,32,128]{2,1,0:T(8,128)(2,1)S(1)}, bf16[8,32,128]{2,1,0:T(8,128)(2,1)S(1)}, u32[]{:S(2)}, u32[]{:S(2)}) collective-permute-start(bf16[8,32,128]{2,1,0:T(8,128)(2,1)S(1)} %multiply_convert_fusion.1.refs_0_), channel_id=1, source_target_pairs={{0,1},{1,0},{2,3},{3,2},{4,5},{5,4},{6,7},{7,6},{8,9},{9,8},{10,11... | collective-permute-start | bytes 196616 | tf_op jit(solution)/shard_map/ppermute | solution.py:34
  180.6 1.5 collective-permute-start.33
  182.1 7.0 %collective-permute-start.34 = (bf16[24,32,128]{2,1,0:T(8,128)(2,1)S(1)}, bf16[24,32,128]{2,1,0:T(8,128)(2,1)S(1)}, u32[]{:S(2)}, u32[]{:S(2)}) collective-permute-start(bf16[24,32,128]{2,1,0:T(8,128)(2,1)S(1)} %add_convert_fusion.1.mine), channel_id=1, source_target_pairs={{0,16},{1,17},{2,18},{3,19},{4,20},{5,21},{6,22},{7,23},{8,24},{9,... | collective-permute-start | bytes 589832 | tf_op jit(solution)/shard_map/ppermute | solution.py:34
  191.8 1.5 collective-permute-start.35
  191.8 1.4 collective-permute-start.36
  195.2 7.2 %collective-permute-start.37 = (bf16[24,32,128]{2,1,0:T(8,128)(2,1)S(1)}, bf16[24,32,128]{2,1,0:T(8,128)(2,1)S(1)}, u32[]{:S(2)}, u32[]{:S(2)}) collective-permute-start(bf16[24,32,128]{2,1,0:T(8,128)(2,1)S(1)} %prior_spread.7.refs_0_), channel_id=1, source_target_pairs={{0,8},{1,9},{2,10},{3,11},{4,12},{5,13},{6,14},{7,15},{8,0},{9,1},... | collective-permute-start | bytes 589832 | tf_op jit(solution)/shard_map/ppermute | solution.py:34
  205.5 4.8 %collective-permute-start.38 = (bf16[8,32,128]{2,1,0:T(8,128)(2,1)S(1)}, bf16[8,32,128]{2,1,0:T(8,128)(2,1)S(1)}, u32[]{:S(2)}, u32[]{:S(2)}) collective-permute-start(bf16[8,32,128]{2,1,0:T(8,128)(2,1)S(1)} %get-tuple-element.77), channel_id=1, source_target_pairs={{0,1},{1,0},{2,3},{3,2},{4,5},{5,4},{6,7},{7,6},{8,9},{9,8},{10,11... | collective-permute-start | bytes 196616 | tf_op jit(solution)/shard_map/ppermute | solution.py:34
  207.3 4.7 %collective-permute-start.39 = (bf16[8,32,128]{2,1,0:T(8,128)(2,1)S(1)}, bf16[8,32,128]{2,1,0:T(8,128)(2,1)S(1)}, u32[]{:S(2)}, u32[]{:S(2)}) collective-permute-start(bf16[8,32,128]{2,1,0:T(8,128)(2,1)S(1)} %get-tuple-element.78), channel_id=1, source_target_pairs={{0,2},{1,3},{2,0},{3,1},{4,6},{5,7},{6,4},{7,5},{8,10},{9,11},{10,... | collective-permute-start | bytes 196616 | tf_op jit(solution)/shard_map/ppermute | solution.py:34
  209.8 5.2 %collective-permute-start.40 = (bf16[8,32,128]{2,1,0:T(8,128)(2,1)S(1)}, bf16[8,32,128]{2,1,0:T(8,128)(2,1)S(1)}, u32[]{:S(2)}, u32[]{:S(2)}) collective-permute-start(bf16[8,32,128]{2,1,0:T(8,128)(2,1)S(1)} %get-tuple-element.79), channel_id=1, source_target_pairs={{0,3},{1,2},{2,1},{3,0},{4,7},{5,6},{6,5},{7,4},{8,11},{9,10},{10,... | collective-permute-start | bytes 196616 | tf_op jit(solution)/shard_map/ppermute | solution.py:34
  215.0 6.5 %collective-permute-start.41 = (bf16[8,32,128]{2,1,0:T(8,128)(2,1)S(1)}, bf16[8,32,128]{2,1,0:T(8,128)(2,1)S(1)}, u32[]{:S(2)}, u32[]{:S(2)}) collective-permute-start(bf16[8,32,128]{2,1,0:T(8,128)(2,1)S(1)} %add_convert_fusion.4), channel_id=1, source_target_pairs={{0,4},{1,5},{2,6},{3,7},{4,0},{5,1},{6,2},{7,3},{8,12},{9,13},{10,... | collective-permute-start | bytes 196616 | tf_op jit(solution)/shard_map/ppermute | solution.py:34
  221.5 5.2 %collective-permute-start.44 = (bf16[8,32,128]{2,1,0:T(8,128)(2,1)S(1)}, bf16[8,32,128]{2,1,0:T(8,128)(2,1)S(1)}, u32[]{:S(2)}, u32[]{:S(2)}) collective-permute-start(bf16[8,32,128]{2,1,0:T(8,128)(2,1)S(1)} %multiply_convert_fusion.refs_0_), channel_id=1, source_target_pairs={{0,3},{1,2},{2,1},{3,0},{4,7},{5,6},{6,5},{7,4},{8,11},{9,10},{10,... | collective-permute-start | bytes 196616 | tf_op jit(solution)/shard_map/ppermute | solution.py:34
  223.0 4.3 %collective-permute-start.43 = (bf16[8,32,128]{2,1,0:T(8,128)(2,1)S(1)}, bf16[8,32,128]{2,1,0:T(8,128)(2,1)S(1)}, u32[]{:S(2)}, u32[]{:S(2)}) collective-permute-start(bf16[8,32,128]{2,1,0:T(8,128)(2,1)S(1)} %multiply_convert_fusion.refs_0_), channel_id=1, source_target_pairs={{0,2},{1,3},{2,0},{3,1},{4,6},{5,7},{6,4},{7,5},{8,10},{9,11},{10,... | collective-permute-start | bytes 196616 | tf_op jit(solution)/shard_map/ppermute | solution.py:34
  223.1 4.3 %collective-permute-start.42 = (bf16[8,32,128]{2,1,0:T(8,128)(2,1)S(1)}, bf16[8,32,128]{2,1,0:T(8,128)(2,1)S(1)}, u32[]{:S(2)}, u32[]{:S(2)}) collective-permute-start(bf16[8,32,128]{2,1,0:T(8,128)(2,1)S(1)} %multiply_convert_fusion.refs_0_), channel_id=1, source_target_pairs={{0,1},{1,0},{2,3},{3,2},{4,5},{5,4},{6,7},{7,6},{8,9},{9,8},{10,11... | collective-permute-start | bytes 196616 | tf_op jit(solution)/shard_map/ppermute | solution.py:34
  230.6 1.5 collective-permute-start.45
  232.1 7.0 %collective-permute-start.46 = (bf16[24,32,128]{2,1,0:T(8,128)(2,1)S(1)}, bf16[24,32,128]{2,1,0:T(8,128)(2,1)S(1)}, u32[]{:S(2)}, u32[]{:S(2)}) collective-permute-start(bf16[24,32,128]{2,1,0:T(8,128)(2,1)S(1)} %add_convert_fusion.mine), channel_id=1, source_target_pairs={{0,16},{1,17},{2,18},{3,19},{4,20},{5,21},{6,22},{7,23},{8,24},{9,... | collective-permute-start | bytes 589832 | tf_op jit(solution)/shard_map/ppermute | solution.py:34
  239.1 12.7 %copy-start.1 = (f32[32,128]{1,0:T(8,128)S(1)}, f32[32,128]{1,0:T(8,128)}, u32[]{:S(2)}) copy-start(f32[32,128]{1,0:T(8,128)} %param.15) | copy-start | bytes 49156
  241.8 3.4 %collective-permute-start.47 = (bf16[24,32,128]{2,1,0:T(8,128)(2,1)S(1)}, bf16[24,32,128]{2,1,0:T(8,128)(2,1)S(1)}, u32[]{:S(2)}, u32[]{:S(2)}) collective-permute-start(bf16[24,32,128]{2,1,0:T(8,128)(2,1)S(1)} %get-tuple-element.83), channel_id=1, source_target_pairs={{1,8},{2,9},{3,10},{4,11},{5,12},{6,13},{7,14},{8,1},{9,2},{10,3},... | collective-permute-start | bytes 589832 | tf_op jit(solution)/shard_map/ppermute | solution.py:34
  242.4 3.8 %collective-permute-start.48 = (bf16[24,32,128]{2,1,0:T(8,128)(2,1)S(1)}, bf16[24,32,128]{2,1,0:T(8,128)(2,1)S(1)}, u32[]{:S(2)}, u32[]{:S(2)}) collective-permute-start(bf16[24,32,128]{2,1,0:T(8,128)(2,1)S(1)} %get-tuple-element.84), channel_id=1, source_target_pairs={{0,8},{1,9},{2,10},{3,11},{4,12},{5,13},{6,14},{7,15},{8,0},{9,1},... | collective-permute-start | bytes 589832 | tf_op jit(solution)/shard_map/ppermute | solution.py:34
  246.3 4.7 %collective-permute-start.49 = (bf16[24,32,128]{2,1,0:T(8,128)(2,1)S(1)}, bf16[24,32,128]{2,1,0:T(8,128)(2,1)S(1)}, u32[]{:S(2)}, u32[]{:S(2)}) collective-permute-start(bf16[24,32,128]{2,1,0:T(8,128)(2,1)S(1)} %fusion.2), channel_id=1, source_target_pairs={{0,8},{1,9},{2,10},{3,11},{4,12},{5,13},{6,14},{7,15},{8,0},{9,1},... | collective-permute-start | bytes 589832 | tf_op jit(solution)/shard_map/ppermute | solution.py:34
  (7 other events, 24.7 us)

commit v4 on v3

--- a/solution.py
+++ b/solution.py
@@ -248,9 +248,6 @@
     fan = neighbours.shape[1]
     prior = prior_tiles.reshape((tile_count * fan,) + prior_tiles.shape[2:])
 
-    prior_plain, prior_turned = setup_blocks(core * (half * fan), half * fan, prior, "prior_setup")
-    jac_plain, jac_turned = setup_blocks(jnp.zeros((1,), jnp.int32), blocks.shape[0], blocks, "jac_setup")
-
     rows = max(obs_rows, tile_count)
     count = max(blocks.shape[0], half * fan)
 
@@ -270,7 +267,6 @@
         rows,
         rows,
     )
-    obs_plan, tile_plan, prior_plan = plans[0], plans[1], plans[2]
 
     def swap_core(value):
         return exchange(value, lambda i, j: (i ^ 1, j))
@@ -288,7 +284,16 @@
     edge = jnp.where(side == 0, probes[:reach], probes[tile_count - reach :])
     beyond = swap_far(edge)
     around = jnp.concatenate([beyond, probes, beyond], axis=0)
-    fields = (lax.dynamic_slice_in_dim(around, side * half, 2 * half, 0),)
+    field = lax.dynamic_slice_in_dim(around, side * half, 2 * half, 0)
+
+    core, begin, nbr, obs_plan, tile_plan, prior_plan, own_rinv, field, blocks, prior = (
+        lax.optimization_barrier(
+            (core, core * (half * fan), nbr, plans[0], plans[1], plans[2], own_rinv, field, blocks, prior)
+        )
+    )
+    prior_plain, prior_turned = setup_blocks(begin, half * fan, prior, "prior_setup")
+    jac_plain, jac_turned = setup_blocks(begin * 0, blocks.shape[0], blocks, "jac_setup")
+    fields = (field,)
     for step in range(STEPS):
         spread = spread_tiles(core, nbr, fields, prior_plain)
         parts = (spread, swap_core(spread))

time: 253 us -> 226 us (0.89)
  local copies, waits for them, and re-layouts: 27.6 us -> 0.54 us
  waiting for transfers between devices: 86 us -> 77.9 us
  starting transfers between devices: 76.1 us -> 82.3 us
    unnamed x42 -> x4, local copies, waits for them, and re-layouts: 27.1 us -> 0.01 us
    ppermute x50, waiting for transfers between devices: 86 us -> 77.9 us  [exchange(): return lax.ppermute(value, ('obs', 'flux'), route)]
    ppermute x50, starting transfers between devices: 76.1 us -> 82.3 us  [exchange(): return lax.ppermute(value, ('obs', 'flux'), route)]
  transfers between devices with their start and end apart: 50 -> 50, of which waited for: 44 -> 44; matrix products, arithmetic and copies ran while one was open for 3% -> 3% of each run, Pallas kernels for 3% -> 2%
where the time goes in v4:
time: 226 us; the launch traced here: 224 us
  starting transfers between devices  82.3 us (36%)
  waiting for transfers between devices  77.9 us (34%)
  Pallas kernels  52 us (23%)
  other arithmetic  9.71 us (4%)
    ppermute x50, starting transfers between devices, exchange(): return lax.ppermute(value, ('obs', 'flux'), route)  82.3 us
    ppermute x50, waiting for transfers between devices, exchange(): return lax.ppermute(value, ('obs', 'flux'), route)  77.9 us
    pallas_call x8, Pallas kernels, jac_pass(): pl.pallas_call(functools.partial(jac_kernel, len(parts), n_outs), in_spec...  25.3 us
    pallas_call x4, Pallas kernels, gather_tiles(): pl.pallas_call(functools.partial(gather_kernel, src_rows), in_specs=[smem...  10.4 us
    pallas_call x2, Pallas kernels, setup_blocks(): pl.pallas_call(functools.partial(setup_kernel, chunk), in_specs=[pl.Block...  8.69 us
    pallas_call x4, Pallas kernels, spread_tiles(): pl.pallas_call(functools.partial(spread_kernel, summed, nbr.shape[0] // t...  7.51 us
  transfers between devices with their start and end apart: 50, of which 44 were waited for; matrix products, arithmetic and copies ran while one was open for 3% of the time, Pallas kernels for 2%

profile of v4, /device:TPU:0, one launch (start us, length us, event | category | flops | bytes accessed | tf_op | source)
XLA Modules:
  0.0 223.6 jit_solution(1478414766003679006)
XLA Ops:
  10.4 3.3 %prior_setup.1 = (bf16[192,128,128]{2,1,0:T(8,128)(2,1)S(1)}, bf16[192,128,128]{2,1,0:T(8,128)(2,1)S(1)}) custom-call(s32[1]{0:T(128)S(6)} %mul.106.first, bf16[384,128,128]{2,1,0:T(8,128)(2,1)} %bitcast.53), custom_call_target="tpu_custom_call" | custom-call | tf_op jit(solution)/shard_map/prior_setup/pallas_call | solution.py:87
  13.7 1.8 prior_spread.4.refs_0_
  15.5 4.4 %collective-permute-start.1 = (bf16[24,32,128]{2,1,0:T(8,128)(2,1)S(1)}, bf16[24,32,128]{2,1,0:T(8,128)(2,1)S(1)}, u32[]{:S(2)}, u32[]{:S(2)}) collective-permute-start(bf16[24,32,128]{2,1,0:T(8,128)(2,1)S(1)} %prior_spread.4.refs_0_), channel_id=1, source_target_pairs={{0,8},{1,9},{2,10},{3,11},{4,12},{5,13},{6,14},{7,15},{8,0},{9,1},... | collective-permute-start | bytes 589832 | tf_op jit(solution)/shard_map/ppermute | solution.py:34
  19.9 5.4 %jac_setup.1 = (bf16[384,128,128]{2,1,0:T(8,128)(2,1)S(1)}, bf16[384,128,128]{2,1,0:T(8,128)(2,1)S(1)}) custom-call(s32[1]{0:T(128)} %constant.117.clone.1.first, bf16[384,128,128]{2,1,0:T(8,128)(2,1)} %bitcast.54), custom_call_target="tpu_custom_call" | custom-call | tf_op jit(solution)/shard_map/jac_setup/pallas_call | solution.py:87
  25.3 3.1 %jac_forward.4 = (f32[8,32,128]{2,1,0:T(8,128)S(1)}, bf16[8,32,128]{2,1,0:T(8,128)(2,1)S(1)}, bf16[8,32,128]{2,1,0:T(8,128)(2,1)S(1)}, bf16[8,32,128]{2,1,0:T(8,128)(2,1)S(1)}) custom-call(s32[1297]{0:T(1024)S(1)} %get-tuple-element.58.plan, bf16[24,32,128]{2,1,0:T(8,128)(2,1)S(1)} %prior_spread.4.refs_0_, ...), custom_call_target="tpu_custom_call" | custom-call | tf_op jit(solution)/shard_map/jac_forward/pallas_call | solution.py:138
  28.5 2.2 collective-permute-start.2
  32.9 2.0 collective-permute-done.3
  36.3 2.2 %collective-permute-start.5 = (bf16[8,32,128]{2,1,0:T(8,128)(2,1)S(1)}, bf16[8,32,128]{2,1,0:T(8,128)(2,1)S(1)}, u32[]{:S(2)}, u32[]{:S(2)}) collective-permute-start(bf16[8,32,128]{2,1,0:T(8,128)(2,1)S(1)} %add_convert_fusion.7), channel_id=1, source_target_pairs={{0,4},{1,5},{2,6},{3,7},{4,0},{5,1},{6,2},{7,3},{8,12},{9,13},{10,... | collective-permute-start | bytes 196616 | tf_op jit(solution)/shard_map/ppermute | solution.py:34
  38.5 3.0 %collective-permute-done.5 = bf16[8,32,128]{2,1,0:T(8,128)(2,1)S(1)} collective-permute-done((bf16[8,32,128]{2,1,0:T(8,128)(2,1)S(1)}, bf16[8,32,128]{2,1,0:T(8,128)(2,1)S(1)}, u32[]{:S(2)}, u32[]{:S(2)}) %collective-permute-start.5) | collective-permute-done | bytes 65568 | tf_op jit(solution)/shard_map/ppermute | solution.py:34
  41.5 1.6 collective-permute-start.8
  43.2 1.9 collective-permute-start.7
  45.1 1.7 collective-permute-done.8.refs_3_
  49.4 3.2 %jac_adjoint.4 = (f32[24,32,128]{2,1,0:T(8,128)S(1)}, bf16[24,32,128]{2,1,0:T(8,128)(2,1)S(1)}) custom-call(s32[1297]{0:T(1024)S(1)} %get-tuple-element.57.plan, bf16[8,32,128]{2,1,0:T(8,128)(2,1)S(1)} %multiply_convert_fusion.3.refs_0_, bf16[8,32,128]{2,1,0:T(8,128)(2,1)S(1)} %collective-permute-done.6.refs_1_, ...), custom_call_target="tpu_custom_call" | custom-call | tf_op jit(solution)/shard_map/jac_adjoint/pallas_call | solution.py:138
  52.6 1.4 collective-permute-done.9
  54.1 1.9 collective-permute-start.10
  56.0 5.2 %collective-permute-done.10.other = bf16[24,32,128]{2,1,0:T(8,128)(2,1)S(1)} collective-permute-done((bf16[24,32,128]{2,1,0:T(8,128)(2,1)S(1)}, bf16[24,32,128]{2,1,0:T(8,128)(2,1)S(1)}, u32[]{:S(2)}, u32[]{:S(2)}) %collective-permute-start.10) | collective-permute-done | bytes 196640 | tf_op jit(solution)/shard_map/ppermute | solution.py:34
  61.2 2.6 %prior_adjoint.4 = (f32[48,32,128]{2,1,0:T(8,128)S(1)}, bf16[24,32,128]{2,1,0:T(8,128)(2,1)S(1)}, bf16[24,32,128]{2,1,0:T(8,128)(2,1)S(1)}) custom-call(s32[1]{0:T(128)} %bitcast.core, s32[1297]{0:T(1024)S(1)} %get-tuple-element.56.plan, bf16[24,32,128]{2,1,0:T(8,128)(2,1)S(1)} %add_convert_fusion.3.mine, ...), custom_call_target="tpu_custom_call" | custom-call | tf_op jit(solution)/shard_map/prior_adjoint/pallas_call | solution.py:167
  65.3 1.9 prior_spread.5.refs_0_
  67.2 6.1 %collective-permute-start.13 = (bf16[24,32,128]{2,1,0:T(8,128)(2,1)S(1)}, bf16[24,32,128]{2,1,0:T(8,128)(2,1)S(1)}, u32[]{:S(2)}, u32[]{:S(2)}) collective-permute-start(bf16[24,32,128]{2,1,0:T(8,128)(2,1)S(1)} %prior_spread.5.refs_0_), channel_id=1, source_target_pairs={{0,8},{1,9},{2,10},{3,11},{4,12},{5,13},{6,14},{7,15},{8,0},{9,1},... | collective-permute-start | bytes 589832 | tf_op jit(solution)/shard_map/ppermute | solution.py:34
  74.4 3.1 %jac_forward.5 = (f32[8,32,128]{2,1,0:T(8,128)S(1)}, bf16[8,32,128]{2,1,0:T(8,128)(2,1)S(1)}, bf16[8,32,128]{2,1,0:T(8,128)(2,1)S(1)}, bf16[8,32,128]{2,1,0:T(8,128)(2,1)S(1)}) custom-call(s32[1297]{0:T(1024)S(1)} %get-tuple-element.58.plan, bf16[24,32,128]{2,1,0:T(8,128)(2,1)S(1)} %prior_spread.5.refs_0_, ...), custom_call_target="tpu_custom_call" | custom-call | tf_op jit(solution)/shard_map/jac_forward/pallas_call | solution.py:138
  77.6 3.3 %collective-permute-start.14 = (bf16[8,32,128]{2,1,0:T(8,128)(2,1)S(1)}, bf16[8,32,128]{2,1,0:T(8,128)(2,1)S(1)}, u32[]{:S(2)}, u32[]{:S(2)}) collective-permute-start(bf16[8,32,128]{2,1,0:T(8,128)(2,1)S(1)} %get-tuple-element.79), channel_id=1, source_target_pairs={{0,1},{1,0},{2,3},{3,2},{4,5},{5,4},{6,7},{7,6},{8,9},{9,8},{10,11... | collective-permute-start | bytes 196616 | tf_op jit(solution)/shard_map/ppermute | solution.py:34
  80.8 1.5 collective-permute-start.16
  83.1 2.0 collective-permute-done.15
  86.1 2.4 %collective-permute-start.17 = (bf16[8,32,128]{2,1,0:T(8,128)(2,1)S(1)}, bf16[8,32,128]{2,1,0:T(8,128)(2,1)S(1)}, u32[]{:S(2)}, u32[]{:S(2)}) collective-permute-start(bf16[8,32,128]{2,1,0:T(8,128)(2,1)S(1)} %add_convert_fusion.6), channel_id=1, source_target_pairs={{0,4},{1,5},{2,6},{3,7},{4,0},{5,1},{6,2},{7,3},{8,12},{9,13},{10,... | collective-permute-start | bytes 196616 | tf_op jit(solution)/shard_map/ppermute | solution.py:34
  88.4 3.1 %collective-permute-done.17 = bf16[8,32,128]{2,1,0:T(8,128)(2,1)S(1)} collective-permute-done((bf16[8,32,128]{2,1,0:T(8,128)(2,1)S(1)}, bf16[8,32,128]{2,1,0:T(8,128)(2,1)S(1)}, u32[]{:S(2)}, u32[]{:S(2)}) %collective-permute-start.17) | collective-permute-done | bytes 65568 | tf_op jit(solution)/shard_map/ppermute | solution.py:34
  91.6 1.6 collective-permute-start.20
  93.2 1.8 collective-permute-start.19
  95.1 1.8 collective-permute-done.20.refs_3_
  99.2 3.2 %jac_adjoint.5 = (f32[24,32,128]{2,1,0:T(8,128)S(1)}, bf16[24,32,128]{2,1,0:T(8,128)(2,1)S(1)}) custom-call(s32[1297]{0:T(1024)S(1)} %get-tuple-element.57.plan, bf16[8,32,128]{2,1,0:T(8,128)(2,1)S(1)} %multiply_convert_fusion.2.refs_0_, bf16[8,32,128]{2,1,0:T(8,128)(2,1)S(1)} %collective-permute-done.18.refs_1_, ...), custom_call_target="tpu_custom_call" | custom-call | tf_op jit(solution)/shard_map/jac_adjoint/pallas_call | solution.py:138
  104.0 2.3 %collective-permute-start.22 = (bf16[24,32,128]{2,1,0:T(8,128)(2,1)S(1)}, bf16[24,32,128]{2,1,0:T(8,128)(2,1)S(1)}, u32[]{:S(2)}, u32[]{:S(2)}) collective-permute-start(bf16[24,32,128]{2,1,0:T(8,128)(2,1)S(1)} %add_convert_fusion.2.mine), channel_id=1, source_target_pairs={{0,16},{1,17},{2,18},{3,19},{4,20},{5,21},{6,22},{7,23},{8,24},{9,... | collective-permute-start | bytes 589832 | tf_op jit(solution)/shard_map/ppermute | solution.py:34
  106.2 5.2 %collective-permute-done.22.other = bf16[24,32,128]{2,1,0:T(8,128)(2,1)S(1)} collective-permute-done((bf16[24,32,128]{2,1,0:T(8,128)(2,1)S(1)}, bf16[24,32,128]{2,1,0:T(8,128)(2,1)S(1)}, u32[]{:S(2)}, u32[]{:S(2)}) %collective-permute-start.22) | collective-permute-done | bytes 196640 | tf_op jit(solution)/shard_map/ppermute | solution.py:34
  111.4 2.6 %prior_adjoint.5 = (f32[48,32,128]{2,1,0:T(8,128)S(1)}, bf16[24,32,128]{2,1,0:T(8,128)(2,1)S(1)}, bf16[24,32,128]{2,1,0:T(8,128)(2,1)S(1)}) custom-call(s32[1]{0:T(128)} %bitcast.core, s32[1297]{0:T(1024)S(1)} %get-tuple-element.56.plan, bf16[24,32,128]{2,1,0:T(8,128)(2,1)S(1)} %add_convert_fusion.2.mine, ...), custom_call_target="tpu_custom_call" | custom-call | tf_op jit(solution)/shard_map/prior_adjoint/pallas_call | solution.py:167
  115.6 1.9 prior_spread.6.refs_0_
  117.5 6.1 %collective-permute-start.25 = (bf16[24,32,128]{2,1,0:T(8,128)(2,1)S(1)}, bf16[24,32,128]{2,1,0:T(8,128)(2,1)S(1)}, u32[]{:S(2)}, u32[]{:S(2)}) collective-permute-start(bf16[24,32,128]{2,1,0:T(8,128)(2,1)S(1)} %prior_spread.6.refs_0_), channel_id=1, source_target_pairs={{0,8},{1,9},{2,10},{3,11},{4,12},{5,13},{6,14},{7,15},{8,0},{9,1},... | collective-permute-start | bytes 589832 | tf_op jit(solution)/shard_map/ppermute | solution.py:34
  124.6 3.3 %jac_forward.6 = (f32[8,32,128]{2,1,0:T(8,128)S(1)}, bf16[8,32,128]{2,1,0:T(8,128)(2,1)S(1)}, bf16[8,32,128]{2,1,0:T(8,128)(2,1)S(1)}, bf16[8,32,128]{2,1,0:T(8,128)(2,1)S(1)}) custom-call(s32[1297]{0:T(1024)S(1)} %get-tuple-element.58.plan, bf16[24,32,128]{2,1,0:T(8,128)(2,1)S(1)} %prior_spread.6.refs_0_, ...), custom_call_target="tpu_custom_call" | custom-call | tf_op jit(solution)/shard_map/jac_forward/pallas_call | solution.py:138
  128.0 3.0 %collective-permute-start.26 = (bf16[8,32,128]{2,1,0:T(8,128)(2,1)S(1)}, bf16[8,32,128]{2,1,0:T(8,128)(2,1)S(1)}, u32[]{:S(2)}, u32[]{:S(2)}) collective-permute-start(bf16[8,32,128]{2,1,0:T(8,128)(2,1)S(1)} %get-tuple-element.88), channel_id=1, source_target_pairs={{0,1},{1,0},{2,3},{3,2},{4,5},{5,4},{6,7},{7,6},{8,9},{9,8},{10,11... | collective-permute-start | bytes 196616 | tf_op jit(solution)/shard_map/ppermute | solution.py:34
  131.0 1.5 collective-permute-start.28
  133.2 2.0 collective-permute-done.27
  136.2 2.4 %collective-permute-start.29 = (bf16[8,32,128]{2,1,0:T(8,128)(2,1)S(1)}, bf16[8,32,128]{2,1,0:T(8,128)(2,1)S(1)}, u32[]{:S(2)}, u32[]{:S(2)}) collective-permute-start(bf16[8,32,128]{2,1,0:T(8,128)(2,1)S(1)} %add_convert_fusion.5), channel_id=1, source_target_pairs={{0,4},{1,5},{2,6},{3,7},{4,0},{5,1},{6,2},{7,3},{8,12},{9,13},{10,... | collective-permute-start | bytes 196616 | tf_op jit(solution)/shard_map/ppermute | solution.py:34
  138.6 3.0 %collective-permute-done.29 = bf16[8,32,128]{2,1,0:T(8,128)(2,1)S(1)} collective-permute-done((bf16[8,32,128]{2,1,0:T(8,128)(2,1)S(1)}, bf16[8,32,128]{2,1,0:T(8,128)(2,1)S(1)}, u32[]{:S(2)}, u32[]{:S(2)}) %collective-permute-start.29) | collective-permute-done | bytes 65568 | tf_op jit(solution)/shard_map/ppermute | solution.py:34
  141.7 1.7 collective-permute-start.32
  143.4 1.7 collective-permute-start.31
  145.2 1.8 collective-permute-done.32.refs_3_
  149.3 3.2 %jac_adjoint.6 = (f32[24,32,128]{2,1,0:T(8,128)S(1)}, bf16[24,32,128]{2,1,0:T(8,128)(2,1)S(1)}) custom-call(s32[1297]{0:T(1024)S(1)} %get-tuple-element.57.plan, bf16[8,32,128]{2,1,0:T(8,128)(2,1)S(1)} %multiply_convert_fusion.1.refs_0_, bf16[8,32,128]{2,1,0:T(8,128)(2,1)S(1)} %collective-permute-done.30.refs_1_, ...), custom_call_target="tpu_custom_call" | custom-call | tf_op jit(solution)/shard_map/jac_adjoint/pallas_call | solution.py:138
  154.1 2.6 %collective-permute-start.34 = (bf16[24,32,128]{2,1,0:T(8,128)(2,1)S(1)}, bf16[24,32,128]{2,1,0:T(8,128)(2,1)S(1)}, u32[]{:S(2)}, u32[]{:S(2)}) collective-permute-start(bf16[24,32,128]{2,1,0:T(8,128)(2,1)S(1)} %add_convert_fusion.1.mine), channel_id=1, source_target_pairs={{0,16},{1,17},{2,18},{3,19},{4,20},{5,21},{6,22},{7,23},{8,24},{9,... | collective-permute-start | bytes 589832 | tf_op jit(solution)/shard_map/ppermute | solution.py:34
  156.6 5.2 %collective-permute-done.34.other = bf16[24,32,128]{2,1,0:T(8,128)(2,1)S(1)} collective-permute-done((bf16[24,32,128]{2,1,0:T(8,128)(2,1)S(1)}, bf16[24,32,128]{2,1,0:T(8,128)(2,1)S(1)}, u32[]{:S(2)}, u32[]{:S(2)}) %collective-permute-start.34) | collective-permute-done | bytes 196640 | tf_op jit(solution)/shard_map/ppermute | solution.py:34
  161.8 2.6 %prior_adjoint.6 = (f32[48,32,128]{2,1,0:T(8,128)S(1)}, bf16[24,32,128]{2,1,0:T(8,128)(2,1)S(1)}, bf16[24,32,128]{2,1,0:T(8,128)(2,1)S(1)}) custom-call(s32[1]{0:T(128)} %bitcast.core, s32[1297]{0:T(1024)S(1)} %get-tuple-element.56.plan, bf16[24,32,128]{2,1,0:T(8,128)(2,1)S(1)} %add_convert_fusion.1.mine, ...), custom_call_target="tpu_custom_call" | custom-call | tf_op jit(solution)/shard_map/prior_adjoint/pallas_call | solution.py:167
  166.0 1.9 prior_spread.7.refs_0_
  167.9 6.1 %collective-permute-start.37 = (bf16[24,32,128]{2,1,0:T(8,128)(2,1)S(1)}, bf16[24,32,128]{2,1,0:T(8,128)(2,1)S(1)}, u32[]{:S(2)}, u32[]{:S(2)}) collective-permute-start(bf16[24,32,128]{2,1,0:T(8,128)(2,1)S(1)} %prior_spread.7.refs_0_), channel_id=1, source_target_pairs={{0,8},{1,9},{2,10},{3,11},{4,12},{5,13},{6,14},{7,15},{8,0},{9,1},... | collective-permute-start | bytes 589832 | tf_op jit(solution)/shard_map/ppermute | solution.py:34
  175.1 3.1 %jac_forward.7 = (f32[8,32,128]{2,1,0:T(8,128)S(1)}, bf16[8,32,128]{2,1,0:T(8,128)(2,1)S(1)}, bf16[8,32,128]{2,1,0:T(8,128)(2,1)S(1)}, bf16[8,32,128]{2,1,0:T(8,128)(2,1)S(1)}) custom-call(s32[1297]{0:T(1024)S(1)} %get-tuple-element.58.plan, bf16[24,32,128]{2,1,0:T(8,128)(2,1)S(1)} %prior_spread.7.refs_0_, ...), custom_call_target="tpu_custom_call" | custom-call | tf_op jit(solution)/shard_map/jac_forward/pallas_call | solution.py:138
  178.2 3.0 %collective-permute-start.38 = (bf16[8,32,128]{2,1,0:T(8,128)(2,1)S(1)}, bf16[8,32,128]{2,1,0:T(8,128)(2,1)S(1)}, u32[]{:S(2)}, u32[]{:S(2)}) collective-permute-start(bf16[8,32,128]{2,1,0:T(8,128)(2,1)S(1)} %get-tuple-element.97), channel_id=1, source_target_pairs={{0,1},{1,0},{2,3},{3,2},{4,5},{5,4},{6,7},{7,6},{8,9},{9,8},{10,11... | collective-permute-start | bytes 196616 | tf_op jit(solution)/shard_map/ppermute | solution.py:34
  181.2 1.5 collective-permute-start.40
  183.5 2.0 collective-permute-done.39
  186.4 2.2 collective-permute-start.41
  188.6 3.0 %collective-permute-done.41 = bf16[8,32,128]{2,1,0:T(8,128)(2,1)S(1)} collective-permute-done((bf16[8,32,128]{2,1,0:T(8,128)(2,1)S(1)}, bf16[8,32,128]{2,1,0:T(8,128)(2,1)S(1)}, u32[]{:S(2)}, u32[]{:S(2)}) %collective-permute-start.41) | collective-permute-done | bytes 65568 | tf_op jit(solution)/shard_map/ppermute | solution.py:34
  191.7 1.7 collective-permute-start.44
  193.4 1.9 collective-permute-start.43
  195.3 1.6 collective-permute-done.44.refs_3_
  199.6 3.2 %jac_adjoint.7 = (f32[24,32,128]{2,1,0:T(8,128)S(1)}, bf16[24,32,128]{2,1,0:T(8,128)(2,1)S(1)}) custom-call(s32[1297]{0:T(1024)S(1)} %get-tuple-element.57.plan, bf16[8,32,128]{2,1,0:T(8,128)(2,1)S(1)} %multiply_convert_fusion.refs_0_, bf16[8,32,128]{2,1,0:T(8,128)(2,1)S(1)} %collective-permute-done.42.refs_1_, ...), custom_call_target="tpu_custom_call" | custom-call | tf_op jit(solution)/shard_map/jac_adjoint/pallas_call | solution.py:138
  204.3 2.6 %collective-permute-start.46 = (bf16[24,32,128]{2,1,0:T(8,128)(2,1)S(1)}, bf16[24,32,128]{2,1,0:T(8,128)(2,1)S(1)}, u32[]{:S(2)}, u32[]{:S(2)}) collective-permute-start(bf16[24,32,128]{2,1,0:T(8,128)(2,1)S(1)} %add_convert_fusion.mine), channel_id=1, source_target_pairs={{0,16},{1,17},{2,18},{3,19},{4,20},{5,21},{6,22},{7,23},{8,24},{9,... | collective-permute-start | bytes 589832 | tf_op jit(solution)/shard_map/ppermute | solution.py:34
  206.9 5.2 %collective-permute-done.46.other = bf16[24,32,128]{2,1,0:T(8,128)(2,1)S(1)} collective-permute-done((bf16[24,32,128]{2,1,0:T(8,128)(2,1)S(1)}, bf16[24,32,128]{2,1,0:T(8,128)(2,1)S(1)}, u32[]{:S(2)}, u32[]{:S(2)}) %collective-permute-start.46) | collective-permute-done | bytes 196640 | tf_op jit(solution)/shard_map/ppermute | solution.py:34
  212.1 2.6 %prior_adjoint.7 = (f32[48,32,128]{2,1,0:T(8,128)S(1)}, bf16[24,32,128]{2,1,0:T(8,128)(2,1)S(1)}, bf16[24,32,128]{2,1,0:T(8,128)(2,1)S(1)}) custom-call(s32[1]{0:T(128)} %bitcast.core, s32[1297]{0:T(1024)S(1)} %get-tuple-element.56.plan, bf16[24,32,128]{2,1,0:T(8,128)(2,1)S(1)} %add_convert_fusion.mine, ...), custom_call_target="tpu_custom_call" | custom-call | tf_op jit(solution)/shard_map/prior_adjoint/pallas_call | solution.py:167
  215.4 1.6 collective-permute-start.48
  218.1 3.6 %collective-permute-start.49 = (bf16[24,32,128]{2,1,0:T(8,128)(2,1)S(1)}, bf16[24,32,128]{2,1,0:T(8,128)(2,1)S(1)}, u32[]{:S(2)}, u32[]{:S(2)}) collective-permute-start(bf16[24,32,128]{2,1,0:T(8,128)(2,1)S(1)} %fusion.2), channel_id=1, source_target_pairs={{0,8},{1,9},{2,10},{3,11},{4,12},{5,13},{6,14},{7,15},{8,0},{9,1},... | collective-permute-start | bytes 589832 | tf_op jit(solution)/shard_map/ppermute | solution.py:34
  (110 shorter events, 44.5 us)
Async XLA Ops:
  0.0 9.2 %copy-start = (f32[32,128]{1,0:T(8,128)S(1)}, f32[32,128]{1,0:T(8,128)}, u32[]{:S(2)}) copy-start(f32[32,128]{1,0:T(8,128)} %param.15) | copy-start | bytes 49156
  1.0 8.2 %collective-permute-start = (bf16[12,32,128]{2,1,0:T(8,128)(2,1)S(1)}, bf16[12,32,128]{2,1,0:T(8,128)(2,1)S(1)}, u32[]{:S(2)}, u32[]{:S(2)}) collective-permute-start(bf16[12,32,128]{2,1,0:T(8,128)(2,1)S(1)} %slice_select_fusion), channel_id=1, source_target_pairs={{1,8},{2,9},{3,10},{4,11},{5,12},{6,13},{7,14},{8,1},{9,2},{10,3},... | collective-permute-start | bytes 294920 | tf_op jit(solution)/shard_map/ppermute | solution.py:34
  15.5 9.8 %collective-permute-start.1 = (bf16[24,32,128]{2,1,0:T(8,128)(2,1)S(1)}, bf16[24,32,128]{2,1,0:T(8,128)(2,1)S(1)}, u32[]{:S(2)}, u32[]{:S(2)}) collective-permute-start(bf16[24,32,128]{2,1,0:T(8,128)(2,1)S(1)} %prior_spread.4.refs_0_), channel_id=1, source_target_pairs={{0,8},{1,9},{2,10},{3,11},{4,12},{5,13},{6,14},{7,15},{8,0},{9,1},... | collective-permute-start | bytes 589832 | tf_op jit(solution)/shard_map/ppermute | solution.py:34
  28.5 4.4 %collective-permute-start.2 = (bf16[8,32,128]{2,1,0:T(8,128)(2,1)S(1)}, bf16[8,32,128]{2,1,0:T(8,128)(2,1)S(1)}, u32[]{:S(2)}, u32[]{:S(2)}) collective-permute-start(bf16[8,32,128]{2,1,0:T(8,128)(2,1)S(1)} %get-tuple-element.67), channel_id=1, source_target_pairs={{0,1},{1,0},{2,3},{3,2},{4,5},{5,4},{6,7},{7,6},{8,9},{9,8},{10,11... | collective-permute-start | bytes 196616 | tf_op jit(solution)/shard_map/ppermute | solution.py:34
  30.7 4.3 %collective-permute-start.3 = (bf16[8,32,128]{2,1,0:T(8,128)(2,1)S(1)}, bf16[8,32,128]{2,1,0:T(8,128)(2,1)S(1)}, u32[]{:S(2)}, u32[]{:S(2)}) collective-permute-start(bf16[8,32,128]{2,1,0:T(8,128)(2,1)S(1)} %get-tuple-element.68), channel_id=1, source_target_pairs={{0,2},{1,3},{2,0},{3,1},{4,6},{5,7},{6,4},{7,5},{8,10},{9,11},{10,... | collective-permute-start | bytes 196616 | tf_op jit(solution)/shard_map/ppermute | solution.py:34
  31.1 5.2 %collective-permute-start.4 = (bf16[8,32,128]{2,1,0:T(8,128)(2,1)S(1)}, bf16[8,32,128]{2,1,0:T(8,128)(2,1)S(1)}, u32[]{:S(2)}, u32[]{:S(2)}) collective-permute-start(bf16[8,32,128]{2,1,0:T(8,128)(2,1)S(1)} %get-tuple-element.69), channel_id=1, source_target_pairs={{0,3},{1,2},{2,1},{3,0},{4,7},{5,6},{6,5},{7,4},{8,11},{9,10},{10,... | collective-permute-start | bytes 196616 | tf_op jit(solution)/shard_map/ppermute | solution.py:34
  36.3 5.2 %collective-permute-start.5 = (bf16[8,32,128]{2,1,0:T(8,128)(2,1)S(1)}, bf16[8,32,128]{2,1,0:T(8,128)(2,1)S(1)}, u32[]{:S(2)}, u32[]{:S(2)}) collective-permute-start(bf16[8,32,128]{2,1,0:T(8,128)(2,1)S(1)} %add_convert_fusion.7), channel_id=1, source_target_pairs={{0,4},{1,5},{2,6},{3,7},{4,0},{5,1},{6,2},{7,3},{8,12},{9,13},{10,... | collective-permute-start | bytes 196616 | tf_op jit(solution)/shard_map/ppermute | solution.py:34
  41.5 5.3 %collective-permute-start.8 = (bf16[8,32,128]{2,1,0:T(8,128)(2,1)S(1)}, bf16[8,32,128]{2,1,0:T(8,128)(2,1)S(1)}, u32[]{:S(2)}, u32[]{:S(2)}) collective-permute-start(bf16[8,32,128]{2,1,0:T(8,128)(2,1)S(1)} %multiply_convert_fusion.3.refs_0_), channel_id=1, source_target_pairs={{0,3},{1,2},{2,1},{3,0},{4,7},{5,6},{6,5},{7,4},{8,11},{9,10},{10,... | collective-permute-start | bytes 196616 | tf_op jit(solution)/shard_map/ppermute | solution.py:34
  43.2 4.9 %collective-permute-start.7 = (bf16[8,32,128]{2,1,0:T(8,128)(2,1)S(1)}, bf16[8,32,128]{2,1,0:T(8,128)(2,1)S(1)}, u32[]{:S(2)}, u32[]{:S(2)}) collective-permute-start(bf16[8,32,128]{2,1,0:T(8,128)(2,1)S(1)} %multiply_convert_fusion.3.refs_0_), channel_id=1, source_target_pairs={{0,2},{1,3},{2,0},{3,1},{4,6},{5,7},{6,4},{7,5},{8,10},{9,11},{10,... | collective-permute-start | bytes 196616 | tf_op jit(solution)/shard_map/ppermute | solution.py:34
  45.1 4.3 %collective-permute-start.6 = (bf16[8,32,128]{2,1,0:T(8,128)(2,1)S(1)}, bf16[8,32,128]{2,1,0:T(8,128)(2,1)S(1)}, u32[]{:S(2)}, u32[]{:S(2)}) collective-permute-start(bf16[8,32,128]{2,1,0:T(8,128)(2,1)S(1)} %multiply_convert_fusion.3.refs_0_), channel_id=1, source_target_pairs={{0,1},{1,0},{2,3},{3,2},{4,5},{5,4},{6,7},{7,6},{8,9},{9,8},{10,11... | collective-permute-start | bytes 196616 | tf_op jit(solution)/shard_map/ppermute | solution.py:34
  52.5 1.5 collective-permute-start.9
  54.1 7.1 %collective-permute-start.10 = (bf16[24,32,128]{2,1,0:T(8,128)(2,1)S(1)}, bf16[24,32,128]{2,1,0:T(8,128)(2,1)S(1)}, u32[]{:S(2)}, u32[]{:S(2)}) collective-permute-start(bf16[24,32,128]{2,1,0:T(8,128)(2,1)S(1)} %add_convert_fusion.3.mine), channel_id=1, source_target_pairs={{0,16},{1,17},{2,18},{3,19},{4,20},{5,21},{6,22},{7,23},{8,24},{9,... | collective-permute-start | bytes 589832 | tf_op jit(solution)/shard_map/ppermute | solution.py:34
  63.8 1.5 collective-permute-start.11
  63.9 1.4 collective-permute-start.12
  67.2 7.2 %collective-permute-start.13 = (bf16[24,32,128]{2,1,0:T(8,128)(2,1)S(1)}, bf16[24,32,128]{2,1,0:T(8,128)(2,1)S(1)}, u32[]{:S(2)}, u32[]{:S(2)}) collective-permute-start(bf16[24,32,128]{2,1,0:T(8,128)(2,1)S(1)} %prior_spread.5.refs_0_), channel_id=1, source_target_pairs={{0,8},{1,9},{2,10},{3,11},{4,12},{5,13},{6,14},{7,15},{8,0},{9,1},... | collective-permute-start | bytes 589832 | tf_op jit(solution)/shard_map/ppermute | solution.py:34
  77.6 5.5 %collective-permute-start.14 = (bf16[8,32,128]{2,1,0:T(8,128)(2,1)S(1)}, bf16[8,32,128]{2,1,0:T(8,128)(2,1)S(1)}, u32[]{:S(2)}, u32[]{:S(2)}) collective-permute-start(bf16[8,32,128]{2,1,0:T(8,128)(2,1)S(1)} %get-tuple-element.79), channel_id=1, source_target_pairs={{0,1},{1,0},{2,3},{3,2},{4,5},{5,4},{6,7},{7,6},{8,9},{9,8},{10,11... | collective-permute-start | bytes 196616 | tf_op jit(solution)/shard_map/ppermute | solution.py:34
  80.8 4.3 %collective-permute-start.15 = (bf16[8,32,128]{2,1,0:T(8,128)(2,1)S(1)}, bf16[8,32,128]{2,1,0:T(8,128)(2,1)S(1)}, u32[]{:S(2)}, u32[]{:S(2)}) collective-permute-start(bf16[8,32,128]{2,1,0:T(8,128)(2,1)S(1)} %get-tuple-element.80), channel_id=1, source_target_pairs={{0,2},{1,3},{2,0},{3,1},{4,6},{5,7},{6,4},{7,5},{8,10},{9,11},{10,... | collective-permute-start | bytes 196616 | tf_op jit(solution)/shard_map/ppermute | solution.py:34
  80.8 5.2 %collective-permute-start.16 = (bf16[8,32,128]{2,1,0:T(8,128)(2,1)S(1)}, bf16[8,32,128]{2,1,0:T(8,128)(2,1)S(1)}, u32[]{:S(2)}, u32[]{:S(2)}) collective-permute-start(bf16[8,32,128]{2,1,0:T(8,128)(2,1)S(1)} %get-tuple-element.81), channel_id=1, source_target_pairs={{0,3},{1,2},{2,1},{3,0},{4,7},{5,6},{6,5},{7,4},{8,11},{9,10},{10,... | collective-permute-start | bytes 196616 | tf_op jit(solution)/shard_map/ppermute | solution.py:34
  86.1 5.5 %collective-permute-start.17 = (bf16[8,32,128]{2,1,0:T(8,128)(2,1)S(1)}, bf16[8,32,128]{2,1,0:T(8,128)(2,1)S(1)}, u32[]{:S(2)}, u32[]{:S(2)}) collective-permute-start(bf16[8,32,128]{2,1,0:T(8,128)(2,1)S(1)} %add_convert_fusion.6), channel_id=1, source_target_pairs={{0,4},{1,5},{2,6},{3,7},{4,0},{5,1},{6,2},{7,3},{8,12},{9,13},{10,... | collective-permute-start | bytes 196616 | tf_op jit(solution)/shard_map/ppermute | solution.py:34
  91.6 5.3 %collective-permute-start.20 = (bf16[8,32,128]{2,1,0:T(8,128)(2,1)S(1)}, bf16[8,32,128]{2,1,0:T(8,128)(2,1)S(1)}, u32[]{:S(2)}, u32[]{:S(2)}) collective-permute-start(bf16[8,32,128]{2,1,0:T(8,128)(2,1)S(1)} %multiply_convert_fusion.2.refs_0_), channel_id=1, source_target_pairs={{0,3},{1,2},{2,1},{3,0},{4,7},{5,6},{6,5},{7,4},{8,11},{9,10},{10,... | collective-permute-start | bytes 196616 | tf_op jit(solution)/shard_map/ppermute | solution.py:34
  93.2 4.7 %collective-permute-start.19 = (bf16[8,32,128]{2,1,0:T(8,128)(2,1)S(1)}, bf16[8,32,128]{2,1,0:T(8,128)(2,1)S(1)}, u32[]{:S(2)}, u32[]{:S(2)}) collective-permute-start(bf16[8,32,128]{2,1,0:T(8,128)(2,1)S(1)} %multiply_convert_fusion.2.refs_0_), channel_id=1, source_target_pairs={{0,2},{1,3},{2,0},{3,1},{4,6},{5,7},{6,4},{7,5},{8,10},{9,11},{10,... | collective-permute-start | bytes 196616 | tf_op jit(solution)/shard_map/ppermute | solution.py:34
  95.0 4.3 %collective-permute-start.18 = (bf16[8,32,128]{2,1,0:T(8,128)(2,1)S(1)}, bf16[8,32,128]{2,1,0:T(8,128)(2,1)S(1)}, u32[]{:S(2)}, u32[]{:S(2)}) collective-permute-start(bf16[8,32,128]{2,1,0:T(8,128)(2,1)S(1)} %multiply_convert_fusion.2.refs_0_), channel_id=1, source_target_pairs={{0,1},{1,0},{2,3},{3,2},{4,5},{5,4},{6,7},{7,6},{8,9},{9,8},{10,11... | collective-permute-start | bytes 196616 | tf_op jit(solution)/shard_map/ppermute | solution.py:34
  102.4 1.5 collective-permute-start.21
  104.0 7.5 %collective-permute-start.22 = (bf16[24,32,128]{2,1,0:T(8,128)(2,1)S(1)}, bf16[24,32,128]{2,1,0:T(8,128)(2,1)S(1)}, u32[]{:S(2)}, u32[]{:S(2)}) collective-permute-start(bf16[24,32,128]{2,1,0:T(8,128)(2,1)S(1)} %add_convert_fusion.2.mine), channel_id=1, source_target_pairs={{0,16},{1,17},{2,18},{3,19},{4,20},{5,21},{6,22},{7,23},{8,24},{9,... | collective-permute-start | bytes 589832 | tf_op jit(solution)/shard_map/ppermute | solution.py:34
  114.0 1.5 collective-permute-start.23
  114.1 1.4 collective-permute-start.24
  117.5 7.2 %collective-permute-start.25 = (bf16[24,32,128]{2,1,0:T(8,128)(2,1)S(1)}, bf16[24,32,128]{2,1,0:T(8,128)(2,1)S(1)}, u32[]{:S(2)}, u32[]{:S(2)}) collective-permute-start(bf16[24,32,128]{2,1,0:T(8,128)(2,1)S(1)} %prior_spread.6.refs_0_), channel_id=1, source_target_pairs={{0,8},{1,9},{2,10},{3,11},{4,12},{5,13},{6,14},{7,15},{8,0},{9,1},... | collective-permute-start | bytes 589832 | tf_op jit(solution)/shard_map/ppermute | solution.py:34
  128.0 5.3 %collective-permute-start.26 = (bf16[8,32,128]{2,1,0:T(8,128)(2,1)S(1)}, bf16[8,32,128]{2,1,0:T(8,128)(2,1)S(1)}, u32[]{:S(2)}, u32[]{:S(2)}) collective-permute-start(bf16[8,32,128]{2,1,0:T(8,128)(2,1)S(1)} %get-tuple-element.88), channel_id=1, source_target_pairs={{0,1},{1,0},{2,3},{3,2},{4,5},{5,4},{6,7},{7,6},{8,9},{9,8},{10,11... | collective-permute-start | bytes 196616 | tf_op jit(solution)/shard_map/ppermute | solution.py:34
  131.0 4.3 %collective-permute-start.27 = (bf16[8,32,128]{2,1,0:T(8,128)(2,1)S(1)}, bf16[8,32,128]{2,1,0:T(8,128)(2,1)S(1)}, u32[]{:S(2)}, u32[]{:S(2)}) collective-permute-start(bf16[8,32,128]{2,1,0:T(8,128)(2,1)S(1)} %get-tuple-element.89), channel_id=1, source_target_pairs={{0,2},{1,3},{2,0},{3,1},{4,6},{5,7},{6,4},{7,5},{8,10},{9,11},{10,... | collective-permute-start | bytes 196616 | tf_op jit(solution)/shard_map/ppermute | solution.py:34
  131.0 5.2 %collective-permute-start.28 = (bf16[8,32,128]{2,1,0:T(8,128)(2,1)S(1)}, bf16[8,32,128]{2,1,0:T(8,128)(2,1)S(1)}, u32[]{:S(2)}, u32[]{:S(2)}) collective-permute-start(bf16[8,32,128]{2,1,0:T(8,128)(2,1)S(1)} %get-tuple-element.90), channel_id=1, source_target_pairs={{0,3},{1,2},{2,1},{3,0},{4,7},{5,6},{6,5},{7,4},{8,11},{9,10},{10,... | collective-permute-start | bytes 196616 | tf_op jit(solution)/shard_map/ppermute | solution.py:34
  136.2 5.4 %collective-permute-start.29 = (bf16[8,32,128]{2,1,0:T(8,128)(2,1)S(1)}, bf16[8,32,128]{2,1,0:T(8,128)(2,1)S(1)}, u32[]{:S(2)}, u32[]{:S(2)}) collective-permute-start(bf16[8,32,128]{2,1,0:T(8,128)(2,1)S(1)} %add_convert_fusion.5), channel_id=1, source_target_pairs={{0,4},{1,5},{2,6},{3,7},{4,0},{5,1},{6,2},{7,3},{8,12},{9,13},{10,... | collective-permute-start | bytes 196616 | tf_op jit(solution)/shard_map/ppermute | solution.py:34
  141.7 5.3 %collective-permute-start.32 = (bf16[8,32,128]{2,1,0:T(8,128)(2,1)S(1)}, bf16[8,32,128]{2,1,0:T(8,128)(2,1)S(1)}, u32[]{:S(2)}, u32[]{:S(2)}) collective-permute-start(bf16[8,32,128]{2,1,0:T(8,128)(2,1)S(1)} %multiply_convert_fusion.1.refs_0_), channel_id=1, source_target_pairs={{0,3},{1,2},{2,1},{3,0},{4,7},{5,6},{6,5},{7,4},{8,11},{9,10},{10,... | collective-permute-start | bytes 196616 | tf_op jit(solution)/shard_map/ppermute | solution.py:34
  143.4 4.7 %collective-permute-start.31 = (bf16[8,32,128]{2,1,0:T(8,128)(2,1)S(1)}, bf16[8,32,128]{2,1,0:T(8,128)(2,1)S(1)}, u32[]{:S(2)}, u32[]{:S(2)}) collective-permute-start(bf16[8,32,128]{2,1,0:T(8,128)(2,1)S(1)} %multiply_convert_fusion.1.refs_0_), channel_id=1, source_target_pairs={{0,2},{1,3},{2,0},{3,1},{4,6},{5,7},{6,4},{7,5},{8,10},{9,11},{10,... | collective-permute-start | bytes 196616 | tf_op jit(solution)/shard_map/ppermute | solution.py:34
  145.1 4.3 %collective-permute-start.30 = (bf16[8,32,128]{2,1,0:T(8,128)(2,1)S(1)}, bf16[8,32,128]{2,1,0:T(8,128)(2,1)S(1)}, u32[]{:S(2)}, u32[]{:S(2)}) collective-permute-start(bf16[8,32,128]{2,1,0:T(8,128)(2,1)S(1)} %multiply_convert_fusion.1.refs_0_), channel_id=1, source_target_pairs={{0,1},{1,0},{2,3},{3,2},{4,5},{5,4},{6,7},{7,6},{8,9},{9,8},{10,11... | collective-permute-start | bytes 196616 | tf_op jit(solution)/shard_map/ppermute | solution.py:34
  152.5 1.5 collective-permute-start.33
  154.1 7.8 %collective-permute-start.34 = (bf16[24,32,128]{2,1,0:T(8,128)(2,1)S(1)}, bf16[24,32,128]{2,1,0:T(8,128)(2,1)S(1)}, u32[]{:S(2)}, u32[]{:S(2)}) collective-permute-start(bf16[24,32,128]{2,1,0:T(8,128)(2,1)S(1)} %add_convert_fusion.1.mine), channel_id=1, source_target_pairs={{0,16},{1,17},{2,18},{3,19},{4,20},{5,21},{6,22},{7,23},{8,24},{9,... | collective-permute-start | bytes 589832 | tf_op jit(solution)/shard_map/ppermute | solution.py:34
  164.5 1.5 collective-permute-start.35
  164.5 1.4 collective-permute-start.36
  167.9 7.2 %collective-permute-start.37 = (bf16[24,32,128]{2,1,0:T(8,128)(2,1)S(1)}, bf16[24,32,128]{2,1,0:T(8,128)(2,1)S(1)}, u32[]{:S(2)}, u32[]{:S(2)}) collective-permute-start(bf16[24,32,128]{2,1,0:T(8,128)(2,1)S(1)} %prior_spread.7.refs_0_), channel_id=1, source_target_pairs={{0,8},{1,9},{2,10},{3,11},{4,12},{5,13},{6,14},{7,15},{8,0},{9,1},... | collective-permute-start | bytes 589832 | tf_op jit(solution)/shard_map/ppermute | solution.py:34
  178.2 5.3 %collective-permute-start.38 = (bf16[8,32,128]{2,1,0:T(8,128)(2,1)S(1)}, bf16[8,32,128]{2,1,0:T(8,128)(2,1)S(1)}, u32[]{:S(2)}, u32[]{:S(2)}) collective-permute-start(bf16[8,32,128]{2,1,0:T(8,128)(2,1)S(1)} %get-tuple-element.97), channel_id=1, source_target_pairs={{0,1},{1,0},{2,3},{3,2},{4,5},{5,4},{6,7},{7,6},{8,9},{9,8},{10,11... | collective-permute-start | bytes 196616 | tf_op jit(solution)/shard_map/ppermute | solution.py:34
  181.2 4.3 %collective-permute-start.39 = (bf16[8,32,128]{2,1,0:T(8,128)(2,1)S(1)}, bf16[8,32,128]{2,1,0:T(8,128)(2,1)S(1)}, u32[]{:S(2)}, u32[]{:S(2)}) collective-permute-start(bf16[8,32,128]{2,1,0:T(8,128)(2,1)S(1)} %get-tuple-element.98), channel_id=1, source_target_pairs={{0,2},{1,3},{2,0},{3,1},{4,6},{5,7},{6,4},{7,5},{8,10},{9,11},{10,... | collective-permute-start | bytes 196616 | tf_op jit(solution)/shard_map/ppermute | solution.py:34
  181.2 5.2 %collective-permute-start.40 = (bf16[8,32,128]{2,1,0:T(8,128)(2,1)S(1)}, bf16[8,32,128]{2,1,0:T(8,128)(2,1)S(1)}, u32[]{:S(2)}, u32[]{:S(2)}) collective-permute-start(bf16[8,32,128]{2,1,0:T(8,128)(2,1)S(1)} %get-tuple-element.99), channel_id=1, source_target_pairs={{0,3},{1,2},{2,1},{3,0},{4,7},{5,6},{6,5},{7,4},{8,11},{9,10},{10,... | collective-permute-start | bytes 196616 | tf_op jit(solution)/shard_map/ppermute | solution.py:34
  186.4 5.2 %collective-permute-start.41 = (bf16[8,32,128]{2,1,0:T(8,128)(2,1)S(1)}, bf16[8,32,128]{2,1,0:T(8,128)(2,1)S(1)}, u32[]{:S(2)}, u32[]{:S(2)}) collective-permute-start(bf16[8,32,128]{2,1,0:T(8,128)(2,1)S(1)} %add_convert_fusion.4), channel_id=1, source_target_pairs={{0,4},{1,5},{2,6},{3,7},{4,0},{5,1},{6,2},{7,3},{8,12},{9,13},{10,... | collective-permute-start | bytes 196616 | tf_op jit(solution)/shard_map/ppermute | solution.py:34
  191.7 5.2 %collective-permute-start.44 = (bf16[8,32,128]{2,1,0:T(8,128)(2,1)S(1)}, bf16[8,32,128]{2,1,0:T(8,128)(2,1)S(1)}, u32[]{:S(2)}, u32[]{:S(2)}) collective-permute-start(bf16[8,32,128]{2,1,0:T(8,128)(2,1)S(1)} %multiply_convert_fusion.refs_0_), channel_id=1, source_target_pairs={{0,3},{1,2},{2,1},{3,0},{4,7},{5,6},{6,5},{7,4},{8,11},{9,10},{10,... | collective-permute-start | bytes 196616 | tf_op jit(solution)/shard_map/ppermute | solution.py:34
  193.4 4.8 %collective-permute-start.43 = (bf16[8,32,128]{2,1,0:T(8,128)(2,1)S(1)}, bf16[8,32,128]{2,1,0:T(8,128)(2,1)S(1)}, u32[]{:S(2)}, u32[]{:S(2)}) collective-permute-start(bf16[8,32,128]{2,1,0:T(8,128)(2,1)S(1)} %multiply_convert_fusion.refs_0_), channel_id=1, source_target_pairs={{0,2},{1,3},{2,0},{3,1},{4,6},{5,7},{6,4},{7,5},{8,10},{9,11},{10,... | collective-permute-start | bytes 196616 | tf_op jit(solution)/shard_map/ppermute | solution.py:34
  195.3 4.3 %collective-permute-start.42 = (bf16[8,32,128]{2,1,0:T(8,128)(2,1)S(1)}, bf16[8,32,128]{2,1,0:T(8,128)(2,1)S(1)}, u32[]{:S(2)}, u32[]{:S(2)}) collective-permute-start(bf16[8,32,128]{2,1,0:T(8,128)(2,1)S(1)} %multiply_convert_fusion.refs_0_), channel_id=1, source_target_pairs={{0,1},{1,0},{2,3},{3,2},{4,5},{5,4},{6,7},{7,6},{8,9},{9,8},{10,11... | collective-permute-start | bytes 196616 | tf_op jit(solution)/shard_map/ppermute | solution.py:34
  202.7 1.5 collective-permute-start.45
  204.3 7.8 %collective-permute-start.46 = (bf16[24,32,128]{2,1,0:T(8,128)(2,1)S(1)}, bf16[24,32,128]{2,1,0:T(8,128)(2,1)S(1)}, u32[]{:S(2)}, u32[]{:S(2)}) collective-permute-start(bf16[24,32,128]{2,1,0:T(8,128)(2,1)S(1)} %add_convert_fusion.mine), channel_id=1, source_target_pairs={{0,16},{1,17},{2,18},{3,19},{4,20},{5,21},{6,22},{7,23},{8,24},{9,... | collective-permute-start | bytes 589832 | tf_op jit(solution)/shard_map/ppermute | solution.py:34
  212.1 11.5 %copy-start.1 = (f32[32,128]{1,0:T(8,128)S(1)}, f32[32,128]{1,0:T(8,128)}, u32[]{:S(2)}) copy-start(f32[32,128]{1,0:T(8,128)} %param.15) | copy-start | bytes 49156
  214.7 2.2 collective-permute-start.47
  215.4 2.6 %collective-permute-start.48 = (bf16[24,32,128]{2,1,0:T(8,128)(2,1)S(1)}, bf16[24,32,128]{2,1,0:T(8,128)(2,1)S(1)}, u32[]{:S(2)}, u32[]{:S(2)}) collective-permute-start(bf16[24,32,128]{2,1,0:T(8,128)(2,1)S(1)} %get-tuple-element.104), channel_id=1, source_target_pairs={{0,8},{1,9},{2,10},{3,11},{4,12},{5,13},{6,14},{7,15},{8,0},{9,1},... | collective-permute-start | bytes 589832 | tf_op jit(solution)/shard_map/ppermute | solution.py:34
  218.1 4.7 %collective-permute-start.49 = (bf16[24,32,128]{2,1,0:T(8,128)(2,1)S(1)}, bf16[24,32,128]{2,1,0:T(8,128)(2,1)S(1)}, u32[]{:S(2)}, u32[]{:S(2)}) collective-permute-start(bf16[24,32,128]{2,1,0:T(8,128)(2,1)S(1)} %fusion.2), channel_id=1, source_target_pairs={{0,8},{1,9},{2,10},{3,11},{4,12},{5,13},{6,14},{7,15},{8,0},{9,1},... | collective-permute-start | bytes 589832 | tf_op jit(solution)/shard_map/ppermute | solution.py:34

commit v5 on v4

--- a/solution.py
+++ b/solution.py
@@ -1,4 +1,5 @@
 import functools
+import math
 
 import jax
 import jax.numpy as jnp
@@ -13,6 +14,7 @@
 VMEM_LIMIT = 8 * 2**20
 GROUP = 4
 ROUND = 24
+LANES = 128
 
 
 def matmul(a, b):
@@ -34,84 +36,153 @@
     return lax.ppermute(value, ("obs", "flux"), route)
 
 
-def plan_groups(src, dst, src_rows, dst_rows):
-    passes, blocks = dst.shape
-    groups = blocks // GROUP + dst_rows
+def plan_sizes(blocks, dst_rows):
+    groups = (blocks + -blocks % LANES) // GROUP + dst_rows
     groups += -groups % ROUND
     slots = groups * GROUP
+    return slots + -slots % LANES, groups + 1 + -(groups + 1) % LANES
+
+
+def columns(row):
+    parts = [
+        jnp.broadcast_to(row[:, k : k + LANES], (LANES, LANES)).T for k in range(0, row.shape[1], LANES)
+    ]
+    return jnp.concatenate(parts, axis=0)
+
+
+def plan_groups(src, dst, rows, out):
+    blocks = dst.shape[1]
+    slots, groups = plan_sizes(blocks, rows)
     i32 = jnp.int32
-    at = jnp.arange(blocks, dtype=i32)
-    rows = jnp.arange(dst_rows, dtype=i32)
-    same = (dst[:, :, None] == dst[:, None, :]) & (at[None, :] < at[:, None])
-    rank = jnp.sum(same.astype(i32), axis=2)
-    member = (dst[:, None, :] == rows[:, None]).astype(i32)
-    fills = (jnp.sum(member, axis=2) + GROUP - 1) // GROUP
-    begin = jnp.sum(jnp.where(rows[None, :] < rows[:, None], fills[:, None, :], 0), axis=2)
-    place = jnp.sum(member * begin[:, :, None], axis=1) * GROUP + rank
-    place = jnp.where(dst < dst_rows, place, slots)
-    hit = place[:, None, :] == jnp.arange(slots, dtype=i32)[:, None]
-    src_of = jnp.sum(jnp.where(hit, (src - src_rows)[:, None, :], 0), axis=2) + src_rows
-    block_of = jnp.sum(jnp.where(hit, at, 0), axis=2)
-    lead = place[:, None, :] == jnp.arange(groups, dtype=i32)[:, None] * GROUP
-    dst_of = jnp.sum(jnp.where(lead, (dst - dst_rows)[:, None, :], 0), axis=2) + dst_rows
-    rounds = (jnp.sum(fills, axis=1, keepdims=True) + ROUND - 1) // ROUND
-    return jnp.concatenate([src_of, block_of, dst_of, rounds], axis=1)
-
-
-def setup_kernel(chunk, first, source, plain, turned, sems):
-    begin = first[0]
-
-    def copy(c):
-        at = pl.ds(c * chunk, chunk)
-        rows = pl.ds(begin + c * chunk, chunk)
-        return pltpu.make_async_copy(source.at[rows], plain.at[at], sems.at[c])
-
-    def start(c, _):
-        copy(c).start()
-        return 0
-
-    def turn(c, _):
-        copy(c).wait()
-        for u in range(chunk):
-            turned[c * chunk + u] = plain[c * chunk + u].T
-        return 0
-
-    lax.fori_loop(0, plain.shape[0] // chunk, start, 0)
-    lax.fori_loop(0, plain.shape[0] // chunk, turn, 0)
-
-
-def setup_blocks(first, count, source, name):
-    shape = (count,) + source.shape[1:]
-    chunk = chunk_of(count, 24)
+    lane = lax.broadcasted_iota(i32, (blocks, LANES), 1)
+    at = lax.broadcasted_iota(i32, (blocks, LANES), 0)
+    src_at, dst_at = columns(src), columns(dst)
+    rank = jnp.zeros((blocks, LANES), F32)
+    for k in range(0, blocks, LANES):
+        same = (dst_at == dst[:, k : k + LANES]) & (lane + k < at)
+        rank += same.astype(F32)
+    rank = jnp.sum(rank, axis=1, keepdims=True)
+    fills = jnp.sum((dst_at == lane).astype(F32), axis=0, keepdims=True)
+    sizes = jnp.where(lane[:1] < rows, jnp.floor((fills + (GROUP - 1)) * (1.0 / GROUP)), 0.0)
+    begin = jnp.sum(jnp.where(lane < dst_at, sizes, 0.0), axis=1, keepdims=True)
+    place = (begin * GROUP + rank).astype(i32)
+    place = jnp.where(dst_at < rows, place, slots)
+    for k in range(0, slots, LANES):
+        hit = place == lane + k
+        of = jnp.sum(jnp.where(hit, (src_at - rows).astype(F32), 0.0), axis=0, keepdims=True)
+        out[:, k : k + LANES] = of.astype(i32) + rows
+        of = jnp.sum(jnp.where(hit, at.astype(F32), 0.0), axis=0, keepdims=True)
+        out[:, slots + k : slots + k + LANES] = of.astype(i32)
+    full = jnp.sum(sizes, axis=1, keepdims=True)
+    rounds = jnp.sum((lane[:1].astype(F32) * ROUND < full).astype(F32), axis=1, keepdims=True)
+    for k in range(0, groups, LANES):
+        lead = place == (lane + k) * GROUP
+        of = jnp.sum(jnp.where(lead, (dst_at - rows).astype(F32), 0.0), axis=0, keepdims=True)
+        of = jnp.where(lane[:1] + k == groups - 1, rounds, of + rows)
+        out[:, 2 * slots + k : 2 * slots + k + LANES] = of.astype(i32)
+
+
+def setup_kernel(
+    rows, chunk, where, obs, flux, nbr, prior, jac,
+    prior_plain, prior_turned, jac_plain, jac_turned, obs_plan, tile_plan, prior_plan, sems
+):
+    side, corner, count = where[0], where[1], where[2]
+    begin = side * prior_plain.shape[0]
+    rounds = (prior_plain.shape[0] // chunk, jac_plain.shape[0] // chunk)
+
+    def copy(c, first, source, plain, offset):
+        to = pl.ds(c * chunk, chunk)
+        return pltpu.make_async_copy(source.at[pl.ds(first + c * chunk, chunk)], plain.at[to], sems.at[offset + c])
+
+    def start(first, source, plain, offset):
+        def one(c, _):
+            copy(c, first, source, plain, offset).start()
+            return 0
+
+        return one
+
+    def turn(first, source, plain, turned, offset):
+        def one(c, _):
+            copy(c, first, source, plain, offset).wait()
+            for u in range(chunk):
+                turned[c * chunk + u] = plain[c * chunk + u].T
+            return 0
+
+        return one
+
+    lax.fori_loop(0, rounds[0], start(begin, prior, prior_plain, 0), 0)
+    lax.fori_loop(0, rounds[1], start(0, jac, jac_plain, rounds[0]), 0)
+
+    blocks = obs.shape[1]
+    obs_rows, tile_rows, fan = rows
+    half = tile_rows // 2
+    quarter = obs_rows // 4
+    most = max(obs_rows, tile_rows)
+    i32 = jnp.int32
+    at = lax.broadcasted_iota(i32, (1, blocks), 1)
+    live = at < count
+    block = sum((obs[...] >= k * quarter).astype(i32) for k in range(1, 4))
+    obs_at = (block ^ corner) * quarter + obs[...] - block * quarter
+    block = (flux[...] >= half).astype(i32)
+    tile_at = (block ^ side) * half + flux[...] - block * half
+    plan_groups(tile_at, jnp.where(live, obs_at, most), most, obs_plan)
+    plan_groups(obs_at, jnp.where(live, tile_at, most), most, tile_plan)
+    at = lax.broadcasted_iota(i32, nbr.shape, 1)
+    tile = sum((at >= k * fan).astype(i32) for k in range(1, half))
+    plan_groups(tile, nbr[...], most, prior_plan)
+
+    lax.fori_loop(0, rounds[0], turn(begin, prior, prior_plain, prior_turned, 0), 0)
+    lax.fori_loop(0, rounds[1], turn(0, jac, jac_plain, jac_turned, rounds[0]), 0)
+
+
+def setup(where, obs, flux, nbr, prior, jac, rows):
+    most = max(rows[:2])
+    tiles = rows[1] // 2 * rows[2]
+    chunk = chunk_of(math.gcd(tiles, jac.shape[0]), 24)
+    smem = pl.BlockSpec(memory_space=pltpu.SMEM)
     vmem = pl.BlockSpec(memory_space=pltpu.VMEM)
+    hbm = pl.BlockSpec(memory_space=pl.ANY)
+    own = pltpu.VMEM((tiles,) + prior.shape[1:], HALF)
+    all_blocks = pltpu.VMEM(jac.shape, HALF)
+    plans = []
+    for width in (obs.shape[1], obs.shape[1], nbr.shape[1]):
+        slots, groups = plan_sizes(width, most)
+        plans.append(jax.ShapeDtypeStruct((1, 2 * slots + groups), jnp.int32))
     return pl.pallas_call(
-        functools.partial(setup_kernel, chunk),
-        in_specs=[pl.BlockSpec(memory_space=pltpu.SMEM), pl.BlockSpec(memory_space=pl.ANY)],
-        out_specs=[vmem, vmem],
-        out_shape=[pltpu.VMEM(shape, HALF), pltpu.VMEM(shape, HALF)],
-        scratch_shapes=[pltpu.SemaphoreType.DMA((count // chunk,))],
+        functools.partial(setup_kernel, rows, chunk),
+        in_specs=[smem, vmem, vmem, vmem, hbm, hbm],
+        out_specs=[vmem] * 7,
+        out_shape=[own, own, all_blocks, all_blocks] + plans,
+        scratch_shapes=[pltpu.SemaphoreType.DMA(((tiles + jac.shape[0]) // chunk,))],
         compiler_params=pltpu.CompilerParams(vmem_limit_bytes=VMEM_LIMIT),
-        name=name,
-    )(first, pltpu.with_memory_space_constraint(source, pltpu.HBM))
+        name="setup",
+    )(
+        where,
+        obs,
+        flux,
+        nbr,
+        pltpu.with_memory_space_constraint(prior, pltpu.HBM),
+        pltpu.with_memory_space_constraint(jac, pltpu.HBM),
+    )
 
 
 def grouped_products(plan, x, blocks, total):
-    slots = (plan.shape[0] - 1) // (2 * GROUP + 1) * GROUP
+    slots, groups = plan_sizes(blocks.shape[0], x.shape[0] - 1)
     total[...] = jnp.zeros_like(total)
 
     def one(c, _):
         products = []
         for u in range(ROUND):
             first = (c * ROUND + u) * GROUP
-            rows = [x[plan[first + g]] for g in range(GROUP)]
-            tiles = [blocks[plan[slots + first + g]] for g in range(GROUP)]
+            rows = [x[plan[0, first + g]] for g in range(GROUP)]
+            tiles = [blocks[plan[0, slots + first + g]] for g in range(GROUP)]
             left = jnp.concatenate(rows, axis=1)
             products.append(matmul(left, jnp.concatenate(tiles, axis=0)))
         for u in range(ROUND):
-            total[plan[2 * slots + c * ROUND + u]] += products[u]
+            total[plan[0, 2 * slots + c * ROUND + u]] += products[u]
         return 0
 
-    lax.fori_loop(0, plan[plan.shape[0] - 1], one, 0)
+    lax.fori_loop(0, plan[0, 2 * slots + groups - 1], one, 0)
 
 
 def jac_kernel(n_parts, n_outs, plan, *refs):
@@ -237,10 +308,6 @@
     corner = lax.rem(flux_at, 4)
     core = side.reshape(1)
 
-    live = jnp.arange(blocks.shape[0], dtype=jnp.int32) < counts[0, 0]
-    obs_all, flux_all = jac_obs[0, 0], jac_flux[0, 0]
-    obs_at = ((obs_all // quarter) ^ corner) * quarter + obs_all % quarter
-    tile_at = ((flux_all // half) ^ side) * half + flux_all % half
     own_rinv = lax.dynamic_slice_in_dim(rinv, corner * quarter, quarter, 0)[:, None, :]
     first_tile = flux_at * tile_count + side * half
     own_nbr = lax.dynamic_slice_in_dim(neighbours, side * half, half, 0)
@@ -249,24 +316,6 @@
     prior = prior_tiles.reshape((tile_count * fan,) + prior_tiles.shape[2:])
 
     rows = max(obs_rows, tile_count)
-    count = max(blocks.shape[0], half * fan)
-
-    def fill(value, more):
-        return jnp.pad(value, (0, count - value.shape[0]), constant_values=more)
-
-    prior_src = jnp.arange(half * fan, dtype=jnp.int32) // fan
-    plans = plan_groups(
-        jnp.stack([fill(tile_at, 0), fill(obs_at, 0), fill(prior_src, 0)]),
-        jnp.stack(
-            [
-                fill(jnp.where(live, obs_at, rows), rows),
-                fill(jnp.where(live, tile_at, rows), rows),
-                fill(nbr, rows),
-            ]
-        ),
-        rows,
-        rows,
-    )
 
     def swap_core(value):
         return exchange(value, lambda i, j: (i ^ 1, j))
@@ -286,13 +335,17 @@
     around = jnp.concatenate([beyond, probes, beyond], axis=0)
     field = lax.dynamic_slice_in_dim(around, side * half, 2 * half, 0)
 
-    core, begin, nbr, obs_plan, tile_plan, prior_plan, own_rinv, field, blocks, prior = (
-        lax.optimization_barrier(
-            (core, core * (half * fan), nbr, plans[0], plans[1], plans[2], own_rinv, field, blocks, prior)
-        )
+    where = jnp.stack([side, corner, counts[0, 0]])
+    width = nbr.shape[0] + -nbr.shape[0] % LANES
+    nbr_row = jnp.pad(nbr, (0, width - nbr.shape[0]), constant_values=rows).reshape(1, width)
+    sizes = (obs_rows, tile_count, fan)
+
+    core, nbr, nbr_row, where, own_rinv, field, prior, blocks = lax.optimization_barrier(
+        (core, nbr, nbr_row, where, own_rinv, field, prior, blocks)
     )
-    prior_plain, prior_turned = setup_blocks(begin, half * fan, prior, "prior_setup")
-    jac_plain, jac_turned = setup_blocks(begin * 0, blocks.shape[0], blocks, "jac_setup")
+    prior_plain, prior_turned, jac_plain, jac_turned, obs_plan, tile_plan, prior_plan = setup(
+        where, jac_obs[0], jac_flux[0], nbr_row, prior, blocks, sizes
+    )
     fields = (field,)
     for step in range(STEPS):
         spread = spread_tiles(core, nbr, fields, prior_plain)
@@ -317,11 +370,14 @@
             if bits < n_obs:
                 mine = (mine.astype(F32) + other.astype(F32)).astype(HALF)
         ext, to_core, to_far = gather_tiles(core, prior_plan, mine, other, prior_turned, rows, rows)
-        fields = (ext, swap_core(to_core), swap_far(to_far))
-    ext, from_core, from_far = fields
-    low = jnp.where(side == 0, from_far, from_core).astype(F32)
-    high = jnp.where(side == 0, from_core, from_far).astype(F32)
-    own = (ext + jnp.concatenate([low, high], axis=0))[reach : reach + half].astype(HALF)
+        if step < STEPS - 1:
+            fields = (ext, swap_core(to_core), swap_far(to_far))
+    lower = side == 0
+    from_core = swap_core(jnp.where(lower, to_core[half - reach :], to_core[:reach])).astype(F32)
+    from_far = swap_far(jnp.where(lower, to_far[:reach], to_far[half - reach :])).astype(F32)
+    low = jnp.where(lower, from_far, from_core)
+    high = jnp.where(lower, from_core, from_far)
+    own = (ext[reach : reach + half] + jnp.concatenate([low, high], axis=0)).astype(HALF)
     other = swap_core(own)
     first = jnp.where(side == 0, own, other)
     second = jnp.where(side == 0, other, own)

time: 226 us -> 221 us (0.978); the launches traced: 224 us -> 221 us
  waiting for transfers between devices: 77.9 us -> 87.1 us
  other arithmetic: 9.71 us -> 4.38 us
  Pallas kernels: 52 us -> 46.8 us
    ppermute x50, waiting for transfers between devices: 77.9 us -> 87.1 us  [exchange(): return lax.ppermute(value, ('obs', 'flux'), route)]
    pallas_call x8, Pallas kernels: 25.3 us -> 20.6 us  [jac_pass(): pl.pallas_call(functools.partial(jac_kernel, len(parts), n_outs), in_spec...]
    reduce_sum x7 -> x0, other arithmetic: 2.47 us -> none  [the longest x1 1.01 us: plan_groups(): block_of = jnp.sum(jnp.where(hit, at, 0), axis=2)]
    pallas_call x2 -> x1, Pallas kernels: 8.69 us -> 8.39 us  [setup(): pl.pallas_call(functools.partial(setup_kernel, rows, chunk), in_specs=[sm...]
  transfers between devices with their start and end apart: 50 -> 50, of which waited for: 44 -> 41; matrix products, arithmetic and copies ran while one was open for 3% -> 0% of each run, Pallas kernels for 2% -> 0%
where the time goes in v5:
time: 221 us
  waiting for transfers between devices  87.1 us (39%)
  starting transfers between devices  80.4 us (36%)
  Pallas kernels  46.8 us (21%)
  other arithmetic  4.38 us (2%)
    ppermute x50, waiting for transfers between devices, exchange(): return lax.ppermute(value, ('obs', 'flux'), route)  87.1 us
    ppermute x50, starting transfers between devices, exchange(): return lax.ppermute(value, ('obs', 'flux'), route)  80.4 us
    pallas_call x8, Pallas kernels, jac_pass(): pl.pallas_call(functools.partial(jac_kernel, len(parts), n_outs), in_spec...  20.6 us
    pallas_call x4, Pallas kernels, gather_tiles(): pl.pallas_call(functools.partial(gather_kernel, src_rows), in_specs=[smem...  10.4 us
    pallas_call x1, Pallas kernels, setup(): pl.pallas_call(functools.partial(setup_kernel, rows, chunk), in_specs=[sm...  8.39 us
    pallas_call x4, Pallas kernels, spread_tiles(): pl.pallas_call(functools.partial(spread_kernel, summed, nbr.shape[0] // t...  7.47 us
  transfers between devices with their start and end apart: 50, of which 41 were waited for; matrix products, arithmetic and copies ran while one was open for 0% of the time, Pallas kernels for 0%

profile of v5, /device:TPU:0, one launch (start us, length us, event | category | flops | bytes accessed | tf_op | source)
XLA Modules:
  0.0 221.3 jit_solution(7336468489469243804)
XLA Ops:
  5.9 8.4 %setup.1 = (bf16[192,128,128]{2,1,0:T(8,128)(2,1)S(1)}, bf16[192,128,128]{2,1,0:T(8,128)(2,1)S(1)}, bf16[384,128,128]{2,1,0:T(8,128)(2,1)S(1)}, bf16[384,128,128...) custom-call(s32[3]{0:T(128)S(1)} %pad_add_fusion.where, ...), custom_call_target="tpu_custom_call" | custom-call | tf_op jit(solution)/shard_map/setup/pallas_call | solution.py:151
  14.3 1.8 prior_spread.4.refs_0_
  16.2 4.9 %collective-permute-start.1 = (bf16[24,32,128]{2,1,0:T(8,128)(2,1)S(1)}, bf16[24,32,128]{2,1,0:T(8,128)(2,1)S(1)}, u32[]{:S(2)}, u32[]{:S(2)}) collective-permute-start(bf16[24,32,128]{2,1,0:T(8,128)(2,1)S(1)} %prior_spread.4.refs_0_), channel_id=1, source_target_pairs={{0,8},{1,9},{2,10},{3,11},{4,12},{5,13},{6,14},{7,15},{8,0},{9,1},... | collective-permute-start | bytes 589832 | tf_op jit(solution)/shard_map/ppermute | solution.py:36
  22.2 2.5 %jac_forward.4 = (f32[8,32,128]{2,1,0:T(8,128)S(1)}, bf16[8,32,128]{2,1,0:T(8,128)(2,1)S(1)}, bf16[8,32,128]{2,1,0:T(8,128)(2,1)S(1)}, bf16[8,32,128]{2,1,0:T(8,128)(2,1)S(1)}) custom-call(s32[1,1536]{1,0:T(1,128)S(1)} %get-tuple-element.63.plan, bf16[24,32,128]{2,1,0:T(8,128)(2,1)S(1)} %prior_spread.4.refs_0_, ...), custom_call_target="tpu_custom_call" | custom-call | tf_op jit(solution)/shard_map/jac_forward/pallas_call | solution.py:209
  24.7 2.5 %collective-permute-start.2 = (bf16[8,32,128]{2,1,0:T(8,128)(2,1)S(1)}, bf16[8,32,128]{2,1,0:T(8,128)(2,1)S(1)}, u32[]{:S(2)}, u32[]{:S(2)}) collective-permute-start(bf16[8,32,128]{2,1,0:T(8,128)(2,1)S(1)} %get-tuple-element.69), channel_id=1, source_target_pairs={{0,1},{1,0},{2,3},{3,2},{4,5},{5,4},{6,7},{7,6},{8,9},{9,8},{10,11... | collective-permute-start | bytes 196616 | tf_op jit(solution)/shard_map/ppermute | solution.py:36
  27.2 2.8 %collective-permute-start.3 = (bf16[8,32,128]{2,1,0:T(8,128)(2,1)S(1)}, bf16[8,32,128]{2,1,0:T(8,128)(2,1)S(1)}, u32[]{:S(2)}, u32[]{:S(2)}) collective-permute-start(bf16[8,32,128]{2,1,0:T(8,128)(2,1)S(1)} %get-tuple-element.70), channel_id=1, source_target_pairs={{0,2},{1,3},{2,0},{3,1},{4,6},{5,7},{6,4},{7,5},{8,10},{9,11},{10,... | collective-permute-start | bytes 196616 | tf_op jit(solution)/shard_map/ppermute | solution.py:36
  30.5 2.2 %collective-permute-done.3 = bf16[8,32,128]{2,1,0:T(8,128)(2,1)S(1)} collective-permute-done((bf16[8,32,128]{2,1,0:T(8,128)(2,1)S(1)}, bf16[8,32,128]{2,1,0:T(8,128)(2,1)S(1)}, u32[]{:S(2)}, u32[]{:S(2)}) %collective-permute-start.3) | collective-permute-done | bytes 65568 | tf_op jit(solution)/shard_map/ppermute | solution.py:36
  32.7 2.4 %collective-permute-done.4 = bf16[8,32,128]{2,1,0:T(8,128)(2,1)S(1)} collective-permute-done((bf16[8,32,128]{2,1,0:T(8,128)(2,1)S(1)}, bf16[8,32,128]{2,1,0:T(8,128)(2,1)S(1)}, u32[]{:S(2)}, u32[]{:S(2)}) %collective-permute-start.4) | collective-permute-done | bytes 65568 | tf_op jit(solution)/shard_map/ppermute | solution.py:36
  35.2 1.5 collective-permute-start.5
  36.7 4.4 %collective-permute-done.5 = bf16[8,32,128]{2,1,0:T(8,128)(2,1)S(1)} collective-permute-done((bf16[8,32,128]{2,1,0:T(8,128)(2,1)S(1)}, bf16[8,32,128]{2,1,0:T(8,128)(2,1)S(1)}, u32[]{:S(2)}, u32[]{:S(2)}) %collective-permute-start.5) | collective-permute-done | bytes 65568 | tf_op jit(solution)/shard_map/ppermute | solution.py:36
  42.2 1.5 collective-permute-start.7
  44.7 1.7 collective-permute-done.8.refs_3_
  48.0 2.6 %jac_adjoint.4 = (f32[24,32,128]{2,1,0:T(8,128)S(1)}, bf16[24,32,128]{2,1,0:T(8,128)(2,1)S(1)}) custom-call(s32[1,1536]{1,0:T(1,128)S(1)} %get-tuple-element.62.plan, bf16[8,32,128]{2,1,0:T(8,128)(2,1)S(1)} %multiply_convert_fusion.3.refs_0_, bf16[8,32,128]{2,1,0:T(8,128)(2,1)S(1)} %collective-permute-done.6.refs_1_, ...), custom_call_target="tpu_custom_call" | custom-call | tf_op jit(solution)/shard_map/jac_adjoint/pallas_call | solution.py:209
  50.7 1.4 collective-permute-done.9
  53.2 5.9 %collective-permute-done.10.other = bf16[24,32,128]{2,1,0:T(8,128)(2,1)S(1)} collective-permute-done((bf16[24,32,128]{2,1,0:T(8,128)(2,1)S(1)}, bf16[24,32,128]{2,1,0:T(8,128)(2,1)S(1)}, u32[]{:S(2)}, u32[]{:S(2)}) %collective-permute-start.10) | collective-permute-done | bytes 196640 | tf_op jit(solution)/shard_map/ppermute | solution.py:36
  59.2 2.6 %prior_adjoint.4 = (f32[48,32,128]{2,1,0:T(8,128)S(1)}, bf16[24,32,128]{2,1,0:T(8,128)(2,1)S(1)}, bf16[24,32,128]{2,1,0:T(8,128)(2,1)S(1)}) custom-call(s32[1]{0:T(128)} %bitcast.core, s32[1,1152]{1,0:T(1,128)S(1)} %get-tuple-element.61.plan, bf16[24,32,128]{2,1,0:T(8,128)(2,1)S(1)} %add_convert_fusion.3.mine, ...), custom_call_target="tpu_custom_call" | custom-call | tf_op jit(solution)/shard_map/prior_adjoint/pallas_call | solution.py:238
  63.3 1.9 prior_spread.5.refs_0_
  65.2 6.1 %collective-permute-start.13 = (bf16[24,32,128]{2,1,0:T(8,128)(2,1)S(1)}, bf16[24,32,128]{2,1,0:T(8,128)(2,1)S(1)}, u32[]{:S(2)}, u32[]{:S(2)}) collective-permute-start(bf16[24,32,128]{2,1,0:T(8,128)(2,1)S(1)} %prior_spread.5.refs_0_), channel_id=1, source_target_pairs={{0,8},{1,9},{2,10},{3,11},{4,12},{5,13},{6,14},{7,15},{8,0},{9,1},... | collective-permute-start | bytes 589832 | tf_op jit(solution)/shard_map/ppermute | solution.py:36
  72.3 2.5 %jac_forward.5 = (f32[8,32,128]{2,1,0:T(8,128)S(1)}, bf16[8,32,128]{2,1,0:T(8,128)(2,1)S(1)}, bf16[8,32,128]{2,1,0:T(8,128)(2,1)S(1)}, bf16[8,32,128]{2,1,0:T(8,128)(2,1)S(1)}) custom-call(s32[1,1536]{1,0:T(1,128)S(1)} %get-tuple-element.63.plan, bf16[24,32,128]{2,1,0:T(8,128)(2,1)S(1)} %prior_spread.5.refs_0_, ...), custom_call_target="tpu_custom_call" | custom-call | tf_op jit(solution)/shard_map/jac_forward/pallas_call | solution.py:209
  74.9 2.0 collective-permute-start.14
  76.9 3.2 %collective-permute-start.15 = (bf16[8,32,128]{2,1,0:T(8,128)(2,1)S(1)}, bf16[8,32,128]{2,1,0:T(8,128)(2,1)S(1)}, u32[]{:S(2)}, u32[]{:S(2)}) collective-permute-start(bf16[8,32,128]{2,1,0:T(8,128)(2,1)S(1)} %get-tuple-element.82), channel_id=1, source_target_pairs={{0,2},{1,3},{2,0},{3,1},{4,6},{5,7},{6,4},{7,5},{8,10},{9,11},{10,... | collective-permute-start | bytes 196616 | tf_op jit(solution)/shard_map/ppermute | solution.py:36
  82.7 2.5 %collective-permute-done.16 = bf16[8,32,128]{2,1,0:T(8,128)(2,1)S(1)} collective-permute-done((bf16[8,32,128]{2,1,0:T(8,128)(2,1)S(1)}, bf16[8,32,128]{2,1,0:T(8,128)(2,1)S(1)}, u32[]{:S(2)}, u32[]{:S(2)}) %collective-permute-start.16) | collective-permute-done | bytes 65568 | tf_op jit(solution)/shard_map/ppermute | solution.py:36
  86.6 3.9 %collective-permute-done.17 = bf16[8,32,128]{2,1,0:T(8,128)(2,1)S(1)} collective-permute-done((bf16[8,32,128]{2,1,0:T(8,128)(2,1)S(1)}, bf16[8,32,128]{2,1,0:T(8,128)(2,1)S(1)}, u32[]{:S(2)}, u32[]{:S(2)}) %collective-permute-start.17) | collective-permute-done | bytes 65568 | tf_op jit(solution)/shard_map/ppermute | solution.py:36
  90.5 1.6 collective-permute-start.20
  92.1 2.2 collective-permute-start.19
  94.3 1.5 collective-permute-done.20.refs_3_
  95.7 1.4 collective-permute-done.19.refs_2_
  98.5 2.6 %jac_adjoint.5 = (f32[24,32,128]{2,1,0:T(8,128)S(1)}, bf16[24,32,128]{2,1,0:T(8,128)(2,1)S(1)}) custom-call(s32[1,1536]{1,0:T(1,128)S(1)} %get-tuple-element.62.plan, bf16[8,32,128]{2,1,0:T(8,128)(2,1)S(1)} %multiply_convert_fusion.2.refs_0_, bf16[8,32,128]{2,1,0:T(8,128)(2,1)S(1)} %collective-permute-done.18.refs_1_, ...), custom_call_target="tpu_custom_call" | custom-call | tf_op jit(solution)/shard_map/jac_adjoint/pallas_call | solution.py:209
  101.2 1.4 collective-permute-done.21
  103.3 6.4 %collective-permute-done.22.other = bf16[24,32,128]{2,1,0:T(8,128)(2,1)S(1)} collective-permute-done((bf16[24,32,128]{2,1,0:T(8,128)(2,1)S(1)}, bf16[24,32,128]{2,1,0:T(8,128)(2,1)S(1)}, u32[]{:S(2)}, u32[]{:S(2)}) %collective-permute-start.22) | collective-permute-done | bytes 196640 | tf_op jit(solution)/shard_map/ppermute | solution.py:36
  109.7 2.6 %prior_adjoint.5 = (f32[48,32,128]{2,1,0:T(8,128)S(1)}, bf16[24,32,128]{2,1,0:T(8,128)(2,1)S(1)}, bf16[24,32,128]{2,1,0:T(8,128)(2,1)S(1)}) custom-call(s32[1]{0:T(128)} %bitcast.core, s32[1,1152]{1,0:T(1,128)S(1)} %get-tuple-element.61.plan, bf16[24,32,128]{2,1,0:T(8,128)(2,1)S(1)} %add_convert_fusion.2.mine, ...), custom_call_target="tpu_custom_call" | custom-call | tf_op jit(solution)/shard_map/prior_adjoint/pallas_call | solution.py:238
  113.8 1.9 prior_spread.6.refs_0_
  115.7 6.1 %collective-permute-start.25 = (bf16[24,32,128]{2,1,0:T(8,128)(2,1)S(1)}, bf16[24,32,128]{2,1,0:T(8,128)(2,1)S(1)}, u32[]{:S(2)}, u32[]{:S(2)}) collective-permute-start(bf16[24,32,128]{2,1,0:T(8,128)(2,1)S(1)} %prior_spread.6.refs_0_), channel_id=1, source_target_pairs={{0,8},{1,9},{2,10},{3,11},{4,12},{5,13},{6,14},{7,15},{8,0},{9,1},... | collective-permute-start | bytes 589832 | tf_op jit(solution)/shard_map/ppermute | solution.py:36
  122.8 2.5 %jac_forward.6 = (f32[8,32,128]{2,1,0:T(8,128)S(1)}, bf16[8,32,128]{2,1,0:T(8,128)(2,1)S(1)}, bf16[8,32,128]{2,1,0:T(8,128)(2,1)S(1)}, bf16[8,32,128]{2,1,0:T(8,128)(2,1)S(1)}) custom-call(s32[1,1536]{1,0:T(1,128)S(1)} %get-tuple-element.63.plan, bf16[24,32,128]{2,1,0:T(8,128)(2,1)S(1)} %prior_spread.6.refs_0_, ...), custom_call_target="tpu_custom_call" | custom-call | tf_op jit(solution)/shard_map/jac_forward/pallas_call | solution.py:209
  125.4 1.8 collective-permute-start.26
  127.2 2.9 %collective-permute-start.27 = (bf16[8,32,128]{2,1,0:T(8,128)(2,1)S(1)}, bf16[8,32,128]{2,1,0:T(8,128)(2,1)S(1)}, u32[]{:S(2)}, u32[]{:S(2)}) collective-permute-start(bf16[8,32,128]{2,1,0:T(8,128)(2,1)S(1)} %get-tuple-element.91), channel_id=1, source_target_pairs={{0,2},{1,3},{2,0},{3,1},{4,6},{5,7},{6,4},{7,5},{8,10},{9,11},{10,... | collective-permute-start | bytes 196616 | tf_op jit(solution)/shard_map/ppermute | solution.py:36
  131.5 1.4 collective-permute-done.27
  132.9 2.5 %collective-permute-done.28 = bf16[8,32,128]{2,1,0:T(8,128)(2,1)S(1)} collective-permute-done((bf16[8,32,128]{2,1,0:T(8,128)(2,1)S(1)}, bf16[8,32,128]{2,1,0:T(8,128)(2,1)S(1)}, u32[]{:S(2)}, u32[]{:S(2)}) %collective-permute-start.28) | collective-permute-done | bytes 65568 | tf_op jit(solution)/shard_map/ppermute | solution.py:36
  135.4 1.7 collective-permute-start.29
  137.1 3.5 %collective-permute-done.29 = bf16[8,32,128]{2,1,0:T(8,128)(2,1)S(1)} collective-permute-done((bf16[8,32,128]{2,1,0:T(8,128)(2,1)S(1)}, bf16[8,32,128]{2,1,0:T(8,128)(2,1)S(1)}, u32[]{:S(2)}, u32[]{:S(2)}) %collective-permute-start.29) | collective-permute-done | bytes 65568 | tf_op jit(solution)/shard_map/ppermute | solution.py:36
  140.6 1.7 collective-permute-start.32
  142.3 2.1 collective-permute-start.31
  145.9 1.6 collective-permute-done.31.refs_2_
  148.8 2.7 %jac_adjoint.6 = (f32[24,32,128]{2,1,0:T(8,128)S(1)}, bf16[24,32,128]{2,1,0:T(8,128)(2,1)S(1)}) custom-call(s32[1,1536]{1,0:T(1,128)S(1)} %get-tuple-element.62.plan, bf16[8,32,128]{2,1,0:T(8,128)(2,1)S(1)} %multiply_convert_fusion.1.refs_0_, bf16[8,32,128]{2,1,0:T(8,128)(2,1)S(1)} %collective-permute-done.30.refs_1_, ...), custom_call_target="tpu_custom_call" | custom-call | tf_op jit(solution)/shard_map/jac_adjoint/pallas_call | solution.py:209
  151.6 1.4 collective-permute-done.33
  153.5 6.6 %collective-permute-done.34.other = bf16[24,32,128]{2,1,0:T(8,128)(2,1)S(1)} collective-permute-done((bf16[24,32,128]{2,1,0:T(8,128)(2,1)S(1)}, bf16[24,32,128]{2,1,0:T(8,128)(2,1)S(1)}, u32[]{:S(2)}, u32[]{:S(2)}) %collective-permute-start.34) | collective-permute-done | bytes 196640 | tf_op jit(solution)/shard_map/ppermute | solution.py:36
  160.1 2.6 %prior_adjoint.6 = (f32[48,32,128]{2,1,0:T(8,128)S(1)}, bf16[24,32,128]{2,1,0:T(8,128)(2,1)S(1)}, bf16[24,32,128]{2,1,0:T(8,128)(2,1)S(1)}) custom-call(s32[1]{0:T(128)} %bitcast.core, s32[1,1152]{1,0:T(1,128)S(1)} %get-tuple-element.61.plan, bf16[24,32,128]{2,1,0:T(8,128)(2,1)S(1)} %add_convert_fusion.1.mine, ...), custom_call_target="tpu_custom_call" | custom-call | tf_op jit(solution)/shard_map/prior_adjoint/pallas_call | solution.py:238
  164.2 1.9 prior_spread.7.refs_0_
  166.1 6.1 %collective-permute-start.37 = (bf16[24,32,128]{2,1,0:T(8,128)(2,1)S(1)}, bf16[24,32,128]{2,1,0:T(8,128)(2,1)S(1)}, u32[]{:S(2)}, u32[]{:S(2)}) collective-permute-start(bf16[24,32,128]{2,1,0:T(8,128)(2,1)S(1)} %prior_spread.7.refs_0_), channel_id=1, source_target_pairs={{0,8},{1,9},{2,10},{3,11},{4,12},{5,13},{6,14},{7,15},{8,0},{9,1},... | collective-permute-start | bytes 589832 | tf_op jit(solution)/shard_map/ppermute | solution.py:36
  173.3 2.5 %jac_forward.7 = (f32[8,32,128]{2,1,0:T(8,128)S(1)}, bf16[8,32,128]{2,1,0:T(8,128)(2,1)S(1)}, bf16[8,32,128]{2,1,0:T(8,128)(2,1)S(1)}, bf16[8,32,128]{2,1,0:T(8,128)(2,1)S(1)}) custom-call(s32[1,1536]{1,0:T(1,128)S(1)} %get-tuple-element.63.plan, bf16[24,32,128]{2,1,0:T(8,128)(2,1)S(1)} %prior_spread.7.refs_0_, ...), custom_call_target="tpu_custom_call" | custom-call | tf_op jit(solution)/shard_map/jac_forward/pallas_call | solution.py:209
  175.8 1.8 collective-permute-start.38
  177.6 2.8 %collective-permute-start.39 = (bf16[8,32,128]{2,1,0:T(8,128)(2,1)S(1)}, bf16[8,32,128]{2,1,0:T(8,128)(2,1)S(1)}, u32[]{:S(2)}, u32[]{:S(2)}) collective-permute-start(bf16[8,32,128]{2,1,0:T(8,128)(2,1)S(1)} %get-tuple-element.100), channel_id=1, source_target_pairs={{0,2},{1,3},{2,0},{3,1},{4,6},{5,7},{6,4},{7,5},{8,10},{9,11},{10,... | collective-permute-start | bytes 196616 | tf_op jit(solution)/shard_map/ppermute | solution.py:36
  183.1 2.6 %collective-permute-done.40 = bf16[8,32,128]{2,1,0:T(8,128)(2,1)S(1)} collective-permute-done((bf16[8,32,128]{2,1,0:T(8,128)(2,1)S(1)}, bf16[8,32,128]{2,1,0:T(8,128)(2,1)S(1)}, u32[]{:S(2)}, u32[]{:S(2)}) %collective-permute-start.40) | collective-permute-done | bytes 65568 | tf_op jit(solution)/shard_map/ppermute | solution.py:36
  185.7 1.9 collective-permute-start.41
  187.6 3.3 %collective-permute-done.41 = bf16[8,32,128]{2,1,0:T(8,128)(2,1)S(1)} collective-permute-done((bf16[8,32,128]{2,1,0:T(8,128)(2,1)S(1)}, bf16[8,32,128]{2,1,0:T(8,128)(2,1)S(1)}, u32[]{:S(2)}, u32[]{:S(2)}) %collective-permute-start.41) | collective-permute-done | bytes 65568 | tf_op jit(solution)/shard_map/ppermute | solution.py:36
  190.9 1.6 collective-permute-start.44
  192.5 2.2 collective-permute-start.43
  194.7 1.5 collective-permute-done.44.refs_3_
  196.2 1.4 collective-permute-done.43.refs_2_
  198.9 2.6 %jac_adjoint.7 = (f32[24,32,128]{2,1,0:T(8,128)S(1)}, bf16[24,32,128]{2,1,0:T(8,128)(2,1)S(1)}) custom-call(s32[1,1536]{1,0:T(1,128)S(1)} %get-tuple-element.62.plan, bf16[8,32,128]{2,1,0:T(8,128)(2,1)S(1)} %multiply_convert_fusion.refs_0_, bf16[8,32,128]{2,1,0:T(8,128)(2,1)S(1)} %collective-permute-done.42.refs_1_, ...), custom_call_target="tpu_custom_call" | custom-call | tf_op jit(solution)/shard_map/jac_adjoint/pallas_call | solution.py:209
  201.6 1.4 collective-permute-done.45
  203.2 6.9 %collective-permute-done.46.other = bf16[24,32,128]{2,1,0:T(8,128)(2,1)S(1)} collective-permute-done((bf16[24,32,128]{2,1,0:T(8,128)(2,1)S(1)}, bf16[24,32,128]{2,1,0:T(8,128)(2,1)S(1)}, u32[]{:S(2)}, u32[]{:S(2)}) %collective-permute-start.46) | collective-permute-done | bytes 196640 | tf_op jit(solution)/shard_map/ppermute | solution.py:36
  210.1 2.6 %prior_adjoint.7 = (f32[48,32,128]{2,1,0:T(8,128)S(1)}, bf16[24,32,128]{2,1,0:T(8,128)(2,1)S(1)}, bf16[24,32,128]{2,1,0:T(8,128)(2,1)S(1)}) custom-call(s32[1]{0:T(128)} %bitcast.core, s32[1,1152]{1,0:T(1,128)S(1)} %get-tuple-element.61.plan, bf16[24,32,128]{2,1,0:T(8,128)(2,1)S(1)} %add_convert_fusion.mine, ...), custom_call_target="tpu_custom_call" | custom-call | tf_op jit(solution)/shard_map/prior_adjoint/pallas_call | solution.py:238
  214.2 5.2 %collective-permute-start.49 = (bf16[24,32,128]{2,1,0:T(8,128)(2,1)S(1)}, bf16[24,32,128]{2,1,0:T(8,128)(2,1)S(1)}, u32[]{:S(2)}, u32[]{:S(2)}) collective-permute-start(bf16[24,32,128]{2,1,0:T(8,128)(2,1)S(1)} %fusion.2), channel_id=1, source_target_pairs={{0,8},{1,9},{2,10},{3,11},{4,12},{5,13},{6,14},{7,15},{8,0},{9,1},... | collective-permute-start | bytes 589832 | tf_op jit(solution)/shard_map/ppermute | solution.py:36
  (87 shorter events, 37.6 us)
Async XLA Ops:
  0.0 3.3 %copy-start = (f32[32,128]{1,0:T(8,128)S(1)}, f32[32,128]{1,0:T(8,128)}, u32[]{:S(2)}) copy-start(f32[32,128]{1,0:T(8,128)} %param.15) | copy-start | bytes 49156
  1.0 2.4 %collective-permute-start = (bf16[12,32,128]{2,1,0:T(8,128)(2,1)S(1)}, bf16[12,32,128]{2,1,0:T(8,128)(2,1)S(1)}, u32[]{:S(2)}, u32[]{:S(2)}) collective-permute-start(bf16[12,32,128]{2,1,0:T(8,128)(2,1)S(1)} %slice_select_fusion.2), channel_id=1, source_target_pairs={{1,8},{2,9},{3,10},{4,11},{5,12},{6,13},{7,14},{8,1},{9,2},{10,3},... | collective-permute-start | bytes 294920 | tf_op jit(solution)/shard_map/ppermute | solution.py:36
  4.6 0.7 copy-start.2
  5.3 0.7 copy-start.3
  16.2 6.0 %collective-permute-start.1 = (bf16[24,32,128]{2,1,0:T(8,128)(2,1)S(1)}, bf16[24,32,128]{2,1,0:T(8,128)(2,1)S(1)}, u32[]{:S(2)}, u32[]{:S(2)}) collective-permute-start(bf16[24,32,128]{2,1,0:T(8,128)(2,1)S(1)} %prior_spread.4.refs_0_), channel_id=1, source_target_pairs={{0,8},{1,9},{2,10},{3,11},{4,12},{5,13},{6,14},{7,15},{8,0},{9,1},... | collective-permute-start | bytes 589832 | tf_op jit(solution)/shard_map/ppermute | solution.py:36
  24.7 5.8 %collective-permute-start.2 = (bf16[8,32,128]{2,1,0:T(8,128)(2,1)S(1)}, bf16[8,32,128]{2,1,0:T(8,128)(2,1)S(1)}, u32[]{:S(2)}, u32[]{:S(2)}) collective-permute-start(bf16[8,32,128]{2,1,0:T(8,128)(2,1)S(1)} %get-tuple-element.69), channel_id=1, source_target_pairs={{0,1},{1,0},{2,3},{3,2},{4,5},{5,4},{6,7},{7,6},{8,9},{9,8},{10,11... | collective-permute-start | bytes 196616 | tf_op jit(solution)/shard_map/ppermute | solution.py:36
  27.2 5.5 %collective-permute-start.3 = (bf16[8,32,128]{2,1,0:T(8,128)(2,1)S(1)}, bf16[8,32,128]{2,1,0:T(8,128)(2,1)S(1)}, u32[]{:S(2)}, u32[]{:S(2)}) collective-permute-start(bf16[8,32,128]{2,1,0:T(8,128)(2,1)S(1)} %get-tuple-element.70), channel_id=1, source_target_pairs={{0,2},{1,3},{2,0},{3,1},{4,6},{5,7},{6,4},{7,5},{8,10},{9,11},{10,... | collective-permute-start | bytes 196616 | tf_op jit(solution)/shard_map/ppermute | solution.py:36
  30.0 5.2 %collective-permute-start.4 = (bf16[8,32,128]{2,1,0:T(8,128)(2,1)S(1)}, bf16[8,32,128]{2,1,0:T(8,128)(2,1)S(1)}, u32[]{:S(2)}, u32[]{:S(2)}) collective-permute-start(bf16[8,32,128]{2,1,0:T(8,128)(2,1)S(1)} %get-tuple-element.71), channel_id=1, source_target_pairs={{0,3},{1,2},{2,1},{3,0},{4,7},{5,6},{6,5},{7,4},{8,11},{9,10},{10,... | collective-permute-start | bytes 196616 | tf_op jit(solution)/shard_map/ppermute | solution.py:36
  35.2 5.9 %collective-permute-start.5 = (bf16[8,32,128]{2,1,0:T(8,128)(2,1)S(1)}, bf16[8,32,128]{2,1,0:T(8,128)(2,1)S(1)}, u32[]{:S(2)}, u32[]{:S(2)}) collective-permute-start(bf16[8,32,128]{2,1,0:T(8,128)(2,1)S(1)} %add_convert_fusion.7), channel_id=1, source_target_pairs={{0,4},{1,5},{2,6},{3,7},{4,0},{5,1},{6,2},{7,3},{8,12},{9,13},{10,... | collective-permute-start | bytes 196616 | tf_op jit(solution)/shard_map/ppermute | solution.py:36
  41.2 5.2 %collective-permute-start.8 = (bf16[8,32,128]{2,1,0:T(8,128)(2,1)S(1)}, bf16[8,32,128]{2,1,0:T(8,128)(2,1)S(1)}, u32[]{:S(2)}, u32[]{:S(2)}) collective-permute-start(bf16[8,32,128]{2,1,0:T(8,128)(2,1)S(1)} %multiply_convert_fusion.3.refs_0_), channel_id=1, source_target_pairs={{0,3},{1,2},{2,1},{3,0},{4,7},{5,6},{6,5},{7,4},{8,11},{9,10},{10,... | collective-permute-start | bytes 196616 | tf_op jit(solution)/shard_map/ppermute | solution.py:36
  42.2 4.5 %collective-permute-start.7 = (bf16[8,32,128]{2,1,0:T(8,128)(2,1)S(1)}, bf16[8,32,128]{2,1,0:T(8,128)(2,1)S(1)}, u32[]{:S(2)}, u32[]{:S(2)}) collective-permute-start(bf16[8,32,128]{2,1,0:T(8,128)(2,1)S(1)} %multiply_convert_fusion.3.refs_0_), channel_id=1, source_target_pairs={{0,2},{1,3},{2,0},{3,1},{4,6},{5,7},{6,4},{7,5},{8,10},{9,11},{10,... | collective-permute-start | bytes 196616 | tf_op jit(solution)/shard_map/ppermute | solution.py:36
  43.8 4.3 %collective-permute-start.6 = (bf16[8,32,128]{2,1,0:T(8,128)(2,1)S(1)}, bf16[8,32,128]{2,1,0:T(8,128)(2,1)S(1)}, u32[]{:S(2)}, u32[]{:S(2)}) collective-permute-start(bf16[8,32,128]{2,1,0:T(8,128)(2,1)S(1)} %multiply_convert_fusion.3.refs_0_), channel_id=1, source_target_pairs={{0,1},{1,0},{2,3},{3,2},{4,5},{5,4},{6,7},{7,6},{8,9},{9,8},{10,11... | collective-permute-start | bytes 196616 | tf_op jit(solution)/shard_map/ppermute | solution.py:36
  50.6 1.5 collective-permute-start.9
  52.1 7.0 %collective-permute-start.10 = (bf16[24,32,128]{2,1,0:T(8,128)(2,1)S(1)}, bf16[24,32,128]{2,1,0:T(8,128)(2,1)S(1)}, u32[]{:S(2)}, u32[]{:S(2)}) collective-permute-start(bf16[24,32,128]{2,1,0:T(8,128)(2,1)S(1)} %add_convert_fusion.3.mine), channel_id=1, source_target_pairs={{0,16},{1,17},{2,18},{3,19},{4,20},{5,21},{6,22},{7,23},{8,24},{9,... | collective-permute-start | bytes 589832 | tf_op jit(solution)/shard_map/ppermute | solution.py:36
  61.8 1.5 collective-permute-start.11
  61.8 1.4 collective-permute-start.12
  65.2 7.2 %collective-permute-start.13 = (bf16[24,32,128]{2,1,0:T(8,128)(2,1)S(1)}, bf16[24,32,128]{2,1,0:T(8,128)(2,1)S(1)}, u32[]{:S(2)}, u32[]{:S(2)}) collective-permute-start(bf16[24,32,128]{2,1,0:T(8,128)(2,1)S(1)} %prior_spread.5.refs_0_), channel_id=1, source_target_pairs={{0,8},{1,9},{2,10},{3,11},{4,12},{5,13},{6,14},{7,15},{8,0},{9,1},... | collective-permute-start | bytes 589832 | tf_op jit(solution)/shard_map/ppermute | solution.py:36
  74.9 6.6 %collective-permute-start.14 = (bf16[8,32,128]{2,1,0:T(8,128)(2,1)S(1)}, bf16[8,32,128]{2,1,0:T(8,128)(2,1)S(1)}, u32[]{:S(2)}, u32[]{:S(2)}) collective-permute-start(bf16[8,32,128]{2,1,0:T(8,128)(2,1)S(1)} %get-tuple-element.81), channel_id=1, source_target_pairs={{0,1},{1,0},{2,3},{3,2},{4,5},{5,4},{6,7},{7,6},{8,9},{9,8},{10,11... | collective-permute-start | bytes 196616 | tf_op jit(solution)/shard_map/ppermute | solution.py:36
  76.9 5.8 %collective-permute-start.15 = (bf16[8,32,128]{2,1,0:T(8,128)(2,1)S(1)}, bf16[8,32,128]{2,1,0:T(8,128)(2,1)S(1)}, u32[]{:S(2)}, u32[]{:S(2)}) collective-permute-start(bf16[8,32,128]{2,1,0:T(8,128)(2,1)S(1)} %get-tuple-element.82), channel_id=1, source_target_pairs={{0,2},{1,3},{2,0},{3,1},{4,6},{5,7},{6,4},{7,5},{8,10},{9,11},{10,... | collective-permute-start | bytes 196616 | tf_op jit(solution)/shard_map/ppermute | solution.py:36
  80.1 5.2 %collective-permute-start.16 = (bf16[8,32,128]{2,1,0:T(8,128)(2,1)S(1)}, bf16[8,32,128]{2,1,0:T(8,128)(2,1)S(1)}, u32[]{:S(2)}, u32[]{:S(2)}) collective-permute-start(bf16[8,32,128]{2,1,0:T(8,128)(2,1)S(1)} %get-tuple-element.83), channel_id=1, source_target_pairs={{0,3},{1,2},{2,1},{3,0},{4,7},{5,6},{6,5},{7,4},{8,11},{9,10},{10,... | collective-permute-start | bytes 196616 | tf_op jit(solution)/shard_map/ppermute | solution.py:36
  85.3 5.2 %collective-permute-start.17 = (bf16[8,32,128]{2,1,0:T(8,128)(2,1)S(1)}, bf16[8,32,128]{2,1,0:T(8,128)(2,1)S(1)}, u32[]{:S(2)}, u32[]{:S(2)}) collective-permute-start(bf16[8,32,128]{2,1,0:T(8,128)(2,1)S(1)} %add_convert_fusion.6), channel_id=1, source_target_pairs={{0,4},{1,5},{2,6},{3,7},{4,0},{5,1},{6,2},{7,3},{8,12},{9,13},{10,... | collective-permute-start | bytes 196616 | tf_op jit(solution)/shard_map/ppermute | solution.py:36
  90.5 5.2 %collective-permute-start.20 = (bf16[8,32,128]{2,1,0:T(8,128)(2,1)S(1)}, bf16[8,32,128]{2,1,0:T(8,128)(2,1)S(1)}, u32[]{:S(2)}, u32[]{:S(2)}) collective-permute-start(bf16[8,32,128]{2,1,0:T(8,128)(2,1)S(1)} %multiply_convert_fusion.2.refs_0_), channel_id=1, source_target_pairs={{0,3},{1,2},{2,1},{3,0},{4,7},{5,6},{6,5},{7,4},{8,11},{9,10},{10,... | collective-permute-start | bytes 196616 | tf_op jit(solution)/shard_map/ppermute | solution.py:36
  92.1 5.1 %collective-permute-start.19 = (bf16[8,32,128]{2,1,0:T(8,128)(2,1)S(1)}, bf16[8,32,128]{2,1,0:T(8,128)(2,1)S(1)}, u32[]{:S(2)}, u32[]{:S(2)}) collective-permute-start(bf16[8,32,128]{2,1,0:T(8,128)(2,1)S(1)} %multiply_convert_fusion.2.refs_0_), channel_id=1, source_target_pairs={{0,2},{1,3},{2,0},{3,1},{4,6},{5,7},{6,4},{7,5},{8,10},{9,11},{10,... | collective-permute-start | bytes 196616 | tf_op jit(solution)/shard_map/ppermute | solution.py:36
  94.3 4.3 %collective-permute-start.18 = (bf16[8,32,128]{2,1,0:T(8,128)(2,1)S(1)}, bf16[8,32,128]{2,1,0:T(8,128)(2,1)S(1)}, u32[]{:S(2)}, u32[]{:S(2)}) collective-permute-start(bf16[8,32,128]{2,1,0:T(8,128)(2,1)S(1)} %multiply_convert_fusion.2.refs_0_), channel_id=1, source_target_pairs={{0,1},{1,0},{2,3},{3,2},{4,5},{5,4},{6,7},{7,6},{8,9},{9,8},{10,11... | collective-permute-start | bytes 196616 | tf_op jit(solution)/shard_map/ppermute | solution.py:36
  101.1 1.5 collective-permute-start.21
  102.7 7.0 %collective-permute-start.22 = (bf16[24,32,128]{2,1,0:T(8,128)(2,1)S(1)}, bf16[24,32,128]{2,1,0:T(8,128)(2,1)S(1)}, u32[]{:S(2)}, u32[]{:S(2)}) collective-permute-start(bf16[24,32,128]{2,1,0:T(8,128)(2,1)S(1)} %add_convert_fusion.2.mine), channel_id=1, source_target_pairs={{0,16},{1,17},{2,18},{3,19},{4,20},{5,21},{6,22},{7,23},{8,24},{9,... | collective-permute-start | bytes 589832 | tf_op jit(solution)/shard_map/ppermute | solution.py:36
  112.3 1.5 collective-permute-start.23
  112.3 1.4 collective-permute-start.24
  115.7 7.2 %collective-permute-start.25 = (bf16[24,32,128]{2,1,0:T(8,128)(2,1)S(1)}, bf16[24,32,128]{2,1,0:T(8,128)(2,1)S(1)}, u32[]{:S(2)}, u32[]{:S(2)}) collective-permute-start(bf16[24,32,128]{2,1,0:T(8,128)(2,1)S(1)} %prior_spread.6.refs_0_), channel_id=1, source_target_pairs={{0,8},{1,9},{2,10},{3,11},{4,12},{5,13},{6,14},{7,15},{8,0},{9,1},... | collective-permute-start | bytes 589832 | tf_op jit(solution)/shard_map/ppermute | solution.py:36
  125.4 6.1 %collective-permute-start.26 = (bf16[8,32,128]{2,1,0:T(8,128)(2,1)S(1)}, bf16[8,32,128]{2,1,0:T(8,128)(2,1)S(1)}, u32[]{:S(2)}, u32[]{:S(2)}) collective-permute-start(bf16[8,32,128]{2,1,0:T(8,128)(2,1)S(1)} %get-tuple-element.90), channel_id=1, source_target_pairs={{0,1},{1,0},{2,3},{3,2},{4,5},{5,4},{6,7},{7,6},{8,9},{9,8},{10,11... | collective-permute-start | bytes 196616 | tf_op jit(solution)/shard_map/ppermute | solution.py:36
  127.2 5.7 %collective-permute-start.27 = (bf16[8,32,128]{2,1,0:T(8,128)(2,1)S(1)}, bf16[8,32,128]{2,1,0:T(8,128)(2,1)S(1)}, u32[]{:S(2)}, u32[]{:S(2)}) collective-permute-start(bf16[8,32,128]{2,1,0:T(8,128)(2,1)S(1)} %get-tuple-element.91), channel_id=1, source_target_pairs={{0,2},{1,3},{2,0},{3,1},{4,6},{5,7},{6,4},{7,5},{8,10},{9,11},{10,... | collective-permute-start | bytes 196616 | tf_op jit(solution)/shard_map/ppermute | solution.py:36
  130.2 5.2 %collective-permute-start.28 = (bf16[8,32,128]{2,1,0:T(8,128)(2,1)S(1)}, bf16[8,32,128]{2,1,0:T(8,128)(2,1)S(1)}, u32[]{:S(2)}, u32[]{:S(2)}) collective-permute-start(bf16[8,32,128]{2,1,0:T(8,128)(2,1)S(1)} %get-tuple-element.92), channel_id=1, source_target_pairs={{0,3},{1,2},{2,1},{3,0},{4,7},{5,6},{6,5},{7,4},{8,11},{9,10},{10,... | collective-permute-start | bytes 196616 | tf_op jit(solution)/shard_map/ppermute | solution.py:36
  135.4 5.2 %collective-permute-start.29 = (bf16[8,32,128]{2,1,0:T(8,128)(2,1)S(1)}, bf16[8,32,128]{2,1,0:T(8,128)(2,1)S(1)}, u32[]{:S(2)}, u32[]{:S(2)}) collective-permute-start(bf16[8,32,128]{2,1,0:T(8,128)(2,1)S(1)} %add_convert_fusion.5), channel_id=1, source_target_pairs={{0,4},{1,5},{2,6},{3,7},{4,0},{5,1},{6,2},{7,3},{8,12},{9,13},{10,... | collective-permute-start | bytes 196616 | tf_op jit(solution)/shard_map/ppermute | solution.py:36
  140.6 5.2 %collective-permute-start.32 = (bf16[8,32,128]{2,1,0:T(8,128)(2,1)S(1)}, bf16[8,32,128]{2,1,0:T(8,128)(2,1)S(1)}, u32[]{:S(2)}, u32[]{:S(2)}) collective-permute-start(bf16[8,32,128]{2,1,0:T(8,128)(2,1)S(1)} %multiply_convert_fusion.1.refs_0_), channel_id=1, source_target_pairs={{0,3},{1,2},{2,1},{3,0},{4,7},{5,6},{6,5},{7,4},{8,11},{9,10},{10,... | collective-permute-start | bytes 196616 | tf_op jit(solution)/shard_map/ppermute | solution.py:36
  142.3 5.1 %collective-permute-start.31 = (bf16[8,32,128]{2,1,0:T(8,128)(2,1)S(1)}, bf16[8,32,128]{2,1,0:T(8,128)(2,1)S(1)}, u32[]{:S(2)}, u32[]{:S(2)}) collective-permute-start(bf16[8,32,128]{2,1,0:T(8,128)(2,1)S(1)} %multiply_convert_fusion.1.refs_0_), channel_id=1, source_target_pairs={{0,2},{1,3},{2,0},{3,1},{4,6},{5,7},{6,4},{7,5},{8,10},{9,11},{10,... | collective-permute-start | bytes 196616 | tf_op jit(solution)/shard_map/ppermute | solution.py:36
  144.5 4.3 %collective-permute-start.30 = (bf16[8,32,128]{2,1,0:T(8,128)(2,1)S(1)}, bf16[8,32,128]{2,1,0:T(8,128)(2,1)S(1)}, u32[]{:S(2)}, u32[]{:S(2)}) collective-permute-start(bf16[8,32,128]{2,1,0:T(8,128)(2,1)S(1)} %multiply_convert_fusion.1.refs_0_), channel_id=1, source_target_pairs={{0,1},{1,0},{2,3},{3,2},{4,5},{5,4},{6,7},{7,6},{8,9},{9,8},{10,11... | collective-permute-start | bytes 196616 | tf_op jit(solution)/shard_map/ppermute | solution.py:36
  151.5 1.5 collective-permute-start.33
  153.1 7.0 %collective-permute-start.34 = (bf16[24,32,128]{2,1,0:T(8,128)(2,1)S(1)}, bf16[24,32,128]{2,1,0:T(8,128)(2,1)S(1)}, u32[]{:S(2)}, u32[]{:S(2)}) collective-permute-start(bf16[24,32,128]{2,1,0:T(8,128)(2,1)S(1)} %add_convert_fusion.1.mine), channel_id=1, source_target_pairs={{0,16},{1,17},{2,18},{3,19},{4,20},{5,21},{6,22},{7,23},{8,24},{9,... | collective-permute-start | bytes 589832 | tf_op jit(solution)/shard_map/ppermute | solution.py:36
  162.7 1.5 collective-permute-start.35
  162.8 1.4 collective-permute-start.36
  166.1 7.2 %collective-permute-start.37 = (bf16[24,32,128]{2,1,0:T(8,128)(2,1)S(1)}, bf16[24,32,128]{2,1,0:T(8,128)(2,1)S(1)}, u32[]{:S(2)}, u32[]{:S(2)}) collective-permute-start(bf16[24,32,128]{2,1,0:T(8,128)(2,1)S(1)} %prior_spread.7.refs_0_), channel_id=1, source_target_pairs={{0,8},{1,9},{2,10},{3,11},{4,12},{5,13},{6,14},{7,15},{8,0},{9,1},... | collective-permute-start | bytes 589832 | tf_op jit(solution)/shard_map/ppermute | solution.py:36
  173.3 48.0 %copy-start.1 = (f32[32,128]{1,0:T(8,128)S(1)}, f32[32,128]{1,0:T(8,128)}, u32[]{:S(2)}) copy-start(f32[32,128]{1,0:T(8,128)} %param.15) | copy-start | bytes 49156
  175.8 6.1 %collective-permute-start.38 = (bf16[8,32,128]{2,1,0:T(8,128)(2,1)S(1)}, bf16[8,32,128]{2,1,0:T(8,128)(2,1)S(1)}, u32[]{:S(2)}, u32[]{:S(2)}) collective-permute-start(bf16[8,32,128]{2,1,0:T(8,128)(2,1)S(1)} %get-tuple-element.99), channel_id=1, source_target_pairs={{0,1},{1,0},{2,3},{3,2},{4,5},{5,4},{6,7},{7,6},{8,9},{9,8},{10,11... | collective-permute-start | bytes 196616 | tf_op jit(solution)/shard_map/ppermute | solution.py:36
  177.6 5.5 %collective-permute-start.39 = (bf16[8,32,128]{2,1,0:T(8,128)(2,1)S(1)}, bf16[8,32,128]{2,1,0:T(8,128)(2,1)S(1)}, u32[]{:S(2)}, u32[]{:S(2)}) collective-permute-start(bf16[8,32,128]{2,1,0:T(8,128)(2,1)S(1)} %get-tuple-element.100), channel_id=1, source_target_pairs={{0,2},{1,3},{2,0},{3,1},{4,6},{5,7},{6,4},{7,5},{8,10},{9,11},{10,... | collective-permute-start | bytes 196616 | tf_op jit(solution)/shard_map/ppermute | solution.py:36
  180.5 5.2 %collective-permute-start.40 = (bf16[8,32,128]{2,1,0:T(8,128)(2,1)S(1)}, bf16[8,32,128]{2,1,0:T(8,128)(2,1)S(1)}, u32[]{:S(2)}, u32[]{:S(2)}) collective-permute-start(bf16[8,32,128]{2,1,0:T(8,128)(2,1)S(1)} %get-tuple-element.101), channel_id=1, source_target_pairs={{0,3},{1,2},{2,1},{3,0},{4,7},{5,6},{6,5},{7,4},{8,11},{9,10},{10,... | collective-permute-start | bytes 196616 | tf_op jit(solution)/shard_map/ppermute | solution.py:36
  185.7 5.2 %collective-permute-start.41 = (bf16[8,32,128]{2,1,0:T(8,128)(2,1)S(1)}, bf16[8,32,128]{2,1,0:T(8,128)(2,1)S(1)}, u32[]{:S(2)}, u32[]{:S(2)}) collective-permute-start(bf16[8,32,128]{2,1,0:T(8,128)(2,1)S(1)} %add_convert_fusion.4), channel_id=1, source_target_pairs={{0,4},{1,5},{2,6},{3,7},{4,0},{5,1},{6,2},{7,3},{8,12},{9,13},{10,... | collective-permute-start | bytes 196616 | tf_op jit(solution)/shard_map/ppermute | solution.py:36
  190.9 5.2 %collective-permute-start.44 = (bf16[8,32,128]{2,1,0:T(8,128)(2,1)S(1)}, bf16[8,32,128]{2,1,0:T(8,128)(2,1)S(1)}, u32[]{:S(2)}, u32[]{:S(2)}) collective-permute-start(bf16[8,32,128]{2,1,0:T(8,128)(2,1)S(1)} %multiply_convert_fusion.refs_0_), channel_id=1, source_target_pairs={{0,3},{1,2},{2,1},{3,0},{4,7},{5,6},{6,5},{7,4},{8,11},{9,10},{10,... | collective-permute-start | bytes 196616 | tf_op jit(solution)/shard_map/ppermute | solution.py:36
  192.5 5.1 %collective-permute-start.43 = (bf16[8,32,128]{2,1,0:T(8,128)(2,1)S(1)}, bf16[8,32,128]{2,1,0:T(8,128)(2,1)S(1)}, u32[]{:S(2)}, u32[]{:S(2)}) collective-permute-start(bf16[8,32,128]{2,1,0:T(8,128)(2,1)S(1)} %multiply_convert_fusion.refs_0_), channel_id=1, source_target_pairs={{0,2},{1,3},{2,0},{3,1},{4,6},{5,7},{6,4},{7,5},{8,10},{9,11},{10,... | collective-permute-start | bytes 196616 | tf_op jit(solution)/shard_map/ppermute | solution.py:36
  194.7 4.3 %collective-permute-start.42 = (bf16[8,32,128]{2,1,0:T(8,128)(2,1)S(1)}, bf16[8,32,128]{2,1,0:T(8,128)(2,1)S(1)}, u32[]{:S(2)}, u32[]{:S(2)}) collective-permute-start(bf16[8,32,128]{2,1,0:T(8,128)(2,1)S(1)} %multiply_convert_fusion.refs_0_), channel_id=1, source_target_pairs={{0,1},{1,0},{2,3},{3,2},{4,5},{5,4},{6,7},{7,6},{8,9},{9,8},{10,11... | collective-permute-start | bytes 196616 | tf_op jit(solution)/shard_map/ppermute | solution.py:36
  201.5 1.5 collective-permute-start.45
  203.1 7.0 %collective-permute-start.46 = (bf16[24,32,128]{2,1,0:T(8,128)(2,1)S(1)}, bf16[24,32,128]{2,1,0:T(8,128)(2,1)S(1)}, u32[]{:S(2)}, u32[]{:S(2)}) collective-permute-start(bf16[24,32,128]{2,1,0:T(8,128)(2,1)S(1)} %add_convert_fusion.mine), channel_id=1, source_target_pairs={{0,16},{1,17},{2,18},{3,19},{4,20},{5,21},{6,22},{7,23},{8,24},{9,... | collective-permute-start | bytes 589832 | tf_op jit(solution)/shard_map/ppermute | solution.py:36
  212.7 1.4 collective-permute-start.48
  212.8 1.3 collective-permute-start.47
  214.2 6.3 %collective-permute-start.49 = (bf16[24,32,128]{2,1,0:T(8,128)(2,1)S(1)}, bf16[24,32,128]{2,1,0:T(8,128)(2,1)S(1)}, u32[]{:S(2)}, u32[]{:S(2)}) collective-permute-start(bf16[24,32,128]{2,1,0:T(8,128)(2,1)S(1)} %fusion.2), channel_id=1, source_target_pairs={{0,8},{1,9},{2,10},{3,11},{4,12},{5,13},{6,14},{7,15},{8,0},{9,1},... | collective-permute-start | bytes 589832 | tf_op jit(solution)/shard_map/ppermute | solution.py:36

commit v6 on v5

v6 whole, which is shorter than its diff:
```python
import functools
import math

import jax
import jax.numpy as jnp
from jax import lax
from jax.experimental import pallas as pl
from jax.experimental.pallas import tpu as pltpu
from jax.sharding import PartitionSpec as P

STEPS = 4
F32 = jnp.float32
HALF = jnp.bfloat16
VMEM_LIMIT = 8 * 2**20
LANES = 128
OBS_PLAN = (4, 57)
TILE_PLAN = (4, 60)
PRIOR_PLAN = (2, 56)


def matmul(a, b):
    return lax.dot_general(a, b, (((1,), (0,)), ((), ())), preferred_element_type=F32)


def chunk_of(count, most):
    return max(c for c in range(1, most + 1) if count % c == 0)


def exchange(value, partner):
    n_obs, n_flux = lax.axis_size("obs"), lax.axis_size("flux")
    route = []
    for i in range(n_obs):
        for j in range(n_flux):
            to = partner(i, j)
            if to is not None:
                route.append((i * n_flux + j, to[0] * n_flux + to[1]))
    return lax.ppermute(value, ("obs", "flux"), route)


def plan_sizes(plan, blocks, dst_rows):
    group, per_round = plan
    groups = blocks // group + dst_rows
    groups += -groups % per_round
    slots = groups * group
    return slots + -slots % LANES, groups + 1 + -(groups + 1) % LANES


def columns(row):
    parts = [
        jnp.broadcast_to(row[:, k : k + LANES], (LANES, LANES)).T for k in range(0, row.shape[1], LANES)
    ]
    return jnp.concatenate(parts, axis=0)


def plan_groups(plan, src, dst, first, rows, out):
    group, per_round = plan
    blocks = dst.shape[1]
    slots, groups = plan_sizes(plan, blocks, rows)
    i32 = jnp.int32
    lane = lax.broadcasted_iota(i32, (blocks, LANES), 1)
    at = lax.broadcasted_iota(i32, (blocks, LANES), 0)
    src_at, dst_at = columns(src), columns(dst)
    rank = jnp.zeros((blocks, LANES), F32)
    for k in range(0, blocks, LANES):
        same = (dst_at == dst[:, k : k + LANES]) & (lane + k < at)
        rank += same.astype(F32)
    rank = jnp.sum(rank, axis=1, keepdims=True)
    fills = jnp.sum((dst_at == lane).astype(F32), axis=0, keepdims=True)
    sizes = jnp.where(lane[:1] < rows, jnp.floor((fills + (group - 1)) * (1.0 / group)), 0.0)
    begin = jnp.sum(jnp.where(lane < dst_at, sizes, 0.0), axis=1, keepdims=True)
    place = (begin * group + rank).astype(i32)
    place = jnp.where(dst_at < rows, place, slots)
    for k in range(0, slots, LANES):
        hit = place == lane + k
        of = jnp.sum(jnp.where(hit, (src_at - rows).astype(F32), 0.0), axis=0, keepdims=True)
        out[:, k : k + LANES] = of.astype(i32) + rows
        of = jnp.sum(jnp.where(hit, (at - first).astype(F32), 0.0), axis=0, keepdims=True)
        out[:, slots + k : slots + k + LANES] = of.astype(i32)
    full = jnp.sum(sizes, axis=1, keepdims=True)
    rounds = jnp.sum((lane[:1].astype(F32) * per_round < full).astype(F32), axis=1, keepdims=True)
    for k in range(0, groups, LANES):
        lead = place == (lane + k) * group
        of = jnp.sum(jnp.where(lead, (dst_at - rows).astype(F32), 0.0), axis=0, keepdims=True)
        of = jnp.where(lane[:1] + k == groups - 1, rounds, of + rows)
        out[:, 2 * slots + k : 2 * slots + k + LANES] = of.astype(i32)


def setup_kernel(
    rows, chunk, where, obs, flux, nbr, prior, jac,
    prior_plain, prior_turned, jac_plain, jac_turned, obs_plan, tile_plan, prior_plan, nbr_list,
    obs_in, flux_in, nbr_in, obs_out, tile_out, prior_out, nbr_out, small_sems, sems
):
    side, corner, count, first_tile = where[0], where[1], where[2], where[3]
    owned = prior_plain.shape[0]
    begin = side * owned
    rounds = (owned // chunk, jac_plain.shape[0] // chunk)

    def copy(c, first, source, plain, offset):
        to = pl.ds(c * chunk, chunk)
        return pltpu.make_async_copy(source.at[pl.ds(first + c * chunk, chunk)], plain.at[to], sems.at[offset + c])

    def start(first, source, plain, offset):
        def one(c, _):
            copy(c, first, source, plain, offset).start()
            return 0

        return one

    def turn(first, source, plain, turned, offset):
        def one(c, _):
            copy(c, first, source, plain, offset).wait()
            for u in range(chunk):
                turned[c * chunk + u] = plain[c * chunk + u].T
            return 0

        return one

    small = ((obs, obs_in), (flux, flux_in), (nbr, nbr_in))
    small = [pltpu.make_async_copy(src, dst, small_sems.at[k]) for k, (src, dst) in enumerate(small)]
    for one in small:
        one.start()
    lax.fori_loop(0, rounds[0], start(begin, prior, prior_plain, 0), 0)
    lax.fori_loop(0, rounds[1], start(0, jac, jac_plain, rounds[0]), 0)
    for one in small:
        one.wait()

    obs_rows, tile_rows, fan = rows
    half = tile_rows // 2
    reach = tile_rows // 4
    quarter = obs_rows // 4
    most = max(obs_rows, tile_rows)
    i32 = jnp.int32
    at = lax.broadcasted_iota(i32, obs_in.shape, 1)
    live = at < count
    block = sum((obs_in[...] >= k * quarter).astype(i32) for k in range(1, 4))
    obs_at = (block ^ corner) * quarter + obs_in[...] - block * quarter
    block = (flux_in[...] >= half).astype(i32)
    tile_at = (block ^ side) * half + flux_in[...] - block * half
    plan_groups(OBS_PLAN, tile_at, jnp.where(live, obs_at, most), 0, most, obs_out)
    plan_groups(TILE_PLAN, obs_at, jnp.where(live, tile_at, most), 0, most, tile_out)
    at = lax.broadcasted_iota(i32, nbr_in.shape, 1)
    tile = sum((at >= k * fan).astype(i32) for k in range(1, tile_rows)) - side * half
    owns = (tile >= 0) & (tile < half)
    ext = nbr_in[...] - first_tile + reach
    plan_groups(PRIOR_PLAN, jnp.where(owns, tile, 0), jnp.where(owns, ext, most), begin, most, prior_out)
    nbr_out[:, : ext.shape[1]] = ext
    nbr_out[:, ext.shape[1] :] = jnp.zeros((1, LANES), i32) + side
    lists = ((obs_out, obs_plan), (tile_out, tile_plan), (prior_out, prior_plan), (nbr_out, nbr_list))
    lists = [pltpu.make_async_copy(src, dst, small_sems.at[3 + k]) for k, (src, dst) in enumerate(lists)]
    for one in lists:
        one.start()

    lax.fori_loop(0, rounds[0], turn(begin, prior, prior_plain, prior_turned, 0), 0)
    lax.fori_loop(0, rounds[1], turn(0, jac, jac_plain, jac_turned, rounds[0]), 0)
    for one in lists:
        one.wait()


def setup(where, obs, flux, nbr, prior, jac, rows):
    most = max(rows[:2])
    owned = rows[1] // 2 * rows[2]
    chunk = chunk_of(math.gcd(owned, jac.shape[0]), 24)
    smem = pl.BlockSpec(memory_space=pltpu.SMEM)
    vmem = pl.BlockSpec(memory_space=pltpu.VMEM)
    hbm = pl.BlockSpec(memory_space=pl.ANY)
    own = pltpu.VMEM((owned,) + prior.shape[1:], HALF)
    all_blocks = pltpu.VMEM(jac.shape, HALF)
    i32 = jnp.int32
    lengths = []
    for plan, width in ((OBS_PLAN, obs), (TILE_PLAN, obs), (PRIOR_PLAN, nbr)):
        slots, groups = plan_sizes(plan, width.shape[1], most)
        lengths.append(2 * slots + groups)
    lengths.append(nbr.shape[1] + LANES)
    return pl.pallas_call(
        functools.partial(setup_kernel, rows, chunk),
        in_specs=[smem] + [hbm] * 5,
        out_specs=[vmem] * 4 + [smem] * 4,
        out_shape=[own, own, all_blocks, all_blocks] + [pltpu.SMEM((1, n), i32) for n in lengths],
        scratch_shapes=[pltpu.VMEM(v.shape, i32) for v in (obs, flux, nbr)]
        + [pltpu.VMEM((1, n), i32) for n in lengths]
        + [
            pltpu.SemaphoreType.DMA((7,)),
            pltpu.SemaphoreType.DMA(((owned + jac.shape[0]) // chunk,)),
        ],
        compiler_params=pltpu.CompilerParams(vmem_limit_bytes=VMEM_LIMIT),
        name="setup",
    )(where, *(pltpu.with_memory_space_constraint(v, pltpu.HBM) for v in (obs, flux, nbr, prior, jac)))


def grouped_products(plan, sizes, lists, x, blocks, total):
    group, per_round = plan
    slots, groups = sizes
    total[...] = jnp.zeros_like(total)

    def one(c, _):
        products = []
        for u in range(per_round):
            first = (c * per_round + u) * group
            rows = [x[lists[0, first + g]] for g in range(group)]
            tiles = [blocks[lists[0, slots + first + g]] for g in range(group)]
            products.append(matmul(jnp.concatenate(rows, axis=1), jnp.concatenate(tiles, axis=0)))
        for u in range(per_round):
            total[lists[0, 2 * slots + c * per_round + u]] += products[u]
        return 0

    lax.fori_loop(0, lists[0, 2 * slots + groups - 1], one, 0)


def jac_kernel(plan, sizes, n_parts, n_outs, lists, *refs):
    parts = refs[:n_parts]
    jac = refs[n_parts]
    outs = refs[n_parts + 1 : n_parts + 1 + n_outs]
    x, total = refs[n_parts + 1 + n_outs :]
    rows = parts[0].shape[0]
    for k, part in enumerate(parts):
        x[k * rows : (k + 1) * rows] = part[...]
    for r in range(n_parts * rows, x.shape[0]):
        x[r] = jnp.zeros(x.shape[1:], HALF)
    grouped_products(plan, sizes, lists, x, jac, total)
    rows = outs[0].shape[0]
    for k, out in enumerate(outs):
        out[...] = total[k * rows : (k + 1) * rows].astype(out.dtype)


def jac_pass(plan, lists, parts, jac, rows, out_rows, n_outs, name):
    probes, width = parts[0].shape[1:]
    smem = pl.BlockSpec(memory_space=pltpu.SMEM)
    vmem = pl.BlockSpec(memory_space=pltpu.VMEM)
    out = (out_rows // n_outs, probes, width)
    return pl.pallas_call(
        functools.partial(jac_kernel, plan, plan_sizes(plan, jac.shape[0], rows), len(parts), n_outs),
        in_specs=[smem] + [vmem] * len(parts) + [vmem],
        out_specs=[vmem] * n_outs,
        out_shape=[jax.ShapeDtypeStruct(out, F32 if k == 0 else HALF) for k in range(n_outs)],
        scratch_shapes=[
            pltpu.VMEM((rows + 1, probes, width), HALF),
            pltpu.VMEM((rows + 1, probes, width), F32),
        ],
        compiler_params=pltpu.CompilerParams(vmem_limit_bytes=VMEM_LIMIT),
        name=name,
    )(lists, *parts, jac)


def gather_kernel(rows, sizes, nbr, lists, mine, other, prior, ext, to_core, to_far, x, total):
    half = mine.shape[0]
    side = nbr[0, nbr.shape[1] - 1]
    x[:half] = (mine[...].astype(F32) + other[...].astype(F32)).astype(HALF)
    x[rows] = jnp.zeros(x.shape[1:], HALF)
    grouped_products(PRIOR_PLAN, sizes, lists, x, prior, total)
    ext[...] = total[: 2 * half]
    to_core[...] = total[pl.ds(half * (1 - side), half)].astype(HALF)
    to_far[...] = total[pl.ds(half * side, half)].astype(HALF)


def gather_tiles(nbr, lists, mine, other, prior, rows):
    tiles, probes, width = mine.shape
    smem = pl.BlockSpec(memory_space=pltpu.SMEM)
    vmem = pl.BlockSpec(memory_space=pltpu.VMEM)
    return pl.pallas_call(
        functools.partial(gather_kernel, rows, plan_sizes(PRIOR_PLAN, nbr.shape[1] - LANES, rows)),
        in_specs=[smem, smem, vmem, vmem, vmem],
        out_specs=[vmem] * 3,
        out_shape=[
            jax.ShapeDtypeStruct((2 * tiles, probes, width), F32),
            jax.ShapeDtypeStruct((tiles, probes, width), HALF),
            jax.ShapeDtypeStruct((tiles, probes, width), HALF),
        ],
        scratch_shapes=[
            pltpu.VMEM((rows + 1, probes, width), HALF),
            pltpu.VMEM((rows + 1, probes, width), F32),
        ],
        compiler_params=pltpu.CompilerParams(vmem_limit_bytes=VMEM_LIMIT),
        name="prior_adjoint",
    )(nbr, lists, mine, other, prior)


def spread_kernel(first, fan, nbr, *refs):
    prior, out, field = refs[-3:]
    tiles = out.shape[0]
    chunk = chunk_of(tiles, 24)
    side = nbr[0, nbr.shape[1] - 1]
    if first:
        probes, beyond = refs[:2]
        reach = beyond.shape[0]
        inner = 2 * tiles - reach
        field[pl.ds(reach * (1 - side), inner)] = probes[pl.ds(reach * side, inner)]
        field[pl.ds(inner * side, reach)] = beyond[...]
    else:
        ext, from_core, from_far = refs[:3]
        for begin, update in ((tiles * (1 - side), from_core), (tiles * side, from_far)):
            at = pl.ds(begin, tiles)
            field[at] = (ext[at] + update[...].astype(F32)).astype(HALF)

    def one(c, _):
        for u in range(chunk):
            t = c * chunk + u
            row = [field[nbr[0, (side * tiles + t) * fan + k]] for k in range(fan)]
            tile = prior[pl.ds(t * fan, fan)]
            tile = tile.reshape(fan * tile.shape[1], tile.shape[2])
            out[t] = matmul(jnp.concatenate(row, axis=1), tile).astype(HALF)
        return 0

    lax.fori_loop(0, tiles // chunk, one, 0)


def spread_tiles(nbr, fields, prior):
    ext_tiles, probes, width = fields[0].shape
    tiles = ext_tiles // 2
    smem = pl.BlockSpec(memory_space=pltpu.SMEM)
    vmem = pl.BlockSpec(memory_space=pltpu.VMEM)
    return pl.pallas_call(
        functools.partial(spread_kernel, len(fields) == 2, prior.shape[0] // tiles),
        in_specs=[smem] + [vmem] * len(fields) + [vmem],
        out_specs=vmem,
        out_shape=jax.ShapeDtypeStruct((tiles, probes, width), HALF),
        scratch_shapes=[pltpu.VMEM(fields[0].shape, HALF)],
        compiler_params=pltpu.CompilerParams(vmem_limit_bytes=VMEM_LIMIT),
        name="prior_spread",
    )(nbr, *fields, prior)


def shards(probes, prior_tiles, neighbours, jac, jac_obs, jac_flux, counts, rinv):
    n_obs, n_flux = lax.axis_size("obs"), lax.axis_size("flux")
    tile_count = probes.shape[0]
    half = tile_count // 2
    reach = tile_count // 4
    obs_rows = rinv.shape[0]
    quarter = obs_rows // 4
    blocks = jac[0, 0]
    flux_at = lax.axis_index("flux")
    side = lax.rem(lax.axis_index("obs"), 2)
    corner = lax.rem(flux_at, 4)
    fan = neighbours.shape[1]
    prior = prior_tiles.reshape((tile_count * fan,) + prior_tiles.shape[2:])
    own_rinv = lax.dynamic_slice_in_dim(rinv, corner * quarter, quarter, 0)[:, None, :]
    rows = max(obs_rows, tile_count)
    sizes = (obs_rows, tile_count, fan)

    def swap_core(value):
        return exchange(value, lambda i, j: (i ^ 1, j))

    def swap_far(value):
        def partner(i, j):
            to = j - 1 if i % 2 == 0 else j + 1
            return (i ^ 1, to) if 0 <= to < n_flux else None

        return exchange(value, partner)

    def swap_flux(value, bits):
        return exchange(value, lambda i, j: (i, j ^ bits))

    edge = jnp.where(side == 0, probes[:reach], probes[tile_count - reach :])
    beyond = swap_far(edge)
    where = jnp.stack([side, corner, counts[0, 0], flux_at * tile_count + side * half])
    nbr = neighbours.reshape(1, tile_count * fan)

    where, own_rinv, nbr, prior, blocks = lax.optimization_barrier((where, own_rinv, nbr, prior, blocks))
    prior_plain, prior_turned, jac_plain, jac_turned, obs_lists, tile_lists, prior_lists, nbr = setup(
        where, jac_obs[0], jac_flux[0], nbr, prior, blocks, sizes
    )
    fields = (probes, beyond)
    for step in range(STEPS):
        spread = spread_tiles(nbr, fields, prior_plain)
        parts = (spread, swap_core(spread))
        pieces = jac_pass(OBS_PLAN, obs_lists, parts, jac_plain, rows, obs_rows, 4, "jac_forward")
        total = pieces[0]
        for bits in range(1, 4):
            total = total + swap_flux(pieces[bits], bits).astype(F32)
        bits = 4
        while bits < n_flux:
            sent = total.astype(HALF)
            total = sent.astype(F32) + swap_flux(sent, bits).astype(F32)
            bits *= 2
        weighted = (total * own_rinv).astype(HALF)
        parts = (weighted,) + tuple(swap_flux(weighted, bits) for bits in range(1, 4))
        mine, theirs = jac_pass(TILE_PLAN, tile_lists, parts, jac_turned, rows, tile_count, 2, "jac_adjoint")
        mine = (mine + swap_core(theirs).astype(F32)).astype(HALF)
        bits = 2
        while bits < n_obs:
            other = exchange(mine, lambda i, j, bits=bits: (i ^ bits, j))
            bits *= 2
            if bits < n_obs:
                mine = (mine.astype(F32) + other.astype(F32)).astype(HALF)
        ext, to_core, to_far = gather_tiles(nbr, prior_lists, mine, other, prior_turned, rows)
        if step < STEPS - 1:
            fields = (ext, swap_core(to_core), swap_far(to_far))
    lower = side == 0
    from_core = swap_core(jnp.where(lower, to_core[half - reach :], to_core[:reach])).astype(F32)
    from_far = swap_far(jnp.where(lower, to_far[:reach], to_far[half - reach :])).astype(F32)
    low = jnp.where(lower, from_far, from_core)
    high = jnp.where(lower, from_core, from_far)
    own = (ext[reach : reach + half] + jnp.concatenate([low, high], axis=0)).astype(HALF)
    other = swap_core(own)
    first = jnp.where(side == 0, own, other)
    second = jnp.where(side == 0, other, own)
    return jnp.concatenate([first, second], axis=0)


def solution(mesh):
    placed = (
        P("flux", None, None),
        P("flux", None, None, None),
        P("flux", None),
        P("obs", "flux", None, None, None),
        P("obs", "flux", None),
        P("obs", "flux", None),
        P("obs", "flux"),
        P("obs", None),
    )
    return jax.shard_map(
        shards, mesh=mesh, in_specs=placed, out_specs=P("flux", None, None), check_vma=False
    )
```

time: 221 us -> 207 us (0.937)
  waiting for transfers between devices: 87.1 us -> 80.9 us
  starting transfers between devices: 80.4 us -> 76.3 us
  Pallas kernels: 46.8 us -> 43.6 us
    ppermute x50, waiting for transfers between devices: 87.1 us -> 80.9 us  [exchange(): return lax.ppermute(value, ('obs', 'flux'), route)]
    pallas_call x16, Pallas kernels: 38.4 us -> 34.3 us  [the longest x8 22.9 us: jac_pass(): pl.pallas_call(functools.partial(jac_kernel, plan, plan_sizes(plan, jac.s...]
    ppermute x50, starting transfers between devices: 80.4 us -> 76.3 us  [exchange(): return lax.ppermute(value, ('obs', 'flux'), route)]
  transfers between devices with their start and end apart: 50 -> 50, of which waited for: 41 -> 41; matrix products, arithmetic and copies ran while one was open for 0% -> 1% of each run, Pallas kernels for 0% -> 5%
where the time goes in v6:
time: 207 us; the launch traced here: 206 us
  waiting for transfers between devices  80.9 us (39%)
  starting transfers between devices  76.3 us (37%)
  Pallas kernels  43.6 us (21%)
  other arithmetic  2.47 us (1%)
    ppermute x50, waiting for transfers between devices, exchange(): return lax.ppermute(value, ('obs', 'flux'), route)  80.9 us
    ppermute x50, starting transfers between devices, exchange(): return lax.ppermute(value, ('obs', 'flux'), route)  76.3 us
    pallas_call x8, Pallas kernels, jac_pass(): pl.pallas_call(functools.partial(jac_kernel, plan, plan_sizes(plan, jac.s...  22.9 us
    pallas_call x1, Pallas kernels, setup(): pl.pallas_call(functools.partial(setup_kernel, rows, chunk), in_specs=[sm...  9.32 us
    pallas_call x4, Pallas kernels, gather_tiles(): pl.pallas_call(functools.partial(gather_kernel, rows, plan_sizes(PRIOR_PL...  6.49 us
    pallas_call x4, Pallas kernels, spread_tiles(): pl.pallas_call(functools.partial(spread_kernel, len(fields) == 2, prior.s...  4.84 us
  transfers between devices with their start and end apart: 50, of which 41 were waited for; matrix products, arithmetic and copies ran while one was open for 1% of the time, Pallas kernels for 5%

profile of v6, /device:TPU:0, one launch (start us, length us, event | category | flops | bytes accessed | tf_op | source)
XLA Modules:
  0.0 205.7 jit_solution(7669767809685096767)
XLA Ops:
  3.8 9.3 %setup.1 = (bf16[192,128,128]{2,1,0:T(8,128)(2,1)S(1)}, bf16[192,128,128]{2,1,0:T(8,128)(2,1)S(1)}, bf16[384,128,128]{2,1,0:T(8,128)(2,1)S(1)}, bf16[384,128,128...) custom-call(s32[4]{0:T(128)S(1)} %pad_add_fusion.where, ...), custom_call_target="tpu_custom_call" | custom-call | tf_op jit(solution)/shard_map/setup/pallas_call | solution.py:174
  14.3 4.4 %collective-permute-start.1 = (bf16[24,32,128]{2,1,0:T(8,128)(2,1)S(1)}, bf16[24,32,128]{2,1,0:T(8,128)(2,1)S(1)}, u32[]{:S(2)}, u32[]{:S(2)}) collective-permute-start(bf16[24,32,128]{2,1,0:T(8,128)(2,1)S(1)} %prior_spread.4.refs_0_), channel_id=1, source_target_pairs={{0,8},{1,9},{2,10},{3,11},{4,12},{5,13},{6,14},{7,15},{8,0},{9,1},... | collective-permute-start | bytes 589832 | tf_op jit(solution)/shard_map/ppermute | solution.py:37
  19.7 2.7 %jac_forward.4 = (f32[8,32,128]{2,1,0:T(8,128)S(1)}, bf16[8,32,128]{2,1,0:T(8,128)(2,1)S(1)}, bf16[8,32,128]{2,1,0:T(8,128)(2,1)S(1)}, bf16[8,32,128]{2,1,0:T(8,128)(2,1)S(1)}) custom-call(s32[1,1792]{1,0:T(1,128)S(4)} %get-tuple-element.61.lists, bf16[24,32,128]{2,1,0:T(8,128)(2,1)S(1)} %prior_spread.4.refs_0_, ...), custom_call_target="tpu_custom_call" | custom-call | tf_op jit(solution)/shard_map/jac_forward/pallas_call | solution.py:230
  22.8 2.9 %collective-permute-start.3 = (bf16[8,32,128]{2,1,0:T(8,128)(2,1)S(1)}, bf16[8,32,128]{2,1,0:T(8,128)(2,1)S(1)}, u32[]{:S(2)}, u32[]{:S(2)}) collective-permute-start(bf16[8,32,128]{2,1,0:T(8,128)(2,1)S(1)} %get-tuple-element.66), channel_id=1, source_target_pairs={{0,2},{1,3},{2,0},{3,1},{4,6},{5,7},{6,4},{7,5},{8,10},{9,11},{10,... | collective-permute-start | bytes 196616 | tf_op jit(solution)/shard_map/ppermute | solution.py:37
  28.0 2.8 %collective-permute-done.4 = bf16[8,32,128]{2,1,0:T(8,128)(2,1)S(1)} collective-permute-done((bf16[8,32,128]{2,1,0:T(8,128)(2,1)S(1)}, bf16[8,32,128]{2,1,0:T(8,128)(2,1)S(1)}, u32[]{:S(2)}, u32[]{:S(2)}) %collective-permute-start.4) | collective-permute-done | bytes 65568 | tf_op jit(solution)/shard_map/ppermute | solution.py:37
  30.9 1.5 collective-permute-start.5
  32.4 4.1 %collective-permute-done.5 = bf16[8,32,128]{2,1,0:T(8,128)(2,1)S(1)} collective-permute-done((bf16[8,32,128]{2,1,0:T(8,128)(2,1)S(1)}, bf16[8,32,128]{2,1,0:T(8,128)(2,1)S(1)}, u32[]{:S(2)}, u32[]{:S(2)}) %collective-permute-start.5) | collective-permute-done | bytes 65568 | tf_op jit(solution)/shard_map/ppermute | solution.py:37
  37.9 2.2 %collective-permute-start.6 = (bf16[8,32,128]{2,1,0:T(8,128)(2,1)S(1)}, bf16[8,32,128]{2,1,0:T(8,128)(2,1)S(1)}, u32[]{:S(2)}, u32[]{:S(2)}) collective-permute-start(bf16[8,32,128]{2,1,0:T(8,128)(2,1)S(1)} %multiply_convert_fusion.3.refs_0_), channel_id=1, source_target_pairs={{0,1},{1,0},{2,3},{3,2},{4,5},{5,4},{6,7},{7,6},{8,9},{9,8},{10,11... | collective-permute-start | bytes 196616 | tf_op jit(solution)/shard_map/ppermute | solution.py:37
  40.1 1.7 collective-permute-done.8.refs_3_
  42.5 2.9 %jac_adjoint.4 = (f32[24,32,128]{2,1,0:T(8,128)S(1)}, bf16[24,32,128]{2,1,0:T(8,128)(2,1)S(1)}) custom-call(s32[1,1792]{1,0:T(1,128)S(4)} %get-tuple-element.60.lists, bf16[8,32,128]{2,1,0:T(8,128)(2,1)S(1)} %multiply_convert_fusion.3.refs_0_, bf16[8,32,128]{2,1,0:T(8,128)(2,1)S(1)} %collective-permute-done.6.refs_1_, ...), custom_call_target="tpu_custom_call" | custom-call | tf_op jit(solution)/shard_map/jac_adjoint/pallas_call | solution.py:230
  45.4 1.4 collective-permute-done.9
  46.9 2.2 %collective-permute-start.10 = (bf16[24,32,128]{2,1,0:T(8,128)(2,1)S(1)}, bf16[24,32,128]{2,1,0:T(8,128)(2,1)S(1)}, u32[]{:S(2)}, u32[]{:S(2)}) collective-permute-start(bf16[24,32,128]{2,1,0:T(8,128)(2,1)S(1)} %add_convert_fusion.3.mine), channel_id=1, source_target_pairs={{0,16},{1,17},{2,18},{3,19},{4,20},{5,21},{6,22},{7,23},{8,24},{9,... | collective-permute-start | bytes 589832 | tf_op jit(solution)/shard_map/ppermute | solution.py:37
  49.1 5.2 %collective-permute-done.10.other = bf16[24,32,128]{2,1,0:T(8,128)(2,1)S(1)} collective-permute-done((bf16[24,32,128]{2,1,0:T(8,128)(2,1)S(1)}, bf16[24,32,128]{2,1,0:T(8,128)(2,1)S(1)}, u32[]{:S(2)}, u32[]{:S(2)}) %collective-permute-start.10) | collective-permute-done | bytes 196640 | tf_op jit(solution)/shard_map/ppermute | solution.py:37
  54.4 1.6 prior_adjoint.4
  57.5 1.2 prior_spread.5.refs_0_
  58.7 6.3 %collective-permute-start.13 = (bf16[24,32,128]{2,1,0:T(8,128)(2,1)S(1)}, bf16[24,32,128]{2,1,0:T(8,128)(2,1)S(1)}, u32[]{:S(2)}, u32[]{:S(2)}) collective-permute-start(bf16[24,32,128]{2,1,0:T(8,128)(2,1)S(1)} %prior_spread.5.refs_0_), channel_id=1, source_target_pairs={{0,8},{1,9},{2,10},{3,11},{4,12},{5,13},{6,14},{7,15},{8,0},{9,1},... | collective-permute-start | bytes 589832 | tf_op jit(solution)/shard_map/ppermute | solution.py:37
  66.1 2.7 %jac_forward.5 = (f32[8,32,128]{2,1,0:T(8,128)S(1)}, bf16[8,32,128]{2,1,0:T(8,128)(2,1)S(1)}, bf16[8,32,128]{2,1,0:T(8,128)(2,1)S(1)}, bf16[8,32,128]{2,1,0:T(8,128)(2,1)S(1)}) custom-call(s32[1,1792]{1,0:T(1,128)S(4)} %get-tuple-element.61.lists, bf16[24,32,128]{2,1,0:T(8,128)(2,1)S(1)} %prior_spread.5.refs_0_, ...), custom_call_target="tpu_custom_call" | custom-call | tf_op jit(solution)/shard_map/jac_forward/pallas_call | solution.py:230
  68.9 1.5 collective-permute-start.14
  70.4 1.8 collective-permute-start.15
  73.3 1.3 collective-permute-done.15
  74.6 2.7 %collective-permute-done.16 = bf16[8,32,128]{2,1,0:T(8,128)(2,1)S(1)} collective-permute-done((bf16[8,32,128]{2,1,0:T(8,128)(2,1)S(1)}, bf16[8,32,128]{2,1,0:T(8,128)(2,1)S(1)}, u32[]{:S(2)}, u32[]{:S(2)}) %collective-permute-start.16) | collective-permute-done | bytes 65568 | tf_op jit(solution)/shard_map/ppermute | solution.py:37
  77.4 1.9 collective-permute-start.17
  79.3 4.1 %collective-permute-done.17 = bf16[8,32,128]{2,1,0:T(8,128)(2,1)S(1)} collective-permute-done((bf16[8,32,128]{2,1,0:T(8,128)(2,1)S(1)}, bf16[8,32,128]{2,1,0:T(8,128)(2,1)S(1)}, u32[]{:S(2)}, u32[]{:S(2)}) %collective-permute-start.17) | collective-permute-done | bytes 65568 | tf_op jit(solution)/shard_map/ppermute | solution.py:37
  83.8 1.5 collective-permute-start.19
  85.4 1.6 collective-permute-start.18
  86.9 1.7 collective-permute-done.20.refs_3_
  89.6 3.1 %jac_adjoint.5 = (f32[24,32,128]{2,1,0:T(8,128)S(1)}, bf16[24,32,128]{2,1,0:T(8,128)(2,1)S(1)}) custom-call(s32[1,1792]{1,0:T(1,128)S(4)} %get-tuple-element.60.lists, bf16[8,32,128]{2,1,0:T(8,128)(2,1)S(1)} %multiply_convert_fusion.2.refs_0_, bf16[8,32,128]{2,1,0:T(8,128)(2,1)S(1)} %collective-permute-done.18.refs_1_, ...), custom_call_target="tpu_custom_call" | custom-call | tf_op jit(solution)/shard_map/jac_adjoint/pallas_call | solution.py:230
  92.8 1.4 collective-permute-done.21
  94.3 2.3 %collective-permute-start.22 = (bf16[24,32,128]{2,1,0:T(8,128)(2,1)S(1)}, bf16[24,32,128]{2,1,0:T(8,128)(2,1)S(1)}, u32[]{:S(2)}, u32[]{:S(2)}) collective-permute-start(bf16[24,32,128]{2,1,0:T(8,128)(2,1)S(1)} %add_convert_fusion.2.mine), channel_id=1, source_target_pairs={{0,16},{1,17},{2,18},{3,19},{4,20},{5,21},{6,22},{7,23},{8,24},{9,... | collective-permute-start | bytes 589832 | tf_op jit(solution)/shard_map/ppermute | solution.py:37
  96.6 5.2 %collective-permute-done.22.other = bf16[24,32,128]{2,1,0:T(8,128)(2,1)S(1)} collective-permute-done((bf16[24,32,128]{2,1,0:T(8,128)(2,1)S(1)}, bf16[24,32,128]{2,1,0:T(8,128)(2,1)S(1)}, u32[]{:S(2)}, u32[]{:S(2)}) %collective-permute-start.22) | collective-permute-done | bytes 196640 | tf_op jit(solution)/shard_map/ppermute | solution.py:37
  101.8 1.6 prior_adjoint.5
  105.0 1.2 prior_spread.6.refs_0_
  106.2 6.1 %collective-permute-start.25 = (bf16[24,32,128]{2,1,0:T(8,128)(2,1)S(1)}, bf16[24,32,128]{2,1,0:T(8,128)(2,1)S(1)}, u32[]{:S(2)}, u32[]{:S(2)}) collective-permute-start(bf16[24,32,128]{2,1,0:T(8,128)(2,1)S(1)} %prior_spread.6.refs_0_), channel_id=1, source_target_pairs={{0,8},{1,9},{2,10},{3,11},{4,12},{5,13},{6,14},{7,15},{8,0},{9,1},... | collective-permute-start | bytes 589832 | tf_op jit(solution)/shard_map/ppermute | solution.py:37
  113.4 2.7 %jac_forward.6 = (f32[8,32,128]{2,1,0:T(8,128)S(1)}, bf16[8,32,128]{2,1,0:T(8,128)(2,1)S(1)}, bf16[8,32,128]{2,1,0:T(8,128)(2,1)S(1)}, bf16[8,32,128]{2,1,0:T(8,128)(2,1)S(1)}) custom-call(s32[1,1792]{1,0:T(1,128)S(4)} %get-tuple-element.61.lists, bf16[24,32,128]{2,1,0:T(8,128)(2,1)S(1)} %prior_spread.6.refs_0_, ...), custom_call_target="tpu_custom_call" | custom-call | tf_op jit(solution)/shard_map/jac_forward/pallas_call | solution.py:230
  117.2 2.0 collective-permute-start.27
  121.5 2.9 %collective-permute-done.28 = bf16[8,32,128]{2,1,0:T(8,128)(2,1)S(1)} collective-permute-done((bf16[8,32,128]{2,1,0:T(8,128)(2,1)S(1)}, bf16[8,32,128]{2,1,0:T(8,128)(2,1)S(1)}, u32[]{:S(2)}, u32[]{:S(2)}) %collective-permute-start.28) | collective-permute-done | bytes 65568 | tf_op jit(solution)/shard_map/ppermute | solution.py:37
  124.5 2.0 collective-permute-start.29
  126.5 4.0 %collective-permute-done.29 = bf16[8,32,128]{2,1,0:T(8,128)(2,1)S(1)} collective-permute-done((bf16[8,32,128]{2,1,0:T(8,128)(2,1)S(1)}, bf16[8,32,128]{2,1,0:T(8,128)(2,1)S(1)}, u32[]{:S(2)}, u32[]{:S(2)}) %collective-permute-start.29) | collective-permute-done | bytes 65568 | tf_op jit(solution)/shard_map/ppermute | solution.py:37
  130.9 1.6 collective-permute-start.31
  132.6 1.4 collective-permute-start.30
  134.0 1.7 collective-permute-done.32.refs_3_
  135.7 1.2 collective-permute-done.30.refs_1_
  136.9 2.9 %jac_adjoint.6 = (f32[24,32,128]{2,1,0:T(8,128)S(1)}, bf16[24,32,128]{2,1,0:T(8,128)(2,1)S(1)}) custom-call(s32[1,1792]{1,0:T(1,128)S(4)} %get-tuple-element.60.lists, bf16[8,32,128]{2,1,0:T(8,128)(2,1)S(1)} %multiply_convert_fusion.1.refs_0_, bf16[8,32,128]{2,1,0:T(8,128)(2,1)S(1)} %collective-permute-done.30.refs_1_, ...), custom_call_target="tpu_custom_call" | custom-call | tf_op jit(solution)/shard_map/jac_adjoint/pallas_call | solution.py:230
  139.8 1.4 collective-permute-done.33
  141.3 2.0 collective-permute-start.34
  143.3 5.2 %collective-permute-done.34.other = bf16[24,32,128]{2,1,0:T(8,128)(2,1)S(1)} collective-permute-done((bf16[24,32,128]{2,1,0:T(8,128)(2,1)S(1)}, bf16[24,32,128]{2,1,0:T(8,128)(2,1)S(1)}, u32[]{:S(2)}, u32[]{:S(2)}) %collective-permute-start.34) | collective-permute-done | bytes 196640 | tf_op jit(solution)/shard_map/ppermute | solution.py:37
  148.5 1.6 prior_adjoint.6
  151.7 1.2 prior_spread.7.refs_0_
  152.9 6.1 %collective-permute-start.37 = (bf16[24,32,128]{2,1,0:T(8,128)(2,1)S(1)}, bf16[24,32,128]{2,1,0:T(8,128)(2,1)S(1)}, u32[]{:S(2)}, u32[]{:S(2)}) collective-permute-start(bf16[24,32,128]{2,1,0:T(8,128)(2,1)S(1)} %prior_spread.7.refs_0_), channel_id=1, source_target_pairs={{0,8},{1,9},{2,10},{3,11},{4,12},{5,13},{6,14},{7,15},{8,0},{9,1},... | collective-permute-start | bytes 589832 | tf_op jit(solution)/shard_map/ppermute | solution.py:37
  160.1 2.7 %jac_forward.7 = (f32[8,32,128]{2,1,0:T(8,128)S(1)}, bf16[8,32,128]{2,1,0:T(8,128)(2,1)S(1)}, bf16[8,32,128]{2,1,0:T(8,128)(2,1)S(1)}, bf16[8,32,128]{2,1,0:T(8,128)(2,1)S(1)}) custom-call(s32[1,1792]{1,0:T(1,128)S(4)} %get-tuple-element.61.lists, bf16[24,32,128]{2,1,0:T(8,128)(2,1)S(1)} %prior_spread.7.refs_0_, ...), custom_call_target="tpu_custom_call" | custom-call | tf_op jit(solution)/shard_map/jac_forward/pallas_call | solution.py:230
  162.8 1.1 collective-permute-start.38
  164.0 2.3 %collective-permute-start.39 = (bf16[8,32,128]{2,1,0:T(8,128)(2,1)S(1)}, bf16[8,32,128]{2,1,0:T(8,128)(2,1)S(1)}, u32[]{:S(2)}, u32[]{:S(2)}) collective-permute-start(bf16[8,32,128]{2,1,0:T(8,128)(2,1)S(1)} %get-tuple-element.96), channel_id=1, source_target_pairs={{0,2},{1,3},{2,0},{3,1},{4,6},{5,7},{6,4},{7,5},{8,10},{9,11},{10,... | collective-permute-start | bytes 196616 | tf_op jit(solution)/shard_map/ppermute | solution.py:37
  167.3 1.2 collective-permute-done.39
  168.5 2.9 %collective-permute-done.40 = bf16[8,32,128]{2,1,0:T(8,128)(2,1)S(1)} collective-permute-done((bf16[8,32,128]{2,1,0:T(8,128)(2,1)S(1)}, bf16[8,32,128]{2,1,0:T(8,128)(2,1)S(1)}, u32[]{:S(2)}, u32[]{:S(2)}) %collective-permute-start.40) | collective-permute-done | bytes 65568 | tf_op jit(solution)/shard_map/ppermute | solution.py:37
  171.4 1.6 collective-permute-start.41
  173.1 4.3 %collective-permute-done.41 = bf16[8,32,128]{2,1,0:T(8,128)(2,1)S(1)} collective-permute-done((bf16[8,32,128]{2,1,0:T(8,128)(2,1)S(1)}, bf16[8,32,128]{2,1,0:T(8,128)(2,1)S(1)}, u32[]{:S(2)}, u32[]{:S(2)}) %collective-permute-start.41) | collective-permute-done | bytes 65568 | tf_op jit(solution)/shard_map/ppermute | solution.py:37
  178.6 2.4 %collective-permute-start.42 = (bf16[8,32,128]{2,1,0:T(8,128)(2,1)S(1)}, bf16[8,32,128]{2,1,0:T(8,128)(2,1)S(1)}, u32[]{:S(2)}, u32[]{:S(2)}) collective-permute-start(bf16[8,32,128]{2,1,0:T(8,128)(2,1)S(1)} %multiply_convert_fusion.refs_0_), channel_id=1, source_target_pairs={{0,1},{1,0},{2,3},{3,2},{4,5},{5,4},{6,7},{7,6},{8,9},{9,8},{10,11... | collective-permute-start | bytes 196616 | tf_op jit(solution)/shard_map/ppermute | solution.py:37
  181.0 1.7 collective-permute-done.44.refs_3_
  183.3 3.1 %jac_adjoint.7 = (f32[24,32,128]{2,1,0:T(8,128)S(1)}, bf16[24,32,128]{2,1,0:T(8,128)(2,1)S(1)}) custom-call(s32[1,1792]{1,0:T(1,128)S(4)} %get-tuple-element.60.lists, bf16[8,32,128]{2,1,0:T(8,128)(2,1)S(1)} %multiply_convert_fusion.refs_0_, bf16[8,32,128]{2,1,0:T(8,128)(2,1)S(1)} %collective-permute-done.42.refs_1_, ...), custom_call_target="tpu_custom_call" | custom-call | tf_op jit(solution)/shard_map/jac_adjoint/pallas_call | solution.py:230
  186.5 1.4 collective-permute-done.45
  188.0 2.2 %collective-permute-start.46 = (bf16[24,32,128]{2,1,0:T(8,128)(2,1)S(1)}, bf16[24,32,128]{2,1,0:T(8,128)(2,1)S(1)}, u32[]{:S(2)}, u32[]{:S(2)}) collective-permute-start(bf16[24,32,128]{2,1,0:T(8,128)(2,1)S(1)} %add_convert_fusion.mine), channel_id=1, source_target_pairs={{0,16},{1,17},{2,18},{3,19},{4,20},{5,21},{6,22},{7,23},{8,24},{9,... | collective-permute-start | bytes 589832 | tf_op jit(solution)/shard_map/ppermute | solution.py:37
  190.3 5.2 %collective-permute-done.46.other = bf16[24,32,128]{2,1,0:T(8,128)(2,1)S(1)} collective-permute-done((bf16[24,32,128]{2,1,0:T(8,128)(2,1)S(1)}, bf16[24,32,128]{2,1,0:T(8,128)(2,1)S(1)}, u32[]{:S(2)}, u32[]{:S(2)}) %collective-permute-start.46) | collective-permute-done | bytes 196640 | tf_op jit(solution)/shard_map/ppermute | solution.py:37
  195.5 1.6 prior_adjoint.7
  198.6 5.2 %collective-permute-start.49 = (bf16[24,32,128]{2,1,0:T(8,128)(2,1)S(1)}, bf16[24,32,128]{2,1,0:T(8,128)(2,1)S(1)}, u32[]{:S(2)}, u32[]{:S(2)}) collective-permute-start(bf16[24,32,128]{2,1,0:T(8,128)(2,1)S(1)} %fusion), channel_id=1, source_target_pairs={{0,8},{1,9},{2,10},{3,11},{4,12},{5,13},{6,14},{7,15},{8,0},{9,1},... | collective-permute-start | bytes 589832 | tf_op jit(solution)/shard_map/ppermute | solution.py:37
  (82 shorter events, 31.2 us)
Async XLA Ops:
  0.0 3.7 %copy-start = (f32[32,128]{1,0:T(8,128)S(1)}, f32[32,128]{1,0:T(8,128)}, u32[]{:S(2)}) copy-start(f32[32,128]{1,0:T(8,128)} %param.15) | copy-start | bytes 49156
  1.0 12.2 %collective-permute-start = (bf16[12,32,128]{2,1,0:T(8,128)(2,1)S(1)}, bf16[12,32,128]{2,1,0:T(8,128)(2,1)S(1)}, u32[]{:S(2)}, u32[]{:S(2)}) collective-permute-start(bf16[12,32,128]{2,1,0:T(8,128)(2,1)S(1)} %slice_select_fusion.2), channel_id=1, source_target_pairs={{1,8},{2,9},{3,10},{4,11},{5,12},{6,13},{7,14},{8,1},{9,2},{10,3},... | collective-permute-start | bytes 294920 | tf_op jit(solution)/shard_map/ppermute | solution.py:37
  3.8 9.3 %copy-start.2 = (bf16[48,32,128]{2,1,0:T(8,128)(2,1)S(1)}, bf16[48,32,128]{2,1,0:T(8,128)(2,1)}, u32[]{:S(2)}) copy-start(bf16[48,32,128]{2,1,0:T(8,128)(2,1)} %refs_0_.1) | copy-start | bytes 1179652
  14.3 5.5 %collective-permute-start.1 = (bf16[24,32,128]{2,1,0:T(8,128)(2,1)S(1)}, bf16[24,32,128]{2,1,0:T(8,128)(2,1)S(1)}, u32[]{:S(2)}, u32[]{:S(2)}) collective-permute-start(bf16[24,32,128]{2,1,0:T(8,128)(2,1)S(1)} %prior_spread.4.refs_0_), channel_id=1, source_target_pairs={{0,8},{1,9},{2,10},{3,11},{4,12},{5,13},{6,14},{7,15},{8,0},{9,1},... | collective-permute-start | bytes 589832 | tf_op jit(solution)/shard_map/ppermute | solution.py:37
  22.5 4.4 %collective-permute-start.2 = (bf16[8,32,128]{2,1,0:T(8,128)(2,1)S(1)}, bf16[8,32,128]{2,1,0:T(8,128)(2,1)S(1)}, u32[]{:S(2)}, u32[]{:S(2)}) collective-permute-start(bf16[8,32,128]{2,1,0:T(8,128)(2,1)S(1)} %get-tuple-element.65), channel_id=1, source_target_pairs={{0,1},{1,0},{2,3},{3,2},{4,5},{5,4},{6,7},{7,6},{8,9},{9,8},{10,11... | collective-permute-start | bytes 196616 | tf_op jit(solution)/shard_map/ppermute | solution.py:37
  22.8 5.2 %collective-permute-start.3 = (bf16[8,32,128]{2,1,0:T(8,128)(2,1)S(1)}, bf16[8,32,128]{2,1,0:T(8,128)(2,1)S(1)}, u32[]{:S(2)}, u32[]{:S(2)}) collective-permute-start(bf16[8,32,128]{2,1,0:T(8,128)(2,1)S(1)} %get-tuple-element.66), channel_id=1, source_target_pairs={{0,2},{1,3},{2,0},{3,1},{4,6},{5,7},{6,4},{7,5},{8,10},{9,11},{10,... | collective-permute-start | bytes 196616 | tf_op jit(solution)/shard_map/ppermute | solution.py:37
  25.7 5.2 %collective-permute-start.4 = (bf16[8,32,128]{2,1,0:T(8,128)(2,1)S(1)}, bf16[8,32,128]{2,1,0:T(8,128)(2,1)S(1)}, u32[]{:S(2)}, u32[]{:S(2)}) collective-permute-start(bf16[8,32,128]{2,1,0:T(8,128)(2,1)S(1)} %get-tuple-element.67), channel_id=1, source_target_pairs={{0,3},{1,2},{2,1},{3,0},{4,7},{5,6},{6,5},{7,4},{8,11},{9,10},{10,... | collective-permute-start | bytes 196616 | tf_op jit(solution)/shard_map/ppermute | solution.py:37
  30.9 5.6 %collective-permute-start.5 = (bf16[8,32,128]{2,1,0:T(8,128)(2,1)S(1)}, bf16[8,32,128]{2,1,0:T(8,128)(2,1)S(1)}, u32[]{:S(2)}, u32[]{:S(2)}) collective-permute-start(bf16[8,32,128]{2,1,0:T(8,128)(2,1)S(1)} %add_convert_fusion.7), channel_id=1, source_target_pairs={{0,4},{1,5},{2,6},{3,7},{4,0},{5,1},{6,2},{7,3},{8,12},{9,13},{10,... | collective-permute-start | bytes 196616 | tf_op jit(solution)/shard_map/ppermute | solution.py:37
  36.5 5.2 %collective-permute-start.8 = (bf16[8,32,128]{2,1,0:T(8,128)(2,1)S(1)}, bf16[8,32,128]{2,1,0:T(8,128)(2,1)S(1)}, u32[]{:S(2)}, u32[]{:S(2)}) collective-permute-start(bf16[8,32,128]{2,1,0:T(8,128)(2,1)S(1)} %multiply_convert_fusion.3.refs_0_), channel_id=1, source_target_pairs={{0,3},{1,2},{2,1},{3,0},{4,7},{5,6},{6,5},{7,4},{8,11},{9,10},{10,... | collective-permute-start | bytes 196616 | tf_op jit(solution)/shard_map/ppermute | solution.py:37
  37.4 4.4 %collective-permute-start.7 = (bf16[8,32,128]{2,1,0:T(8,128)(2,1)S(1)}, bf16[8,32,128]{2,1,0:T(8,128)(2,1)S(1)}, u32[]{:S(2)}, u32[]{:S(2)}) collective-permute-start(bf16[8,32,128]{2,1,0:T(8,128)(2,1)S(1)} %multiply_convert_fusion.3.refs_0_), channel_id=1, source_target_pairs={{0,2},{1,3},{2,0},{3,1},{4,6},{5,7},{6,4},{7,5},{8,10},{9,11},{10,... | collective-permute-start | bytes 196616 | tf_op jit(solution)/shard_map/ppermute | solution.py:37
  37.9 4.6 %collective-permute-start.6 = (bf16[8,32,128]{2,1,0:T(8,128)(2,1)S(1)}, bf16[8,32,128]{2,1,0:T(8,128)(2,1)S(1)}, u32[]{:S(2)}, u32[]{:S(2)}) collective-permute-start(bf16[8,32,128]{2,1,0:T(8,128)(2,1)S(1)} %multiply_convert_fusion.3.refs_0_), channel_id=1, source_target_pairs={{0,1},{1,0},{2,3},{3,2},{4,5},{5,4},{6,7},{7,6},{8,9},{9,8},{10,11... | collective-permute-start | bytes 196616 | tf_op jit(solution)/shard_map/ppermute | solution.py:37
  45.4 1.5 collective-permute-start.9
  46.9 7.4 %collective-permute-start.10 = (bf16[24,32,128]{2,1,0:T(8,128)(2,1)S(1)}, bf16[24,32,128]{2,1,0:T(8,128)(2,1)S(1)}, u32[]{:S(2)}, u32[]{:S(2)}) collective-permute-start(bf16[24,32,128]{2,1,0:T(8,128)(2,1)S(1)} %add_convert_fusion.3.mine), channel_id=1, source_target_pairs={{0,16},{1,17},{2,18},{3,19},{4,20},{5,21},{6,22},{7,23},{8,24},{9,... | collective-permute-start | bytes 589832 | tf_op jit(solution)/shard_map/ppermute | solution.py:37
  56.0 1.5 collective-permute-start.11
  56.1 1.4 collective-permute-start.12
  58.7 7.4 %collective-permute-start.13 = (bf16[24,32,128]{2,1,0:T(8,128)(2,1)S(1)}, bf16[24,32,128]{2,1,0:T(8,128)(2,1)S(1)}, u32[]{:S(2)}, u32[]{:S(2)}) collective-permute-start(bf16[24,32,128]{2,1,0:T(8,128)(2,1)S(1)} %prior_spread.5.refs_0_), channel_id=1, source_target_pairs={{0,8},{1,9},{2,10},{3,11},{4,12},{5,13},{6,14},{7,15},{8,0},{9,1},... | collective-permute-start | bytes 589832 | tf_op jit(solution)/shard_map/ppermute | solution.py:37
  68.9 4.4 %collective-permute-start.14 = (bf16[8,32,128]{2,1,0:T(8,128)(2,1)S(1)}, bf16[8,32,128]{2,1,0:T(8,128)(2,1)S(1)}, u32[]{:S(2)}, u32[]{:S(2)}) collective-permute-start(bf16[8,32,128]{2,1,0:T(8,128)(2,1)S(1)} %get-tuple-element.77), channel_id=1, source_target_pairs={{0,1},{1,0},{2,3},{3,2},{4,5},{5,4},{6,7},{7,6},{8,9},{9,8},{10,11... | collective-permute-start | bytes 196616 | tf_op jit(solution)/shard_map/ppermute | solution.py:37
  70.4 4.3 %collective-permute-start.15 = (bf16[8,32,128]{2,1,0:T(8,128)(2,1)S(1)}, bf16[8,32,128]{2,1,0:T(8,128)(2,1)S(1)}, u32[]{:S(2)}, u32[]{:S(2)}) collective-permute-start(bf16[8,32,128]{2,1,0:T(8,128)(2,1)S(1)} %get-tuple-element.78), channel_id=1, source_target_pairs={{0,2},{1,3},{2,0},{3,1},{4,6},{5,7},{6,4},{7,5},{8,10},{9,11},{10,... | collective-permute-start | bytes 196616 | tf_op jit(solution)/shard_map/ppermute | solution.py:37
  72.2 5.2 %collective-permute-start.16 = (bf16[8,32,128]{2,1,0:T(8,128)(2,1)S(1)}, bf16[8,32,128]{2,1,0:T(8,128)(2,1)S(1)}, u32[]{:S(2)}, u32[]{:S(2)}) collective-permute-start(bf16[8,32,128]{2,1,0:T(8,128)(2,1)S(1)} %get-tuple-element.79), channel_id=1, source_target_pairs={{0,3},{1,2},{2,1},{3,0},{4,7},{5,6},{6,5},{7,4},{8,11},{9,10},{10,... | collective-permute-start | bytes 196616 | tf_op jit(solution)/shard_map/ppermute | solution.py:37
  77.4 5.9 %collective-permute-start.17 = (bf16[8,32,128]{2,1,0:T(8,128)(2,1)S(1)}, bf16[8,32,128]{2,1,0:T(8,128)(2,1)S(1)}, u32[]{:S(2)}, u32[]{:S(2)}) collective-permute-start(bf16[8,32,128]{2,1,0:T(8,128)(2,1)S(1)} %add_convert_fusion.6), channel_id=1, source_target_pairs={{0,4},{1,5},{2,6},{3,7},{4,0},{5,1},{6,2},{7,3},{8,12},{9,13},{10,... | collective-permute-start | bytes 196616 | tf_op jit(solution)/shard_map/ppermute | solution.py:37
  83.4 5.2 %collective-permute-start.20 = (bf16[8,32,128]{2,1,0:T(8,128)(2,1)S(1)}, bf16[8,32,128]{2,1,0:T(8,128)(2,1)S(1)}, u32[]{:S(2)}, u32[]{:S(2)}) collective-permute-start(bf16[8,32,128]{2,1,0:T(8,128)(2,1)S(1)} %multiply_convert_fusion.2.refs_0_), channel_id=1, source_target_pairs={{0,3},{1,2},{2,1},{3,0},{4,7},{5,6},{6,5},{7,4},{8,11},{9,10},{10,... | collective-permute-start | bytes 196616 | tf_op jit(solution)/shard_map/ppermute | solution.py:37
  83.8 4.8 %collective-permute-start.19 = (bf16[8,32,128]{2,1,0:T(8,128)(2,1)S(1)}, bf16[8,32,128]{2,1,0:T(8,128)(2,1)S(1)}, u32[]{:S(2)}, u32[]{:S(2)}) collective-permute-start(bf16[8,32,128]{2,1,0:T(8,128)(2,1)S(1)} %multiply_convert_fusion.2.refs_0_), channel_id=1, source_target_pairs={{0,2},{1,3},{2,0},{3,1},{4,6},{5,7},{6,4},{7,5},{8,10},{9,11},{10,... | collective-permute-start | bytes 196616 | tf_op jit(solution)/shard_map/ppermute | solution.py:37
  85.4 4.3 %collective-permute-start.18 = (bf16[8,32,128]{2,1,0:T(8,128)(2,1)S(1)}, bf16[8,32,128]{2,1,0:T(8,128)(2,1)S(1)}, u32[]{:S(2)}, u32[]{:S(2)}) collective-permute-start(bf16[8,32,128]{2,1,0:T(8,128)(2,1)S(1)} %multiply_convert_fusion.2.refs_0_), channel_id=1, source_target_pairs={{0,1},{1,0},{2,3},{3,2},{4,5},{5,4},{6,7},{7,6},{8,9},{9,8},{10,11... | collective-permute-start | bytes 196616 | tf_op jit(solution)/shard_map/ppermute | solution.py:37
  92.7 1.5 collective-permute-start.21
  94.3 7.5 %collective-permute-start.22 = (bf16[24,32,128]{2,1,0:T(8,128)(2,1)S(1)}, bf16[24,32,128]{2,1,0:T(8,128)(2,1)S(1)}, u32[]{:S(2)}, u32[]{:S(2)}) collective-permute-start(bf16[24,32,128]{2,1,0:T(8,128)(2,1)S(1)} %add_convert_fusion.2.mine), channel_id=1, source_target_pairs={{0,16},{1,17},{2,18},{3,19},{4,20},{5,21},{6,22},{7,23},{8,24},{9,... | collective-permute-start | bytes 589832 | tf_op jit(solution)/shard_map/ppermute | solution.py:37
  103.5 1.5 collective-permute-start.23
  103.5 1.4 collective-permute-start.24
  106.2 7.2 %collective-permute-start.25 = (bf16[24,32,128]{2,1,0:T(8,128)(2,1)S(1)}, bf16[24,32,128]{2,1,0:T(8,128)(2,1)S(1)}, u32[]{:S(2)}, u32[]{:S(2)}) collective-permute-start(bf16[24,32,128]{2,1,0:T(8,128)(2,1)S(1)} %prior_spread.6.refs_0_), channel_id=1, source_target_pairs={{0,8},{1,9},{2,10},{3,11},{4,12},{5,13},{6,14},{7,15},{8,0},{9,1},... | collective-permute-start | bytes 589832 | tf_op jit(solution)/shard_map/ppermute | solution.py:37
  116.1 4.4 %collective-permute-start.26 = (bf16[8,32,128]{2,1,0:T(8,128)(2,1)S(1)}, bf16[8,32,128]{2,1,0:T(8,128)(2,1)S(1)}, u32[]{:S(2)}, u32[]{:S(2)}) collective-permute-start(bf16[8,32,128]{2,1,0:T(8,128)(2,1)S(1)} %get-tuple-element.86), channel_id=1, source_target_pairs={{0,1},{1,0},{2,3},{3,2},{4,5},{5,4},{6,7},{7,6},{8,9},{9,8},{10,11... | collective-permute-start | bytes 196616 | tf_op jit(solution)/shard_map/ppermute | solution.py:37
  117.2 4.3 %collective-permute-start.27 = (bf16[8,32,128]{2,1,0:T(8,128)(2,1)S(1)}, bf16[8,32,128]{2,1,0:T(8,128)(2,1)S(1)}, u32[]{:S(2)}, u32[]{:S(2)}) collective-permute-start(bf16[8,32,128]{2,1,0:T(8,128)(2,1)S(1)} %get-tuple-element.87), channel_id=1, source_target_pairs={{0,2},{1,3},{2,0},{3,1},{4,6},{5,7},{6,4},{7,5},{8,10},{9,11},{10,... | collective-permute-start | bytes 196616 | tf_op jit(solution)/shard_map/ppermute | solution.py:37
  119.3 5.2 %collective-permute-start.28 = (bf16[8,32,128]{2,1,0:T(8,128)(2,1)S(1)}, bf16[8,32,128]{2,1,0:T(8,128)(2,1)S(1)}, u32[]{:S(2)}, u32[]{:S(2)}) collective-permute-start(bf16[8,32,128]{2,1,0:T(8,128)(2,1)S(1)} %get-tuple-element.88), channel_id=1, source_target_pairs={{0,3},{1,2},{2,1},{3,0},{4,7},{5,6},{6,5},{7,4},{8,11},{9,10},{10,... | collective-permute-start | bytes 196616 | tf_op jit(solution)/shard_map/ppermute | solution.py:37
  124.5 5.9 %collective-permute-start.29 = (bf16[8,32,128]{2,1,0:T(8,128)(2,1)S(1)}, bf16[8,32,128]{2,1,0:T(8,128)(2,1)S(1)}, u32[]{:S(2)}, u32[]{:S(2)}) collective-permute-start(bf16[8,32,128]{2,1,0:T(8,128)(2,1)S(1)} %add_convert_fusion.5), channel_id=1, source_target_pairs={{0,4},{1,5},{2,6},{3,7},{4,0},{5,1},{6,2},{7,3},{8,12},{9,13},{10,... | collective-permute-start | bytes 196616 | tf_op jit(solution)/shard_map/ppermute | solution.py:37
  130.5 5.2 %collective-permute-start.32 = (bf16[8,32,128]{2,1,0:T(8,128)(2,1)S(1)}, bf16[8,32,128]{2,1,0:T(8,128)(2,1)S(1)}, u32[]{:S(2)}, u32[]{:S(2)}) collective-permute-start(bf16[8,32,128]{2,1,0:T(8,128)(2,1)S(1)} %multiply_convert_fusion.1.refs_0_), channel_id=1, source_target_pairs={{0,3},{1,2},{2,1},{3,0},{4,7},{5,6},{6,5},{7,4},{8,11},{9,10},{10,... | collective-permute-start | bytes 196616 | tf_op jit(solution)/shard_map/ppermute | solution.py:37
  130.9 4.7 %collective-permute-start.31 = (bf16[8,32,128]{2,1,0:T(8,128)(2,1)S(1)}, bf16[8,32,128]{2,1,0:T(8,128)(2,1)S(1)}, u32[]{:S(2)}, u32[]{:S(2)}) collective-permute-start(bf16[8,32,128]{2,1,0:T(8,128)(2,1)S(1)} %multiply_convert_fusion.1.refs_0_), channel_id=1, source_target_pairs={{0,2},{1,3},{2,0},{3,1},{4,6},{5,7},{6,4},{7,5},{8,10},{9,11},{10,... | collective-permute-start | bytes 196616 | tf_op jit(solution)/shard_map/ppermute | solution.py:37
  132.6 4.3 %collective-permute-start.30 = (bf16[8,32,128]{2,1,0:T(8,128)(2,1)S(1)}, bf16[8,32,128]{2,1,0:T(8,128)(2,1)S(1)}, u32[]{:S(2)}, u32[]{:S(2)}) collective-permute-start(bf16[8,32,128]{2,1,0:T(8,128)(2,1)S(1)} %multiply_convert_fusion.1.refs_0_), channel_id=1, source_target_pairs={{0,1},{1,0},{2,3},{3,2},{4,5},{5,4},{6,7},{7,6},{8,9},{9,8},{10,11... | collective-permute-start | bytes 196616 | tf_op jit(solution)/shard_map/ppermute | solution.py:37
  139.7 1.5 collective-permute-start.33
  141.3 7.2 %collective-permute-start.34 = (bf16[24,32,128]{2,1,0:T(8,128)(2,1)S(1)}, bf16[24,32,128]{2,1,0:T(8,128)(2,1)S(1)}, u32[]{:S(2)}, u32[]{:S(2)}) collective-permute-start(bf16[24,32,128]{2,1,0:T(8,128)(2,1)S(1)} %add_convert_fusion.1.mine), channel_id=1, source_target_pairs={{0,16},{1,17},{2,18},{3,19},{4,20},{5,21},{6,22},{7,23},{8,24},{9,... | collective-permute-start | bytes 589832 | tf_op jit(solution)/shard_map/ppermute | solution.py:37
  150.2 1.5 collective-permute-start.35
  150.2 1.4 collective-permute-start.36
  152.9 7.2 %collective-permute-start.37 = (bf16[24,32,128]{2,1,0:T(8,128)(2,1)S(1)}, bf16[24,32,128]{2,1,0:T(8,128)(2,1)S(1)}, u32[]{:S(2)}, u32[]{:S(2)}) collective-permute-start(bf16[24,32,128]{2,1,0:T(8,128)(2,1)S(1)} %prior_spread.7.refs_0_), channel_id=1, source_target_pairs={{0,8},{1,9},{2,10},{3,11},{4,12},{5,13},{6,14},{7,15},{8,0},{9,1},... | collective-permute-start | bytes 589832 | tf_op jit(solution)/shard_map/ppermute | solution.py:37
  160.1 45.6 %copy-start.1 = (f32[32,128]{1,0:T(8,128)S(1)}, f32[32,128]{1,0:T(8,128)}, u32[]{:S(2)}) copy-start(f32[32,128]{1,0:T(8,128)} %param.15) | copy-start | bytes 49156
  162.8 4.4 %collective-permute-start.38 = (bf16[8,32,128]{2,1,0:T(8,128)(2,1)S(1)}, bf16[8,32,128]{2,1,0:T(8,128)(2,1)S(1)}, u32[]{:S(2)}, u32[]{:S(2)}) collective-permute-start(bf16[8,32,128]{2,1,0:T(8,128)(2,1)S(1)} %get-tuple-element.95), channel_id=1, source_target_pairs={{0,1},{1,0},{2,3},{3,2},{4,5},{5,4},{6,7},{7,6},{8,9},{9,8},{10,11... | collective-permute-start | bytes 196616 | tf_op jit(solution)/shard_map/ppermute | solution.py:37
  164.0 4.5 %collective-permute-start.39 = (bf16[8,32,128]{2,1,0:T(8,128)(2,1)S(1)}, bf16[8,32,128]{2,1,0:T(8,128)(2,1)S(1)}, u32[]{:S(2)}, u32[]{:S(2)}) collective-permute-start(bf16[8,32,128]{2,1,0:T(8,128)(2,1)S(1)} %get-tuple-element.96), channel_id=1, source_target_pairs={{0,2},{1,3},{2,0},{3,1},{4,6},{5,7},{6,4},{7,5},{8,10},{9,11},{10,... | collective-permute-start | bytes 196616 | tf_op jit(solution)/shard_map/ppermute | solution.py:37
  166.2 5.2 %collective-permute-start.40 = (bf16[8,32,128]{2,1,0:T(8,128)(2,1)S(1)}, bf16[8,32,128]{2,1,0:T(8,128)(2,1)S(1)}, u32[]{:S(2)}, u32[]{:S(2)}) collective-permute-start(bf16[8,32,128]{2,1,0:T(8,128)(2,1)S(1)} %get-tuple-element.97), channel_id=1, source_target_pairs={{0,3},{1,2},{2,1},{3,0},{4,7},{5,6},{6,5},{7,4},{8,11},{9,10},{10,... | collective-permute-start | bytes 196616 | tf_op jit(solution)/shard_map/ppermute | solution.py:37
  171.4 5.9 %collective-permute-start.41 = (bf16[8,32,128]{2,1,0:T(8,128)(2,1)S(1)}, bf16[8,32,128]{2,1,0:T(8,128)(2,1)S(1)}, u32[]{:S(2)}, u32[]{:S(2)}) collective-permute-start(bf16[8,32,128]{2,1,0:T(8,128)(2,1)S(1)} %add_convert_fusion.4), channel_id=1, source_target_pairs={{0,4},{1,5},{2,6},{3,7},{4,0},{5,1},{6,2},{7,3},{8,12},{9,13},{10,... | collective-permute-start | bytes 196616 | tf_op jit(solution)/shard_map/ppermute | solution.py:37
  177.4 5.2 %collective-permute-start.44 = (bf16[8,32,128]{2,1,0:T(8,128)(2,1)S(1)}, bf16[8,32,128]{2,1,0:T(8,128)(2,1)S(1)}, u32[]{:S(2)}, u32[]{:S(2)}) collective-permute-start(bf16[8,32,128]{2,1,0:T(8,128)(2,1)S(1)} %multiply_convert_fusion.refs_0_), channel_id=1, source_target_pairs={{0,3},{1,2},{2,1},{3,0},{4,7},{5,6},{6,5},{7,4},{8,11},{9,10},{10,... | collective-permute-start | bytes 196616 | tf_op jit(solution)/shard_map/ppermute | solution.py:37
  177.8 4.8 %collective-permute-start.43 = (bf16[8,32,128]{2,1,0:T(8,128)(2,1)S(1)}, bf16[8,32,128]{2,1,0:T(8,128)(2,1)S(1)}, u32[]{:S(2)}, u32[]{:S(2)}) collective-permute-start(bf16[8,32,128]{2,1,0:T(8,128)(2,1)S(1)} %multiply_convert_fusion.refs_0_), channel_id=1, source_target_pairs={{0,2},{1,3},{2,0},{3,1},{4,6},{5,7},{6,4},{7,5},{8,10},{9,11},{10,... | collective-permute-start | bytes 196616 | tf_op jit(solution)/shard_map/ppermute | solution.py:37
  178.6 4.7 %collective-permute-start.42 = (bf16[8,32,128]{2,1,0:T(8,128)(2,1)S(1)}, bf16[8,32,128]{2,1,0:T(8,128)(2,1)S(1)}, u32[]{:S(2)}, u32[]{:S(2)}) collective-permute-start(bf16[8,32,128]{2,1,0:T(8,128)(2,1)S(1)} %multiply_convert_fusion.refs_0_), channel_id=1, source_target_pairs={{0,1},{1,0},{2,3},{3,2},{4,5},{5,4},{6,7},{7,6},{8,9},{9,8},{10,11... | collective-permute-start | bytes 196616 | tf_op jit(solution)/shard_map/ppermute | solution.py:37
  186.5 1.5 collective-permute-start.45
  188.0 7.4 %collective-permute-start.46 = (bf16[24,32,128]{2,1,0:T(8,128)(2,1)S(1)}, bf16[24,32,128]{2,1,0:T(8,128)(2,1)S(1)}, u32[]{:S(2)}, u32[]{:S(2)}) collective-permute-start(bf16[24,32,128]{2,1,0:T(8,128)(2,1)S(1)} %add_convert_fusion.mine), channel_id=1, source_target_pairs={{0,16},{1,17},{2,18},{3,19},{4,20},{5,21},{6,22},{7,23},{8,24},{9,... | collective-permute-start | bytes 589832 | tf_op jit(solution)/shard_map/ppermute | solution.py:37
  197.1 1.4 collective-permute-start.48
  197.2 1.3 collective-permute-start.47
  198.6 6.3 %collective-permute-start.49 = (bf16[24,32,128]{2,1,0:T(8,128)(2,1)S(1)}, bf16[24,32,128]{2,1,0:T(8,128)(2,1)S(1)}, u32[]{:S(2)}, u32[]{:S(2)}) collective-permute-start(bf16[24,32,128]{2,1,0:T(8,128)(2,1)S(1)} %fusion), channel_id=1, source_target_pairs={{0,8},{1,9},{2,10},{3,11},{4,12},{5,13},{6,14},{7,15},{8,0},{9,1},... | collective-permute-start | bytes 589832 | tf_op jit(solution)/shard_map/ppermute | solution.py:37

commit v7 on v6

--- a/solution.py
+++ b/solution.py
@@ -87,7 +87,7 @@
 
 def setup_kernel(
     rows, chunk, where, obs, flux, nbr, prior, jac,
-    prior_plain, prior_turned, jac_plain, jac_turned, obs_plan, tile_plan, prior_plan, nbr_list,
+    prior_plain, jac_plain, obs_plan, tile_plan, prior_plan, nbr_list,
     obs_in, flux_in, nbr_in, obs_out, tile_out, prior_out, nbr_out, small_sems, sems
 ):
     side, corner, count, first_tile = where[0], where[1], where[2], where[3]
@@ -106,11 +106,9 @@
 
         return one
 
-    def turn(first, source, plain, turned, offset):
+    def wait(first, source, plain, offset):
         def one(c, _):
             copy(c, first, source, plain, offset).wait()
-            for u in range(chunk):
-                turned[c * chunk + u] = plain[c * chunk + u].T
             return 0
 
         return one
@@ -150,10 +148,32 @@
     for one in lists:
         one.start()
 
-    lax.fori_loop(0, rounds[0], turn(begin, prior, prior_plain, prior_turned, 0), 0)
-    lax.fori_loop(0, rounds[1], turn(0, jac, jac_plain, jac_turned, rounds[0]), 0)
+    lax.fori_loop(0, rounds[0], wait(begin, prior, prior_plain, 0), 0)
+    lax.fori_loop(0, rounds[1], wait(0, jac, jac_plain, rounds[0]), 0)
     for one in lists:
         one.wait()
+
+
+def turn_kernel(chunk, plain, turned):
+    def one(c, _):
+        for u in range(chunk):
+            turned[c * chunk + u] = plain[c * chunk + u].T
+        return 0
+
+    lax.fori_loop(0, plain.shape[0] // chunk, one, 0)
+
+
+def turn_blocks(plain, name):
+    vmem = pl.BlockSpec(memory_space=pltpu.VMEM)
+    return pl.pallas_call(
+        functools.partial(turn_kernel, chunk_of(plain.shape[0], 48)),
+        in_specs=[vmem],
+        out_specs=vmem,
+        out_shape=pltpu.VMEM(plain.shape, HALF),
+        compiler_params=pltpu.CompilerParams(vmem_limit_bytes=VMEM_LIMIT),
+        cost_estimate=pl.CostEstimate(flops=0, bytes_accessed=2 * plain.size, transcendentals=0),
+        name=name,
+    )(plain)
 
 
 def setup(where, obs, flux, nbr, prior, jac, rows):
@@ -174,8 +194,8 @@
     return pl.pallas_call(
         functools.partial(setup_kernel, rows, chunk),
         in_specs=[smem] + [hbm] * 5,
-        out_specs=[vmem] * 4 + [smem] * 4,
-        out_shape=[own, own, all_blocks, all_blocks] + [pltpu.SMEM((1, n), i32) for n in lengths],
+        out_specs=[vmem] * 2 + [smem] * 4,
+        out_shape=[own, all_blocks] + [pltpu.SMEM((1, n), i32) for n in lengths],
         scratch_shapes=[pltpu.VMEM(v.shape, i32) for v in (obs, flux, nbr)]
         + [pltpu.VMEM((1, n), i32) for n in lengths]
         + [
@@ -355,7 +375,7 @@
     nbr = neighbours.reshape(1, tile_count * fan)
 
     where, own_rinv, nbr, prior, blocks = lax.optimization_barrier((where, own_rinv, nbr, prior, blocks))
-    prior_plain, prior_turned, jac_plain, jac_turned, obs_lists, tile_lists, prior_lists, nbr = setup(
+    prior_plain, jac_plain, obs_lists, tile_lists, prior_lists, nbr = setup(
         where, jac_obs[0], jac_flux[0], nbr, prior, blocks, sizes
     )
     fields = (probes, beyond)
@@ -363,6 +383,9 @@
         spread = spread_tiles(nbr, fields, prior_plain)
         parts = (spread, swap_core(spread))
         pieces = jac_pass(OBS_PLAN, obs_lists, parts, jac_plain, rows, obs_rows, 4, "jac_forward")
+        if step == 0:
+            pieces, jac_plain = lax.optimization_barrier((pieces, jac_plain))
+            jac_turned = turn_blocks(jac_plain, "jac_turn")
         total = pieces[0]
         for bits in range(1, 4):
             total = total + swap_flux(pieces[bits], bits).astype(F32)
@@ -375,6 +398,9 @@
         parts = (weighted,) + tuple(swap_flux(weighted, bits) for bits in range(1, 4))
         mine, theirs = jac_pass(TILE_PLAN, tile_lists, parts, jac_turned, rows, tile_count, 2, "jac_adjoint")
         mine = (mine + swap_core(theirs).astype(F32)).astype(HALF)
+        if step == 0:
+            mine, prior_plain = lax.optimization_barrier((mine, prior_plain))
+            prior_turned = turn_blocks(prior_plain, "prior_turn")
         bits = 2
         while bits < n_obs:
             other = exchange(mine, lambda i, j, bits=bits: (i ^ bits, j))

time: 207 us -> 206 us (level)
  waiting for transfers between devices: 80.9 us -> 77.3 us
  Pallas kernels: 43.6 us -> 46.1 us
    pallas_call x0 -> x2, Pallas kernels: none -> 5.5 us  [turn_blocks(): pl.pallas_call(functools.partial(turn_kernel, chunk_of(plain.shape[0], 48...]
    ppermute x50, waiting for transfers between devices: 80.9 us -> 77.3 us  [exchange(): return lax.ppermute(value, ('obs', 'flux'), route)]
  transfers between devices with their start and end apart: 50 -> 50, of which waited for: 41 -> 41; matrix products, arithmetic and copies ran while one was open for 1% -> 1% of each run, Pallas kernels for 5% -> 6%
where the time goes in v7:
time: 206 us; the launch traced here: 205 us
  waiting for transfers between devices  77.3 us (38%)
  starting transfers between devices  76.4 us (37%)
  Pallas kernels  46.1 us (22%)
  other arithmetic  2.47 us (1%)
    ppermute x50, waiting for transfers between devices, exchange(): return lax.ppermute(value, ('obs', 'flux'), route)  77.3 us
    ppermute x50, starting transfers between devices, exchange(): return lax.ppermute(value, ('obs', 'flux'), route)  76.4 us
    pallas_call x8, Pallas kernels, jac_pass(): pl.pallas_call(functools.partial(jac_kernel, plan, plan_sizes(plan, jac.s...  22 us
    pallas_call x1, Pallas kernels, setup(): pl.pallas_call(functools.partial(setup_kernel, rows, chunk), in_specs=[sm...  7.3 us
    pallas_call x4, Pallas kernels, gather_tiles(): pl.pallas_call(functools.partial(gather_kernel, rows, plan_sizes(PRIOR_PL...  6.51 us
    pallas_call x2, Pallas kernels, turn_blocks(): pl.pallas_call(functools.partial(turn_kernel, chunk_of(plain.shape[0], 48...  5.5 us
    pallas_call x4, Pallas kernels, spread_tiles(): pl.pallas_call(functools.partial(spread_kernel, len(fields) == 2, prior.s...  4.83 us
  transfers between devices with their start and end apart: 50, of which 41 were waited for; matrix products, arithmetic and copies ran while one was open for 1% of the time, Pallas kernels for 6%

profile of v7, /device:TPU:0, one launch (start us, length us, event | category | flops | bytes accessed | tf_op | source)
XLA Modules:
  0.0 204.9 jit_solution(16799210259965990621)
XLA Ops:
  3.8 7.3 %setup.1 = (bf16[192,128,128]{2,1,0:T(8,128)(2,1)S(1)}, bf16[384,128,128]{2,1,0:T(8,128)(2,1)S(1)}, s32[1,1792]{1,0:T(1,128)S(4)}, s32[1,1792]{1,0:T(1,128)S(4)}...) custom-call(s32[4]{0:T(128)S(1)} %pad_add_fusion.where, s32[1,384]{1,0:T(1,128)} %bitcast.20, s32[1,384]{1,0:T(1,128)} %bitcast.21, ...), custom_call_target="tpu_custom_call" | custom-call | tf_op jit(solution)/shard_map/setup/pallas_call | solution.py:194
  12.2 4.4 %collective-permute-start.1 = (bf16[24,32,128]{2,1,0:T(8,128)(2,1)S(1)}, bf16[24,32,128]{2,1,0:T(8,128)(2,1)S(1)}, u32[]{:S(2)}, u32[]{:S(2)}) collective-permute-start(bf16[24,32,128]{2,1,0:T(8,128)(2,1)S(1)} %prior_spread.4.refs_0_), channel_id=1, source_target_pairs={{0,8},{1,9},{2,10},{3,11},{4,12},{5,13},{6,14},{7,15},{8,0},{9,1},... | collective-permute-start | bytes 589832 | tf_op jit(solution)/shard_map/ppermute | solution.py:37
  17.7 2.6 %jac_forward.4 = (f32[8,32,128]{2,1,0:T(8,128)S(1)}, bf16[8,32,128]{2,1,0:T(8,128)(2,1)S(1)}, bf16[8,32,128]{2,1,0:T(8,128)(2,1)S(1)}, bf16[8,32,128]{2,1,0:T(8,128)(2,1)S(1)}) custom-call(s32[1,1792]{1,0:T(1,128)S(4)} %get-tuple-element.66.lists, bf16[24,32,128]{2,1,0:T(8,128)(2,1)S(1)} %prior_spread.4.refs_0_, ...), custom_call_target="tpu_custom_call" | custom-call | tf_op jit(solution)/shard_map/jac_forward/pallas_call | solution.py:250
  20.7 2.9 %collective-permute-start.3 = (bf16[8,32,128]{2,1,0:T(8,128)(2,1)S(1)}, bf16[8,32,128]{2,1,0:T(8,128)(2,1)S(1)}, u32[]{:S(2)}, u32[]{:S(2)}) collective-permute-start(bf16[8,32,128]{2,1,0:T(8,128)(2,1)S(1)} %get-tuple-element.75), channel_id=1, source_target_pairs={{0,2},{1,3},{2,0},{3,1},{4,6},{5,7},{6,4},{7,5},{8,10},{9,11},{10,... | collective-permute-start | bytes 196616 | tf_op jit(solution)/shard_map/ppermute | solution.py:37
  24.7 1.5 collective-permute-done.3
  26.2 2.5 %collective-permute-done.4 = bf16[8,32,128]{2,1,0:T(8,128)(2,1)S(1)} collective-permute-done((bf16[8,32,128]{2,1,0:T(8,128)(2,1)S(1)}, bf16[8,32,128]{2,1,0:T(8,128)(2,1)S(1)}, u32[]{:S(2)}, u32[]{:S(2)}) %collective-permute-start.4) | collective-permute-done | bytes 65568 | tf_op jit(solution)/shard_map/ppermute | solution.py:37
  28.7 1.5 collective-permute-start.5
  30.2 4.3 %collective-permute-done.5 = bf16[8,32,128]{2,1,0:T(8,128)(2,1)S(1)} collective-permute-done((bf16[8,32,128]{2,1,0:T(8,128)(2,1)S(1)}, bf16[8,32,128]{2,1,0:T(8,128)(2,1)S(1)}, u32[]{:S(2)}, u32[]{:S(2)}) %collective-permute-start.5) | collective-permute-done | bytes 65568 | tf_op jit(solution)/shard_map/ppermute | solution.py:37
  36.0 2.1 %collective-permute-start.6 = (bf16[8,32,128]{2,1,0:T(8,128)(2,1)S(1)}, bf16[8,32,128]{2,1,0:T(8,128)(2,1)S(1)}, u32[]{:S(2)}, u32[]{:S(2)}) collective-permute-start(bf16[8,32,128]{2,1,0:T(8,128)(2,1)S(1)} %multiply_convert_fusion.3.refs_0_), channel_id=1, source_target_pairs={{0,1},{1,0},{2,3},{3,2},{4,5},{5,4},{6,7},{7,6},{8,9},{9,8},{10,11... | collective-permute-start | bytes 196616 | tf_op jit(solution)/shard_map/ppermute | solution.py:37
  38.1 3.7 %jac_turn.1.refs_4_ = bf16[384,128,128]{2,1,0:T(8,128)(2,1)S(1)} custom-call(bf16[384,128,128]{2,1,0:T(8,128)(2,1)S(1)} %get-tuple-element.78.refs_2_.plain), custom_call_target="tpu_custom_call" | custom-call | bytes 12582912 | tf_op jit(solution)/shard_map/jac_turn/pallas_call | solution.py:168
  41.9 2.8 %jac_adjoint.4 = (f32[24,32,128]{2,1,0:T(8,128)S(1)}, bf16[24,32,128]{2,1,0:T(8,128)(2,1)S(1)}) custom-call(s32[1,1792]{1,0:T(1,128)S(4)} %get-tuple-element.65.lists, bf16[8,32,128]{2,1,0:T(8,128)(2,1)S(1)} %multiply_convert_fusion.3.refs_0_, bf16[8,32,128]{2,1,0:T(8,128)(2,1)S(1)} %collective-permute-done.6.refs_1_, ...), custom_call_target="tpu_custom_call" | custom-call | tf_op jit(solution)/shard_map/jac_adjoint/pallas_call | solution.py:250
  44.7 1.4 collective-permute-done.9
  47.3 1.8 prior_turn.1.prior
  49.1 4.1 %collective-permute-done.10.other = bf16[24,32,128]{2,1,0:T(8,128)(2,1)S(1)} collective-permute-done((bf16[24,32,128]{2,1,0:T(8,128)(2,1)S(1)}, bf16[24,32,128]{2,1,0:T(8,128)(2,1)S(1)}, u32[]{:S(2)}, u32[]{:S(2)}) %collective-permute-start.10) | collective-permute-done | bytes 196640 | tf_op jit(solution)/shard_map/ppermute | solution.py:37
  53.2 1.6 prior_adjoint.4
  56.4 1.2 prior_spread.5.refs_0_
  57.6 6.1 %collective-permute-start.13 = (bf16[24,32,128]{2,1,0:T(8,128)(2,1)S(1)}, bf16[24,32,128]{2,1,0:T(8,128)(2,1)S(1)}, u32[]{:S(2)}, u32[]{:S(2)}) collective-permute-start(bf16[24,32,128]{2,1,0:T(8,128)(2,1)S(1)} %prior_spread.5.refs_0_), channel_id=1, source_target_pairs={{0,8},{1,9},{2,10},{3,11},{4,12},{5,13},{6,14},{7,15},{8,0},{9,1},... | collective-permute-start | bytes 589832 | tf_op jit(solution)/shard_map/ppermute | solution.py:37
  64.8 2.6 %jac_forward.5 = (f32[8,32,128]{2,1,0:T(8,128)S(1)}, bf16[8,32,128]{2,1,0:T(8,128)(2,1)S(1)}, bf16[8,32,128]{2,1,0:T(8,128)(2,1)S(1)}, bf16[8,32,128]{2,1,0:T(8,128)(2,1)S(1)}) custom-call(s32[1,1792]{1,0:T(1,128)S(4)} %get-tuple-element.66.lists, bf16[24,32,128]{2,1,0:T(8,128)(2,1)S(1)} %prior_spread.5.refs_0_, ...), custom_call_target="tpu_custom_call" | custom-call | tf_op jit(solution)/shard_map/jac_forward/pallas_call | solution.py:250
  68.6 2.1 %collective-permute-start.15 = (bf16[8,32,128]{2,1,0:T(8,128)(2,1)S(1)}, bf16[8,32,128]{2,1,0:T(8,128)(2,1)S(1)}, u32[]{:S(2)}, u32[]{:S(2)}) collective-permute-start(bf16[8,32,128]{2,1,0:T(8,128)(2,1)S(1)} %get-tuple-element.88), channel_id=1, source_target_pairs={{0,2},{1,3},{2,0},{3,1},{4,6},{5,7},{6,4},{7,5},{8,10},{9,11},{10,... | collective-permute-start | bytes 196616 | tf_op jit(solution)/shard_map/ppermute | solution.py:37
  72.3 1.2 collective-permute-done.15
  73.5 2.3 %collective-permute-done.16 = bf16[8,32,128]{2,1,0:T(8,128)(2,1)S(1)} collective-permute-done((bf16[8,32,128]{2,1,0:T(8,128)(2,1)S(1)}, bf16[8,32,128]{2,1,0:T(8,128)(2,1)S(1)}, u32[]{:S(2)}, u32[]{:S(2)}) %collective-permute-start.16) | collective-permute-done | bytes 65568 | tf_op jit(solution)/shard_map/ppermute | solution.py:37
  75.9 2.1 %collective-permute-start.17 = (bf16[8,32,128]{2,1,0:T(8,128)(2,1)S(1)}, bf16[8,32,128]{2,1,0:T(8,128)(2,1)S(1)}, u32[]{:S(2)}, u32[]{:S(2)}) collective-permute-start(bf16[8,32,128]{2,1,0:T(8,128)(2,1)S(1)} %add_convert_fusion.6), channel_id=1, source_target_pairs={{0,4},{1,5},{2,6},{3,7},{4,0},{5,1},{6,2},{7,3},{8,12},{9,13},{10,... | collective-permute-start | bytes 196616 | tf_op jit(solution)/shard_map/ppermute | solution.py:37
  78.0 3.8 %collective-permute-done.17 = bf16[8,32,128]{2,1,0:T(8,128)(2,1)S(1)} collective-permute-done((bf16[8,32,128]{2,1,0:T(8,128)(2,1)S(1)}, bf16[8,32,128]{2,1,0:T(8,128)(2,1)S(1)}, u32[]{:S(2)}, u32[]{:S(2)}) %collective-permute-start.17) | collective-permute-done | bytes 65568 | tf_op jit(solution)/shard_map/ppermute | solution.py:37
  82.3 2.1 %collective-permute-start.19 = (bf16[8,32,128]{2,1,0:T(8,128)(2,1)S(1)}, bf16[8,32,128]{2,1,0:T(8,128)(2,1)S(1)}, u32[]{:S(2)}, u32[]{:S(2)}) collective-permute-start(bf16[8,32,128]{2,1,0:T(8,128)(2,1)S(1)} %multiply_convert_fusion.2.refs_0_), channel_id=1, source_target_pairs={{0,2},{1,3},{2,0},{3,1},{4,6},{5,7},{6,4},{7,5},{8,10},{9,11},{10,... | collective-permute-start | bytes 196616 | tf_op jit(solution)/shard_map/ppermute | solution.py:37
  85.4 1.7 collective-permute-done.20.refs_3_
  87.4 1.3 collective-permute-done.18.refs_1_
  88.7 2.9 %jac_adjoint.5 = (f32[24,32,128]{2,1,0:T(8,128)S(1)}, bf16[24,32,128]{2,1,0:T(8,128)(2,1)S(1)}) custom-call(s32[1,1792]{1,0:T(1,128)S(4)} %get-tuple-element.65.lists, bf16[8,32,128]{2,1,0:T(8,128)(2,1)S(1)} %multiply_convert_fusion.2.refs_0_, bf16[8,32,128]{2,1,0:T(8,128)(2,1)S(1)} %collective-permute-done.18.refs_1_, ...), custom_call_target="tpu_custom_call" | custom-call | tf_op jit(solution)/shard_map/jac_adjoint/pallas_call | solution.py:250
  91.7 1.4 collective-permute-done.21
  93.2 1.4 collective-permute-start.22
  94.7 5.6 %collective-permute-done.22.other = bf16[24,32,128]{2,1,0:T(8,128)(2,1)S(1)} collective-permute-done((bf16[24,32,128]{2,1,0:T(8,128)(2,1)S(1)}, bf16[24,32,128]{2,1,0:T(8,128)(2,1)S(1)}, u32[]{:S(2)}, u32[]{:S(2)}) %collective-permute-start.22) | collective-permute-done | bytes 196640 | tf_op jit(solution)/shard_map/ppermute | solution.py:37
  100.2 1.6 prior_adjoint.5
  103.4 1.2 prior_spread.6.refs_0_
  104.6 6.1 %collective-permute-start.25 = (bf16[24,32,128]{2,1,0:T(8,128)(2,1)S(1)}, bf16[24,32,128]{2,1,0:T(8,128)(2,1)S(1)}, u32[]{:S(2)}, u32[]{:S(2)}) collective-permute-start(bf16[24,32,128]{2,1,0:T(8,128)(2,1)S(1)} %prior_spread.6.refs_0_), channel_id=1, source_target_pairs={{0,8},{1,9},{2,10},{3,11},{4,12},{5,13},{6,14},{7,15},{8,0},{9,1},... | collective-permute-start | bytes 589832 | tf_op jit(solution)/shard_map/ppermute | solution.py:37
  111.8 2.6 %jac_forward.6 = (f32[8,32,128]{2,1,0:T(8,128)S(1)}, bf16[8,32,128]{2,1,0:T(8,128)(2,1)S(1)}, bf16[8,32,128]{2,1,0:T(8,128)(2,1)S(1)}, bf16[8,32,128]{2,1,0:T(8,128)(2,1)S(1)}) custom-call(s32[1,1792]{1,0:T(1,128)S(4)} %get-tuple-element.66.lists, bf16[24,32,128]{2,1,0:T(8,128)(2,1)S(1)} %prior_spread.6.refs_0_, ...), custom_call_target="tpu_custom_call" | custom-call | tf_op jit(solution)/shard_map/jac_forward/pallas_call | solution.py:250
  115.6 2.3 %collective-permute-start.27 = (bf16[8,32,128]{2,1,0:T(8,128)(2,1)S(1)}, bf16[8,32,128]{2,1,0:T(8,128)(2,1)S(1)}, u32[]{:S(2)}, u32[]{:S(2)}) collective-permute-start(bf16[8,32,128]{2,1,0:T(8,128)(2,1)S(1)} %get-tuple-element.97), channel_id=1, source_target_pairs={{0,2},{1,3},{2,0},{3,1},{4,6},{5,7},{6,4},{7,5},{8,10},{9,11},{10,... | collective-permute-start | bytes 196616 | tf_op jit(solution)/shard_map/ppermute | solution.py:37
  119.3 1.6 collective-permute-done.27
  120.9 2.2 %collective-permute-done.28 = bf16[8,32,128]{2,1,0:T(8,128)(2,1)S(1)} collective-permute-done((bf16[8,32,128]{2,1,0:T(8,128)(2,1)S(1)}, bf16[8,32,128]{2,1,0:T(8,128)(2,1)S(1)}, u32[]{:S(2)}, u32[]{:S(2)}) %collective-permute-start.28) | collective-permute-done | bytes 65568 | tf_op jit(solution)/shard_map/ppermute | solution.py:37
  123.2 2.3 %collective-permute-start.29 = (bf16[8,32,128]{2,1,0:T(8,128)(2,1)S(1)}, bf16[8,32,128]{2,1,0:T(8,128)(2,1)S(1)}, u32[]{:S(2)}, u32[]{:S(2)}) collective-permute-start(bf16[8,32,128]{2,1,0:T(8,128)(2,1)S(1)} %add_convert_fusion.5), channel_id=1, source_target_pairs={{0,4},{1,5},{2,6},{3,7},{4,0},{5,1},{6,2},{7,3},{8,12},{9,13},{10,... | collective-permute-start | bytes 196616 | tf_op jit(solution)/shard_map/ppermute | solution.py:37
  125.4 3.7 %collective-permute-done.29 = bf16[8,32,128]{2,1,0:T(8,128)(2,1)S(1)} collective-permute-done((bf16[8,32,128]{2,1,0:T(8,128)(2,1)S(1)}, bf16[8,32,128]{2,1,0:T(8,128)(2,1)S(1)}, u32[]{:S(2)}, u32[]{:S(2)}) %collective-permute-start.29) | collective-permute-done | bytes 65568 | tf_op jit(solution)/shard_map/ppermute | solution.py:37
  130.6 2.0 collective-permute-start.30
  132.7 1.7 collective-permute-done.32.refs_3_
  135.1 2.8 %jac_adjoint.6 = (f32[24,32,128]{2,1,0:T(8,128)S(1)}, bf16[24,32,128]{2,1,0:T(8,128)(2,1)S(1)}) custom-call(s32[1,1792]{1,0:T(1,128)S(4)} %get-tuple-element.65.lists, bf16[8,32,128]{2,1,0:T(8,128)(2,1)S(1)} %multiply_convert_fusion.1.refs_0_, bf16[8,32,128]{2,1,0:T(8,128)(2,1)S(1)} %collective-permute-done.30.refs_1_, ...), custom_call_target="tpu_custom_call" | custom-call | tf_op jit(solution)/shard_map/jac_adjoint/pallas_call | solution.py:250
  137.9 1.4 collective-permute-done.33
  139.4 1.7 collective-permute-start.34
  141.1 5.4 %collective-permute-done.34.other = bf16[24,32,128]{2,1,0:T(8,128)(2,1)S(1)} collective-permute-done((bf16[24,32,128]{2,1,0:T(8,128)(2,1)S(1)}, bf16[24,32,128]{2,1,0:T(8,128)(2,1)S(1)}, u32[]{:S(2)}, u32[]{:S(2)}) %collective-permute-start.34) | collective-permute-done | bytes 196640 | tf_op jit(solution)/shard_map/ppermute | solution.py:37
  146.4 1.6 prior_adjoint.6
  149.6 1.2 prior_spread.7.refs_0_
  150.8 7.0 %collective-permute-start.37 = (bf16[24,32,128]{2,1,0:T(8,128)(2,1)S(1)}, bf16[24,32,128]{2,1,0:T(8,128)(2,1)S(1)}, u32[]{:S(2)}, u32[]{:S(2)}) collective-permute-start(bf16[24,32,128]{2,1,0:T(8,128)(2,1)S(1)} %prior_spread.7.refs_0_), channel_id=1, source_target_pairs={{0,8},{1,9},{2,10},{3,11},{4,12},{5,13},{6,14},{7,15},{8,0},{9,1},... | collective-permute-start | bytes 589832 | tf_op jit(solution)/shard_map/ppermute | solution.py:37
  158.8 2.6 %jac_forward.7 = (f32[8,32,128]{2,1,0:T(8,128)S(1)}, bf16[8,32,128]{2,1,0:T(8,128)(2,1)S(1)}, bf16[8,32,128]{2,1,0:T(8,128)(2,1)S(1)}, bf16[8,32,128]{2,1,0:T(8,128)(2,1)S(1)}) custom-call(s32[1,1792]{1,0:T(1,128)S(4)} %get-tuple-element.66.lists, bf16[24,32,128]{2,1,0:T(8,128)(2,1)S(1)} %prior_spread.7.refs_0_, ...), custom_call_target="tpu_custom_call" | custom-call | tf_op jit(solution)/shard_map/jac_forward/pallas_call | solution.py:250
  161.5 1.5 collective-permute-start.38
  163.0 1.6 collective-permute-start.39
  166.3 1.5 collective-permute-done.39
  167.8 2.0 collective-permute-done.40
  169.9 2.9 %collective-permute-start.41 = (bf16[8,32,128]{2,1,0:T(8,128)(2,1)S(1)}, bf16[8,32,128]{2,1,0:T(8,128)(2,1)S(1)}, u32[]{:S(2)}, u32[]{:S(2)}) collective-permute-start(bf16[8,32,128]{2,1,0:T(8,128)(2,1)S(1)} %add_convert_fusion.4), channel_id=1, source_target_pairs={{0,4},{1,5},{2,6},{3,7},{4,0},{5,1},{6,2},{7,3},{8,12},{9,13},{10,... | collective-permute-start | bytes 196616 | tf_op jit(solution)/shard_map/ppermute | solution.py:37
  172.8 3.3 %collective-permute-done.41 = bf16[8,32,128]{2,1,0:T(8,128)(2,1)S(1)} collective-permute-done((bf16[8,32,128]{2,1,0:T(8,128)(2,1)S(1)}, bf16[8,32,128]{2,1,0:T(8,128)(2,1)S(1)}, u32[]{:S(2)}, u32[]{:S(2)}) %collective-permute-start.41) | collective-permute-done | bytes 65568 | tf_op jit(solution)/shard_map/ppermute | solution.py:37
  176.6 2.1 %collective-permute-start.43 = (bf16[8,32,128]{2,1,0:T(8,128)(2,1)S(1)}, bf16[8,32,128]{2,1,0:T(8,128)(2,1)S(1)}, u32[]{:S(2)}, u32[]{:S(2)}) collective-permute-start(bf16[8,32,128]{2,1,0:T(8,128)(2,1)S(1)} %multiply_convert_fusion.refs_0_), channel_id=1, source_target_pairs={{0,2},{1,3},{2,0},{3,1},{4,6},{5,7},{6,4},{7,5},{8,10},{9,11},{10,... | collective-permute-start | bytes 196616 | tf_op jit(solution)/shard_map/ppermute | solution.py:37
  179.6 1.7 collective-permute-done.44.refs_3_
  181.7 1.3 collective-permute-done.42.refs_1_
  183.0 3.0 %jac_adjoint.7 = (f32[24,32,128]{2,1,0:T(8,128)S(1)}, bf16[24,32,128]{2,1,0:T(8,128)(2,1)S(1)}) custom-call(s32[1,1792]{1,0:T(1,128)S(4)} %get-tuple-element.65.lists, bf16[8,32,128]{2,1,0:T(8,128)(2,1)S(1)} %multiply_convert_fusion.refs_0_, bf16[8,32,128]{2,1,0:T(8,128)(2,1)S(1)} %collective-permute-done.42.refs_1_, ...), custom_call_target="tpu_custom_call" | custom-call | tf_op jit(solution)/shard_map/jac_adjoint/pallas_call | solution.py:250
  186.1 1.4 collective-permute-done.45
  187.6 1.7 collective-permute-start.46
  189.3 5.3 %collective-permute-done.46.other = bf16[24,32,128]{2,1,0:T(8,128)(2,1)S(1)} collective-permute-done((bf16[24,32,128]{2,1,0:T(8,128)(2,1)S(1)}, bf16[24,32,128]{2,1,0:T(8,128)(2,1)S(1)}, u32[]{:S(2)}, u32[]{:S(2)}) %collective-permute-start.46) | collective-permute-done | bytes 196640 | tf_op jit(solution)/shard_map/ppermute | solution.py:37
  194.6 1.6 prior_adjoint.7
  197.8 5.2 %collective-permute-start.49 = (bf16[24,32,128]{2,1,0:T(8,128)(2,1)S(1)}, bf16[24,32,128]{2,1,0:T(8,128)(2,1)S(1)}, u32[]{:S(2)}, u32[]{:S(2)}) collective-permute-start(bf16[24,32,128]{2,1,0:T(8,128)(2,1)S(1)} %fusion), channel_id=1, source_target_pairs={{0,8},{1,9},{2,10},{3,11},{4,12},{5,13},{6,14},{7,15},{8,0},{9,1},... | collective-permute-start | bytes 589832 | tf_op jit(solution)/shard_map/ppermute | solution.py:37
  (91 shorter events, 33.9 us)
Async XLA Ops:
  0.0 3.7 %copy-start = (f32[32,128]{1,0:T(8,128)S(1)}, f32[32,128]{1,0:T(8,128)}, u32[]{:S(2)}) copy-start(f32[32,128]{1,0:T(8,128)} %param.15) | copy-start | bytes 49156
  1.0 10.1 %collective-permute-start = (bf16[12,32,128]{2,1,0:T(8,128)(2,1)S(1)}, bf16[12,32,128]{2,1,0:T(8,128)(2,1)S(1)}, u32[]{:S(2)}, u32[]{:S(2)}) collective-permute-start(bf16[12,32,128]{2,1,0:T(8,128)(2,1)S(1)} %slice_select_fusion.2), channel_id=1, source_target_pairs={{1,8},{2,9},{3,10},{4,11},{5,12},{6,13},{7,14},{8,1},{9,2},{10,3},... | collective-permute-start | bytes 294920 | tf_op jit(solution)/shard_map/ppermute | solution.py:37
  3.8 7.3 %copy-start.3 = (bf16[48,32,128]{2,1,0:T(8,128)(2,1)S(1)}, bf16[48,32,128]{2,1,0:T(8,128)(2,1)}, u32[]{:S(2)}) copy-start(bf16[48,32,128]{2,1,0:T(8,128)(2,1)} %refs_0_.1) | copy-start | bytes 1179652
  12.2 5.5 %collective-permute-start.1 = (bf16[24,32,128]{2,1,0:T(8,128)(2,1)S(1)}, bf16[24,32,128]{2,1,0:T(8,128)(2,1)S(1)}, u32[]{:S(2)}, u32[]{:S(2)}) collective-permute-start(bf16[24,32,128]{2,1,0:T(8,128)(2,1)S(1)} %prior_spread.4.refs_0_), channel_id=1, source_target_pairs={{0,8},{1,9},{2,10},{3,11},{4,12},{5,13},{6,14},{7,15},{8,0},{9,1},... | collective-permute-start | bytes 589832 | tf_op jit(solution)/shard_map/ppermute | solution.py:37
  20.3 4.3 %collective-permute-start.2 = (bf16[8,32,128]{2,1,0:T(8,128)(2,1)S(1)}, bf16[8,32,128]{2,1,0:T(8,128)(2,1)S(1)}, u32[]{:S(2)}, u32[]{:S(2)}) collective-permute-start(bf16[8,32,128]{2,1,0:T(8,128)(2,1)S(1)} %get-tuple-element.74), channel_id=1, source_target_pairs={{0,1},{1,0},{2,3},{3,2},{4,5},{5,4},{6,7},{7,6},{8,9},{9,8},{10,11... | collective-permute-start | bytes 196616 | tf_op jit(solution)/shard_map/ppermute | solution.py:37
  20.7 5.5 %collective-permute-start.3 = (bf16[8,32,128]{2,1,0:T(8,128)(2,1)S(1)}, bf16[8,32,128]{2,1,0:T(8,128)(2,1)S(1)}, u32[]{:S(2)}, u32[]{:S(2)}) collective-permute-start(bf16[8,32,128]{2,1,0:T(8,128)(2,1)S(1)} %get-tuple-element.75), channel_id=1, source_target_pairs={{0,2},{1,3},{2,0},{3,1},{4,6},{5,7},{6,4},{7,5},{8,10},{9,11},{10,... | collective-permute-start | bytes 196616 | tf_op jit(solution)/shard_map/ppermute | solution.py:37
  23.5 5.2 %collective-permute-start.4 = (bf16[8,32,128]{2,1,0:T(8,128)(2,1)S(1)}, bf16[8,32,128]{2,1,0:T(8,128)(2,1)S(1)}, u32[]{:S(2)}, u32[]{:S(2)}) collective-permute-start(bf16[8,32,128]{2,1,0:T(8,128)(2,1)S(1)} %get-tuple-element.76), channel_id=1, source_target_pairs={{0,3},{1,2},{2,1},{3,0},{4,7},{5,6},{6,5},{7,4},{8,11},{9,10},{10,... | collective-permute-start | bytes 196616 | tf_op jit(solution)/shard_map/ppermute | solution.py:37
  28.7 5.8 %collective-permute-start.5 = (bf16[8,32,128]{2,1,0:T(8,128)(2,1)S(1)}, bf16[8,32,128]{2,1,0:T(8,128)(2,1)S(1)}, u32[]{:S(2)}, u32[]{:S(2)}) collective-permute-start(bf16[8,32,128]{2,1,0:T(8,128)(2,1)S(1)} %add_convert_fusion.7), channel_id=1, source_target_pairs={{0,4},{1,5},{2,6},{3,7},{4,0},{5,1},{6,2},{7,3},{8,12},{9,13},{10,... | collective-permute-start | bytes 196616 | tf_op jit(solution)/shard_map/ppermute | solution.py:37
  34.6 7.2 %collective-permute-start.8 = (bf16[8,32,128]{2,1,0:T(8,128)(2,1)S(1)}, bf16[8,32,128]{2,1,0:T(8,128)(2,1)S(1)}, u32[]{:S(2)}, u32[]{:S(2)}) collective-permute-start(bf16[8,32,128]{2,1,0:T(8,128)(2,1)S(1)} %multiply_convert_fusion.3.refs_0_), channel_id=1, source_target_pairs={{0,3},{1,2},{2,1},{3,0},{4,7},{5,6},{6,5},{7,4},{8,11},{9,10},{10,... | collective-permute-start | bytes 196616 | tf_op jit(solution)/shard_map/ppermute | solution.py:37
  35.3 6.6 %collective-permute-start.7 = (bf16[8,32,128]{2,1,0:T(8,128)(2,1)S(1)}, bf16[8,32,128]{2,1,0:T(8,128)(2,1)S(1)}, u32[]{:S(2)}, u32[]{:S(2)}) collective-permute-start(bf16[8,32,128]{2,1,0:T(8,128)(2,1)S(1)} %multiply_convert_fusion.3.refs_0_), channel_id=1, source_target_pairs={{0,2},{1,3},{2,0},{3,1},{4,6},{5,7},{6,4},{7,5},{8,10},{9,11},{10,... | collective-permute-start | bytes 196616 | tf_op jit(solution)/shard_map/ppermute | solution.py:37
  36.0 5.8 %collective-permute-start.6 = (bf16[8,32,128]{2,1,0:T(8,128)(2,1)S(1)}, bf16[8,32,128]{2,1,0:T(8,128)(2,1)S(1)}, u32[]{:S(2)}, u32[]{:S(2)}) collective-permute-start(bf16[8,32,128]{2,1,0:T(8,128)(2,1)S(1)} %multiply_convert_fusion.3.refs_0_), channel_id=1, source_target_pairs={{0,1},{1,0},{2,3},{3,2},{4,5},{5,4},{6,7},{7,6},{8,9},{9,8},{10,11... | collective-permute-start | bytes 196616 | tf_op jit(solution)/shard_map/ppermute | solution.py:37
  44.6 1.5 collective-permute-start.9
  46.2 7.0 %collective-permute-start.10 = (bf16[24,32,128]{2,1,0:T(8,128)(2,1)S(1)}, bf16[24,32,128]{2,1,0:T(8,128)(2,1)S(1)}, u32[]{:S(2)}, u32[]{:S(2)}) collective-permute-start(bf16[24,32,128]{2,1,0:T(8,128)(2,1)S(1)} %add_convert_fusion.3.mine), channel_id=1, source_target_pairs={{0,16},{1,17},{2,18},{3,19},{4,20},{5,21},{6,22},{7,23},{8,24},{9,... | collective-permute-start | bytes 589832 | tf_op jit(solution)/shard_map/ppermute | solution.py:37
  49.1 97.3 %copy-start.2 = (bf16[192,128,128]{2,1,0:T(8,128)(2,1)}, bf16[192,128,128]{2,1,0:T(8,128)(2,1)S(1)}, u32[]{:S(2)}) copy-start(bf16[192,128,128]{2,1,0:T(8,128)(2,1)S(1)} %prior_turn.1.prior) | copy-start | bytes 18874372
  54.8 1.5 collective-permute-start.11
  54.9 1.4 collective-permute-start.12
  57.6 7.2 %collective-permute-start.13 = (bf16[24,32,128]{2,1,0:T(8,128)(2,1)S(1)}, bf16[24,32,128]{2,1,0:T(8,128)(2,1)S(1)}, u32[]{:S(2)}, u32[]{:S(2)}) collective-permute-start(bf16[24,32,128]{2,1,0:T(8,128)(2,1)S(1)} %prior_spread.5.refs_0_), channel_id=1, source_target_pairs={{0,8},{1,9},{2,10},{3,11},{4,12},{5,13},{6,14},{7,15},{8,0},{9,1},... | collective-permute-start | bytes 589832 | tf_op jit(solution)/shard_map/ppermute | solution.py:37
  67.4 4.8 %collective-permute-start.14 = (bf16[8,32,128]{2,1,0:T(8,128)(2,1)S(1)}, bf16[8,32,128]{2,1,0:T(8,128)(2,1)S(1)}, u32[]{:S(2)}, u32[]{:S(2)}) collective-permute-start(bf16[8,32,128]{2,1,0:T(8,128)(2,1)S(1)} %get-tuple-element.87), channel_id=1, source_target_pairs={{0,1},{1,0},{2,3},{3,2},{4,5},{5,4},{6,7},{7,6},{8,9},{9,8},{10,11... | collective-permute-start | bytes 196616 | tf_op jit(solution)/shard_map/ppermute | solution.py:37
  68.6 4.9 %collective-permute-start.15 = (bf16[8,32,128]{2,1,0:T(8,128)(2,1)S(1)}, bf16[8,32,128]{2,1,0:T(8,128)(2,1)S(1)}, u32[]{:S(2)}, u32[]{:S(2)}) collective-permute-start(bf16[8,32,128]{2,1,0:T(8,128)(2,1)S(1)} %get-tuple-element.88), channel_id=1, source_target_pairs={{0,2},{1,3},{2,0},{3,1},{4,6},{5,7},{6,4},{7,5},{8,10},{9,11},{10,... | collective-permute-start | bytes 196616 | tf_op jit(solution)/shard_map/ppermute | solution.py:37
  70.7 5.2 %collective-permute-start.16 = (bf16[8,32,128]{2,1,0:T(8,128)(2,1)S(1)}, bf16[8,32,128]{2,1,0:T(8,128)(2,1)S(1)}, u32[]{:S(2)}, u32[]{:S(2)}) collective-permute-start(bf16[8,32,128]{2,1,0:T(8,128)(2,1)S(1)} %get-tuple-element.89), channel_id=1, source_target_pairs={{0,3},{1,2},{2,1},{3,0},{4,7},{5,6},{6,5},{7,4},{8,11},{9,10},{10,... | collective-permute-start | bytes 196616 | tf_op jit(solution)/shard_map/ppermute | solution.py:37
  75.9 5.9 %collective-permute-start.17 = (bf16[8,32,128]{2,1,0:T(8,128)(2,1)S(1)}, bf16[8,32,128]{2,1,0:T(8,128)(2,1)S(1)}, u32[]{:S(2)}, u32[]{:S(2)}) collective-permute-start(bf16[8,32,128]{2,1,0:T(8,128)(2,1)S(1)} %add_convert_fusion.6), channel_id=1, source_target_pairs={{0,4},{1,5},{2,6},{3,7},{4,0},{5,1},{6,2},{7,3},{8,12},{9,13},{10,... | collective-permute-start | bytes 196616 | tf_op jit(solution)/shard_map/ppermute | solution.py:37
  81.9 5.2 %collective-permute-start.20 = (bf16[8,32,128]{2,1,0:T(8,128)(2,1)S(1)}, bf16[8,32,128]{2,1,0:T(8,128)(2,1)S(1)}, u32[]{:S(2)}, u32[]{:S(2)}) collective-permute-start(bf16[8,32,128]{2,1,0:T(8,128)(2,1)S(1)} %multiply_convert_fusion.2.refs_0_), channel_id=1, source_target_pairs={{0,3},{1,2},{2,1},{3,0},{4,7},{5,6},{6,5},{7,4},{8,11},{9,10},{10,... | collective-permute-start | bytes 196616 | tf_op jit(solution)/shard_map/ppermute | solution.py:37
  82.3 5.1 %collective-permute-start.19 = (bf16[8,32,128]{2,1,0:T(8,128)(2,1)S(1)}, bf16[8,32,128]{2,1,0:T(8,128)(2,1)S(1)}, u32[]{:S(2)}, u32[]{:S(2)}) collective-permute-start(bf16[8,32,128]{2,1,0:T(8,128)(2,1)S(1)} %multiply_convert_fusion.2.refs_0_), channel_id=1, source_target_pairs={{0,2},{1,3},{2,0},{3,1},{4,6},{5,7},{6,4},{7,5},{8,10},{9,11},{10,... | collective-permute-start | bytes 196616 | tf_op jit(solution)/shard_map/ppermute | solution.py:37
  84.4 4.3 %collective-permute-start.18 = (bf16[8,32,128]{2,1,0:T(8,128)(2,1)S(1)}, bf16[8,32,128]{2,1,0:T(8,128)(2,1)S(1)}, u32[]{:S(2)}, u32[]{:S(2)}) collective-permute-start(bf16[8,32,128]{2,1,0:T(8,128)(2,1)S(1)} %multiply_convert_fusion.2.refs_0_), channel_id=1, source_target_pairs={{0,1},{1,0},{2,3},{3,2},{4,5},{5,4},{6,7},{7,6},{8,9},{9,8},{10,11... | collective-permute-start | bytes 196616 | tf_op jit(solution)/shard_map/ppermute | solution.py:37
  91.7 1.5 collective-permute-start.21
  93.2 7.0 %collective-permute-start.22 = (bf16[24,32,128]{2,1,0:T(8,128)(2,1)S(1)}, bf16[24,32,128]{2,1,0:T(8,128)(2,1)S(1)}, u32[]{:S(2)}, u32[]{:S(2)}) collective-permute-start(bf16[24,32,128]{2,1,0:T(8,128)(2,1)S(1)} %add_convert_fusion.2.mine), channel_id=1, source_target_pairs={{0,16},{1,17},{2,18},{3,19},{4,20},{5,21},{6,22},{7,23},{8,24},{9,... | collective-permute-start | bytes 589832 | tf_op jit(solution)/shard_map/ppermute | solution.py:37
  101.9 1.5 collective-permute-start.23
  101.9 1.4 collective-permute-start.24
  104.6 7.2 %collective-permute-start.25 = (bf16[24,32,128]{2,1,0:T(8,128)(2,1)S(1)}, bf16[24,32,128]{2,1,0:T(8,128)(2,1)S(1)}, u32[]{:S(2)}, u32[]{:S(2)}) collective-permute-start(bf16[24,32,128]{2,1,0:T(8,128)(2,1)S(1)} %prior_spread.6.refs_0_), channel_id=1, source_target_pairs={{0,8},{1,9},{2,10},{3,11},{4,12},{5,13},{6,14},{7,15},{8,0},{9,1},... | collective-permute-start | bytes 589832 | tf_op jit(solution)/shard_map/ppermute | solution.py:37
  114.5 4.8 %collective-permute-start.26 = (bf16[8,32,128]{2,1,0:T(8,128)(2,1)S(1)}, bf16[8,32,128]{2,1,0:T(8,128)(2,1)S(1)}, u32[]{:S(2)}, u32[]{:S(2)}) collective-permute-start(bf16[8,32,128]{2,1,0:T(8,128)(2,1)S(1)} %get-tuple-element.96), channel_id=1, source_target_pairs={{0,1},{1,0},{2,3},{3,2},{4,5},{5,4},{6,7},{7,6},{8,9},{9,8},{10,11... | collective-permute-start | bytes 196616 | tf_op jit(solution)/shard_map/ppermute | solution.py:37
  115.6 5.3 %collective-permute-start.27 = (bf16[8,32,128]{2,1,0:T(8,128)(2,1)S(1)}, bf16[8,32,128]{2,1,0:T(8,128)(2,1)S(1)}, u32[]{:S(2)}, u32[]{:S(2)}) collective-permute-start(bf16[8,32,128]{2,1,0:T(8,128)(2,1)S(1)} %get-tuple-element.97), channel_id=1, source_target_pairs={{0,2},{1,3},{2,0},{3,1},{4,6},{5,7},{6,4},{7,5},{8,10},{9,11},{10,... | collective-permute-start | bytes 196616 | tf_op jit(solution)/shard_map/ppermute | solution.py:37
  118.0 5.2 %collective-permute-start.28 = (bf16[8,32,128]{2,1,0:T(8,128)(2,1)S(1)}, bf16[8,32,128]{2,1,0:T(8,128)(2,1)S(1)}, u32[]{:S(2)}, u32[]{:S(2)}) collective-permute-start(bf16[8,32,128]{2,1,0:T(8,128)(2,1)S(1)} %get-tuple-element.98), channel_id=1, source_target_pairs={{0,3},{1,2},{2,1},{3,0},{4,7},{5,6},{6,5},{7,4},{8,11},{9,10},{10,... | collective-permute-start | bytes 196616 | tf_op jit(solution)/shard_map/ppermute | solution.py:37
  123.2 5.9 %collective-permute-start.29 = (bf16[8,32,128]{2,1,0:T(8,128)(2,1)S(1)}, bf16[8,32,128]{2,1,0:T(8,128)(2,1)S(1)}, u32[]{:S(2)}, u32[]{:S(2)}) collective-permute-start(bf16[8,32,128]{2,1,0:T(8,128)(2,1)S(1)} %add_convert_fusion.5), channel_id=1, source_target_pairs={{0,4},{1,5},{2,6},{3,7},{4,0},{5,1},{6,2},{7,3},{8,12},{9,13},{10,... | collective-permute-start | bytes 196616 | tf_op jit(solution)/shard_map/ppermute | solution.py:37
  129.1 5.2 %collective-permute-start.32 = (bf16[8,32,128]{2,1,0:T(8,128)(2,1)S(1)}, bf16[8,32,128]{2,1,0:T(8,128)(2,1)S(1)}, u32[]{:S(2)}, u32[]{:S(2)}) collective-permute-start(bf16[8,32,128]{2,1,0:T(8,128)(2,1)S(1)} %multiply_convert_fusion.1.refs_0_), channel_id=1, source_target_pairs={{0,3},{1,2},{2,1},{3,0},{4,7},{5,6},{6,5},{7,4},{8,11},{9,10},{10,... | collective-permute-start | bytes 196616 | tf_op jit(solution)/shard_map/ppermute | solution.py:37
  130.0 4.4 %collective-permute-start.31 = (bf16[8,32,128]{2,1,0:T(8,128)(2,1)S(1)}, bf16[8,32,128]{2,1,0:T(8,128)(2,1)S(1)}, u32[]{:S(2)}, u32[]{:S(2)}) collective-permute-start(bf16[8,32,128]{2,1,0:T(8,128)(2,1)S(1)} %multiply_convert_fusion.1.refs_0_), channel_id=1, source_target_pairs={{0,2},{1,3},{2,0},{3,1},{4,6},{5,7},{6,4},{7,5},{8,10},{9,11},{10,... | collective-permute-start | bytes 196616 | tf_op jit(solution)/shard_map/ppermute | solution.py:37
  130.6 4.4 %collective-permute-start.30 = (bf16[8,32,128]{2,1,0:T(8,128)(2,1)S(1)}, bf16[8,32,128]{2,1,0:T(8,128)(2,1)S(1)}, u32[]{:S(2)}, u32[]{:S(2)}) collective-permute-start(bf16[8,32,128]{2,1,0:T(8,128)(2,1)S(1)} %multiply_convert_fusion.1.refs_0_), channel_id=1, source_target_pairs={{0,1},{1,0},{2,3},{3,2},{4,5},{5,4},{6,7},{7,6},{8,9},{9,8},{10,11... | collective-permute-start | bytes 196616 | tf_op jit(solution)/shard_map/ppermute | solution.py:37
  137.8 1.5 collective-permute-start.33
  139.4 7.0 %collective-permute-start.34 = (bf16[24,32,128]{2,1,0:T(8,128)(2,1)S(1)}, bf16[24,32,128]{2,1,0:T(8,128)(2,1)S(1)}, u32[]{:S(2)}, u32[]{:S(2)}) collective-permute-start(bf16[24,32,128]{2,1,0:T(8,128)(2,1)S(1)} %add_convert_fusion.1.mine), channel_id=1, source_target_pairs={{0,16},{1,17},{2,18},{3,19},{4,20},{5,21},{6,22},{7,23},{8,24},{9,... | collective-permute-start | bytes 589832 | tf_op jit(solution)/shard_map/ppermute | solution.py:37
  148.0 1.5 collective-permute-start.35
  148.1 1.4 collective-permute-start.36
  150.8 43.8 %slice-start = ((s8[6291456]{0:T(1024)(128)(4,1)}), s8[4194304]{0:T(1024)(128)(4,1)S(1)}, s32[]{:S(2)}) async-start(s8[6291456]{0:T(1024)(128)(4,1)} %bitcast.12), calls=%async_computation | async-start | bytes 8388608
  150.8 8.0 %collective-permute-start.37 = (bf16[24,32,128]{2,1,0:T(8,128)(2,1)S(1)}, bf16[24,32,128]{2,1,0:T(8,128)(2,1)S(1)}, u32[]{:S(2)}, u32[]{:S(2)}) collective-permute-start(bf16[24,32,128]{2,1,0:T(8,128)(2,1)S(1)} %prior_spread.7.refs_0_), channel_id=1, source_target_pairs={{0,8},{1,9},{2,10},{3,11},{4,12},{5,13},{6,14},{7,15},{8,0},{9,1},... | collective-permute-start | bytes 589832 | tf_op jit(solution)/shard_map/ppermute | solution.py:37
  158.8 46.0 %copy-start.1 = (f32[32,128]{1,0:T(8,128)S(1)}, f32[32,128]{1,0:T(8,128)}, u32[]{:S(2)}) copy-start(f32[32,128]{1,0:T(8,128)} %param.15) | copy-start | bytes 49156
  161.5 4.9 %collective-permute-start.38 = (bf16[8,32,128]{2,1,0:T(8,128)(2,1)S(1)}, bf16[8,32,128]{2,1,0:T(8,128)(2,1)S(1)}, u32[]{:S(2)}, u32[]{:S(2)}) collective-permute-start(bf16[8,32,128]{2,1,0:T(8,128)(2,1)S(1)} %get-tuple-element.105), channel_id=1, source_target_pairs={{0,1},{1,0},{2,3},{3,2},{4,5},{5,4},{6,7},{7,6},{8,9},{9,8},{10,11... | collective-permute-start | bytes 196616 | tf_op jit(solution)/shard_map/ppermute | solution.py:37
  163.0 4.8 %collective-permute-start.39 = (bf16[8,32,128]{2,1,0:T(8,128)(2,1)S(1)}, bf16[8,32,128]{2,1,0:T(8,128)(2,1)S(1)}, u32[]{:S(2)}, u32[]{:S(2)}) collective-permute-start(bf16[8,32,128]{2,1,0:T(8,128)(2,1)S(1)} %get-tuple-element.106), channel_id=1, source_target_pairs={{0,2},{1,3},{2,0},{3,1},{4,6},{5,7},{6,4},{7,5},{8,10},{9,11},{10,... | collective-permute-start | bytes 196616 | tf_op jit(solution)/shard_map/ppermute | solution.py:37
  164.7 5.2 %collective-permute-start.40 = (bf16[8,32,128]{2,1,0:T(8,128)(2,1)S(1)}, bf16[8,32,128]{2,1,0:T(8,128)(2,1)S(1)}, u32[]{:S(2)}, u32[]{:S(2)}) collective-permute-start(bf16[8,32,128]{2,1,0:T(8,128)(2,1)S(1)} %get-tuple-element.107), channel_id=1, source_target_pairs={{0,3},{1,2},{2,1},{3,0},{4,7},{5,6},{6,5},{7,4},{8,11},{9,10},{10,... | collective-permute-start | bytes 196616 | tf_op jit(solution)/shard_map/ppermute | solution.py:37
  169.9 6.2 %collective-permute-start.41 = (bf16[8,32,128]{2,1,0:T(8,128)(2,1)S(1)}, bf16[8,32,128]{2,1,0:T(8,128)(2,1)S(1)}, u32[]{:S(2)}, u32[]{:S(2)}) collective-permute-start(bf16[8,32,128]{2,1,0:T(8,128)(2,1)S(1)} %add_convert_fusion.4), channel_id=1, source_target_pairs={{0,4},{1,5},{2,6},{3,7},{4,0},{5,1},{6,2},{7,3},{8,12},{9,13},{10,... | collective-permute-start | bytes 196616 | tf_op jit(solution)/shard_map/ppermute | solution.py:37
  176.1 18.5 %slice-start.1 = ((s8[6291456]{0:T(1024)(128)(4,1)}), s8[2097152]{0:T(1024)(128)(4,1)S(1)}, s32[]{:S(2)}) async-start(s8[6291456]{0:T(1024)(128)(4,1)} %bitcast.12), calls=%async_computation.1 | async-start | bytes 4194304
  176.1 5.2 %collective-permute-start.44 = (bf16[8,32,128]{2,1,0:T(8,128)(2,1)S(1)}, bf16[8,32,128]{2,1,0:T(8,128)(2,1)S(1)}, u32[]{:S(2)}, u32[]{:S(2)}) collective-permute-start(bf16[8,32,128]{2,1,0:T(8,128)(2,1)S(1)} %multiply_convert_fusion.refs_0_), channel_id=1, source_target_pairs={{0,3},{1,2},{2,1},{3,0},{4,7},{5,6},{6,5},{7,4},{8,11},{9,10},{10,... | collective-permute-start | bytes 196616 | tf_op jit(solution)/shard_map/ppermute | solution.py:37
  176.6 5.1 %collective-permute-start.43 = (bf16[8,32,128]{2,1,0:T(8,128)(2,1)S(1)}, bf16[8,32,128]{2,1,0:T(8,128)(2,1)S(1)}, u32[]{:S(2)}, u32[]{:S(2)}) collective-permute-start(bf16[8,32,128]{2,1,0:T(8,128)(2,1)S(1)} %multiply_convert_fusion.refs_0_), channel_id=1, source_target_pairs={{0,2},{1,3},{2,0},{3,1},{4,6},{5,7},{6,4},{7,5},{8,10},{9,11},{10,... | collective-permute-start | bytes 196616 | tf_op jit(solution)/shard_map/ppermute | solution.py:37
  178.8 4.3 %collective-permute-start.42 = (bf16[8,32,128]{2,1,0:T(8,128)(2,1)S(1)}, bf16[8,32,128]{2,1,0:T(8,128)(2,1)S(1)}, u32[]{:S(2)}, u32[]{:S(2)}) collective-permute-start(bf16[8,32,128]{2,1,0:T(8,128)(2,1)S(1)} %multiply_convert_fusion.refs_0_), channel_id=1, source_target_pairs={{0,1},{1,0},{2,3},{3,2},{4,5},{5,4},{6,7},{7,6},{8,9},{9,8},{10,11... | collective-permute-start | bytes 196616 | tf_op jit(solution)/shard_map/ppermute | solution.py:37
  186.0 1.5 collective-permute-start.45
  187.6 7.0 %collective-permute-start.46 = (bf16[24,32,128]{2,1,0:T(8,128)(2,1)S(1)}, bf16[24,32,128]{2,1,0:T(8,128)(2,1)S(1)}, u32[]{:S(2)}, u32[]{:S(2)}) collective-permute-start(bf16[24,32,128]{2,1,0:T(8,128)(2,1)S(1)} %add_convert_fusion.mine), channel_id=1, source_target_pairs={{0,16},{1,17},{2,18},{3,19},{4,20},{5,21},{6,22},{7,23},{8,24},{9,... | collective-permute-start | bytes 589832 | tf_op jit(solution)/shard_map/ppermute | solution.py:37
  196.3 1.4 collective-permute-start.48
  196.4 1.3 collective-permute-start.47
  197.8 6.3 %collective-permute-start.49 = (bf16[24,32,128]{2,1,0:T(8,128)(2,1)S(1)}, bf16[24,32,128]{2,1,0:T(8,128)(2,1)S(1)}, u32[]{:S(2)}, u32[]{:S(2)}) collective-permute-start(bf16[24,32,128]{2,1,0:T(8,128)(2,1)S(1)} %fusion), channel_id=1, source_target_pairs={{0,8},{1,9},{2,10},{3,11},{4,12},{5,13},{6,14},{7,15},{8,0},{9,1},... | collective-permute-start | bytes 589832 | tf_op jit(solution)/shard_map/ppermute | solution.py:37

commit v8 on v7

--- a/solution.py
+++ b/solution.py
@@ -13,8 +13,9 @@
 HALF = jnp.bfloat16
 VMEM_LIMIT = 8 * 2**20
 LANES = 128
-OBS_PLAN = (4, 57)
-TILE_PLAN = (4, 60)
+FORWARD_PLAN = (2, 56)
+NEAR_PLAN = (2, 32)
+REST_PLAN = (2, 42)
 PRIOR_PLAN = (2, 56)
 
 
@@ -87,9 +88,10 @@
 
 def setup_kernel(
     rows, chunk, where, obs, flux, nbr, prior, jac,
-    prior_plain, jac_plain, obs_plan, tile_plan, prior_plan, nbr_list,
-    obs_in, flux_in, nbr_in, obs_out, tile_out, prior_out, nbr_out, small_sems, sems
+    prior_plain, jac_plain, *refs
 ):
+    plans, (obs_in, flux_in, nbr_in) = refs[:7], refs[7:10]
+    built, (small_sems, sems) = refs[10:17], refs[17:]
     side, corner, count, first_tile = where[0], where[1], where[2], where[3]
     owned = prior_plain.shape[0]
     begin = side * owned
@@ -134,17 +136,27 @@
     obs_at = (block ^ corner) * quarter + obs_in[...] - block * quarter
     block = (flux_in[...] >= half).astype(i32)
     tile_at = (block ^ side) * half + flux_in[...] - block * half
-    plan_groups(OBS_PLAN, tile_at, jnp.where(live, obs_at, most), 0, most, obs_out)
-    plan_groups(TILE_PLAN, obs_at, jnp.where(live, tile_at, most), 0, most, tile_out)
+    own, near = tile_at < half, obs_at < quarter
+    for plan, src, dst, use, out in (
+        (FORWARD_PLAN, tile_at, obs_at, own, built[0]),
+        (FORWARD_PLAN, tile_at - half, obs_at, ~own, built[1]),
+        (NEAR_PLAN, obs_at, tile_at, near, built[2]),
+        (REST_PLAN, obs_at - quarter, tile_at - half, ~near & ~own, built[3]),
+        (REST_PLAN, obs_at - quarter, tile_at, ~near & own, built[4]),
+    ):
+        use = live & use
+        plan_groups(plan, jnp.where(use, src, 0), jnp.where(use, dst, most), 0, most, out)
     at = lax.broadcasted_iota(i32, nbr_in.shape, 1)
     tile = sum((at >= k * fan).astype(i32) for k in range(1, tile_rows)) - side * half
     owns = (tile >= 0) & (tile < half)
     ext = nbr_in[...] - first_tile + reach
-    plan_groups(PRIOR_PLAN, jnp.where(owns, tile, 0), jnp.where(owns, ext, most), begin, most, prior_out)
-    nbr_out[:, : ext.shape[1]] = ext
-    nbr_out[:, ext.shape[1] :] = jnp.zeros((1, LANES), i32) + side
-    lists = ((obs_out, obs_plan), (tile_out, tile_plan), (prior_out, prior_plan), (nbr_out, nbr_list))
-    lists = [pltpu.make_async_copy(src, dst, small_sems.at[3 + k]) for k, (src, dst) in enumerate(lists)]
+    plan_groups(PRIOR_PLAN, jnp.where(owns, tile, 0), jnp.where(owns, ext, most), begin, most, built[5])
+    built[6][:, : ext.shape[1]] = ext
+    built[6][:, ext.shape[1] :] = jnp.zeros((1, LANES), i32) + side
+    lists = [
+        pltpu.make_async_copy(src, dst, small_sems.at[3 + k])
+        for k, (src, dst) in enumerate(zip(built, plans))
+    ]
     for one in lists:
         one.start()
 
@@ -187,19 +199,20 @@
     all_blocks = pltpu.VMEM(jac.shape, HALF)
     i32 = jnp.int32
     lengths = []
-    for plan, width in ((OBS_PLAN, obs), (TILE_PLAN, obs), (PRIOR_PLAN, nbr)):
-        slots, groups = plan_sizes(plan, width.shape[1], most)
+    used = (FORWARD_PLAN, FORWARD_PLAN, NEAR_PLAN, REST_PLAN, REST_PLAN, PRIOR_PLAN)
+    for plan in used:
+        slots, groups = plan_sizes(plan, (nbr if plan is used[-1] else obs).shape[1], most)
         lengths.append(2 * slots + groups)
     lengths.append(nbr.shape[1] + LANES)
     return pl.pallas_call(
         functools.partial(setup_kernel, rows, chunk),
         in_specs=[smem] + [hbm] * 5,
-        out_specs=[vmem] * 2 + [smem] * 4,
+        out_specs=[vmem] * 2 + [smem] * 7,
         out_shape=[own, all_blocks] + [pltpu.SMEM((1, n), i32) for n in lengths],
         scratch_shapes=[pltpu.VMEM(v.shape, i32) for v in (obs, flux, nbr)]
         + [pltpu.VMEM((1, n), i32) for n in lengths]
         + [
-            pltpu.SemaphoreType.DMA((7,)),
+            pltpu.SemaphoreType.DMA((10,)),
             pltpu.SemaphoreType.DMA(((owned + jac.shape[0]) // chunk,)),
         ],
         compiler_params=pltpu.CompilerParams(vmem_limit_bytes=VMEM_LIMIT),
@@ -210,7 +223,6 @@
 def grouped_products(plan, sizes, lists, x, blocks, total):
     group, per_round = plan
     slots, groups = sizes
-    total[...] = jnp.zeros_like(total)
 
     def one(c, _):
         products = []
@@ -226,39 +238,45 @@
     lax.fori_loop(0, lists[0, 2 * slots + groups - 1], one, 0)
 
 
-def jac_kernel(plan, sizes, n_parts, n_outs, lists, *refs):
-    parts = refs[:n_parts]
-    jac = refs[n_parts]
-    outs = refs[n_parts + 1 : n_parts + 1 + n_outs]
-    x, total = refs[n_parts + 1 + n_outs :]
+def jac_kernel(plan, sizes, n_parts, started, n_outs, lists, *refs):
+    parts, refs = refs[:n_parts], refs[n_parts:]
+    if started:
+        begun, refs = refs[0], refs[1:]
+    jac, outs, (x, total) = refs[0], refs[1 : 1 + n_outs], refs[1 + n_outs :]
     rows = parts[0].shape[0]
     for k, part in enumerate(parts):
         x[k * rows : (k + 1) * rows] = part[...]
-    for r in range(n_parts * rows, x.shape[0]):
-        x[r] = jnp.zeros(x.shape[1:], HALF)
+    x[x.shape[0] - 1] = jnp.zeros(x.shape[1:], HALF)
+    if started:
+        total[: begun.shape[0]] = begun[...]
+    else:
+        total[...] = jnp.zeros_like(total)
     grouped_products(plan, sizes, lists, x, jac, total)
     rows = outs[0].shape[0]
     for k, out in enumerate(outs):
         out[...] = total[k * rows : (k + 1) * rows].astype(out.dtype)
 
 
-def jac_pass(plan, lists, parts, jac, rows, out_rows, n_outs, name):
+def jac_pass(plan, lists, parts, begun, jac, rows, out_rows, out_types, name):
     probes, width = parts[0].shape[1:]
+    n_outs = len(out_types)
     smem = pl.BlockSpec(memory_space=pltpu.SMEM)
     vmem = pl.BlockSpec(memory_space=pltpu.VMEM)
-    out = (out_rows // n_outs, probes, width)
+    operands = (lists, *parts) + (() if begun is None else (begun,)) + (jac,)
+    sizes = plan_sizes(plan, jac.shape[0], rows)
     return pl.pallas_call(
-        functools.partial(jac_kernel, plan, plan_sizes(plan, jac.shape[0], rows), len(parts), n_outs),
-        in_specs=[smem] + [vmem] * len(parts) + [vmem],
+        functools.partial(jac_kernel, plan, sizes, len(parts), begun is not None, n_outs),
+        in_specs=[smem] + [vmem] * (len(operands) - 1),
         out_specs=[vmem] * n_outs,
-        out_shape=[jax.ShapeDtypeStruct(out, F32 if k == 0 else HALF) for k in range(n_outs)],
+        out_shape=[jax.ShapeDtypeStruct((out_rows // n_outs, probes, width), t) for t in out_types],
         scratch_shapes=[
             pltpu.VMEM((rows + 1, probes, width), HALF),
             pltpu.VMEM((rows + 1, probes, width), F32),
         ],
         compiler_params=pltpu.CompilerParams(vmem_limit_bytes=VMEM_LIMIT),
+        cost_estimate=pl.CostEstimate(flops=0, bytes_accessed=jac.size, transcendentals=0),
         name=name,
-    )(lists, *parts, jac)
+    )(*operands)
 
 
 def gather_kernel(rows, sizes, nbr, lists, mine, other, prior, ext, to_core, to_far, x, total):
@@ -266,6 +284,7 @@
     side = nbr[0, nbr.shape[1] - 1]
     x[:half] = (mine[...].astype(F32) + other[...].astype(F32)).astype(HALF)
     x[rows] = jnp.zeros(x.shape[1:], HALF)
+    total[...] = jnp.zeros_like(total)
     grouped_products(PRIOR_PLAN, sizes, lists, x, prior, total)
     ext[...] = total[: 2 * half]
     to_core[...] = total[pl.ds(half * (1 - side), half)].astype(HALF)
@@ -375,14 +394,20 @@
     nbr = neighbours.reshape(1, tile_count * fan)
 
     where, own_rinv, nbr, prior, blocks = lax.optimization_barrier((where, own_rinv, nbr, prior, blocks))
-    prior_plain, jac_plain, obs_lists, tile_lists, prior_lists, nbr = setup(
+    prior_plain, jac_plain, *jac_lists, prior_lists, nbr = setup(
         where, jac_obs[0], jac_flux[0], nbr, prior, blocks, sizes
     )
     fields = (probes, beyond)
     for step in range(STEPS):
         spread = spread_tiles(nbr, fields, prior_plain)
-        parts = (spread, swap_core(spread))
-        pieces = jac_pass(OBS_PLAN, obs_lists, parts, jac_plain, rows, obs_rows, 4, "jac_forward")
+        other = swap_core(spread)
+        (begun,) = jac_pass(
+            FORWARD_PLAN, jac_lists[0], (spread,), None, jac_plain, rows, obs_rows, [F32], "forward_own"
+        )
+        types = [F32, HALF, HALF, HALF]
+        pieces = jac_pass(
+            FORWARD_PLAN, jac_lists[1], (other,), begun, jac_plain, rows, obs_rows, types, "forward_other"
+        )
         if step == 0:
             pieces, jac_plain = lax.optimization_barrier((pieces, jac_plain))
             jac_turned = turn_blocks(jac_plain, "jac_turn")
@@ -395,8 +420,14 @@
             total = sent.astype(F32) + swap_flux(sent, bits).astype(F32)
             bits *= 2
         weighted = (total * own_rinv).astype(HALF)
-        parts = (weighted,) + tuple(swap_flux(weighted, bits) for bits in range(1, 4))
-        mine, theirs = jac_pass(TILE_PLAN, tile_lists, parts, jac_turned, rows, tile_count, 2, "jac_adjoint")
+        rest = tuple(swap_flux(weighted, bits) for bits in range(1, 4))
+        mine, theirs = jac_pass(
+            NEAR_PLAN, jac_lists[2], (weighted,), None, jac_turned, rows, tile_count, [F32, F32], "adjoint_near"
+        )
+        (theirs,) = jac_pass(
+            REST_PLAN, jac_lists[3], rest, theirs, jac_turned, rows, half, [HALF], "adjoint_other"
+        )
+        (mine,) = jac_pass(REST_PLAN, jac_lists[4], rest, mine, jac_turned, rows, half, [F32], "adjoint_own")
         mine = (mine + swap_core(theirs).astype(F32)).astype(HALF)
         if step == 0:
             mine, prior_plain = lax.optimization_barrier((mine, prior_plain))

time: 206 us -> 198 us (0.961)
  waiting for transfers between devices: 77.3 us -> 65.7 us
  starting transfers between devices: 76.4 us -> 80.6 us
    ppermute x50, waiting for transfers between devices: 77.3 us -> 65.7 us  [exchange(): return lax.ppermute(value, ('obs', 'flux'), route)]
    ppermute x50, starting transfers between devices: 76.4 us -> 80.6 us  [exchange(): return lax.ppermute(value, ('obs', 'flux'), route)]
    pallas_call x8 -> x20, Pallas kernels: 22 us -> 21.8 us  [jac_pass(): pl.pallas_call(functools.partial(jac_kernel, plan, sizes, len(parts), beg...]
  transfers between devices with their start and end apart: 50 -> 50, of which waited for: 41 -> 37; matrix products, arithmetic and copies ran while one was open for 1% -> 1% of each run, Pallas kernels for 6% -> 13%
where the time goes in v8:
time: 198 us; the launch traced here: 197 us
  starting transfers between devices  80.6 us (41%)
  waiting for transfers between devices  65.7 us (33%)
  Pallas kernels  46 us (23%)
  other arithmetic  2.45 us (1%)
    ppermute x50, starting transfers between devices, exchange(): return lax.ppermute(value, ('obs', 'flux'), route)  80.6 us
    ppermute x50, waiting for transfers between devices, exchange(): return lax.ppermute(value, ('obs', 'flux'), route)  65.7 us
    pallas_call x20, Pallas kernels, jac_pass(): pl.pallas_call(functools.partial(jac_kernel, plan, sizes, len(parts), beg...  21.8 us
    pallas_call x1, Pallas kernels, setup(): pl.pallas_call(functools.partial(setup_kernel, rows, chunk), in_specs=[sm...  7.35 us
    pallas_call x4, Pallas kernels, gather_tiles(): pl.pallas_call(functools.partial(gather_kernel, rows, plan_sizes(PRIOR_PL...  6.5 us
    pallas_call x2, Pallas kernels, turn_blocks(): pl.pallas_call(functools.partial(turn_kernel, chunk_of(plain.shape[0], 48...  5.5 us
    pallas_call x4, Pallas kernels, spread_tiles(): pl.pallas_call(functools.partial(spread_kernel, len(fields) == 2, prior.s...  4.82 us
  transfers between devices with their start and end apart: 50, of which 37 were waited for; matrix products, arithmetic and copies ran while one was open for 1% of the time, Pallas kernels for 13%

profile of v8, /device:TPU:0, one launch (start us, length us, event | category | flops | bytes accessed | tf_op | source)
XLA Modules:
  0.0 197.4 jit_solution(1096528171278775549)
XLA Ops:
  3.8 7.3 %setup.1 = (bf16[192,128,128]{2,1,0:T(8,128)(2,1)S(1)}, bf16[384,128,128]{2,1,0:T(8,128)(2,1)S(1)}, s32[1,1664]{1,0:T(1,128)S(4)}, s32[1,1664]{1,0:T(1,128)S(4)}...) custom-call(s32[4]{0:T(128)S(1)} %pad_add_fusion.where, ...), custom_call_target="tpu_custom_call" | custom-call | tf_op jit(solution)/shard_map/setup/pallas_call | solution.py:207
  11.2 1.1 prior_spread.4.refs_0_
  12.3 4.4 %collective-permute-start.1 = (bf16[24,32,128]{2,1,0:T(8,128)(2,1)S(1)}, bf16[24,32,128]{2,1,0:T(8,128)(2,1)S(1)}, u32[]{:S(2)}, u32[]{:S(2)}) collective-permute-start(bf16[24,32,128]{2,1,0:T(8,128)(2,1)S(1)} %prior_spread.4.refs_0_), channel_id=1, source_target_pairs={{0,8},{1,9},{2,10},{3,11},{4,12},{5,13},{6,14},{7,15},{8,0},{9,1},... | collective-permute-start | bytes 589832 | tf_op jit(solution)/shard_map/ppermute | solution.py:38
  16.7 1.6 forward_own.4.refs_1_
  18.3 1.5 forward_other.4
  20.1 2.8 %collective-permute-start.3 = (bf16[8,32,128]{2,1,0:T(8,128)(2,1)S(1)}, bf16[8,32,128]{2,1,0:T(8,128)(2,1)S(1)}, u32[]{:S(2)}, u32[]{:S(2)}) collective-permute-start(bf16[8,32,128]{2,1,0:T(8,128)(2,1)S(1)} %get-tuple-element.79), channel_id=1, source_target_pairs={{0,2},{1,3},{2,0},{3,1},{4,6},{5,7},{6,4},{7,5},{8,10},{9,11},{10,... | collective-permute-start | bytes 196616 | tf_op jit(solution)/shard_map/ppermute | solution.py:38
  24.1 1.4 collective-permute-done.3
  25.5 2.6 %collective-permute-done.4 = bf16[8,32,128]{2,1,0:T(8,128)(2,1)S(1)} collective-permute-done((bf16[8,32,128]{2,1,0:T(8,128)(2,1)S(1)}, bf16[8,32,128]{2,1,0:T(8,128)(2,1)S(1)}, u32[]{:S(2)}, u32[]{:S(2)}) %collective-permute-start.4) | collective-permute-done | bytes 65568 | tf_op jit(solution)/shard_map/ppermute | solution.py:38
  28.1 1.4 collective-permute-start.5
  29.6 4.3 %collective-permute-done.5 = bf16[8,32,128]{2,1,0:T(8,128)(2,1)S(1)} collective-permute-done((bf16[8,32,128]{2,1,0:T(8,128)(2,1)S(1)}, bf16[8,32,128]{2,1,0:T(8,128)(2,1)S(1)}, u32[]{:S(2)}, u32[]{:S(2)}) %collective-permute-start.5) | collective-permute-done | bytes 65568 | tf_op jit(solution)/shard_map/ppermute | solution.py:38
  34.5 1.7 collective-permute-start.7
  36.2 1.3 collective-permute-start.6
  37.5 3.7 %jac_turn.1.refs_1_.refs_4_ = bf16[384,128,128]{2,1,0:T(8,128)(2,1)S(1)} custom-call(bf16[384,128,128]{2,1,0:T(8,128)(2,1)S(1)} %get-tuple-element.83.refs_1_.refs_2_.plain), custom_call_target="tpu_custom_call" | custom-call | bytes 12582912 | tf_op jit(solution)/shard_map/jac_turn/pallas_call | solution.py:180
  44.4 2.2 %collective-permute-start.10 = (bf16[24,32,128]{2,1,0:T(8,128)(2,1)S(1)}, bf16[24,32,128]{2,1,0:T(8,128)(2,1)S(1)}, u32[]{:S(2)}, u32[]{:S(2)}) collective-permute-start(bf16[24,32,128]{2,1,0:T(8,128)(2,1)S(1)} %add_convert_fusion.3.mine), channel_id=1, source_target_pairs={{0,16},{1,17},{2,18},{3,19},{4,20},{5,21},{6,22},{7,23},{8,24},{9,... | collective-permute-start | bytes 589832 | tf_op jit(solution)/shard_map/ppermute | solution.py:38
  46.7 1.8 prior_turn.1.prior
  48.5 3.5 %collective-permute-done.10.other = bf16[24,32,128]{2,1,0:T(8,128)(2,1)S(1)} collective-permute-done((bf16[24,32,128]{2,1,0:T(8,128)(2,1)S(1)}, bf16[24,32,128]{2,1,0:T(8,128)(2,1)S(1)}, u32[]{:S(2)}, u32[]{:S(2)}) %collective-permute-start.10) | collective-permute-done | bytes 196640 | tf_op jit(solution)/shard_map/ppermute | solution.py:38
  52.0 1.6 prior_adjoint.4
  55.2 1.2 prior_spread.5.refs_0_
  56.4 6.1 %collective-permute-start.13 = (bf16[24,32,128]{2,1,0:T(8,128)(2,1)S(1)}, bf16[24,32,128]{2,1,0:T(8,128)(2,1)S(1)}, u32[]{:S(2)}, u32[]{:S(2)}) collective-permute-start(bf16[24,32,128]{2,1,0:T(8,128)(2,1)S(1)} %prior_spread.5.refs_0_), channel_id=1, source_target_pairs={{0,8},{1,9},{2,10},{3,11},{4,12},{5,13},{6,14},{7,15},{8,0},{9,1},... | collective-permute-start | bytes 589832 | tf_op jit(solution)/shard_map/ppermute | solution.py:38
  62.5 1.7 forward_own.5.refs_1_
  64.3 1.5 forward_other.5
  65.8 1.1 collective-permute-start.14
  67.0 1.8 collective-permute-start.15
  69.6 1.2 collective-permute-done.14
  71.6 2.3 %collective-permute-done.16 = bf16[8,32,128]{2,1,0:T(8,128)(2,1)S(1)} collective-permute-done((bf16[8,32,128]{2,1,0:T(8,128)(2,1)S(1)}, bf16[8,32,128]{2,1,0:T(8,128)(2,1)S(1)}, u32[]{:S(2)}, u32[]{:S(2)}) %collective-permute-start.16) | collective-permute-done | bytes 65568 | tf_op jit(solution)/shard_map/ppermute | solution.py:38
  74.0 2.4 %collective-permute-start.17 = (bf16[8,32,128]{2,1,0:T(8,128)(2,1)S(1)}, bf16[8,32,128]{2,1,0:T(8,128)(2,1)S(1)}, u32[]{:S(2)}, u32[]{:S(2)}) collective-permute-start(bf16[8,32,128]{2,1,0:T(8,128)(2,1)S(1)} %add_convert_fusion.6), channel_id=1, source_target_pairs={{0,4},{1,5},{2,6},{3,7},{4,0},{5,1},{6,2},{7,3},{8,12},{9,13},{10,... | collective-permute-start | bytes 196616 | tf_op jit(solution)/shard_map/ppermute | solution.py:38
  76.4 3.8 %collective-permute-done.17 = bf16[8,32,128]{2,1,0:T(8,128)(2,1)S(1)} collective-permute-done((bf16[8,32,128]{2,1,0:T(8,128)(2,1)S(1)}, bf16[8,32,128]{2,1,0:T(8,128)(2,1)S(1)}, u32[]{:S(2)}, u32[]{:S(2)}) %collective-permute-start.17) | collective-permute-done | bytes 65568 | tf_op jit(solution)/shard_map/ppermute | solution.py:38
  80.9 2.0 collective-permute-start.19
  85.8 1.3 collective-permute-done.18.refs_0_
  89.3 2.1 %collective-permute-start.22 = (bf16[24,32,128]{2,1,0:T(8,128)(2,1)S(1)}, bf16[24,32,128]{2,1,0:T(8,128)(2,1)S(1)}, u32[]{:S(2)}, u32[]{:S(2)}) collective-permute-start(bf16[24,32,128]{2,1,0:T(8,128)(2,1)S(1)} %add_convert_fusion.2.mine), channel_id=1, source_target_pairs={{0,16},{1,17},{2,18},{3,19},{4,20},{5,21},{6,22},{7,23},{8,24},{9,... | collective-permute-start | bytes 589832 | tf_op jit(solution)/shard_map/ppermute | solution.py:38
  91.5 5.4 %collective-permute-done.22.other = bf16[24,32,128]{2,1,0:T(8,128)(2,1)S(1)} collective-permute-done((bf16[24,32,128]{2,1,0:T(8,128)(2,1)S(1)}, bf16[24,32,128]{2,1,0:T(8,128)(2,1)S(1)}, u32[]{:S(2)}, u32[]{:S(2)}) %collective-permute-start.22) | collective-permute-done | bytes 196640 | tf_op jit(solution)/shard_map/ppermute | solution.py:38
  96.9 1.6 prior_adjoint.5
  100.0 1.2 prior_spread.6.refs_0_
  101.3 6.1 %collective-permute-start.25 = (bf16[24,32,128]{2,1,0:T(8,128)(2,1)S(1)}, bf16[24,32,128]{2,1,0:T(8,128)(2,1)S(1)}, u32[]{:S(2)}, u32[]{:S(2)}) collective-permute-start(bf16[24,32,128]{2,1,0:T(8,128)(2,1)S(1)} %prior_spread.6.refs_0_), channel_id=1, source_target_pairs={{0,8},{1,9},{2,10},{3,11},{4,12},{5,13},{6,14},{7,15},{8,0},{9,1},... | collective-permute-start | bytes 589832 | tf_op jit(solution)/shard_map/ppermute | solution.py:38
  107.4 1.6 forward_own.6.refs_1_
  108.9 1.5 forward_other.6
  110.5 1.3 collective-permute-start.26
  111.8 2.0 %collective-permute-start.27 = (bf16[8,32,128]{2,1,0:T(8,128)(2,1)S(1)}, bf16[8,32,128]{2,1,0:T(8,128)(2,1)S(1)}, u32[]{:S(2)}, u32[]{:S(2)}) collective-permute-start(bf16[8,32,128]{2,1,0:T(8,128)(2,1)S(1)} %get-tuple-element.103), channel_id=1, source_target_pairs={{0,2},{1,3},{2,0},{3,1},{4,6},{5,7},{6,4},{7,5},{8,10},{9,11},{10,... | collective-permute-start | bytes 196616 | tf_op jit(solution)/shard_map/ppermute | solution.py:38
  115.5 1.2 collective-permute-done.27
  116.7 2.3 %collective-permute-done.28 = bf16[8,32,128]{2,1,0:T(8,128)(2,1)S(1)} collective-permute-done((bf16[8,32,128]{2,1,0:T(8,128)(2,1)S(1)}, bf16[8,32,128]{2,1,0:T(8,128)(2,1)S(1)}, u32[]{:S(2)}, u32[]{:S(2)}) %collective-permute-start.28) | collective-permute-done | bytes 65568 | tf_op jit(solution)/shard_map/ppermute | solution.py:38
  119.0 2.7 %collective-permute-start.29 = (bf16[8,32,128]{2,1,0:T(8,128)(2,1)S(1)}, bf16[8,32,128]{2,1,0:T(8,128)(2,1)S(1)}, u32[]{:S(2)}, u32[]{:S(2)}) collective-permute-start(bf16[8,32,128]{2,1,0:T(8,128)(2,1)S(1)} %add_convert_fusion.5), channel_id=1, source_target_pairs={{0,4},{1,5},{2,6},{3,7},{4,0},{5,1},{6,2},{7,3},{8,12},{9,13},{10,... | collective-permute-start | bytes 196616 | tf_op jit(solution)/shard_map/ppermute | solution.py:38
  121.7 3.2 %collective-permute-done.29 = bf16[8,32,128]{2,1,0:T(8,128)(2,1)S(1)} collective-permute-done((bf16[8,32,128]{2,1,0:T(8,128)(2,1)S(1)}, bf16[8,32,128]{2,1,0:T(8,128)(2,1)S(1)}, u32[]{:S(2)}, u32[]{:S(2)}) %collective-permute-start.29) | collective-permute-done | bytes 65568 | tf_op jit(solution)/shard_map/ppermute | solution.py:38
  125.0 1.2 collective-permute-start.32
  127.0 1.6 collective-permute-start.30
  133.5 3.0 %collective-permute-start.34 = (bf16[24,32,128]{2,1,0:T(8,128)(2,1)S(1)}, bf16[24,32,128]{2,1,0:T(8,128)(2,1)S(1)}, u32[]{:S(2)}, u32[]{:S(2)}) collective-permute-start(bf16[24,32,128]{2,1,0:T(8,128)(2,1)S(1)} %add_convert_fusion.1.mine), channel_id=1, source_target_pairs={{0,16},{1,17},{2,18},{3,19},{4,20},{5,21},{6,22},{7,23},{8,24},{9,... | collective-permute-start | bytes 589832 | tf_op jit(solution)/shard_map/ppermute | solution.py:38
  136.5 5.4 %collective-permute-done.34.other = bf16[24,32,128]{2,1,0:T(8,128)(2,1)S(1)} collective-permute-done((bf16[24,32,128]{2,1,0:T(8,128)(2,1)S(1)}, bf16[24,32,128]{2,1,0:T(8,128)(2,1)S(1)}, u32[]{:S(2)}, u32[]{:S(2)}) %collective-permute-start.34) | collective-permute-done | bytes 196640 | tf_op jit(solution)/shard_map/ppermute | solution.py:38
  141.8 1.6 prior_adjoint.6
  145.0 1.2 prior_spread.7.refs_0_
  146.2 6.8 %collective-permute-start.37 = (bf16[24,32,128]{2,1,0:T(8,128)(2,1)S(1)}, bf16[24,32,128]{2,1,0:T(8,128)(2,1)S(1)}, u32[]{:S(2)}, u32[]{:S(2)}) collective-permute-start(bf16[24,32,128]{2,1,0:T(8,128)(2,1)S(1)} %prior_spread.7.refs_0_), channel_id=1, source_target_pairs={{0,8},{1,9},{2,10},{3,11},{4,12},{5,13},{6,14},{7,15},{8,0},{9,1},... | collective-permute-start | bytes 589832 | tf_op jit(solution)/shard_map/ppermute | solution.py:38
  153.0 1.6 forward_own.7.refs_1_
  154.6 1.5 forward_other.7
  156.1 1.6 collective-permute-start.38
  159.7 1.2 collective-permute-done.38
  161.0 1.5 collective-permute-done.39
  162.5 1.5 collective-permute-done.40
  164.0 2.5 %collective-permute-start.41 = (bf16[8,32,128]{2,1,0:T(8,128)(2,1)S(1)}, bf16[8,32,128]{2,1,0:T(8,128)(2,1)S(1)}, u32[]{:S(2)}, u32[]{:S(2)}) collective-permute-start(bf16[8,32,128]{2,1,0:T(8,128)(2,1)S(1)} %add_convert_fusion.4), channel_id=1, source_target_pairs={{0,4},{1,5},{2,6},{3,7},{4,0},{5,1},{6,2},{7,3},{8,12},{9,13},{10,... | collective-permute-start | bytes 196616 | tf_op jit(solution)/shard_map/ppermute | solution.py:38
  166.5 4.0 %collective-permute-done.41 = bf16[8,32,128]{2,1,0:T(8,128)(2,1)S(1)} collective-permute-done((bf16[8,32,128]{2,1,0:T(8,128)(2,1)S(1)}, bf16[8,32,128]{2,1,0:T(8,128)(2,1)S(1)}, u32[]{:S(2)}, u32[]{:S(2)}) %collective-permute-start.41) | collective-permute-done | bytes 65568 | tf_op jit(solution)/shard_map/ppermute | solution.py:38
  170.9 2.0 %collective-permute-start.43 = (bf16[8,32,128]{2,1,0:T(8,128)(2,1)S(1)}, bf16[8,32,128]{2,1,0:T(8,128)(2,1)S(1)}, u32[]{:S(2)}, u32[]{:S(2)}) collective-permute-start(bf16[8,32,128]{2,1,0:T(8,128)(2,1)S(1)} %multiply_convert_fusion.refs_0_), channel_id=1, source_target_pairs={{0,2},{1,3},{2,0},{3,1},{4,6},{5,7},{6,4},{7,5},{8,10},{9,11},{10,... | collective-permute-start | bytes 196616 | tf_op jit(solution)/shard_map/ppermute | solution.py:38
  172.9 1.2 collective-permute-start.42
  175.8 1.3 collective-permute-done.42.refs_0_
  179.3 2.4 %collective-permute-start.46 = (bf16[24,32,128]{2,1,0:T(8,128)(2,1)S(1)}, bf16[24,32,128]{2,1,0:T(8,128)(2,1)S(1)}, u32[]{:S(2)}, u32[]{:S(2)}) collective-permute-start(bf16[24,32,128]{2,1,0:T(8,128)(2,1)S(1)} %add_convert_fusion.mine), channel_id=1, source_target_pairs={{0,16},{1,17},{2,18},{3,19},{4,20},{5,21},{6,22},{7,23},{8,24},{9,... | collective-permute-start | bytes 589832 | tf_op jit(solution)/shard_map/ppermute | solution.py:38
  181.7 5.4 %collective-permute-done.46.other = bf16[24,32,128]{2,1,0:T(8,128)(2,1)S(1)} collective-permute-done((bf16[24,32,128]{2,1,0:T(8,128)(2,1)S(1)}, bf16[24,32,128]{2,1,0:T(8,128)(2,1)S(1)}, u32[]{:S(2)}, u32[]{:S(2)}) %collective-permute-start.46) | collective-permute-done | bytes 196640 | tf_op jit(solution)/shard_map/ppermute | solution.py:38
  187.1 1.6 prior_adjoint.7
  190.3 5.2 %collective-permute-start.49 = (bf16[24,32,128]{2,1,0:T(8,128)(2,1)S(1)}, bf16[24,32,128]{2,1,0:T(8,128)(2,1)S(1)}, u32[]{:S(2)}, u32[]{:S(2)}) collective-permute-start(bf16[24,32,128]{2,1,0:T(8,128)(2,1)S(1)} %fusion), channel_id=1, source_target_pairs={{0,8},{1,9},{2,10},{3,11},{4,12},{5,13},{6,14},{7,15},{8,0},{9,1},... | collective-permute-start | bytes 589832 | tf_op jit(solution)/shard_map/ppermute | solution.py:38
  (96 shorter events, 37.7 us)
Async XLA Ops:
  0.0 3.7 %copy-start = (f32[32,128]{1,0:T(8,128)S(1)}, f32[32,128]{1,0:T(8,128)}, u32[]{:S(2)}) copy-start(f32[32,128]{1,0:T(8,128)} %param.15) | copy-start | bytes 49156
  1.0 10.2 %collective-permute-start = (bf16[12,32,128]{2,1,0:T(8,128)(2,1)S(1)}, bf16[12,32,128]{2,1,0:T(8,128)(2,1)S(1)}, u32[]{:S(2)}, u32[]{:S(2)}) collective-permute-start(bf16[12,32,128]{2,1,0:T(8,128)(2,1)S(1)} %slice_select_fusion.2), channel_id=1, source_target_pairs={{1,8},{2,9},{3,10},{4,11},{5,12},{6,13},{7,14},{8,1},{9,2},{10,3},... | collective-permute-start | bytes 294920 | tf_op jit(solution)/shard_map/ppermute | solution.py:38
  3.8 7.4 %copy-start.2 = (bf16[48,32,128]{2,1,0:T(8,128)(2,1)S(1)}, bf16[48,32,128]{2,1,0:T(8,128)(2,1)}, u32[]{:S(2)}) copy-start(bf16[48,32,128]{2,1,0:T(8,128)(2,1)} %refs_0_.1) | copy-start | bytes 1179652
  12.3 6.0 %collective-permute-start.1 = (bf16[24,32,128]{2,1,0:T(8,128)(2,1)S(1)}, bf16[24,32,128]{2,1,0:T(8,128)(2,1)S(1)}, u32[]{:S(2)}, u32[]{:S(2)}) collective-permute-start(bf16[24,32,128]{2,1,0:T(8,128)(2,1)S(1)} %prior_spread.4.refs_0_), channel_id=1, source_target_pairs={{0,8},{1,9},{2,10},{3,11},{4,12},{5,13},{6,14},{7,15},{8,0},{9,1},... | collective-permute-start | bytes 589832 | tf_op jit(solution)/shard_map/ppermute | solution.py:38
  19.8 4.3 %collective-permute-start.2 = (bf16[8,32,128]{2,1,0:T(8,128)(2,1)S(1)}, bf16[8,32,128]{2,1,0:T(8,128)(2,1)S(1)}, u32[]{:S(2)}, u32[]{:S(2)}) collective-permute-start(bf16[8,32,128]{2,1,0:T(8,128)(2,1)S(1)} %get-tuple-element.78), channel_id=1, source_target_pairs={{0,1},{1,0},{2,3},{3,2},{4,5},{5,4},{6,7},{7,6},{8,9},{9,8},{10,11... | collective-permute-start | bytes 196616 | tf_op jit(solution)/shard_map/ppermute | solution.py:38
  20.1 5.4 %collective-permute-start.3 = (bf16[8,32,128]{2,1,0:T(8,128)(2,1)S(1)}, bf16[8,32,128]{2,1,0:T(8,128)(2,1)S(1)}, u32[]{:S(2)}, u32[]{:S(2)}) collective-permute-start(bf16[8,32,128]{2,1,0:T(8,128)(2,1)S(1)} %get-tuple-element.79), channel_id=1, source_target_pairs={{0,2},{1,3},{2,0},{3,1},{4,6},{5,7},{6,4},{7,5},{8,10},{9,11},{10,... | collective-permute-start | bytes 196616 | tf_op jit(solution)/shard_map/ppermute | solution.py:38
  22.9 5.2 %collective-permute-start.4 = (bf16[8,32,128]{2,1,0:T(8,128)(2,1)S(1)}, bf16[8,32,128]{2,1,0:T(8,128)(2,1)S(1)}, u32[]{:S(2)}, u32[]{:S(2)}) collective-permute-start(bf16[8,32,128]{2,1,0:T(8,128)(2,1)S(1)} %get-tuple-element.80), channel_id=1, source_target_pairs={{0,3},{1,2},{2,1},{3,0},{4,7},{5,6},{6,5},{7,4},{8,11},{9,10},{10,... | collective-permute-start | bytes 196616 | tf_op jit(solution)/shard_map/ppermute | solution.py:38
  28.1 5.7 %collective-permute-start.5 = (bf16[8,32,128]{2,1,0:T(8,128)(2,1)S(1)}, bf16[8,32,128]{2,1,0:T(8,128)(2,1)S(1)}, u32[]{:S(2)}, u32[]{:S(2)}) collective-permute-start(bf16[8,32,128]{2,1,0:T(8,128)(2,1)S(1)} %add_convert_fusion.7), channel_id=1, source_target_pairs={{0,4},{1,5},{2,6},{3,7},{4,0},{5,1},{6,2},{7,3},{8,12},{9,13},{10,... | collective-permute-start | bytes 196616 | tf_op jit(solution)/shard_map/ppermute | solution.py:38
  33.9 8.3 %collective-permute-start.8 = (bf16[8,32,128]{2,1,0:T(8,128)(2,1)S(1)}, bf16[8,32,128]{2,1,0:T(8,128)(2,1)S(1)}, u32[]{:S(2)}, u32[]{:S(2)}) collective-permute-start(bf16[8,32,128]{2,1,0:T(8,128)(2,1)S(1)} %multiply_convert_fusion.3.refs_0_), channel_id=1, source_target_pairs={{0,3},{1,2},{2,1},{3,0},{4,7},{5,6},{6,5},{7,4},{8,11},{9,10},{10,... | collective-permute-start | bytes 196616 | tf_op jit(solution)/shard_map/ppermute | solution.py:38
  34.5 7.7 %collective-permute-start.7 = (bf16[8,32,128]{2,1,0:T(8,128)(2,1)S(1)}, bf16[8,32,128]{2,1,0:T(8,128)(2,1)S(1)}, u32[]{:S(2)}, u32[]{:S(2)}) collective-permute-start(bf16[8,32,128]{2,1,0:T(8,128)(2,1)S(1)} %multiply_convert_fusion.3.refs_0_), channel_id=1, source_target_pairs={{0,2},{1,3},{2,0},{3,1},{4,6},{5,7},{6,4},{7,5},{8,10},{9,11},{10,... | collective-permute-start | bytes 196616 | tf_op jit(solution)/shard_map/ppermute | solution.py:38
  36.2 6.1 %collective-permute-start.6 = (bf16[8,32,128]{2,1,0:T(8,128)(2,1)S(1)}, bf16[8,32,128]{2,1,0:T(8,128)(2,1)S(1)}, u32[]{:S(2)}, u32[]{:S(2)}) collective-permute-start(bf16[8,32,128]{2,1,0:T(8,128)(2,1)S(1)} %multiply_convert_fusion.3.refs_0_), channel_id=1, source_target_pairs={{0,1},{1,0},{2,3},{3,2},{4,5},{5,4},{6,7},{7,6},{8,9},{9,8},{10,11... | collective-permute-start | bytes 196616 | tf_op jit(solution)/shard_map/ppermute | solution.py:38
  42.9 1.5 collective-permute-start.9
  44.4 7.6 %collective-permute-start.10 = (bf16[24,32,128]{2,1,0:T(8,128)(2,1)S(1)}, bf16[24,32,128]{2,1,0:T(8,128)(2,1)S(1)}, u32[]{:S(2)}, u32[]{:S(2)}) collective-permute-start(bf16[24,32,128]{2,1,0:T(8,128)(2,1)S(1)} %add_convert_fusion.3.mine), channel_id=1, source_target_pairs={{0,16},{1,17},{2,18},{3,19},{4,20},{5,21},{6,22},{7,23},{8,24},{9,... | collective-permute-start | bytes 589832 | tf_op jit(solution)/shard_map/ppermute | solution.py:38
  53.7 1.5 collective-permute-start.11
  53.7 1.4 collective-permute-start.12
  56.4 7.9 %collective-permute-start.13 = (bf16[24,32,128]{2,1,0:T(8,128)(2,1)S(1)}, bf16[24,32,128]{2,1,0:T(8,128)(2,1)S(1)}, u32[]{:S(2)}, u32[]{:S(2)}) collective-permute-start(bf16[24,32,128]{2,1,0:T(8,128)(2,1)S(1)} %prior_spread.5.refs_0_), channel_id=1, source_target_pairs={{0,8},{1,9},{2,10},{3,11},{4,12},{5,13},{6,14},{7,15},{8,0},{9,1},... | collective-permute-start | bytes 589832 | tf_op jit(solution)/shard_map/ppermute | solution.py:38
  65.8 5.0 %collective-permute-start.14 = (bf16[8,32,128]{2,1,0:T(8,128)(2,1)S(1)}, bf16[8,32,128]{2,1,0:T(8,128)(2,1)S(1)}, u32[]{:S(2)}, u32[]{:S(2)}) collective-permute-start(bf16[8,32,128]{2,1,0:T(8,128)(2,1)S(1)} %get-tuple-element.93), channel_id=1, source_target_pairs={{0,1},{1,0},{2,3},{3,2},{4,5},{5,4},{6,7},{7,6},{8,9},{9,8},{10,11... | collective-permute-start | bytes 196616 | tf_op jit(solution)/shard_map/ppermute | solution.py:38
  67.0 4.6 %collective-permute-start.15 = (bf16[8,32,128]{2,1,0:T(8,128)(2,1)S(1)}, bf16[8,32,128]{2,1,0:T(8,128)(2,1)S(1)}, u32[]{:S(2)}, u32[]{:S(2)}) collective-permute-start(bf16[8,32,128]{2,1,0:T(8,128)(2,1)S(1)} %get-tuple-element.94), channel_id=1, source_target_pairs={{0,2},{1,3},{2,0},{3,1},{4,6},{5,7},{6,4},{7,5},{8,10},{9,11},{10,... | collective-permute-start | bytes 196616 | tf_op jit(solution)/shard_map/ppermute | solution.py:38
  68.8 5.2 %collective-permute-start.16 = (bf16[8,32,128]{2,1,0:T(8,128)(2,1)S(1)}, bf16[8,32,128]{2,1,0:T(8,128)(2,1)S(1)}, u32[]{:S(2)}, u32[]{:S(2)}) collective-permute-start(bf16[8,32,128]{2,1,0:T(8,128)(2,1)S(1)} %get-tuple-element.95), channel_id=1, source_target_pairs={{0,3},{1,2},{2,1},{3,0},{4,7},{5,6},{6,5},{7,4},{8,11},{9,10},{10,... | collective-permute-start | bytes 196616 | tf_op jit(solution)/shard_map/ppermute | solution.py:38
  74.0 6.2 %collective-permute-start.17 = (bf16[8,32,128]{2,1,0:T(8,128)(2,1)S(1)}, bf16[8,32,128]{2,1,0:T(8,128)(2,1)S(1)}, u32[]{:S(2)}, u32[]{:S(2)}) collective-permute-start(bf16[8,32,128]{2,1,0:T(8,128)(2,1)S(1)} %add_convert_fusion.6), channel_id=1, source_target_pairs={{0,4},{1,5},{2,6},{3,7},{4,0},{5,1},{6,2},{7,3},{8,12},{9,13},{10,... | collective-permute-start | bytes 196616 | tf_op jit(solution)/shard_map/ppermute | solution.py:38
  80.2 5.2 %collective-permute-start.20 = (bf16[8,32,128]{2,1,0:T(8,128)(2,1)S(1)}, bf16[8,32,128]{2,1,0:T(8,128)(2,1)S(1)}, u32[]{:S(2)}, u32[]{:S(2)}) collective-permute-start(bf16[8,32,128]{2,1,0:T(8,128)(2,1)S(1)} %multiply_convert_fusion.2.refs_0_), channel_id=1, source_target_pairs={{0,3},{1,2},{2,1},{3,0},{4,7},{5,6},{6,5},{7,4},{8,11},{9,10},{10,... | collective-permute-start | bytes 196616 | tf_op jit(solution)/shard_map/ppermute | solution.py:38
  80.9 4.9 %collective-permute-start.19 = (bf16[8,32,128]{2,1,0:T(8,128)(2,1)S(1)}, bf16[8,32,128]{2,1,0:T(8,128)(2,1)S(1)}, u32[]{:S(2)}, u32[]{:S(2)}) collective-permute-start(bf16[8,32,128]{2,1,0:T(8,128)(2,1)S(1)} %multiply_convert_fusion.2.refs_0_), channel_id=1, source_target_pairs={{0,2},{1,3},{2,0},{3,1},{4,6},{5,7},{6,4},{7,5},{8,10},{9,11},{10,... | collective-permute-start | bytes 196616 | tf_op jit(solution)/shard_map/ppermute | solution.py:38
  82.9 4.3 %collective-permute-start.18 = (bf16[8,32,128]{2,1,0:T(8,128)(2,1)S(1)}, bf16[8,32,128]{2,1,0:T(8,128)(2,1)S(1)}, u32[]{:S(2)}, u32[]{:S(2)}) collective-permute-start(bf16[8,32,128]{2,1,0:T(8,128)(2,1)S(1)} %multiply_convert_fusion.2.refs_0_), channel_id=1, source_target_pairs={{0,1},{1,0},{2,3},{3,2},{4,5},{5,4},{6,7},{7,6},{8,9},{9,8},{10,11... | collective-permute-start | bytes 196616 | tf_op jit(solution)/shard_map/ppermute | solution.py:38
  87.8 1.5 collective-permute-start.21
  89.3 7.5 %collective-permute-start.22 = (bf16[24,32,128]{2,1,0:T(8,128)(2,1)S(1)}, bf16[24,32,128]{2,1,0:T(8,128)(2,1)S(1)}, u32[]{:S(2)}, u32[]{:S(2)}) collective-permute-start(bf16[24,32,128]{2,1,0:T(8,128)(2,1)S(1)} %add_convert_fusion.2.mine), channel_id=1, source_target_pairs={{0,16},{1,17},{2,18},{3,19},{4,20},{5,21},{6,22},{7,23},{8,24},{9,... | collective-permute-start | bytes 589832 | tf_op jit(solution)/shard_map/ppermute | solution.py:38
  98.5 1.5 collective-permute-start.23
  98.6 1.4 collective-permute-start.24
  101.3 7.7 %collective-permute-start.25 = (bf16[24,32,128]{2,1,0:T(8,128)(2,1)S(1)}, bf16[24,32,128]{2,1,0:T(8,128)(2,1)S(1)}, u32[]{:S(2)}, u32[]{:S(2)}) collective-permute-start(bf16[24,32,128]{2,1,0:T(8,128)(2,1)S(1)} %prior_spread.6.refs_0_), channel_id=1, source_target_pairs={{0,8},{1,9},{2,10},{3,11},{4,12},{5,13},{6,14},{7,15},{8,0},{9,1},... | collective-permute-start | bytes 589832 | tf_op jit(solution)/shard_map/ppermute | solution.py:38
  110.5 5.0 %collective-permute-start.26 = (bf16[8,32,128]{2,1,0:T(8,128)(2,1)S(1)}, bf16[8,32,128]{2,1,0:T(8,128)(2,1)S(1)}, u32[]{:S(2)}, u32[]{:S(2)}) collective-permute-start(bf16[8,32,128]{2,1,0:T(8,128)(2,1)S(1)} %get-tuple-element.102), channel_id=1, source_target_pairs={{0,1},{1,0},{2,3},{3,2},{4,5},{5,4},{6,7},{7,6},{8,9},{9,8},{10,11... | collective-permute-start | bytes 196616 | tf_op jit(solution)/shard_map/ppermute | solution.py:38
  111.8 4.8 %collective-permute-start.27 = (bf16[8,32,128]{2,1,0:T(8,128)(2,1)S(1)}, bf16[8,32,128]{2,1,0:T(8,128)(2,1)S(1)}, u32[]{:S(2)}, u32[]{:S(2)}) collective-permute-start(bf16[8,32,128]{2,1,0:T(8,128)(2,1)S(1)} %get-tuple-element.103), channel_id=1, source_target_pairs={{0,2},{1,3},{2,0},{3,1},{4,6},{5,7},{6,4},{7,5},{8,10},{9,11},{10,... | collective-permute-start | bytes 196616 | tf_op jit(solution)/shard_map/ppermute | solution.py:38
  113.8 5.2 %collective-permute-start.28 = (bf16[8,32,128]{2,1,0:T(8,128)(2,1)S(1)}, bf16[8,32,128]{2,1,0:T(8,128)(2,1)S(1)}, u32[]{:S(2)}, u32[]{:S(2)}) collective-permute-start(bf16[8,32,128]{2,1,0:T(8,128)(2,1)S(1)} %get-tuple-element.104), channel_id=1, source_target_pairs={{0,3},{1,2},{2,1},{3,0},{4,7},{5,6},{6,5},{7,4},{8,11},{9,10},{10,... | collective-permute-start | bytes 196616 | tf_op jit(solution)/shard_map/ppermute | solution.py:38
  119.0 5.9 %collective-permute-start.29 = (bf16[8,32,128]{2,1,0:T(8,128)(2,1)S(1)}, bf16[8,32,128]{2,1,0:T(8,128)(2,1)S(1)}, u32[]{:S(2)}, u32[]{:S(2)}) collective-permute-start(bf16[8,32,128]{2,1,0:T(8,128)(2,1)S(1)} %add_convert_fusion.5), channel_id=1, source_target_pairs={{0,4},{1,5},{2,6},{3,7},{4,0},{5,1},{6,2},{7,3},{8,12},{9,13},{10,... | collective-permute-start | bytes 196616 | tf_op jit(solution)/shard_map/ppermute | solution.py:38
  125.0 5.2 %collective-permute-start.32 = (bf16[8,32,128]{2,1,0:T(8,128)(2,1)S(1)}, bf16[8,32,128]{2,1,0:T(8,128)(2,1)S(1)}, u32[]{:S(2)}, u32[]{:S(2)}) collective-permute-start(bf16[8,32,128]{2,1,0:T(8,128)(2,1)S(1)} %multiply_convert_fusion.1.refs_0_), channel_id=1, source_target_pairs={{0,3},{1,2},{2,1},{3,0},{4,7},{5,6},{6,5},{7,4},{8,11},{9,10},{10,... | collective-permute-start | bytes 196616 | tf_op jit(solution)/shard_map/ppermute | solution.py:38
  126.2 4.3 %collective-permute-start.31 = (bf16[8,32,128]{2,1,0:T(8,128)(2,1)S(1)}, bf16[8,32,128]{2,1,0:T(8,128)(2,1)S(1)}, u32[]{:S(2)}, u32[]{:S(2)}) collective-permute-start(bf16[8,32,128]{2,1,0:T(8,128)(2,1)S(1)} %multiply_convert_fusion.1.refs_0_), channel_id=1, source_target_pairs={{0,2},{1,3},{2,0},{3,1},{4,6},{5,7},{6,4},{7,5},{8,10},{9,11},{10,... | collective-permute-start | bytes 196616 | tf_op jit(solution)/shard_map/ppermute | solution.py:38
  127.0 4.3 %collective-permute-start.30 = (bf16[8,32,128]{2,1,0:T(8,128)(2,1)S(1)}, bf16[8,32,128]{2,1,0:T(8,128)(2,1)S(1)}, u32[]{:S(2)}, u32[]{:S(2)}) collective-permute-start(bf16[8,32,128]{2,1,0:T(8,128)(2,1)S(1)} %multiply_convert_fusion.1.refs_0_), channel_id=1, source_target_pairs={{0,1},{1,0},{2,3},{3,2},{4,5},{5,4},{6,7},{7,6},{8,9},{9,8},{10,11... | collective-permute-start | bytes 196616 | tf_op jit(solution)/shard_map/ppermute | solution.py:38
  131.9 1.5 collective-permute-start.33
  133.5 8.4 %collective-permute-start.34 = (bf16[24,32,128]{2,1,0:T(8,128)(2,1)S(1)}, bf16[24,32,128]{2,1,0:T(8,128)(2,1)S(1)}, u32[]{:S(2)}, u32[]{:S(2)}) collective-permute-start(bf16[24,32,128]{2,1,0:T(8,128)(2,1)S(1)} %add_convert_fusion.1.mine), channel_id=1, source_target_pairs={{0,16},{1,17},{2,18},{3,19},{4,20},{5,21},{6,22},{7,23},{8,24},{9,... | collective-permute-start | bytes 589832 | tf_op jit(solution)/shard_map/ppermute | solution.py:38
  143.5 1.5 collective-permute-start.35
  143.6 1.4 collective-permute-start.36
  146.2 8.3 %collective-permute-start.37 = (bf16[24,32,128]{2,1,0:T(8,128)(2,1)S(1)}, bf16[24,32,128]{2,1,0:T(8,128)(2,1)S(1)}, u32[]{:S(2)}, u32[]{:S(2)}) collective-permute-start(bf16[24,32,128]{2,1,0:T(8,128)(2,1)S(1)} %prior_spread.7.refs_0_), channel_id=1, source_target_pairs={{0,8},{1,9},{2,10},{3,11},{4,12},{5,13},{6,14},{7,15},{8,0},{9,1},... | collective-permute-start | bytes 589832 | tf_op jit(solution)/shard_map/ppermute | solution.py:38
  156.1 4.9 %collective-permute-start.38 = (bf16[8,32,128]{2,1,0:T(8,128)(2,1)S(1)}, bf16[8,32,128]{2,1,0:T(8,128)(2,1)S(1)}, u32[]{:S(2)}, u32[]{:S(2)}) collective-permute-start(bf16[8,32,128]{2,1,0:T(8,128)(2,1)S(1)} %get-tuple-element.111), channel_id=1, source_target_pairs={{0,1},{1,0},{2,3},{3,2},{4,5},{5,4},{6,7},{7,6},{8,9},{9,8},{10,11... | collective-permute-start | bytes 196616 | tf_op jit(solution)/shard_map/ppermute | solution.py:38
  157.7 4.8 %collective-permute-start.39 = (bf16[8,32,128]{2,1,0:T(8,128)(2,1)S(1)}, bf16[8,32,128]{2,1,0:T(8,128)(2,1)S(1)}, u32[]{:S(2)}, u32[]{:S(2)}) collective-permute-start(bf16[8,32,128]{2,1,0:T(8,128)(2,1)S(1)} %get-tuple-element.112), channel_id=1, source_target_pairs={{0,2},{1,3},{2,0},{3,1},{4,6},{5,7},{6,4},{7,5},{8,10},{9,11},{10,... | collective-permute-start | bytes 196616 | tf_op jit(solution)/shard_map/ppermute | solution.py:38
  158.7 5.2 %collective-permute-start.40 = (bf16[8,32,128]{2,1,0:T(8,128)(2,1)S(1)}, bf16[8,32,128]{2,1,0:T(8,128)(2,1)S(1)}, u32[]{:S(2)}, u32[]{:S(2)}) collective-permute-start(bf16[8,32,128]{2,1,0:T(8,128)(2,1)S(1)} %get-tuple-element.113), channel_id=1, source_target_pairs={{0,3},{1,2},{2,1},{3,0},{4,7},{5,6},{6,5},{7,4},{8,11},{9,10},{10,... | collective-permute-start | bytes 196616 | tf_op jit(solution)/shard_map/ppermute | solution.py:38
  164.0 6.5 %collective-permute-start.41 = (bf16[8,32,128]{2,1,0:T(8,128)(2,1)S(1)}, bf16[8,32,128]{2,1,0:T(8,128)(2,1)S(1)}, u32[]{:S(2)}, u32[]{:S(2)}) collective-permute-start(bf16[8,32,128]{2,1,0:T(8,128)(2,1)S(1)} %add_convert_fusion.4), channel_id=1, source_target_pairs={{0,4},{1,5},{2,6},{3,7},{4,0},{5,1},{6,2},{7,3},{8,12},{9,13},{10,... | collective-permute-start | bytes 196616 | tf_op jit(solution)/shard_map/ppermute | solution.py:38
  170.5 5.2 %collective-permute-start.44 = (bf16[8,32,128]{2,1,0:T(8,128)(2,1)S(1)}, bf16[8,32,128]{2,1,0:T(8,128)(2,1)S(1)}, u32[]{:S(2)}, u32[]{:S(2)}) collective-permute-start(bf16[8,32,128]{2,1,0:T(8,128)(2,1)S(1)} %multiply_convert_fusion.refs_0_), channel_id=1, source_target_pairs={{0,3},{1,2},{2,1},{3,0},{4,7},{5,6},{6,5},{7,4},{8,11},{9,10},{10,... | collective-permute-start | bytes 196616 | tf_op jit(solution)/shard_map/ppermute | solution.py:38
  170.9 4.9 %collective-permute-start.43 = (bf16[8,32,128]{2,1,0:T(8,128)(2,1)S(1)}, bf16[8,32,128]{2,1,0:T(8,128)(2,1)S(1)}, u32[]{:S(2)}, u32[]{:S(2)}) collective-permute-start(bf16[8,32,128]{2,1,0:T(8,128)(2,1)S(1)} %multiply_convert_fusion.refs_0_), channel_id=1, source_target_pairs={{0,2},{1,3},{2,0},{3,1},{4,6},{5,7},{6,4},{7,5},{8,10},{9,11},{10,... | collective-permute-start | bytes 196616 | tf_op jit(solution)/shard_map/ppermute | solution.py:38
  172.9 4.3 %collective-permute-start.42 = (bf16[8,32,128]{2,1,0:T(8,128)(2,1)S(1)}, bf16[8,32,128]{2,1,0:T(8,128)(2,1)S(1)}, u32[]{:S(2)}, u32[]{:S(2)}) collective-permute-start(bf16[8,32,128]{2,1,0:T(8,128)(2,1)S(1)} %multiply_convert_fusion.refs_0_), channel_id=1, source_target_pairs={{0,1},{1,0},{2,3},{3,2},{4,5},{5,4},{6,7},{7,6},{8,9},{9,8},{10,11... | collective-permute-start | bytes 196616 | tf_op jit(solution)/shard_map/ppermute | solution.py:38
  177.1 20.2 %copy-start.1 = (f32[32,128]{1,0:T(8,128)S(1)}, f32[32,128]{1,0:T(8,128)}, u32[]{:S(2)}) copy-start(f32[32,128]{1,0:T(8,128)} %param.15) | copy-start | bytes 49156
  177.8 1.5 collective-permute-start.45
  179.3 7.8 %collective-permute-start.46 = (bf16[24,32,128]{2,1,0:T(8,128)(2,1)S(1)}, bf16[24,32,128]{2,1,0:T(8,128)(2,1)S(1)}, u32[]{:S(2)}, u32[]{:S(2)}) collective-permute-start(bf16[24,32,128]{2,1,0:T(8,128)(2,1)S(1)} %add_convert_fusion.mine), channel_id=1, source_target_pairs={{0,16},{1,17},{2,18},{3,19},{4,20},{5,21},{6,22},{7,23},{8,24},{9,... | collective-permute-start | bytes 589832 | tf_op jit(solution)/shard_map/ppermute | solution.py:38
  188.8 1.4 collective-permute-start.48
  188.9 1.3 collective-permute-start.47
  190.3 6.3 %collective-permute-start.49 = (bf16[24,32,128]{2,1,0:T(8,128)(2,1)S(1)}, bf16[24,32,128]{2,1,0:T(8,128)(2,1)S(1)}, u32[]{:S(2)}, u32[]{:S(2)}) collective-permute-start(bf16[24,32,128]{2,1,0:T(8,128)(2,1)S(1)} %fusion), channel_id=1, source_target_pairs={{0,8},{1,9},{2,10},{3,11},{4,12},{5,13},{6,14},{7,15},{8,0},{9,1},... | collective-permute-start | bytes 589832 | tf_op jit(solution)/shard_map/ppermute | solution.py:38

commit v9 on v8

--- a/solution.py
+++ b/solution.py
@@ -87,15 +87,15 @@
 
 
 def setup_kernel(
-    rows, chunk, where, obs, flux, nbr, prior, jac,
-    prior_plain, jac_plain, *refs
+    rows, chunk, where, obs, flux, nbr, prior,
+    prior_plain, *refs
 ):
     plans, (obs_in, flux_in, nbr_in) = refs[:7], refs[7:10]
     built, (small_sems, sems) = refs[10:17], refs[17:]
     side, corner, count, first_tile = where[0], where[1], where[2], where[3]
     owned = prior_plain.shape[0]
     begin = side * owned
-    rounds = (owned // chunk, jac_plain.shape[0] // chunk)
+    rounds = (owned // chunk,)
 
     def copy(c, first, source, plain, offset):
         to = pl.ds(c * chunk, chunk)
@@ -120,7 +120,6 @@
     for one in small:
         one.start()
     lax.fori_loop(0, rounds[0], start(begin, prior, prior_plain, 0), 0)
-    lax.fori_loop(0, rounds[1], start(0, jac, jac_plain, rounds[0]), 0)
     for one in small:
         one.wait()
 
@@ -161,7 +160,6 @@
         one.start()
 
     lax.fori_loop(0, rounds[0], wait(begin, prior, prior_plain, 0), 0)
-    lax.fori_loop(0, rounds[1], wait(0, jac, jac_plain, rounds[0]), 0)
     for one in lists:
         one.wait()
 
@@ -188,15 +186,14 @@
     )(plain)
 
 
-def setup(where, obs, flux, nbr, prior, jac, rows):
+def setup(where, obs, flux, nbr, prior, rows):
     most = max(rows[:2])
     owned = rows[1] // 2 * rows[2]
-    chunk = chunk_of(math.gcd(owned, jac.shape[0]), 24)
+    chunk = chunk_of(owned, 24)
     smem = pl.BlockSpec(memory_space=pltpu.SMEM)
     vmem = pl.BlockSpec(memory_space=pltpu.VMEM)
     hbm = pl.BlockSpec(memory_space=pl.ANY)
     own = pltpu.VMEM((owned,) + prior.shape[1:], HALF)
-    all_blocks = pltpu.VMEM(jac.shape, HALF)
     i32 = jnp.int32
     lengths = []
     used = (FORWARD_PLAN, FORWARD_PLAN, NEAR_PLAN, REST_PLAN, REST_PLAN, PRIOR_PLAN)
@@ -206,18 +203,18 @@
     lengths.append(nbr.shape[1] + LANES)
     return pl.pallas_call(
         functools.partial(setup_kernel, rows, chunk),
-        in_specs=[smem] + [hbm] * 5,
-        out_specs=[vmem] * 2 + [smem] * 7,
-        out_shape=[own, all_blocks] + [pltpu.SMEM((1, n), i32) for n in lengths],
+        in_specs=[smem] + [hbm] * 4,
+        out_specs=[vmem] + [smem] * 7,
+        out_shape=[own] + [pltpu.SMEM((1, n), i32) for n in lengths],
         scratch_shapes=[pltpu.VMEM(v.shape, i32) for v in (obs, flux, nbr)]
         + [pltpu.VMEM((1, n), i32) for n in lengths]
         + [
             pltpu.SemaphoreType.DMA((10,)),
-            pltpu.SemaphoreType.DMA(((owned + jac.shape[0]) // chunk,)),
+            pltpu.SemaphoreType.DMA((owned // chunk,)),
         ],
         compiler_params=pltpu.CompilerParams(vmem_limit_bytes=VMEM_LIMIT),
         name="setup",
-    )(where, *(pltpu.with_memory_space_constraint(v, pltpu.HBM) for v in (obs, flux, nbr, prior, jac)))
+    )(where, *(pltpu.with_memory_space_constraint(v, pltpu.HBM) for v in (obs, flux, nbr, prior)))
 
 
 def grouped_products(plan, sizes, lists, x, blocks, total):
@@ -394,8 +391,9 @@
     nbr = neighbours.reshape(1, tile_count * fan)
 
     where, own_rinv, nbr, prior, blocks = lax.optimization_barrier((where, own_rinv, nbr, prior, blocks))
-    prior_plain, jac_plain, *jac_lists, prior_lists, nbr = setup(
-        where, jac_obs[0], jac_flux[0], nbr, prior, blocks, sizes
+    jac_plain = blocks
+    prior_plain, *jac_lists, prior_lists, nbr = setup(
+        where, jac_obs[0], jac_flux[0], nbr, prior, sizes
     )
     fields = (probes, beyond)
     for step in range(STEPS):
@@ -414,6 +412,8 @@
         total = pieces[0]
         for bits in range(1, 4):
             total = total + swap_flux(pieces[bits], bits).astype(F32)
+        if step == 0:
+            total, jac_turned = lax.optimization_barrier((total, jac_turned))
         bits = 4
         while bits < n_flux:
             sent = total.astype(HALF)

time: 198 us -> 194 us (0.980)
  starting transfers between devices: 80.6 us -> 70.5 us
  waiting for transfers between devices: 65.7 us -> 69.7 us
  Pallas kernels: 46 us -> 48.4 us
    ppermute x50, starting transfers between devices: 80.6 us -> 70.5 us  [exchange(): return lax.ppermute(value, ('obs', 'flux'), route)]
    pallas_call x20, Pallas kernels: 21.8 us -> 26.4 us  [jac_pass(): pl.pallas_call(functools.partial(jac_kernel, plan, sizes, len(parts), beg...]
    ppermute x50, waiting for transfers between devices: 65.7 us -> 69.7 us  [exchange(): return lax.ppermute(value, ('obs', 'flux'), route)]
    pallas_call x1, Pallas kernels: 7.35 us -> 5.14 us  [setup(): pl.pallas_call(functools.partial(setup_kernel, rows, chunk), in_specs=[sm...]
where the time goes in v9:
time: 194 us
  starting transfers between devices  70.5 us (36%)
  waiting for transfers between devices  69.7 us (36%)
  Pallas kernels  48.4 us (25%)
  other arithmetic  2.49 us (1%)
    ppermute x50, starting transfers between devices, exchange(): return lax.ppermute(value, ('obs', 'flux'), route)  70.5 us
    ppermute x50, waiting for transfers between devices, exchange(): return lax.ppermute(value, ('obs', 'flux'), route)  69.7 us
    pallas_call x20, Pallas kernels, jac_pass(): pl.pallas_call(functools.partial(jac_kernel, plan, sizes, len(parts), beg...  26.4 us
    pallas_call x4, Pallas kernels, gather_tiles(): pl.pallas_call(functools.partial(gather_kernel, rows, plan_sizes(PRIOR_PL...  6.52 us
    pallas_call x2, Pallas kernels, turn_blocks(): pl.pallas_call(functools.partial(turn_kernel, chunk_of(plain.shape[0], 48...  5.5 us
    pallas_call x1, Pallas kernels, setup(): pl.pallas_call(functools.partial(setup_kernel, rows, chunk), in_specs=[sm...  5.14 us
    pallas_call x4, Pallas kernels, spread_tiles(): pl.pallas_call(functools.partial(spread_kernel, len(fields) == 2, prior.s...  4.8 us
  transfers between devices with their start and end apart: 50, of which 37 were waited for; matrix products, arithmetic and copies ran while one was open for 1% of the time, Pallas kernels for 13%

profile of v9, /device:TPU:0, one launch (start us, length us, event | category | flops | bytes accessed | tf_op | source)
XLA Modules:
  0.0 193.7 jit_solution(290520873481268391)
XLA Ops:
  3.9 5.1 %setup.1 = (bf16[192,128,128]{2,1,0:T(8,128)(2,1)S(1)}, s32[1,1664]{1,0:T(1,128)S(4)}, s32[1,1664]{1,0:T(1,128)S(4)}, s32[1,1408]{1,0:T(1,128)S(4)}, s32[1,1280]...) custom-call(s32[4]{0:T(128)S(1)} %pad_add_fusion.where, s32[1,384]{1,0:T(1,128)} %bitcast.26, ...), custom_call_target="tpu_custom_call" | custom-call | tf_op jit(solution)/shard_map/setup/pallas_call | solution.py:204
  10.1 4.4 %collective-permute-start.1 = (bf16[24,32,128]{2,1,0:T(8,128)(2,1)S(1)}, bf16[24,32,128]{2,1,0:T(8,128)(2,1)S(1)}, u32[]{:S(2)}, u32[]{:S(2)}) collective-permute-start(bf16[24,32,128]{2,1,0:T(8,128)(2,1)S(1)} %prior_spread.4.refs_0_), channel_id=1, source_target_pairs={{0,8},{1,9},{2,10},{3,11},{4,12},{5,13},{6,14},{7,15},{8,0},{9,1},... | collective-permute-start | bytes 589832 | tf_op jit(solution)/shard_map/ppermute | solution.py:38
  14.5 1.5 forward_own.4.refs_1_
  16.1 1.5 forward_other.4
  17.6 1.6 collective-permute-start.2
  19.2 1.6 collective-permute-start.3
  21.2 3.7 %jac_turn.1.refs_1_.refs_4_ = bf16[384,128,128]{2,1,0:T(8,128)(2,1)S(1)} custom-call(bf16[384,128,128]{2,1,0:T(8,128)(2,1)S(1)} %bitcast.14), custom_call_target="tpu_custom_call" | custom-call | bytes 12582912 | tf_op jit(solution)/shard_map/jac_turn/pallas_call | solution.py:178
  27.1 4.8 %collective-permute-done.5 = bf16[8,32,128]{2,1,0:T(8,128)(2,1)S(1)} collective-permute-done((bf16[8,32,128]{2,1,0:T(8,128)(2,1)S(1)}, bf16[8,32,128]{2,1,0:T(8,128)(2,1)S(1)}, u32[]{:S(2)}, u32[]{:S(2)}) %collective-permute-start.5) | collective-permute-done | bytes 65568 | tf_op jit(solution)/shard_map/ppermute | solution.py:38
  33.3 2.2 %collective-permute-start.6 = (bf16[8,32,128]{2,1,0:T(8,128)(2,1)S(1)}, bf16[8,32,128]{2,1,0:T(8,128)(2,1)S(1)}, u32[]{:S(2)}, u32[]{:S(2)}) collective-permute-start(bf16[8,32,128]{2,1,0:T(8,128)(2,1)S(1)} %multiply_convert_fusion.3.refs_0_), channel_id=1, source_target_pairs={{0,1},{1,0},{2,3},{3,2},{4,5},{5,4},{6,7},{7,6},{8,9},{9,8},{10,11... | collective-permute-start | bytes 196616 | tf_op jit(solution)/shard_map/ppermute | solution.py:38
  37.8 1.2 adjoint_other.4
  39.1 1.2 adjoint_own.4
  40.6 1.9 collective-permute-start.10
  42.6 1.8 prior_turn.1.prior
  44.4 3.5 %collective-permute-done.10.other = bf16[24,32,128]{2,1,0:T(8,128)(2,1)S(1)} collective-permute-done((bf16[24,32,128]{2,1,0:T(8,128)(2,1)S(1)}, bf16[24,32,128]{2,1,0:T(8,128)(2,1)S(1)}, u32[]{:S(2)}, u32[]{:S(2)}) %collective-permute-start.10) | collective-permute-done | bytes 196640 | tf_op jit(solution)/shard_map/ppermute | solution.py:38
  47.9 1.6 prior_adjoint.4
  51.1 1.2 prior_spread.5.refs_0_
  52.3 7.1 %collective-permute-start.13 = (bf16[24,32,128]{2,1,0:T(8,128)(2,1)S(1)}, bf16[24,32,128]{2,1,0:T(8,128)(2,1)S(1)}, u32[]{:S(2)}, u32[]{:S(2)}) collective-permute-start(bf16[24,32,128]{2,1,0:T(8,128)(2,1)S(1)} %prior_spread.5.refs_0_), channel_id=1, source_target_pairs={{0,8},{1,9},{2,10},{3,11},{4,12},{5,13},{6,14},{7,15},{8,0},{9,1},... | collective-permute-start | bytes 589832 | tf_op jit(solution)/shard_map/ppermute | solution.py:38
  59.5 1.7 forward_own.5.refs_1_
  61.2 1.5 forward_other.5
  62.7 2.4 %collective-permute-start.14 = (bf16[8,32,128]{2,1,0:T(8,128)(2,1)S(1)}, bf16[8,32,128]{2,1,0:T(8,128)(2,1)S(1)}, u32[]{:S(2)}, u32[]{:S(2)}) collective-permute-start(bf16[8,32,128]{2,1,0:T(8,128)(2,1)S(1)} %get-tuple-element.95), channel_id=1, source_target_pairs={{0,1},{1,0},{2,3},{3,2},{4,5},{5,4},{6,7},{7,6},{8,9},{9,8},{10,11... | collective-permute-start | bytes 196616 | tf_op jit(solution)/shard_map/ppermute | solution.py:38
  65.2 1.5 collective-permute-start.16
  67.9 2.2 %collective-permute-done.15 = bf16[8,32,128]{2,1,0:T(8,128)(2,1)S(1)} collective-permute-done((bf16[8,32,128]{2,1,0:T(8,128)(2,1)S(1)}, bf16[8,32,128]{2,1,0:T(8,128)(2,1)S(1)}, u32[]{:S(2)}, u32[]{:S(2)}) %collective-permute-start.15) | collective-permute-done | bytes 65568 | tf_op jit(solution)/shard_map/ppermute | solution.py:38
  71.8 4.2 %collective-permute-done.17 = bf16[8,32,128]{2,1,0:T(8,128)(2,1)S(1)} collective-permute-done((bf16[8,32,128]{2,1,0:T(8,128)(2,1)S(1)}, bf16[8,32,128]{2,1,0:T(8,128)(2,1)S(1)}, u32[]{:S(2)}, u32[]{:S(2)}) %collective-permute-start.17) | collective-permute-done | bytes 65568 | tf_op jit(solution)/shard_map/ppermute | solution.py:38
  76.0 1.4 collective-permute-start.20
  77.4 2.1 %collective-permute-start.19 = (bf16[8,32,128]{2,1,0:T(8,128)(2,1)S(1)}, bf16[8,32,128]{2,1,0:T(8,128)(2,1)S(1)}, u32[]{:S(2)}, u32[]{:S(2)}) collective-permute-start(bf16[8,32,128]{2,1,0:T(8,128)(2,1)S(1)} %multiply_convert_fusion.2.refs_0_), channel_id=1, source_target_pairs={{0,2},{1,3},{2,0},{3,1},{4,6},{5,7},{6,4},{7,5},{8,10},{9,11},{10,... | collective-permute-start | bytes 196616 | tf_op jit(solution)/shard_map/ppermute | solution.py:38
  82.5 1.3 collective-permute-done.18.refs_0_
  83.8 1.2 adjoint_other.5
  85.1 1.2 adjoint_own.5
  87.7 5.8 %collective-permute-done.22.other = bf16[24,32,128]{2,1,0:T(8,128)(2,1)S(1)} collective-permute-done((bf16[24,32,128]{2,1,0:T(8,128)(2,1)S(1)}, bf16[24,32,128]{2,1,0:T(8,128)(2,1)S(1)}, u32[]{:S(2)}, u32[]{:S(2)}) %collective-permute-start.22) | collective-permute-done | bytes 196640 | tf_op jit(solution)/shard_map/ppermute | solution.py:38
  93.6 1.6 prior_adjoint.5
  96.7 1.2 prior_spread.6.refs_0_
  98.0 6.1 %collective-permute-start.25 = (bf16[24,32,128]{2,1,0:T(8,128)(2,1)S(1)}, bf16[24,32,128]{2,1,0:T(8,128)(2,1)S(1)}, u32[]{:S(2)}, u32[]{:S(2)}) collective-permute-start(bf16[24,32,128]{2,1,0:T(8,128)(2,1)S(1)} %prior_spread.6.refs_0_), channel_id=1, source_target_pairs={{0,8},{1,9},{2,10},{3,11},{4,12},{5,13},{6,14},{7,15},{8,0},{9,1},... | collective-permute-start | bytes 589832 | tf_op jit(solution)/shard_map/ppermute | solution.py:38
  104.1 1.5 forward_own.6.refs_1_
  105.7 1.5 forward_other.6
  107.2 2.1 %collective-permute-start.26 = (bf16[8,32,128]{2,1,0:T(8,128)(2,1)S(1)}, bf16[8,32,128]{2,1,0:T(8,128)(2,1)S(1)}, u32[]{:S(2)}, u32[]{:S(2)}) collective-permute-start(bf16[8,32,128]{2,1,0:T(8,128)(2,1)S(1)} %get-tuple-element.104), channel_id=1, source_target_pairs={{0,1},{1,0},{2,3},{3,2},{4,5},{5,4},{6,7},{7,6},{8,9},{9,8},{10,11... | collective-permute-start | bytes 196616 | tf_op jit(solution)/shard_map/ppermute | solution.py:38
  109.3 1.5 collective-permute-start.27
  112.0 2.0 %collective-permute-done.27 = bf16[8,32,128]{2,1,0:T(8,128)(2,1)S(1)} collective-permute-done((bf16[8,32,128]{2,1,0:T(8,128)(2,1)S(1)}, bf16[8,32,128]{2,1,0:T(8,128)(2,1)S(1)}, u32[]{:S(2)}, u32[]{:S(2)}) %collective-permute-start.27) | collective-permute-done | bytes 65568 | tf_op jit(solution)/shard_map/ppermute | solution.py:38
  114.0 1.9 %collective-permute-done.28 = bf16[8,32,128]{2,1,0:T(8,128)(2,1)S(1)} collective-permute-done((bf16[8,32,128]{2,1,0:T(8,128)(2,1)S(1)}, bf16[8,32,128]{2,1,0:T(8,128)(2,1)S(1)}, u32[]{:S(2)}, u32[]{:S(2)}) %collective-permute-start.28) | collective-permute-done | bytes 65568 | tf_op jit(solution)/shard_map/ppermute | solution.py:38
  116.2 5.7 %collective-permute-done.29 = bf16[8,32,128]{2,1,0:T(8,128)(2,1)S(1)} collective-permute-done((bf16[8,32,128]{2,1,0:T(8,128)(2,1)S(1)}, bf16[8,32,128]{2,1,0:T(8,128)(2,1)S(1)}, u32[]{:S(2)}, u32[]{:S(2)}) %collective-permute-start.29) | collective-permute-done | bytes 65568 | tf_op jit(solution)/shard_map/ppermute | solution.py:38
  122.8 1.5 collective-permute-start.31
  124.3 1.3 collective-permute-start.30
  127.2 1.3 collective-permute-done.30.refs_0_
  128.5 1.2 adjoint_other.6
  129.8 1.2 adjoint_own.6
  131.7 6.6 %collective-permute-done.34.other = bf16[24,32,128]{2,1,0:T(8,128)(2,1)S(1)} collective-permute-done((bf16[24,32,128]{2,1,0:T(8,128)(2,1)S(1)}, bf16[24,32,128]{2,1,0:T(8,128)(2,1)S(1)}, u32[]{:S(2)}, u32[]{:S(2)}) %collective-permute-start.34) | collective-permute-done | bytes 196640 | tf_op jit(solution)/shard_map/ppermute | solution.py:38
  138.3 1.6 prior_adjoint.6
  141.5 1.2 prior_spread.7.refs_0_
  142.7 6.8 %collective-permute-start.37 = (bf16[24,32,128]{2,1,0:T(8,128)(2,1)S(1)}, bf16[24,32,128]{2,1,0:T(8,128)(2,1)S(1)}, u32[]{:S(2)}, u32[]{:S(2)}) collective-permute-start(bf16[24,32,128]{2,1,0:T(8,128)(2,1)S(1)} %prior_spread.7.refs_0_), channel_id=1, source_target_pairs={{0,8},{1,9},{2,10},{3,11},{4,12},{5,13},{6,14},{7,15},{8,0},{9,1},... | collective-permute-start | bytes 589832 | tf_op jit(solution)/shard_map/ppermute | solution.py:38
  149.5 1.5 forward_own.7.refs_1_
  151.1 1.5 forward_other.7
  152.6 2.4 %collective-permute-start.38 = (bf16[8,32,128]{2,1,0:T(8,128)(2,1)S(1)}, bf16[8,32,128]{2,1,0:T(8,128)(2,1)S(1)}, u32[]{:S(2)}, u32[]{:S(2)}) collective-permute-start(bf16[8,32,128]{2,1,0:T(8,128)(2,1)S(1)} %get-tuple-element.113), channel_id=1, source_target_pairs={{0,1},{1,0},{2,3},{3,2},{4,5},{5,4},{6,7},{7,6},{8,9},{9,8},{10,11... | collective-permute-start | bytes 196616 | tf_op jit(solution)/shard_map/ppermute | solution.py:38
  155.2 1.4 collective-permute-start.40
  156.6 1.2 collective-permute-done.38
  157.8 2.2 %collective-permute-done.39 = bf16[8,32,128]{2,1,0:T(8,128)(2,1)S(1)} collective-permute-done((bf16[8,32,128]{2,1,0:T(8,128)(2,1)S(1)}, bf16[8,32,128]{2,1,0:T(8,128)(2,1)S(1)}, u32[]{:S(2)}, u32[]{:S(2)}) %collective-permute-start.39) | collective-permute-done | bytes 65568 | tf_op jit(solution)/shard_map/ppermute | solution.py:38
  160.7 5.1 %collective-permute-done.41 = bf16[8,32,128]{2,1,0:T(8,128)(2,1)S(1)} collective-permute-done((bf16[8,32,128]{2,1,0:T(8,128)(2,1)S(1)}, bf16[8,32,128]{2,1,0:T(8,128)(2,1)S(1)}, u32[]{:S(2)}, u32[]{:S(2)}) %collective-permute-start.41) | collective-permute-done | bytes 65568 | tf_op jit(solution)/shard_map/ppermute | solution.py:38
  165.8 1.5 collective-permute-start.44
  167.3 2.1 %collective-permute-start.43 = (bf16[8,32,128]{2,1,0:T(8,128)(2,1)S(1)}, bf16[8,32,128]{2,1,0:T(8,128)(2,1)S(1)}, u32[]{:S(2)}, u32[]{:S(2)}) collective-permute-start(bf16[8,32,128]{2,1,0:T(8,128)(2,1)S(1)} %multiply_convert_fusion.refs_0_), channel_id=1, source_target_pairs={{0,2},{1,3},{2,0},{3,1},{4,6},{5,7},{6,4},{7,5},{8,10},{9,11},{10,... | collective-permute-start | bytes 196616 | tf_op jit(solution)/shard_map/ppermute | solution.py:38
  171.1 1.3 collective-permute-done.43.refs_1_
  172.3 1.3 collective-permute-done.42.refs_0_
  173.7 1.2 adjoint_other.7
  175.0 1.2 adjoint_own.7
  177.4 6.0 %collective-permute-done.46.other = bf16[24,32,128]{2,1,0:T(8,128)(2,1)S(1)} collective-permute-done((bf16[24,32,128]{2,1,0:T(8,128)(2,1)S(1)}, bf16[24,32,128]{2,1,0:T(8,128)(2,1)S(1)}, u32[]{:S(2)}, u32[]{:S(2)}) %collective-permute-start.46) | collective-permute-done | bytes 196640 | tf_op jit(solution)/shard_map/ppermute | solution.py:38
  183.5 1.6 prior_adjoint.7
  186.6 5.2 %collective-permute-start.49 = (bf16[24,32,128]{2,1,0:T(8,128)(2,1)S(1)}, bf16[24,32,128]{2,1,0:T(8,128)(2,1)S(1)}, u32[]{:S(2)}, u32[]{:S(2)}) collective-permute-start(bf16[24,32,128]{2,1,0:T(8,128)(2,1)S(1)} %fusion), channel_id=1, source_target_pairs={{0,8},{1,9},{2,10},{3,11},{4,12},{5,13},{6,14},{7,15},{8,0},{9,1},... | collective-permute-start | bytes 589832 | tf_op jit(solution)/shard_map/ppermute | solution.py:38
  (98 shorter events, 34.7 us)
Async XLA Ops:
  0.0 3.8 %copy-start = (f32[32,128]{1,0:T(8,128)S(1)}, f32[32,128]{1,0:T(8,128)}, u32[]{:S(2)}) copy-start(f32[32,128]{1,0:T(8,128)} %param.15) | copy-start | bytes 49156
  0.0 9.0 %copy-start.3 = (bf16[48,32,128]{2,1,0:T(8,128)(2,1)S(1)}, bf16[48,32,128]{2,1,0:T(8,128)(2,1)}, u32[]{:S(2)}) copy-start(bf16[48,32,128]{2,1,0:T(8,128)(2,1)} %refs_0_.1) | copy-start | bytes 1179652
  1.0 8.0 %collective-permute-start = (bf16[12,32,128]{2,1,0:T(8,128)(2,1)S(1)}, bf16[12,32,128]{2,1,0:T(8,128)(2,1)S(1)}, u32[]{:S(2)}, u32[]{:S(2)}) collective-permute-start(bf16[12,32,128]{2,1,0:T(8,128)(2,1)S(1)} %slice_select_fusion.2), channel_id=1, source_target_pairs={{1,8},{2,9},{3,10},{4,11},{5,12},{6,13},{7,14},{8,1},{9,2},{10,3},... | collective-permute-start | bytes 294920 | tf_op jit(solution)/shard_map/ppermute | solution.py:38
  3.8 10.7 %copy-start.2 = (bf16[1,1,384,128,128]{4,3,2,1,0:T(8,128)(2,1)S(1)}, bf16[1,1,384,128,128]{4,3,2,1,0:T(8,128)(2,1)}, u32[]{:S(2)}) copy-start(bf16[1,1,384,128,128]{4,3,2,1,0:T(8,128)(2,1)} %param.11) | copy-start | bytes 37748740
  10.1 6.0 %collective-permute-start.1 = (bf16[24,32,128]{2,1,0:T(8,128)(2,1)S(1)}, bf16[24,32,128]{2,1,0:T(8,128)(2,1)S(1)}, u32[]{:S(2)}, u32[]{:S(2)}) collective-permute-start(bf16[24,32,128]{2,1,0:T(8,128)(2,1)S(1)} %prior_spread.4.refs_0_), channel_id=1, source_target_pairs={{0,8},{1,9},{2,10},{3,11},{4,12},{5,13},{6,14},{7,15},{8,0},{9,1},... | collective-permute-start | bytes 589832 | tf_op jit(solution)/shard_map/ppermute | solution.py:38
  17.6 7.2 %collective-permute-start.2 = (bf16[8,32,128]{2,1,0:T(8,128)(2,1)S(1)}, bf16[8,32,128]{2,1,0:T(8,128)(2,1)S(1)}, u32[]{:S(2)}, u32[]{:S(2)}) collective-permute-start(bf16[8,32,128]{2,1,0:T(8,128)(2,1)S(1)} %get-tuple-element.78), channel_id=1, source_target_pairs={{0,1},{1,0},{2,3},{3,2},{4,5},{5,4},{6,7},{7,6},{8,9},{9,8},{10,11... | collective-permute-start | bytes 196616 | tf_op jit(solution)/shard_map/ppermute | solution.py:38
  19.2 5.7 %collective-permute-start.3 = (bf16[8,32,128]{2,1,0:T(8,128)(2,1)S(1)}, bf16[8,32,128]{2,1,0:T(8,128)(2,1)S(1)}, u32[]{:S(2)}, u32[]{:S(2)}) collective-permute-start(bf16[8,32,128]{2,1,0:T(8,128)(2,1)S(1)} %get-tuple-element.79), channel_id=1, source_target_pairs={{0,2},{1,3},{2,0},{3,1},{4,6},{5,7},{6,4},{7,5},{8,10},{9,11},{10,... | collective-permute-start | bytes 196616 | tf_op jit(solution)/shard_map/ppermute | solution.py:38
  20.8 5.2 %collective-permute-start.4 = (bf16[8,32,128]{2,1,0:T(8,128)(2,1)S(1)}, bf16[8,32,128]{2,1,0:T(8,128)(2,1)S(1)}, u32[]{:S(2)}, u32[]{:S(2)}) collective-permute-start(bf16[8,32,128]{2,1,0:T(8,128)(2,1)S(1)} %get-tuple-element.80), channel_id=1, source_target_pairs={{0,3},{1,2},{2,1},{3,0},{4,7},{5,6},{6,5},{7,4},{8,11},{9,10},{10,... | collective-permute-start | bytes 196616 | tf_op jit(solution)/shard_map/ppermute | solution.py:38
  26.0 5.9 %collective-permute-start.5 = (bf16[8,32,128]{2,1,0:T(8,128)(2,1)S(1)}, bf16[8,32,128]{2,1,0:T(8,128)(2,1)S(1)}, u32[]{:S(2)}, u32[]{:S(2)}) collective-permute-start(bf16[8,32,128]{2,1,0:T(8,128)(2,1)S(1)} %convert_add_fusion), channel_id=1, source_target_pairs={{0,4},{1,5},{2,6},{3,7},{4,0},{5,1},{6,2},{7,3},{8,12},{9,13},{10,... | collective-permute-start | bytes 196616 | tf_op jit(solution)/shard_map/ppermute | solution.py:38
  31.9 5.2 %collective-permute-start.8 = (bf16[8,32,128]{2,1,0:T(8,128)(2,1)S(1)}, bf16[8,32,128]{2,1,0:T(8,128)(2,1)S(1)}, u32[]{:S(2)}, u32[]{:S(2)}) collective-permute-start(bf16[8,32,128]{2,1,0:T(8,128)(2,1)S(1)} %multiply_convert_fusion.3.refs_0_), channel_id=1, source_target_pairs={{0,3},{1,2},{2,1},{3,0},{4,7},{5,6},{6,5},{7,4},{8,11},{9,10},{10,... | collective-permute-start | bytes 196616 | tf_op jit(solution)/shard_map/ppermute | solution.py:38
  32.8 4.4 %collective-permute-start.7 = (bf16[8,32,128]{2,1,0:T(8,128)(2,1)S(1)}, bf16[8,32,128]{2,1,0:T(8,128)(2,1)S(1)}, u32[]{:S(2)}, u32[]{:S(2)}) collective-permute-start(bf16[8,32,128]{2,1,0:T(8,128)(2,1)S(1)} %multiply_convert_fusion.3.refs_0_), channel_id=1, source_target_pairs={{0,2},{1,3},{2,0},{3,1},{4,6},{5,7},{6,4},{7,5},{8,10},{9,11},{10,... | collective-permute-start | bytes 196616 | tf_op jit(solution)/shard_map/ppermute | solution.py:38
  33.3 4.6 %collective-permute-start.6 = (bf16[8,32,128]{2,1,0:T(8,128)(2,1)S(1)}, bf16[8,32,128]{2,1,0:T(8,128)(2,1)S(1)}, u32[]{:S(2)}, u32[]{:S(2)}) collective-permute-start(bf16[8,32,128]{2,1,0:T(8,128)(2,1)S(1)} %multiply_convert_fusion.3.refs_0_), channel_id=1, source_target_pairs={{0,1},{1,0},{2,3},{3,2},{4,5},{5,4},{6,7},{7,6},{8,9},{9,8},{10,11... | collective-permute-start | bytes 196616 | tf_op jit(solution)/shard_map/ppermute | solution.py:38
  39.1 1.5 collective-permute-start.9
  40.6 7.3 %collective-permute-start.10 = (bf16[24,32,128]{2,1,0:T(8,128)(2,1)S(1)}, bf16[24,32,128]{2,1,0:T(8,128)(2,1)S(1)}, u32[]{:S(2)}, u32[]{:S(2)}) collective-permute-start(bf16[24,32,128]{2,1,0:T(8,128)(2,1)S(1)} %add_convert_fusion.3.mine), channel_id=1, source_target_pairs={{0,16},{1,17},{2,18},{3,19},{4,20},{5,21},{6,22},{7,23},{8,24},{9,... | collective-permute-start | bytes 589832 | tf_op jit(solution)/shard_map/ppermute | solution.py:38
  49.6 1.5 collective-permute-start.11
  49.7 1.4 collective-permute-start.12
  52.3 8.9 %collective-permute-start.13 = (bf16[24,32,128]{2,1,0:T(8,128)(2,1)S(1)}, bf16[24,32,128]{2,1,0:T(8,128)(2,1)S(1)}, u32[]{:S(2)}, u32[]{:S(2)}) collective-permute-start(bf16[24,32,128]{2,1,0:T(8,128)(2,1)S(1)} %prior_spread.5.refs_0_), channel_id=1, source_target_pairs={{0,8},{1,9},{2,10},{3,11},{4,12},{5,13},{6,14},{7,15},{8,0},{9,1},... | collective-permute-start | bytes 589832 | tf_op jit(solution)/shard_map/ppermute | solution.py:38
  62.7 5.2 %collective-permute-start.14 = (bf16[8,32,128]{2,1,0:T(8,128)(2,1)S(1)}, bf16[8,32,128]{2,1,0:T(8,128)(2,1)S(1)}, u32[]{:S(2)}, u32[]{:S(2)}) collective-permute-start(bf16[8,32,128]{2,1,0:T(8,128)(2,1)S(1)} %get-tuple-element.95), channel_id=1, source_target_pairs={{0,1},{1,0},{2,3},{3,2},{4,5},{5,4},{6,7},{7,6},{8,9},{9,8},{10,11... | collective-permute-start | bytes 196616 | tf_op jit(solution)/shard_map/ppermute | solution.py:38
  65.2 4.9 %collective-permute-start.15 = (bf16[8,32,128]{2,1,0:T(8,128)(2,1)S(1)}, bf16[8,32,128]{2,1,0:T(8,128)(2,1)S(1)}, u32[]{:S(2)}, u32[]{:S(2)}) collective-permute-start(bf16[8,32,128]{2,1,0:T(8,128)(2,1)S(1)} %get-tuple-element.96), channel_id=1, source_target_pairs={{0,2},{1,3},{2,0},{3,1},{4,6},{5,7},{6,4},{7,5},{8,10},{9,11},{10,... | collective-permute-start | bytes 196616 | tf_op jit(solution)/shard_map/ppermute | solution.py:38
  65.2 5.4 %collective-permute-start.16 = (bf16[8,32,128]{2,1,0:T(8,128)(2,1)S(1)}, bf16[8,32,128]{2,1,0:T(8,128)(2,1)S(1)}, u32[]{:S(2)}, u32[]{:S(2)}) collective-permute-start(bf16[8,32,128]{2,1,0:T(8,128)(2,1)S(1)} %get-tuple-element.97), channel_id=1, source_target_pairs={{0,3},{1,2},{2,1},{3,0},{4,7},{5,6},{6,5},{7,4},{8,11},{9,10},{10,... | collective-permute-start | bytes 196616 | tf_op jit(solution)/shard_map/ppermute | solution.py:38
  70.6 5.4 %collective-permute-start.17 = (bf16[8,32,128]{2,1,0:T(8,128)(2,1)S(1)}, bf16[8,32,128]{2,1,0:T(8,128)(2,1)S(1)}, u32[]{:S(2)}, u32[]{:S(2)}) collective-permute-start(bf16[8,32,128]{2,1,0:T(8,128)(2,1)S(1)} %add_convert_fusion.6), channel_id=1, source_target_pairs={{0,4},{1,5},{2,6},{3,7},{4,0},{5,1},{6,2},{7,3},{8,12},{9,13},{10,... | collective-permute-start | bytes 196616 | tf_op jit(solution)/shard_map/ppermute | solution.py:38
  76.0 5.2 %collective-permute-start.20 = (bf16[8,32,128]{2,1,0:T(8,128)(2,1)S(1)}, bf16[8,32,128]{2,1,0:T(8,128)(2,1)S(1)}, u32[]{:S(2)}, u32[]{:S(2)}) collective-permute-start(bf16[8,32,128]{2,1,0:T(8,128)(2,1)S(1)} %multiply_convert_fusion.2.refs_0_), channel_id=1, source_target_pairs={{0,3},{1,2},{2,1},{3,0},{4,7},{5,6},{6,5},{7,4},{8,11},{9,10},{10,... | collective-permute-start | bytes 196616 | tf_op jit(solution)/shard_map/ppermute | solution.py:38
  77.4 5.1 %collective-permute-start.19 = (bf16[8,32,128]{2,1,0:T(8,128)(2,1)S(1)}, bf16[8,32,128]{2,1,0:T(8,128)(2,1)S(1)}, u32[]{:S(2)}, u32[]{:S(2)}) collective-permute-start(bf16[8,32,128]{2,1,0:T(8,128)(2,1)S(1)} %multiply_convert_fusion.2.refs_0_), channel_id=1, source_target_pairs={{0,2},{1,3},{2,0},{3,1},{4,6},{5,7},{6,4},{7,5},{8,10},{9,11},{10,... | collective-permute-start | bytes 196616 | tf_op jit(solution)/shard_map/ppermute | solution.py:38
  79.5 4.3 %collective-permute-start.18 = (bf16[8,32,128]{2,1,0:T(8,128)(2,1)S(1)}, bf16[8,32,128]{2,1,0:T(8,128)(2,1)S(1)}, u32[]{:S(2)}, u32[]{:S(2)}) collective-permute-start(bf16[8,32,128]{2,1,0:T(8,128)(2,1)S(1)} %multiply_convert_fusion.2.refs_0_), channel_id=1, source_target_pairs={{0,1},{1,0},{2,3},{3,2},{4,5},{5,4},{6,7},{7,6},{8,9},{9,8},{10,11... | collective-permute-start | bytes 196616 | tf_op jit(solution)/shard_map/ppermute | solution.py:38
  85.0 1.5 collective-permute-start.21
  86.6 7.0 %collective-permute-start.22 = (bf16[24,32,128]{2,1,0:T(8,128)(2,1)S(1)}, bf16[24,32,128]{2,1,0:T(8,128)(2,1)S(1)}, u32[]{:S(2)}, u32[]{:S(2)}) collective-permute-start(bf16[24,32,128]{2,1,0:T(8,128)(2,1)S(1)} %add_convert_fusion.2.mine), channel_id=1, source_target_pairs={{0,16},{1,17},{2,18},{3,19},{4,20},{5,21},{6,22},{7,23},{8,24},{9,... | collective-permute-start | bytes 589832 | tf_op jit(solution)/shard_map/ppermute | solution.py:38
  95.2 1.5 collective-permute-start.23
  95.3 1.4 collective-permute-start.24
  98.0 7.7 %collective-permute-start.25 = (bf16[24,32,128]{2,1,0:T(8,128)(2,1)S(1)}, bf16[24,32,128]{2,1,0:T(8,128)(2,1)S(1)}, u32[]{:S(2)}, u32[]{:S(2)}) collective-permute-start(bf16[24,32,128]{2,1,0:T(8,128)(2,1)S(1)} %prior_spread.6.refs_0_), channel_id=1, source_target_pairs={{0,8},{1,9},{2,10},{3,11},{4,12},{5,13},{6,14},{7,15},{8,0},{9,1},... | collective-permute-start | bytes 589832 | tf_op jit(solution)/shard_map/ppermute | solution.py:38
  107.2 4.8 %collective-permute-start.26 = (bf16[8,32,128]{2,1,0:T(8,128)(2,1)S(1)}, bf16[8,32,128]{2,1,0:T(8,128)(2,1)S(1)}, u32[]{:S(2)}, u32[]{:S(2)}) collective-permute-start(bf16[8,32,128]{2,1,0:T(8,128)(2,1)S(1)} %get-tuple-element.104), channel_id=1, source_target_pairs={{0,1},{1,0},{2,3},{3,2},{4,5},{5,4},{6,7},{7,6},{8,9},{9,8},{10,11... | collective-permute-start | bytes 196616 | tf_op jit(solution)/shard_map/ppermute | solution.py:38
  109.3 4.7 %collective-permute-start.27 = (bf16[8,32,128]{2,1,0:T(8,128)(2,1)S(1)}, bf16[8,32,128]{2,1,0:T(8,128)(2,1)S(1)}, u32[]{:S(2)}, u32[]{:S(2)}) collective-permute-start(bf16[8,32,128]{2,1,0:T(8,128)(2,1)S(1)} %get-tuple-element.105), channel_id=1, source_target_pairs={{0,2},{1,3},{2,0},{3,1},{4,6},{5,7},{6,4},{7,5},{8,10},{9,11},{10,... | collective-permute-start | bytes 196616 | tf_op jit(solution)/shard_map/ppermute | solution.py:38
  110.8 5.2 %collective-permute-start.28 = (bf16[8,32,128]{2,1,0:T(8,128)(2,1)S(1)}, bf16[8,32,128]{2,1,0:T(8,128)(2,1)S(1)}, u32[]{:S(2)}, u32[]{:S(2)}) collective-permute-start(bf16[8,32,128]{2,1,0:T(8,128)(2,1)S(1)} %get-tuple-element.106), channel_id=1, source_target_pairs={{0,3},{1,2},{2,1},{3,0},{4,7},{5,6},{6,5},{7,4},{8,11},{9,10},{10,... | collective-permute-start | bytes 196616 | tf_op jit(solution)/shard_map/ppermute | solution.py:38
  116.0 5.9 %collective-permute-start.29 = (bf16[8,32,128]{2,1,0:T(8,128)(2,1)S(1)}, bf16[8,32,128]{2,1,0:T(8,128)(2,1)S(1)}, u32[]{:S(2)}, u32[]{:S(2)}) collective-permute-start(bf16[8,32,128]{2,1,0:T(8,128)(2,1)S(1)} %add_convert_fusion.5), channel_id=1, source_target_pairs={{0,4},{1,5},{2,6},{3,7},{4,0},{5,1},{6,2},{7,3},{8,12},{9,13},{10,... | collective-permute-start | bytes 196616 | tf_op jit(solution)/shard_map/ppermute | solution.py:38
  122.0 5.2 %collective-permute-start.32 = (bf16[8,32,128]{2,1,0:T(8,128)(2,1)S(1)}, bf16[8,32,128]{2,1,0:T(8,128)(2,1)S(1)}, u32[]{:S(2)}, u32[]{:S(2)}) collective-permute-start(bf16[8,32,128]{2,1,0:T(8,128)(2,1)S(1)} %multiply_convert_fusion.1.refs_0_), channel_id=1, source_target_pairs={{0,3},{1,2},{2,1},{3,0},{4,7},{5,6},{6,5},{7,4},{8,11},{9,10},{10,... | collective-permute-start | bytes 196616 | tf_op jit(solution)/shard_map/ppermute | solution.py:38
  122.8 4.4 %collective-permute-start.31 = (bf16[8,32,128]{2,1,0:T(8,128)(2,1)S(1)}, bf16[8,32,128]{2,1,0:T(8,128)(2,1)S(1)}, u32[]{:S(2)}, u32[]{:S(2)}) collective-permute-start(bf16[8,32,128]{2,1,0:T(8,128)(2,1)S(1)} %multiply_convert_fusion.1.refs_0_), channel_id=1, source_target_pairs={{0,2},{1,3},{2,0},{3,1},{4,6},{5,7},{6,4},{7,5},{8,10},{9,11},{10,... | collective-permute-start | bytes 196616 | tf_op jit(solution)/shard_map/ppermute | solution.py:38
  124.3 4.3 %collective-permute-start.30 = (bf16[8,32,128]{2,1,0:T(8,128)(2,1)S(1)}, bf16[8,32,128]{2,1,0:T(8,128)(2,1)S(1)}, u32[]{:S(2)}, u32[]{:S(2)}) collective-permute-start(bf16[8,32,128]{2,1,0:T(8,128)(2,1)S(1)} %multiply_convert_fusion.1.refs_0_), channel_id=1, source_target_pairs={{0,1},{1,0},{2,3},{3,2},{4,5},{5,4},{6,7},{7,6},{8,9},{9,8},{10,11... | collective-permute-start | bytes 196616 | tf_op jit(solution)/shard_map/ppermute | solution.py:38
  129.8 1.5 collective-permute-start.33
  131.3 7.0 %collective-permute-start.34 = (bf16[24,32,128]{2,1,0:T(8,128)(2,1)S(1)}, bf16[24,32,128]{2,1,0:T(8,128)(2,1)S(1)}, u32[]{:S(2)}, u32[]{:S(2)}) collective-permute-start(bf16[24,32,128]{2,1,0:T(8,128)(2,1)S(1)} %add_convert_fusion.1.mine), channel_id=1, source_target_pairs={{0,16},{1,17},{2,18},{3,19},{4,20},{5,21},{6,22},{7,23},{8,24},{9,... | collective-permute-start | bytes 589832 | tf_op jit(solution)/shard_map/ppermute | solution.py:38
  140.0 1.5 collective-permute-start.35
  140.0 1.4 collective-permute-start.36
  142.7 8.4 %collective-permute-start.37 = (bf16[24,32,128]{2,1,0:T(8,128)(2,1)S(1)}, bf16[24,32,128]{2,1,0:T(8,128)(2,1)S(1)}, u32[]{:S(2)}, u32[]{:S(2)}) collective-permute-start(bf16[24,32,128]{2,1,0:T(8,128)(2,1)S(1)} %prior_spread.7.refs_0_), channel_id=1, source_target_pairs={{0,8},{1,9},{2,10},{3,11},{4,12},{5,13},{6,14},{7,15},{8,0},{9,1},... | collective-permute-start | bytes 589832 | tf_op jit(solution)/shard_map/ppermute | solution.py:38
  152.6 5.2 %collective-permute-start.38 = (bf16[8,32,128]{2,1,0:T(8,128)(2,1)S(1)}, bf16[8,32,128]{2,1,0:T(8,128)(2,1)S(1)}, u32[]{:S(2)}, u32[]{:S(2)}) collective-permute-start(bf16[8,32,128]{2,1,0:T(8,128)(2,1)S(1)} %get-tuple-element.113), channel_id=1, source_target_pairs={{0,1},{1,0},{2,3},{3,2},{4,5},{5,4},{6,7},{7,6},{8,9},{9,8},{10,11... | collective-permute-start | bytes 196616 | tf_op jit(solution)/shard_map/ppermute | solution.py:38
  155.1 4.9 %collective-permute-start.39 = (bf16[8,32,128]{2,1,0:T(8,128)(2,1)S(1)}, bf16[8,32,128]{2,1,0:T(8,128)(2,1)S(1)}, u32[]{:S(2)}, u32[]{:S(2)}) collective-permute-start(bf16[8,32,128]{2,1,0:T(8,128)(2,1)S(1)} %get-tuple-element.114), channel_id=1, source_target_pairs={{0,2},{1,3},{2,0},{3,1},{4,6},{5,7},{6,4},{7,5},{8,10},{9,11},{10,... | collective-permute-start | bytes 196616 | tf_op jit(solution)/shard_map/ppermute | solution.py:38
  155.2 5.3 %collective-permute-start.40 = (bf16[8,32,128]{2,1,0:T(8,128)(2,1)S(1)}, bf16[8,32,128]{2,1,0:T(8,128)(2,1)S(1)}, u32[]{:S(2)}, u32[]{:S(2)}) collective-permute-start(bf16[8,32,128]{2,1,0:T(8,128)(2,1)S(1)} %get-tuple-element.115), channel_id=1, source_target_pairs={{0,3},{1,2},{2,1},{3,0},{4,7},{5,6},{6,5},{7,4},{8,11},{9,10},{10,... | collective-permute-start | bytes 196616 | tf_op jit(solution)/shard_map/ppermute | solution.py:38
  160.5 5.2 %collective-permute-start.41 = (bf16[8,32,128]{2,1,0:T(8,128)(2,1)S(1)}, bf16[8,32,128]{2,1,0:T(8,128)(2,1)S(1)}, u32[]{:S(2)}, u32[]{:S(2)}) collective-permute-start(bf16[8,32,128]{2,1,0:T(8,128)(2,1)S(1)} %add_convert_fusion.4), channel_id=1, source_target_pairs={{0,4},{1,5},{2,6},{3,7},{4,0},{5,1},{6,2},{7,3},{8,12},{9,13},{10,... | collective-permute-start | bytes 196616 | tf_op jit(solution)/shard_map/ppermute | solution.py:38
  165.8 5.3 %collective-permute-start.44 = (bf16[8,32,128]{2,1,0:T(8,128)(2,1)S(1)}, bf16[8,32,128]{2,1,0:T(8,128)(2,1)S(1)}, u32[]{:S(2)}, u32[]{:S(2)}) collective-permute-start(bf16[8,32,128]{2,1,0:T(8,128)(2,1)S(1)} %multiply_convert_fusion.refs_0_), channel_id=1, source_target_pairs={{0,3},{1,2},{2,1},{3,0},{4,7},{5,6},{6,5},{7,4},{8,11},{9,10},{10,... | collective-permute-start | bytes 196616 | tf_op jit(solution)/shard_map/ppermute | solution.py:38
  167.3 5.1 %collective-permute-start.43 = (bf16[8,32,128]{2,1,0:T(8,128)(2,1)S(1)}, bf16[8,32,128]{2,1,0:T(8,128)(2,1)S(1)}, u32[]{:S(2)}, u32[]{:S(2)}) collective-permute-start(bf16[8,32,128]{2,1,0:T(8,128)(2,1)S(1)} %multiply_convert_fusion.refs_0_), channel_id=1, source_target_pairs={{0,2},{1,3},{2,0},{3,1},{4,6},{5,7},{6,4},{7,5},{8,10},{9,11},{10,... | collective-permute-start | bytes 196616 | tf_op jit(solution)/shard_map/ppermute | solution.py:38
  169.4 4.3 %collective-permute-start.42 = (bf16[8,32,128]{2,1,0:T(8,128)(2,1)S(1)}, bf16[8,32,128]{2,1,0:T(8,128)(2,1)S(1)}, u32[]{:S(2)}, u32[]{:S(2)}) collective-permute-start(bf16[8,32,128]{2,1,0:T(8,128)(2,1)S(1)} %multiply_convert_fusion.refs_0_), channel_id=1, source_target_pairs={{0,1},{1,0},{2,3},{3,2},{4,5},{5,4},{6,7},{7,6},{8,9},{9,8},{10,11... | collective-permute-start | bytes 196616 | tf_op jit(solution)/shard_map/ppermute | solution.py:38
  173.7 20.1 %copy-start.1 = (f32[32,128]{1,0:T(8,128)S(1)}, f32[32,128]{1,0:T(8,128)}, u32[]{:S(2)}) copy-start(f32[32,128]{1,0:T(8,128)} %param.15) | copy-start | bytes 49156
  174.9 1.5 collective-permute-start.45
  176.5 7.0 %collective-permute-start.46 = (bf16[24,32,128]{2,1,0:T(8,128)(2,1)S(1)}, bf16[24,32,128]{2,1,0:T(8,128)(2,1)S(1)}, u32[]{:S(2)}, u32[]{:S(2)}) collective-permute-start(bf16[24,32,128]{2,1,0:T(8,128)(2,1)S(1)} %add_convert_fusion.mine), channel_id=1, source_target_pairs={{0,16},{1,17},{2,18},{3,19},{4,20},{5,21},{6,22},{7,23},{8,24},{9,... | collective-permute-start | bytes 589832 | tf_op jit(solution)/shard_map/ppermute | solution.py:38
  185.2 1.4 collective-permute-start.48
  185.2 1.3 collective-permute-start.47
  186.6 6.3 %collective-permute-start.49 = (bf16[24,32,128]{2,1,0:T(8,128)(2,1)S(1)}, bf16[24,32,128]{2,1,0:T(8,128)(2,1)S(1)}, u32[]{:S(2)}, u32[]{:S(2)}) collective-permute-start(bf16[24,32,128]{2,1,0:T(8,128)(2,1)S(1)} %fusion), channel_id=1, source_target_pairs={{0,8},{1,9},{2,10},{3,11},{4,12},{5,13},{6,14},{7,15},{8,0},{9,1},... | collective-permute-start | bytes 589832 | tf_op jit(solution)/shard_map/ppermute | solution.py:38

commit v10 on v9

--- a/solution.py
+++ b/solution.py
@@ -13,9 +13,8 @@
 HALF = jnp.bfloat16
 VMEM_LIMIT = 8 * 2**20
 LANES = 128
-FORWARD_PLAN = (2, 56)
-NEAR_PLAN = (2, 32)
-REST_PLAN = (2, 42)
+FORWARD_PLANS = ((2, 42), (2, 42), (2, 28))
+ADJOINT_PLANS = ((2, 32), (2, 32), (2, 32), (2, 18), (2, 18))
 PRIOR_PLAN = (2, 56)
 
 
@@ -90,8 +89,8 @@
     rows, chunk, where, obs, flux, nbr, prior,
     prior_plain, *refs
 ):
-    plans, (obs_in, flux_in, nbr_in) = refs[:7], refs[7:10]
-    built, (small_sems, sems) = refs[10:17], refs[17:]
+    (obs_row, tile_row, ext_row), plans, refs = refs[:3], refs[3:7], refs[7:]
+    (obs_in, flux_in, nbr_in), built, (small_sems, sems) = refs[:3], refs[3:7], refs[7:]
     side, corner, count, first_tile = where[0], where[1], where[2], where[3]
     owned = prior_plain.shape[0]
     begin = side * owned
@@ -135,23 +134,20 @@
     obs_at = (block ^ corner) * quarter + obs_in[...] - block * quarter
     block = (flux_in[...] >= half).astype(i32)
     tile_at = (block ^ side) * half + flux_in[...] - block * half
+    obs_at, tile_at = jnp.where(live, obs_at, 2 * most), jnp.where(live, tile_at, 2 * most)
+    obs_row[...], tile_row[...] = obs_at, tile_at
     own, near = tile_at < half, obs_at < quarter
-    for plan, src, dst, use, out in (
-        (FORWARD_PLAN, tile_at, obs_at, own, built[0]),
-        (FORWARD_PLAN, tile_at - half, obs_at, ~own, built[1]),
-        (NEAR_PLAN, obs_at, tile_at, near, built[2]),
-        (REST_PLAN, obs_at - quarter, tile_at - half, ~near & ~own, built[3]),
-        (REST_PLAN, obs_at - quarter, tile_at, ~near & own, built[4]),
-    ):
-        use = live & use
+    uses = (
+        (tile_at, obs_at - quarter, live & own & ~near),
+        (tile_at - half, obs_at - quarter, live & ~own & ~near),
+        (tile_at, obs_at, near),
+    )
+    for plan, (src, dst, use), out in zip(FORWARD_PLANS, uses, built):
         plan_groups(plan, jnp.where(use, src, 0), jnp.where(use, dst, most), 0, most, out)
-    at = lax.broadcasted_iota(i32, nbr_in.shape, 1)
-    tile = sum((at >= k * fan).astype(i32) for k in range(1, tile_rows)) - side * half
-    owns = (tile >= 0) & (tile < half)
     ext = nbr_in[...] - first_tile + reach
-    plan_groups(PRIOR_PLAN, jnp.where(owns, tile, 0), jnp.where(owns, ext, most), begin, most, built[5])
-    built[6][:, : ext.shape[1]] = ext
-    built[6][:, ext.shape[1] :] = jnp.zeros((1, LANES), i32) + side
+    ext_row[...] = ext
+    built[3][:, : ext.shape[1]] = ext
+    built[3][:, ext.shape[1] :] = jnp.zeros((1, LANES), i32) + side
     lists = [
         pltpu.make_async_copy(src, dst, small_sems.at[3 + k])
         for k, (src, dst) in enumerate(zip(built, plans))
@@ -186,35 +182,82 @@
     )(plain)
 
 
+def plan_lengths(plans, width, most):
+    sizes = (plan_sizes(plan, width, most) for plan in plans)
+    return [2 * slots + groups for slots, groups in sizes]
+
+
 def setup(where, obs, flux, nbr, prior, rows):
-    most = max(rows[:2])
     owned = rows[1] // 2 * rows[2]
     chunk = chunk_of(owned, 24)
     smem = pl.BlockSpec(memory_space=pltpu.SMEM)
     vmem = pl.BlockSpec(memory_space=pltpu.VMEM)
     hbm = pl.BlockSpec(memory_space=pl.ANY)
-    own = pltpu.VMEM((owned,) + prior.shape[1:], HALF)
     i32 = jnp.int32
-    lengths = []
-    used = (FORWARD_PLAN, FORWARD_PLAN, NEAR_PLAN, REST_PLAN, REST_PLAN, PRIOR_PLAN)
-    for plan in used:
-        slots, groups = plan_sizes(plan, (nbr if plan is used[-1] else obs).shape[1], most)
-        lengths.append(2 * slots + groups)
-    lengths.append(nbr.shape[1] + LANES)
+    lengths = plan_lengths(FORWARD_PLANS, obs.shape[1], max(rows[:2])) + [nbr.shape[1] + LANES]
     return pl.pallas_call(
         functools.partial(setup_kernel, rows, chunk),
         in_specs=[smem] + [hbm] * 4,
-        out_specs=[vmem] + [smem] * 7,
-        out_shape=[own] + [pltpu.SMEM((1, n), i32) for n in lengths],
+        out_specs=[vmem] * 4 + [smem] * 4,
+        out_shape=[pltpu.VMEM((owned,) + prior.shape[1:], HALF)]
+        + [pltpu.VMEM(v.shape, i32) for v in (obs, flux, nbr)]
+        + [pltpu.SMEM((1, n), i32) for n in lengths],
         scratch_shapes=[pltpu.VMEM(v.shape, i32) for v in (obs, flux, nbr)]
         + [pltpu.VMEM((1, n), i32) for n in lengths]
         + [
-            pltpu.SemaphoreType.DMA((10,)),
+            pltpu.SemaphoreType.DMA((7,)),
             pltpu.SemaphoreType.DMA((owned // chunk,)),
         ],
         compiler_params=pltpu.CompilerParams(vmem_limit_bytes=VMEM_LIMIT),
         name="setup",
     )(where, *(pltpu.with_memory_space_constraint(v, pltpu.HBM) for v in (obs, flux, nbr, prior)))
+
+
+def late_kernel(rows, nbr, obs_row, tile_row, ext_row, *refs):
+    plans, built, sems = refs[:6], refs[6:12], refs[12]
+    obs_rows, tile_rows, fan = rows
+    half, quarter, most = tile_rows // 2, obs_rows // 4, max(obs_rows, tile_rows)
+    side = nbr[0, nbr.shape[1] - 1]
+    obs_at, tile_at, ext = obs_row[...], tile_row[...], ext_row[...]
+    part = [(obs_at >= k * quarter) & (obs_at < (k + 1) * quarter) for k in range(4)]
+    uses = (
+        (obs_at, tile_at, part[0]),
+        (obs_at - 3 * quarter, tile_at, part[3]),
+        (obs_at - 2 * quarter, tile_at, part[2]),
+        (obs_at - quarter, tile_at - half, part[1] & (tile_at >= half)),
+        (obs_at - quarter, tile_at, part[1] & (tile_at < half)),
+    )
+    for plan, (src, dst, use), out in zip(ADJOINT_PLANS, uses, built):
+        plan_groups(plan, jnp.where(use, src, 0), jnp.where(use, dst, most), 0, most, out)
+    at = lax.broadcasted_iota(jnp.int32, ext.shape, 1)
+    tile = sum((at >= k * fan).astype(jnp.int32) for k in range(1, tile_rows)) - side * half
+    owns = (tile >= 0) & (tile < half)
+    src, dst = jnp.where(owns, tile, 0), jnp.where(owns, ext, most)
+    plan_groups(PRIOR_PLAN, src, dst, side * (half * fan), most, built[5])
+    lists = [pltpu.make_async_copy(a, b, sems.at[k]) for k, (a, b) in enumerate(zip(built, plans))]
+    for one in lists:
+        one.start()
+    for one in lists:
+        one.wait()
+
+
+def late_plans(nbr, obs_row, tile_row, ext_row, rows):
+    smem = pl.BlockSpec(memory_space=pltpu.SMEM)
+    vmem = pl.BlockSpec(memory_space=pltpu.VMEM)
+    most = max(rows[:2])
+    lengths = plan_lengths(ADJOINT_PLANS, obs_row.shape[1], most)
+    lengths += plan_lengths((PRIOR_PLAN,), ext_row.shape[1], most)
+    return pl.pallas_call(
+        functools.partial(late_kernel, rows),
+        in_specs=[smem] + [vmem] * 3,
+        out_specs=[smem] * 6,
+        out_shape=[pltpu.SMEM((1, n), jnp.int32) for n in lengths],
+        scratch_shapes=[pltpu.VMEM((1, n), jnp.int32) for n in lengths]
+        + [pltpu.SemaphoreType.DMA((6,))],
+        compiler_params=pltpu.CompilerParams(vmem_limit_bytes=VMEM_LIMIT),
+        cost_estimate=pl.CostEstimate(flops=0, bytes_accessed=2**23, transcendentals=0),
+        name="late_plans",
+    )(nbr, obs_row, tile_row, ext_row)
 
 
 def grouped_products(plan, sizes, lists, x, blocks, total):
@@ -392,42 +435,62 @@
 
     where, own_rinv, nbr, prior, blocks = lax.optimization_barrier((where, own_rinv, nbr, prior, blocks))
     jac_plain = blocks
-    prior_plain, *jac_lists, prior_lists, nbr = setup(
+    prior_plain, *index_rows, own_lists, other_lists, near_lists, nbr = setup(
         where, jac_obs[0], jac_flux[0], nbr, prior, sizes
     )
     fields = (probes, beyond)
     for step in range(STEPS):
         spread = spread_tiles(nbr, fields, prior_plain)
         other = swap_core(spread)
+        far_rows = obs_rows - quarter
         (begun,) = jac_pass(
-            FORWARD_PLAN, jac_lists[0], (spread,), None, jac_plain, rows, obs_rows, [F32], "forward_own"
+            FORWARD_PLANS[0], own_lists, (spread,), None, jac_plain, rows, far_rows, [F32], "forward_own"
         )
-        types = [F32, HALF, HALF, HALF]
         pieces = jac_pass(
-            FORWARD_PLAN, jac_lists[1], (other,), begun, jac_plain, rows, obs_rows, types, "forward_other"
+            FORWARD_PLANS[1], other_lists, (other,), begun, jac_plain, rows, far_rows, [HALF] * 3, "forward_other"
+        )
+        (total,) = jac_pass(
+            FORWARD_PLANS[2], near_lists, (spread, other), None, jac_plain, rows, quarter, [F32], "forward_near"
         )
         if step == 0:
             pieces, jac_plain = lax.optimization_barrier((pieces, jac_plain))
             jac_turned = turn_blocks(jac_plain, "jac_turn")
-        total = pieces[0]
         for bits in range(1, 4):
-            total = total + swap_flux(pieces[bits], bits).astype(F32)
+            total = total + swap_flux(pieces[bits - 1], bits).astype(F32)
         if step == 0:
-            total, jac_turned = lax.optimization_barrier((total, jac_turned))
+            total, jac_turned, index_rows = lax.optimization_barrier((total, jac_turned, index_rows))
+            adjoint_lists = late_plans(nbr, *index_rows, sizes)
         bits = 4
         while bits < n_flux:
             sent = total.astype(HALF)
             total = sent.astype(F32) + swap_flux(sent, bits).astype(F32)
             bits *= 2
+        if step == 0:
+            total, adjoint_lists = lax.optimization_barrier((total, adjoint_lists))
+            prior_lists = adjoint_lists[5]
         weighted = (total * own_rinv).astype(HALF)
-        rest = tuple(swap_flux(weighted, bits) for bits in range(1, 4))
-        mine, theirs = jac_pass(
-            NEAR_PLAN, jac_lists[2], (weighted,), None, jac_turned, rows, tile_count, [F32, F32], "adjoint_near"
+        quarters = [weighted] + [swap_flux(weighted, bits) for bits in range(1, 4)]
+        begun = None
+        for part, at in enumerate((0, 3, 2)):
+            types = [F32] * (2 if part == 2 else 1)
+            begun = jac_pass(
+                ADJOINT_PLANS[part],
+                adjoint_lists[part],
+                (quarters[at],),
+                None if part == 0 else begun[0],
+                jac_turned,
+                rows,
+                tile_count,
+                types,
+                f"adjoint_quarter{at}",
+            )
+        mine, theirs = begun
+        (theirs,) = jac_pass(
+            ADJOINT_PLANS[3], adjoint_lists[3], (quarters[1],), theirs, jac_turned, rows, half, [HALF], "adjoint_other"
         )
-        (theirs,) = jac_pass(
-            REST_PLAN, jac_lists[3], rest, theirs, jac_turned, rows, half, [HALF], "adjoint_other"
+        (mine,) = jac_pass(
+            ADJOINT_PLANS[4], adjoint_lists[4], (quarters[1],), mine, jac_turned, rows, half, [F32], "adjoint_own"
         )
-        (mine,) = jac_pass(REST_PLAN, jac_lists[4], rest, mine, jac_turned, rows, half, [F32], "adjoint_own")
         mine = (mine + swap_core(theirs).astype(F32)).astype(HALF)
         if step == 0:
             mine, prior_plain = lax.optimization_barrier((mine, prior_plain))

time: 194 us -> 192 us (0.990)
  waiting for transfers between devices: 69.7 us -> 52 us
  Pallas kernels: 48.4 us -> 56 us
  starting transfers between devices: 70.5 us -> 78.1 us
    ppermute x50, waiting for transfers between devices: 69.7 us -> 52 us  [exchange(): return lax.ppermute(value, ('obs', 'flux'), route)]
    ppermute x50, starting transfers between devices: 70.5 us -> 78.1 us  [exchange(): return lax.ppermute(value, ('obs', 'flux'), route)]
    pallas_call x20 -> x32, Pallas kernels: 26.4 us -> 31.8 us  [jac_pass(): pl.pallas_call(functools.partial(jac_kernel, plan, sizes, len(parts), beg...]
    pallas_call x0 -> x1, Pallas kernels: none -> 3.39 us  [late_plans(): pl.pallas_call(functools.partial(late_kernel, rows), in_specs=[smem] + [v...]
  transfers between devices with their start and end apart: 50 -> 50, of which waited for: 37 -> 37; matrix products, arithmetic and copies ran while one was open for 1% -> 1% of each run, Pallas kernels for 13% -> 19%
where the time goes in v10:
time: 192 us; the launch traced here: 191 us
  starting transfers between devices  78.1 us (41%)
  Pallas kernels  56 us (29%)
  waiting for transfers between devices  52 us (27%)
  other arithmetic  2.46 us (1%)
    ppermute x50, starting transfers between devices, exchange(): return lax.ppermute(value, ('obs', 'flux'), route)  78.1 us
    ppermute x50, waiting for transfers between devices, exchange(): return lax.ppermute(value, ('obs', 'flux'), route)  52 us
    pallas_call x32, Pallas kernels, jac_pass(): pl.pallas_call(functools.partial(jac_kernel, plan, sizes, len(parts), beg...  31.8 us
    pallas_call x4, Pallas kernels, gather_tiles(): pl.pallas_call(functools.partial(gather_kernel, rows, plan_sizes(PRIOR_PL...  6.69 us
    pallas_call x2, Pallas kernels, turn_blocks(): pl.pallas_call(functools.partial(turn_kernel, chunk_of(plain.shape[0], 48...  5.5 us
    pallas_call x4, Pallas kernels, spread_tiles(): pl.pallas_call(functools.partial(spread_kernel, len(fields) == 2, prior.s...  4.83 us
  transfers between devices with their start and end apart: 50, of which 37 were waited for; matrix products, arithmetic and copies ran while one was open for 1% of the time, Pallas kernels for 19%

profile of v10, /device:TPU:0, one launch (start us, length us, event | category | flops | bytes accessed | tf_op | source)
XLA Modules:
  0.0 191.3 jit_solution(1416548440296447885)
XLA Ops:
  3.9 3.8 %setup.1 = (bf16[192,128,128]{2,1,0:T(8,128)(2,1)S(1)}, s32[1,384]{1,0:T(1,128)S(1)}, s32[1,384]{1,0:T(1,128)S(1)}, s32[1,384]{1,0:T(1,128)S(1)}, s32[1,1280]{1,...) custom-call(s32[4]{0:T(128)S(1)} %pad_add_fusion.where, s32[1,384]{1,0:T(1,128)} %bitcast.30, ...), custom_call_target="tpu_custom_call" | custom-call | tf_op jit(solution)/shard_map/setup/pallas_call | solution.py:198
  7.7 1.1 prior_spread.4.refs_0_
  8.8 4.4 %collective-permute-start.1 = (bf16[24,32,128]{2,1,0:T(8,128)(2,1)S(1)}, bf16[24,32,128]{2,1,0:T(8,128)(2,1)S(1)}, u32[]{:S(2)}, u32[]{:S(2)}) collective-permute-start(bf16[24,32,128]{2,1,0:T(8,128)(2,1)S(1)} %prior_spread.4.refs_0_), channel_id=1, source_target_pairs={{0,8},{1,9},{2,10},{3,11},{4,12},{5,13},{6,14},{7,15},{8,0},{9,1},... | collective-permute-start | bytes 589832 | tf_op jit(solution)/shard_map/ppermute | solution.py:37
  13.2 1.3 forward_own.4.refs_1_
  14.4 1.2 forward_other.4
  16.5 2.4 %collective-permute-start.3 = (bf16[8,32,128]{2,1,0:T(8,128)(2,1)S(1)}, bf16[8,32,128]{2,1,0:T(8,128)(2,1)S(1)}, u32[]{:S(2)}, u32[]{:S(2)}) collective-permute-start(bf16[8,32,128]{2,1,0:T(8,128)(2,1)S(1)} %get-tuple-element.87), channel_id=1, source_target_pairs={{0,2},{1,3},{2,0},{3,1},{4,6},{5,7},{6,4},{7,5},{8,10},{9,11},{10,... | collective-permute-start | bytes 196616 | tf_op jit(solution)/shard_map/ppermute | solution.py:37
  19.2 3.7 %jac_turn.1.refs_1_.refs_2_ = bf16[384,128,128]{2,1,0:T(8,128)(2,1)S(1)} custom-call(bf16[384,128,128]{2,1,0:T(8,128)(2,1)S(1)} %bitcast.14), custom_call_target="tpu_custom_call" | custom-call | bytes 12582912 | tf_op jit(solution)/shard_map/jac_turn/pallas_call | solution.py:174
  24.7 2.6 %collective-permute-start.5 = (bf16[8,32,128]{2,1,0:T(8,128)(2,1)S(1)}, bf16[8,32,128]{2,1,0:T(8,128)(2,1)S(1)}, u32[]{:S(2)}, u32[]{:S(2)}) collective-permute-start(bf16[8,32,128]{2,1,0:T(8,128)(2,1)S(1)} %convert_add_fusion.1), channel_id=1, source_target_pairs={{0,4},{1,5},{2,6},{3,7},{4,0},{5,1},{6,2},{7,3},{8,12},{9,13},{10,... | collective-permute-start | bytes 196616 | tf_op jit(solution)/shard_map/ppermute | solution.py:37
  27.3 3.4 %late_plans.1 = (s32[1,1408]{1,0:T(1,128)S(4)}, s32[1,1408]{1,0:T(1,128)S(4)}, s32[1,1408]{1,0:T(1,128)S(4)}, s32[1,1280]{1,0:T(1,128)S(4)}, s32[1,1280]{1,0:T(1,128)S(4)}, /*index=5*/s32[1,1664]{1,0:T(1,128)S(4)}) custom-call(s32[1,512]{1,0:T(1,128)S(4)} %get-tuple-element.77.nbr, s32[1,384]{1,0:T(1,128)S(1)} %get-tuple-element.94.obs_row, ...), custom_call_target="tpu_custom_call" | custom-call | bytes 8388608 | tf_op jit(solution)/shard_map/late_plans/pallas_call | solution.py:250
  32.8 2.0 %collective-permute-start.6 = (bf16[8,32,128]{2,1,0:T(8,128)(2,1)S(1)}, bf16[8,32,128]{2,1,0:T(8,128)(2,1)S(1)}, u32[]{:S(2)}, u32[]{:S(2)}) collective-permute-start(bf16[8,32,128]{2,1,0:T(8,128)(2,1)S(1)} %multiply_convert_fusion.3.refs_0_), channel_id=1, source_target_pairs={{0,1},{1,0},{2,3},{3,2},{4,5},{5,4},{6,7},{7,6},{8,9},{9,8},{10,11... | collective-permute-start | bytes 196616 | tf_op jit(solution)/shard_map/ppermute | solution.py:37
  41.1 1.5 collective-permute-start.10
  42.5 1.8 prior_turn.1.prior
  44.4 3.7 %collective-permute-done.10.other = bf16[24,32,128]{2,1,0:T(8,128)(2,1)S(1)} collective-permute-done((bf16[24,32,128]{2,1,0:T(8,128)(2,1)S(1)}, bf16[24,32,128]{2,1,0:T(8,128)(2,1)S(1)}, u32[]{:S(2)}, u32[]{:S(2)}) %collective-permute-start.10) | collective-permute-done | bytes 196640 | tf_op jit(solution)/shard_map/ppermute | solution.py:37
  48.1 1.8 prior_adjoint.4
  51.4 1.2 prior_spread.5.refs_0_
  52.6 6.1 %collective-permute-start.13 = (bf16[24,32,128]{2,1,0:T(8,128)(2,1)S(1)}, bf16[24,32,128]{2,1,0:T(8,128)(2,1)S(1)}, u32[]{:S(2)}, u32[]{:S(2)}) collective-permute-start(bf16[24,32,128]{2,1,0:T(8,128)(2,1)S(1)} %prior_spread.5.refs_0_), channel_id=1, source_target_pairs={{0,8},{1,9},{2,10},{3,11},{4,12},{5,13},{6,14},{7,15},{8,0},{9,1},... | collective-permute-start | bytes 589832 | tf_op jit(solution)/shard_map/ppermute | solution.py:37
  58.8 1.3 forward_own.5.refs_1_
  60.0 1.2 forward_other.5
  61.3 1.6 collective-permute-start.14
  62.9 2.1 %collective-permute-start.15 = (bf16[8,32,128]{2,1,0:T(8,128)(2,1)S(1)}, bf16[8,32,128]{2,1,0:T(8,128)(2,1)S(1)}, u32[]{:S(2)}, u32[]{:S(2)}) collective-permute-start(bf16[8,32,128]{2,1,0:T(8,128)(2,1)S(1)} %get-tuple-element.120), channel_id=1, source_target_pairs={{0,2},{1,3},{2,0},{3,1},{4,6},{5,7},{6,4},{7,5},{8,10},{9,11},{10,... | collective-permute-start | bytes 196616 | tf_op jit(solution)/shard_map/ppermute | solution.py:37
  66.1 1.7 collective-permute-done.15
  67.8 2.4 %collective-permute-done.16 = bf16[8,32,128]{2,1,0:T(8,128)(2,1)S(1)} collective-permute-done((bf16[8,32,128]{2,1,0:T(8,128)(2,1)S(1)}, bf16[8,32,128]{2,1,0:T(8,128)(2,1)S(1)}, u32[]{:S(2)}, u32[]{:S(2)}) %collective-permute-start.16) | collective-permute-done | bytes 65568 | tf_op jit(solution)/shard_map/ppermute | solution.py:37
  70.2 2.7 %collective-permute-start.17 = (bf16[8,32,128]{2,1,0:T(8,128)(2,1)S(1)}, bf16[8,32,128]{2,1,0:T(8,128)(2,1)S(1)}, u32[]{:S(2)}, u32[]{:S(2)}) collective-permute-start(bf16[8,32,128]{2,1,0:T(8,128)(2,1)S(1)} %add_convert_fusion.6), channel_id=1, source_target_pairs={{0,4},{1,5},{2,6},{3,7},{4,0},{5,1},{6,2},{7,3},{8,12},{9,13},{10,... | collective-permute-start | bytes 196616 | tf_op jit(solution)/shard_map/ppermute | solution.py:37
  72.9 2.6 %collective-permute-done.17 = bf16[8,32,128]{2,1,0:T(8,128)(2,1)S(1)} collective-permute-done((bf16[8,32,128]{2,1,0:T(8,128)(2,1)S(1)}, bf16[8,32,128]{2,1,0:T(8,128)(2,1)S(1)}, u32[]{:S(2)}, u32[]{:S(2)}) %collective-permute-start.17) | collective-permute-done | bytes 65568 | tf_op jit(solution)/shard_map/ppermute | solution.py:37
  75.5 1.3 collective-permute-start.20
  76.8 2.1 %collective-permute-start.19 = (bf16[8,32,128]{2,1,0:T(8,128)(2,1)S(1)}, bf16[8,32,128]{2,1,0:T(8,128)(2,1)S(1)}, u32[]{:S(2)}, u32[]{:S(2)}) collective-permute-start(bf16[8,32,128]{2,1,0:T(8,128)(2,1)S(1)} %multiply_convert_fusion.2.refs_0_), channel_id=1, source_target_pairs={{0,2},{1,3},{2,0},{3,1},{4,6},{5,7},{6,4},{7,5},{8,10},{9,11},{10,... | collective-permute-start | bytes 196616 | tf_op jit(solution)/shard_map/ppermute | solution.py:37
  80.7 1.0 adjoint_quarter3.5.refs_1_
  85.5 2.0 %collective-permute-start.22 = (bf16[24,32,128]{2,1,0:T(8,128)(2,1)S(1)}, bf16[24,32,128]{2,1,0:T(8,128)(2,1)S(1)}, u32[]{:S(2)}, u32[]{:S(2)}) collective-permute-start(bf16[24,32,128]{2,1,0:T(8,128)(2,1)S(1)} %add_convert_fusion.2.mine), channel_id=1, source_target_pairs={{0,16},{1,17},{2,18},{3,19},{4,20},{5,21},{6,22},{7,23},{8,24},{9,... | collective-permute-start | bytes 589832 | tf_op jit(solution)/shard_map/ppermute | solution.py:37
  87.5 5.2 %collective-permute-done.22.other = bf16[24,32,128]{2,1,0:T(8,128)(2,1)S(1)} collective-permute-done((bf16[24,32,128]{2,1,0:T(8,128)(2,1)S(1)}, bf16[24,32,128]{2,1,0:T(8,128)(2,1)S(1)}, u32[]{:S(2)}, u32[]{:S(2)}) %collective-permute-start.22) | collective-permute-done | bytes 196640 | tf_op jit(solution)/shard_map/ppermute | solution.py:37
  92.7 1.6 prior_adjoint.5
  95.8 1.2 prior_spread.6.refs_0_
  97.1 6.1 %collective-permute-start.25 = (bf16[24,32,128]{2,1,0:T(8,128)(2,1)S(1)}, bf16[24,32,128]{2,1,0:T(8,128)(2,1)S(1)}, u32[]{:S(2)}, u32[]{:S(2)}) collective-permute-start(bf16[24,32,128]{2,1,0:T(8,128)(2,1)S(1)} %prior_spread.6.refs_0_), channel_id=1, source_target_pairs={{0,8},{1,9},{2,10},{3,11},{4,12},{5,13},{6,14},{7,15},{8,0},{9,1},... | collective-permute-start | bytes 589832 | tf_op jit(solution)/shard_map/ppermute | solution.py:37
  103.2 1.3 forward_own.6.refs_1_
  104.5 1.2 forward_other.6
  105.7 1.6 collective-permute-start.26
  107.3 1.7 collective-permute-start.27
  110.5 1.8 collective-permute-done.27
  112.3 1.9 %collective-permute-done.28 = bf16[8,32,128]{2,1,0:T(8,128)(2,1)S(1)} collective-permute-done((bf16[8,32,128]{2,1,0:T(8,128)(2,1)S(1)}, bf16[8,32,128]{2,1,0:T(8,128)(2,1)S(1)}, u32[]{:S(2)}, u32[]{:S(2)}) %collective-permute-start.28) | collective-permute-done | bytes 65568 | tf_op jit(solution)/shard_map/ppermute | solution.py:37
  114.2 3.6 %collective-permute-start.29 = (bf16[8,32,128]{2,1,0:T(8,128)(2,1)S(1)}, bf16[8,32,128]{2,1,0:T(8,128)(2,1)S(1)}, u32[]{:S(2)}, u32[]{:S(2)}) collective-permute-start(bf16[8,32,128]{2,1,0:T(8,128)(2,1)S(1)} %add_convert_fusion.5), channel_id=1, source_target_pairs={{0,4},{1,5},{2,6},{3,7},{4,0},{5,1},{6,2},{7,3},{8,12},{9,13},{10,... | collective-permute-start | bytes 196616 | tf_op jit(solution)/shard_map/ppermute | solution.py:37
  117.8 2.4 %collective-permute-done.29 = bf16[8,32,128]{2,1,0:T(8,128)(2,1)S(1)} collective-permute-done((bf16[8,32,128]{2,1,0:T(8,128)(2,1)S(1)}, bf16[8,32,128]{2,1,0:T(8,128)(2,1)S(1)}, u32[]{:S(2)}, u32[]{:S(2)}) %collective-permute-start.29) | collective-permute-done | bytes 65568 | tf_op jit(solution)/shard_map/ppermute | solution.py:37
  120.3 1.4 collective-permute-start.32
  121.7 2.1 %collective-permute-start.31 = (bf16[8,32,128]{2,1,0:T(8,128)(2,1)S(1)}, bf16[8,32,128]{2,1,0:T(8,128)(2,1)S(1)}, u32[]{:S(2)}, u32[]{:S(2)}) collective-permute-start(bf16[8,32,128]{2,1,0:T(8,128)(2,1)S(1)} %multiply_convert_fusion.1.refs_0_), channel_id=1, source_target_pairs={{0,2},{1,3},{2,0},{3,1},{4,6},{5,7},{6,4},{7,5},{8,10},{9,11},{10,... | collective-permute-start | bytes 196616 | tf_op jit(solution)/shard_map/ppermute | solution.py:37
  126.8 1.2 adjoint_quarter2.6
  130.4 1.7 collective-permute-start.34
  132.0 5.3 %collective-permute-done.34.other = bf16[24,32,128]{2,1,0:T(8,128)(2,1)S(1)} collective-permute-done((bf16[24,32,128]{2,1,0:T(8,128)(2,1)S(1)}, bf16[24,32,128]{2,1,0:T(8,128)(2,1)S(1)}, u32[]{:S(2)}, u32[]{:S(2)}) %collective-permute-start.34) | collective-permute-done | bytes 196640 | tf_op jit(solution)/shard_map/ppermute | solution.py:37
  137.4 1.6 prior_adjoint.6
  140.5 1.2 prior_spread.7.refs_0_
  141.8 6.1 %collective-permute-start.37 = (bf16[24,32,128]{2,1,0:T(8,128)(2,1)S(1)}, bf16[24,32,128]{2,1,0:T(8,128)(2,1)S(1)}, u32[]{:S(2)}, u32[]{:S(2)}) collective-permute-start(bf16[24,32,128]{2,1,0:T(8,128)(2,1)S(1)} %prior_spread.7.refs_0_), channel_id=1, source_target_pairs={{0,8},{1,9},{2,10},{3,11},{4,12},{5,13},{6,14},{7,15},{8,0},{9,1},... | collective-permute-start | bytes 589832 | tf_op jit(solution)/shard_map/ppermute | solution.py:37
  147.9 1.3 forward_own.7.refs_1_
  149.1 1.2 forward_other.7
  150.4 1.8 collective-permute-start.38
  152.2 1.8 collective-permute-start.39
  155.4 1.5 collective-permute-done.39
  156.9 2.2 %collective-permute-done.40 = bf16[8,32,128]{2,1,0:T(8,128)(2,1)S(1)} collective-permute-done((bf16[8,32,128]{2,1,0:T(8,128)(2,1)S(1)}, bf16[8,32,128]{2,1,0:T(8,128)(2,1)S(1)}, u32[]{:S(2)}, u32[]{:S(2)}) %collective-permute-start.40) | collective-permute-done | bytes 65568 | tf_op jit(solution)/shard_map/ppermute | solution.py:37
  159.1 3.7 %collective-permute-start.41 = (bf16[8,32,128]{2,1,0:T(8,128)(2,1)S(1)}, bf16[8,32,128]{2,1,0:T(8,128)(2,1)S(1)}, u32[]{:S(2)}, u32[]{:S(2)}) collective-permute-start(bf16[8,32,128]{2,1,0:T(8,128)(2,1)S(1)} %add_convert_fusion.4), channel_id=1, source_target_pairs={{0,4},{1,5},{2,6},{3,7},{4,0},{5,1},{6,2},{7,3},{8,12},{9,13},{10,... | collective-permute-start | bytes 196616 | tf_op jit(solution)/shard_map/ppermute | solution.py:37
  162.8 2.2 %collective-permute-done.41 = bf16[8,32,128]{2,1,0:T(8,128)(2,1)S(1)} collective-permute-done((bf16[8,32,128]{2,1,0:T(8,128)(2,1)S(1)}, bf16[8,32,128]{2,1,0:T(8,128)(2,1)S(1)}, u32[]{:S(2)}, u32[]{:S(2)}) %collective-permute-start.41) | collective-permute-done | bytes 65568 | tf_op jit(solution)/shard_map/ppermute | solution.py:37
  165.1 1.6 collective-permute-start.44
  166.7 2.1 %collective-permute-start.43 = (bf16[8,32,128]{2,1,0:T(8,128)(2,1)S(1)}, bf16[8,32,128]{2,1,0:T(8,128)(2,1)S(1)}, u32[]{:S(2)}, u32[]{:S(2)}) collective-permute-start(bf16[8,32,128]{2,1,0:T(8,128)(2,1)S(1)} %multiply_convert_fusion.refs_0_), channel_id=1, source_target_pairs={{0,2},{1,3},{2,0},{3,1},{4,6},{5,7},{6,4},{7,5},{8,10},{9,11},{10,... | collective-permute-start | bytes 196616 | tf_op jit(solution)/shard_map/ppermute | solution.py:37
  175.3 1.2 collective-permute-start.46
  176.6 5.8 %collective-permute-done.46.other = bf16[24,32,128]{2,1,0:T(8,128)(2,1)S(1)} collective-permute-done((bf16[24,32,128]{2,1,0:T(8,128)(2,1)S(1)}, bf16[24,32,128]{2,1,0:T(8,128)(2,1)S(1)}, u32[]{:S(2)}, u32[]{:S(2)}) %collective-permute-start.46) | collective-permute-done | bytes 196640 | tf_op jit(solution)/shard_map/ppermute | solution.py:37
  182.3 1.6 prior_adjoint.7
  184.7 1.7 collective-permute-start.48
  187.5 1.9 %collective-permute-start.49 = (bf16[24,32,128]{2,1,0:T(8,128)(2,1)S(1)}, bf16[24,32,128]{2,1,0:T(8,128)(2,1)S(1)}, u32[]{:S(2)}, u32[]{:S(2)}) collective-permute-start(bf16[24,32,128]{2,1,0:T(8,128)(2,1)S(1)} %fusion), channel_id=1, source_target_pairs={{0,8},{1,9},{2,10},{3,11},{4,12},{5,13},{6,14},{7,15},{8,0},{9,1},... | collective-permute-start | bytes 589832 | tf_op jit(solution)/shard_map/ppermute | solution.py:37
  189.4 1.1 collective-permute-done.49
  (112 shorter events, 42.7 us)
Async XLA Ops:
  0.0 3.8 %copy-start = (f32[32,128]{1,0:T(8,128)S(1)}, f32[32,128]{1,0:T(8,128)}, u32[]{:S(2)}) copy-start(f32[32,128]{1,0:T(8,128)} %param.15) | copy-start | bytes 49156
  0.0 7.7 %copy-start.3 = (bf16[48,32,128]{2,1,0:T(8,128)(2,1)S(1)}, bf16[48,32,128]{2,1,0:T(8,128)(2,1)}, u32[]{:S(2)}) copy-start(bf16[48,32,128]{2,1,0:T(8,128)(2,1)} %refs_0_.1) | copy-start | bytes 1179652
  1.0 6.7 %collective-permute-start = (bf16[12,32,128]{2,1,0:T(8,128)(2,1)S(1)}, bf16[12,32,128]{2,1,0:T(8,128)(2,1)S(1)}, u32[]{:S(2)}, u32[]{:S(2)}) collective-permute-start(bf16[12,32,128]{2,1,0:T(8,128)(2,1)S(1)} %slice_select_fusion.2), channel_id=1, source_target_pairs={{1,8},{2,9},{3,10},{4,11},{5,12},{6,13},{7,14},{8,1},{9,2},{10,3},... | collective-permute-start | bytes 294920 | tf_op jit(solution)/shard_map/ppermute | solution.py:37
  3.8 9.4 %copy-start.2 = (bf16[1,1,384,128,128]{4,3,2,1,0:T(8,128)(2,1)S(1)}, bf16[1,1,384,128,128]{4,3,2,1,0:T(8,128)(2,1)}, u32[]{:S(2)}) copy-start(bf16[1,1,384,128,128]{4,3,2,1,0:T(8,128)(2,1)} %param.11) | copy-start | bytes 37748740
  8.8 5.7 %collective-permute-start.1 = (bf16[24,32,128]{2,1,0:T(8,128)(2,1)S(1)}, bf16[24,32,128]{2,1,0:T(8,128)(2,1)S(1)}, u32[]{:S(2)}, u32[]{:S(2)}) collective-permute-start(bf16[24,32,128]{2,1,0:T(8,128)(2,1)S(1)} %prior_spread.4.refs_0_), channel_id=1, source_target_pairs={{0,8},{1,9},{2,10},{3,11},{4,12},{5,13},{6,14},{7,15},{8,0},{9,1},... | collective-permute-start | bytes 589832 | tf_op jit(solution)/shard_map/ppermute | solution.py:37
  15.7 8.2 %collective-permute-start.2 = (bf16[8,32,128]{2,1,0:T(8,128)(2,1)S(1)}, bf16[8,32,128]{2,1,0:T(8,128)(2,1)S(1)}, u32[]{:S(2)}, u32[]{:S(2)}) collective-permute-start(bf16[8,32,128]{2,1,0:T(8,128)(2,1)S(1)} %get-tuple-element.86), channel_id=1, source_target_pairs={{0,1},{1,0},{2,3},{3,2},{4,5},{5,4},{6,7},{7,6},{8,9},{9,8},{10,11... | collective-permute-start | bytes 196616 | tf_op jit(solution)/shard_map/ppermute | solution.py:37
  16.5 7.4 %collective-permute-start.3 = (bf16[8,32,128]{2,1,0:T(8,128)(2,1)S(1)}, bf16[8,32,128]{2,1,0:T(8,128)(2,1)S(1)}, u32[]{:S(2)}, u32[]{:S(2)}) collective-permute-start(bf16[8,32,128]{2,1,0:T(8,128)(2,1)S(1)} %get-tuple-element.87), channel_id=1, source_target_pairs={{0,2},{1,3},{2,0},{3,1},{4,6},{5,7},{6,4},{7,5},{8,10},{9,11},{10,... | collective-permute-start | bytes 196616 | tf_op jit(solution)/shard_map/ppermute | solution.py:37
  18.8 5.8 %collective-permute-start.4 = (bf16[8,32,128]{2,1,0:T(8,128)(2,1)S(1)}, bf16[8,32,128]{2,1,0:T(8,128)(2,1)S(1)}, u32[]{:S(2)}, u32[]{:S(2)}) collective-permute-start(bf16[8,32,128]{2,1,0:T(8,128)(2,1)S(1)} %get-tuple-element.88), channel_id=1, source_target_pairs={{0,3},{1,2},{2,1},{3,0},{4,7},{5,6},{6,5},{7,4},{8,11},{9,10},{10,... | collective-permute-start | bytes 196616 | tf_op jit(solution)/shard_map/ppermute | solution.py:37
  24.7 6.6 %collective-permute-start.5 = (bf16[8,32,128]{2,1,0:T(8,128)(2,1)S(1)}, bf16[8,32,128]{2,1,0:T(8,128)(2,1)S(1)}, u32[]{:S(2)}, u32[]{:S(2)}) collective-permute-start(bf16[8,32,128]{2,1,0:T(8,128)(2,1)S(1)} %convert_add_fusion.1), channel_id=1, source_target_pairs={{0,4},{1,5},{2,6},{3,7},{4,0},{5,1},{6,2},{7,3},{8,12},{9,13},{10,... | collective-permute-start | bytes 196616 | tf_op jit(solution)/shard_map/ppermute | solution.py:37
  31.3 5.4 %collective-permute-start.8 = (bf16[8,32,128]{2,1,0:T(8,128)(2,1)S(1)}, bf16[8,32,128]{2,1,0:T(8,128)(2,1)S(1)}, u32[]{:S(2)}, u32[]{:S(2)}) collective-permute-start(bf16[8,32,128]{2,1,0:T(8,128)(2,1)S(1)} %multiply_convert_fusion.3.refs_0_), channel_id=1, source_target_pairs={{0,3},{1,2},{2,1},{3,0},{4,7},{5,6},{6,5},{7,4},{8,11},{9,10},{10,... | collective-permute-start | bytes 196616 | tf_op jit(solution)/shard_map/ppermute | solution.py:37
  32.3 5.5 %collective-permute-start.7 = (bf16[8,32,128]{2,1,0:T(8,128)(2,1)S(1)}, bf16[8,32,128]{2,1,0:T(8,128)(2,1)S(1)}, u32[]{:S(2)}, u32[]{:S(2)}) collective-permute-start(bf16[8,32,128]{2,1,0:T(8,128)(2,1)S(1)} %multiply_convert_fusion.3.refs_0_), channel_id=1, source_target_pairs={{0,2},{1,3},{2,0},{3,1},{4,6},{5,7},{6,4},{7,5},{8,10},{9,11},{10,... | collective-permute-start | bytes 196616 | tf_op jit(solution)/shard_map/ppermute | solution.py:37
  32.8 6.0 %collective-permute-start.6 = (bf16[8,32,128]{2,1,0:T(8,128)(2,1)S(1)}, bf16[8,32,128]{2,1,0:T(8,128)(2,1)S(1)}, u32[]{:S(2)}, u32[]{:S(2)}) collective-permute-start(bf16[8,32,128]{2,1,0:T(8,128)(2,1)S(1)} %multiply_convert_fusion.3.refs_0_), channel_id=1, source_target_pairs={{0,1},{1,0},{2,3},{3,2},{4,5},{5,4},{6,7},{7,6},{8,9},{9,8},{10,11... | collective-permute-start | bytes 196616 | tf_op jit(solution)/shard_map/ppermute | solution.py:37
  39.5 1.5 collective-permute-start.9
  41.1 7.0 %collective-permute-start.10 = (bf16[24,32,128]{2,1,0:T(8,128)(2,1)S(1)}, bf16[24,32,128]{2,1,0:T(8,128)(2,1)S(1)}, u32[]{:S(2)}, u32[]{:S(2)}) collective-permute-start(bf16[24,32,128]{2,1,0:T(8,128)(2,1)S(1)} %add_convert_fusion.3.mine), channel_id=1, source_target_pairs={{0,16},{1,17},{2,18},{3,19},{4,20},{5,21},{6,22},{7,23},{8,24},{9,... | collective-permute-start | bytes 589832 | tf_op jit(solution)/shard_map/ppermute | solution.py:37
  49.9 1.5 collective-permute-start.11
  50.0 1.4 collective-permute-start.12
  52.6 7.4 %collective-permute-start.13 = (bf16[24,32,128]{2,1,0:T(8,128)(2,1)S(1)}, bf16[24,32,128]{2,1,0:T(8,128)(2,1)S(1)}, u32[]{:S(2)}, u32[]{:S(2)}) collective-permute-start(bf16[24,32,128]{2,1,0:T(8,128)(2,1)S(1)} %prior_spread.5.refs_0_), channel_id=1, source_target_pairs={{0,8},{1,9},{2,10},{3,11},{4,12},{5,13},{6,14},{7,15},{8,0},{9,1},... | collective-permute-start | bytes 589832 | tf_op jit(solution)/shard_map/ppermute | solution.py:37
  61.3 4.8 %collective-permute-start.14 = (bf16[8,32,128]{2,1,0:T(8,128)(2,1)S(1)}, bf16[8,32,128]{2,1,0:T(8,128)(2,1)S(1)}, u32[]{:S(2)}, u32[]{:S(2)}) collective-permute-start(bf16[8,32,128]{2,1,0:T(8,128)(2,1)S(1)} %get-tuple-element.119), channel_id=1, source_target_pairs={{0,1},{1,0},{2,3},{3,2},{4,5},{5,4},{6,7},{7,6},{8,9},{9,8},{10,11... | collective-permute-start | bytes 196616 | tf_op jit(solution)/shard_map/ppermute | solution.py:37
  62.9 4.9 %collective-permute-start.15 = (bf16[8,32,128]{2,1,0:T(8,128)(2,1)S(1)}, bf16[8,32,128]{2,1,0:T(8,128)(2,1)S(1)}, u32[]{:S(2)}, u32[]{:S(2)}) collective-permute-start(bf16[8,32,128]{2,1,0:T(8,128)(2,1)S(1)} %get-tuple-element.120), channel_id=1, source_target_pairs={{0,2},{1,3},{2,0},{3,1},{4,6},{5,7},{6,4},{7,5},{8,10},{9,11},{10,... | collective-permute-start | bytes 196616 | tf_op jit(solution)/shard_map/ppermute | solution.py:37
  65.0 5.2 %collective-permute-start.16 = (bf16[8,32,128]{2,1,0:T(8,128)(2,1)S(1)}, bf16[8,32,128]{2,1,0:T(8,128)(2,1)S(1)}, u32[]{:S(2)}, u32[]{:S(2)}) collective-permute-start(bf16[8,32,128]{2,1,0:T(8,128)(2,1)S(1)} %get-tuple-element.121), channel_id=1, source_target_pairs={{0,3},{1,2},{2,1},{3,0},{4,7},{5,6},{6,5},{7,4},{8,11},{9,10},{10,... | collective-permute-start | bytes 196616 | tf_op jit(solution)/shard_map/ppermute | solution.py:37
  70.2 5.2 %collective-permute-start.17 = (bf16[8,32,128]{2,1,0:T(8,128)(2,1)S(1)}, bf16[8,32,128]{2,1,0:T(8,128)(2,1)S(1)}, u32[]{:S(2)}, u32[]{:S(2)}) collective-permute-start(bf16[8,32,128]{2,1,0:T(8,128)(2,1)S(1)} %add_convert_fusion.6), channel_id=1, source_target_pairs={{0,4},{1,5},{2,6},{3,7},{4,0},{5,1},{6,2},{7,3},{8,12},{9,13},{10,... | collective-permute-start | bytes 196616 | tf_op jit(solution)/shard_map/ppermute | solution.py:37
  75.5 5.2 %collective-permute-start.20 = (bf16[8,32,128]{2,1,0:T(8,128)(2,1)S(1)}, bf16[8,32,128]{2,1,0:T(8,128)(2,1)S(1)}, u32[]{:S(2)}, u32[]{:S(2)}) collective-permute-start(bf16[8,32,128]{2,1,0:T(8,128)(2,1)S(1)} %multiply_convert_fusion.2.refs_0_), channel_id=1, source_target_pairs={{0,3},{1,2},{2,1},{3,0},{4,7},{5,6},{6,5},{7,4},{8,11},{9,10},{10,... | collective-permute-start | bytes 196616 | tf_op jit(solution)/shard_map/ppermute | solution.py:37
  76.8 5.1 %collective-permute-start.19 = (bf16[8,32,128]{2,1,0:T(8,128)(2,1)S(1)}, bf16[8,32,128]{2,1,0:T(8,128)(2,1)S(1)}, u32[]{:S(2)}, u32[]{:S(2)}) collective-permute-start(bf16[8,32,128]{2,1,0:T(8,128)(2,1)S(1)} %multiply_convert_fusion.2.refs_0_), channel_id=1, source_target_pairs={{0,2},{1,3},{2,0},{3,1},{4,6},{5,7},{6,4},{7,5},{8,10},{9,11},{10,... | collective-permute-start | bytes 196616 | tf_op jit(solution)/shard_map/ppermute | solution.py:37
  78.9 4.3 %collective-permute-start.18 = (bf16[8,32,128]{2,1,0:T(8,128)(2,1)S(1)}, bf16[8,32,128]{2,1,0:T(8,128)(2,1)S(1)}, u32[]{:S(2)}, u32[]{:S(2)}) collective-permute-start(bf16[8,32,128]{2,1,0:T(8,128)(2,1)S(1)} %multiply_convert_fusion.2.refs_0_), channel_id=1, source_target_pairs={{0,1},{1,0},{2,3},{3,2},{4,5},{5,4},{6,7},{7,6},{8,9},{9,8},{10,11... | collective-permute-start | bytes 196616 | tf_op jit(solution)/shard_map/ppermute | solution.py:37
  83.9 1.5 collective-permute-start.21
  85.5 7.2 %collective-permute-start.22 = (bf16[24,32,128]{2,1,0:T(8,128)(2,1)S(1)}, bf16[24,32,128]{2,1,0:T(8,128)(2,1)S(1)}, u32[]{:S(2)}, u32[]{:S(2)}) collective-permute-start(bf16[24,32,128]{2,1,0:T(8,128)(2,1)S(1)} %add_convert_fusion.2.mine), channel_id=1, source_target_pairs={{0,16},{1,17},{2,18},{3,19},{4,20},{5,21},{6,22},{7,23},{8,24},{9,... | collective-permute-start | bytes 589832 | tf_op jit(solution)/shard_map/ppermute | solution.py:37
  94.3 1.5 collective-permute-start.23
  94.4 1.4 collective-permute-start.24
  97.1 7.4 %collective-permute-start.25 = (bf16[24,32,128]{2,1,0:T(8,128)(2,1)S(1)}, bf16[24,32,128]{2,1,0:T(8,128)(2,1)S(1)}, u32[]{:S(2)}, u32[]{:S(2)}) collective-permute-start(bf16[24,32,128]{2,1,0:T(8,128)(2,1)S(1)} %prior_spread.6.refs_0_), channel_id=1, source_target_pairs={{0,8},{1,9},{2,10},{3,11},{4,12},{5,13},{6,14},{7,15},{8,0},{9,1},... | collective-permute-start | bytes 589832 | tf_op jit(solution)/shard_map/ppermute | solution.py:37
  105.7 4.8 %collective-permute-start.26 = (bf16[8,32,128]{2,1,0:T(8,128)(2,1)S(1)}, bf16[8,32,128]{2,1,0:T(8,128)(2,1)S(1)}, u32[]{:S(2)}, u32[]{:S(2)}) collective-permute-start(bf16[8,32,128]{2,1,0:T(8,128)(2,1)S(1)} %get-tuple-element.127), channel_id=1, source_target_pairs={{0,1},{1,0},{2,3},{3,2},{4,5},{5,4},{6,7},{7,6},{8,9},{9,8},{10,11... | collective-permute-start | bytes 196616 | tf_op jit(solution)/shard_map/ppermute | solution.py:37
  107.3 5.0 %collective-permute-start.27 = (bf16[8,32,128]{2,1,0:T(8,128)(2,1)S(1)}, bf16[8,32,128]{2,1,0:T(8,128)(2,1)S(1)}, u32[]{:S(2)}, u32[]{:S(2)}) collective-permute-start(bf16[8,32,128]{2,1,0:T(8,128)(2,1)S(1)} %get-tuple-element.128), channel_id=1, source_target_pairs={{0,2},{1,3},{2,0},{3,1},{4,6},{5,7},{6,4},{7,5},{8,10},{9,11},{10,... | collective-permute-start | bytes 196616 | tf_op jit(solution)/shard_map/ppermute | solution.py:37
  109.0 5.2 %collective-permute-start.28 = (bf16[8,32,128]{2,1,0:T(8,128)(2,1)S(1)}, bf16[8,32,128]{2,1,0:T(8,128)(2,1)S(1)}, u32[]{:S(2)}, u32[]{:S(2)}) collective-permute-start(bf16[8,32,128]{2,1,0:T(8,128)(2,1)S(1)} %get-tuple-element.129), channel_id=1, source_target_pairs={{0,3},{1,2},{2,1},{3,0},{4,7},{5,6},{6,5},{7,4},{8,11},{9,10},{10,... | collective-permute-start | bytes 196616 | tf_op jit(solution)/shard_map/ppermute | solution.py:37
  114.2 6.0 %collective-permute-start.29 = (bf16[8,32,128]{2,1,0:T(8,128)(2,1)S(1)}, bf16[8,32,128]{2,1,0:T(8,128)(2,1)S(1)}, u32[]{:S(2)}, u32[]{:S(2)}) collective-permute-start(bf16[8,32,128]{2,1,0:T(8,128)(2,1)S(1)} %add_convert_fusion.5), channel_id=1, source_target_pairs={{0,4},{1,5},{2,6},{3,7},{4,0},{5,1},{6,2},{7,3},{8,12},{9,13},{10,... | collective-permute-start | bytes 196616 | tf_op jit(solution)/shard_map/ppermute | solution.py:37
  120.3 5.2 %collective-permute-start.32 = (bf16[8,32,128]{2,1,0:T(8,128)(2,1)S(1)}, bf16[8,32,128]{2,1,0:T(8,128)(2,1)S(1)}, u32[]{:S(2)}, u32[]{:S(2)}) collective-permute-start(bf16[8,32,128]{2,1,0:T(8,128)(2,1)S(1)} %multiply_convert_fusion.1.refs_0_), channel_id=1, source_target_pairs={{0,3},{1,2},{2,1},{3,0},{4,7},{5,6},{6,5},{7,4},{8,11},{9,10},{10,... | collective-permute-start | bytes 196616 | tf_op jit(solution)/shard_map/ppermute | solution.py:37
  121.7 5.1 %collective-permute-start.31 = (bf16[8,32,128]{2,1,0:T(8,128)(2,1)S(1)}, bf16[8,32,128]{2,1,0:T(8,128)(2,1)S(1)}, u32[]{:S(2)}, u32[]{:S(2)}) collective-permute-start(bf16[8,32,128]{2,1,0:T(8,128)(2,1)S(1)} %multiply_convert_fusion.1.refs_0_), channel_id=1, source_target_pairs={{0,2},{1,3},{2,0},{3,1},{4,6},{5,7},{6,4},{7,5},{8,10},{9,11},{10,... | collective-permute-start | bytes 196616 | tf_op jit(solution)/shard_map/ppermute | solution.py:37
  123.8 4.3 %collective-permute-start.30 = (bf16[8,32,128]{2,1,0:T(8,128)(2,1)S(1)}, bf16[8,32,128]{2,1,0:T(8,128)(2,1)S(1)}, u32[]{:S(2)}, u32[]{:S(2)}) collective-permute-start(bf16[8,32,128]{2,1,0:T(8,128)(2,1)S(1)} %multiply_convert_fusion.1.refs_0_), channel_id=1, source_target_pairs={{0,1},{1,0},{2,3},{3,2},{4,5},{5,4},{6,7},{7,6},{8,9},{9,8},{10,11... | collective-permute-start | bytes 196616 | tf_op jit(solution)/shard_map/ppermute | solution.py:37
  128.8 1.5 collective-permute-start.33
  130.4 7.0 %collective-permute-start.34 = (bf16[24,32,128]{2,1,0:T(8,128)(2,1)S(1)}, bf16[24,32,128]{2,1,0:T(8,128)(2,1)S(1)}, u32[]{:S(2)}, u32[]{:S(2)}) collective-permute-start(bf16[24,32,128]{2,1,0:T(8,128)(2,1)S(1)} %add_convert_fusion.1.mine), channel_id=1, source_target_pairs={{0,16},{1,17},{2,18},{3,19},{4,20},{5,21},{6,22},{7,23},{8,24},{9,... | collective-permute-start | bytes 589832 | tf_op jit(solution)/shard_map/ppermute | solution.py:37
  139.0 1.5 collective-permute-start.35
  139.1 1.4 collective-permute-start.36
  141.8 7.4 %collective-permute-start.37 = (bf16[24,32,128]{2,1,0:T(8,128)(2,1)S(1)}, bf16[24,32,128]{2,1,0:T(8,128)(2,1)S(1)}, u32[]{:S(2)}, u32[]{:S(2)}) collective-permute-start(bf16[24,32,128]{2,1,0:T(8,128)(2,1)S(1)} %prior_spread.7.refs_0_), channel_id=1, source_target_pairs={{0,8},{1,9},{2,10},{3,11},{4,12},{5,13},{6,14},{7,15},{8,0},{9,1},... | collective-permute-start | bytes 589832 | tf_op jit(solution)/shard_map/ppermute | solution.py:37
  150.4 5.0 %collective-permute-start.38 = (bf16[8,32,128]{2,1,0:T(8,128)(2,1)S(1)}, bf16[8,32,128]{2,1,0:T(8,128)(2,1)S(1)}, u32[]{:S(2)}, u32[]{:S(2)}) collective-permute-start(bf16[8,32,128]{2,1,0:T(8,128)(2,1)S(1)} %get-tuple-element.135), channel_id=1, source_target_pairs={{0,1},{1,0},{2,3},{3,2},{4,5},{5,4},{6,7},{7,6},{8,9},{9,8},{10,11... | collective-permute-start | bytes 196616 | tf_op jit(solution)/shard_map/ppermute | solution.py:37
  152.2 4.7 %collective-permute-start.39 = (bf16[8,32,128]{2,1,0:T(8,128)(2,1)S(1)}, bf16[8,32,128]{2,1,0:T(8,128)(2,1)S(1)}, u32[]{:S(2)}, u32[]{:S(2)}) collective-permute-start(bf16[8,32,128]{2,1,0:T(8,128)(2,1)S(1)} %get-tuple-element.136), channel_id=1, source_target_pairs={{0,2},{1,3},{2,0},{3,1},{4,6},{5,7},{6,4},{7,5},{8,10},{9,11},{10,... | collective-permute-start | bytes 196616 | tf_op jit(solution)/shard_map/ppermute | solution.py:37
  153.9 5.2 %collective-permute-start.40 = (bf16[8,32,128]{2,1,0:T(8,128)(2,1)S(1)}, bf16[8,32,128]{2,1,0:T(8,128)(2,1)S(1)}, u32[]{:S(2)}, u32[]{:S(2)}) collective-permute-start(bf16[8,32,128]{2,1,0:T(8,128)(2,1)S(1)} %get-tuple-element.137), channel_id=1, source_target_pairs={{0,3},{1,2},{2,1},{3,0},{4,7},{5,6},{6,5},{7,4},{8,11},{9,10},{10,... | collective-permute-start | bytes 196616 | tf_op jit(solution)/shard_map/ppermute | solution.py:37
  159.1 6.0 %collective-permute-start.41 = (bf16[8,32,128]{2,1,0:T(8,128)(2,1)S(1)}, bf16[8,32,128]{2,1,0:T(8,128)(2,1)S(1)}, u32[]{:S(2)}, u32[]{:S(2)}) collective-permute-start(bf16[8,32,128]{2,1,0:T(8,128)(2,1)S(1)} %add_convert_fusion.4), channel_id=1, source_target_pairs={{0,4},{1,5},{2,6},{3,7},{4,0},{5,1},{6,2},{7,3},{8,12},{9,13},{10,... | collective-permute-start | bytes 196616 | tf_op jit(solution)/shard_map/ppermute | solution.py:37
  165.1 5.2 %collective-permute-start.44 = (bf16[8,32,128]{2,1,0:T(8,128)(2,1)S(1)}, bf16[8,32,128]{2,1,0:T(8,128)(2,1)S(1)}, u32[]{:S(2)}, u32[]{:S(2)}) collective-permute-start(bf16[8,32,128]{2,1,0:T(8,128)(2,1)S(1)} %multiply_convert_fusion.refs_0_), channel_id=1, source_target_pairs={{0,3},{1,2},{2,1},{3,0},{4,7},{5,6},{6,5},{7,4},{8,11},{9,10},{10,... | collective-permute-start | bytes 196616 | tf_op jit(solution)/shard_map/ppermute | solution.py:37
  166.7 5.1 %collective-permute-start.43 = (bf16[8,32,128]{2,1,0:T(8,128)(2,1)S(1)}, bf16[8,32,128]{2,1,0:T(8,128)(2,1)S(1)}, u32[]{:S(2)}, u32[]{:S(2)}) collective-permute-start(bf16[8,32,128]{2,1,0:T(8,128)(2,1)S(1)} %multiply_convert_fusion.refs_0_), channel_id=1, source_target_pairs={{0,2},{1,3},{2,0},{3,1},{4,6},{5,7},{6,4},{7,5},{8,10},{9,11},{10,... | collective-permute-start | bytes 196616 | tf_op jit(solution)/shard_map/ppermute | solution.py:37
  168.8 4.3 %collective-permute-start.42 = (bf16[8,32,128]{2,1,0:T(8,128)(2,1)S(1)}, bf16[8,32,128]{2,1,0:T(8,128)(2,1)S(1)}, u32[]{:S(2)}, u32[]{:S(2)}) collective-permute-start(bf16[8,32,128]{2,1,0:T(8,128)(2,1)S(1)} %multiply_convert_fusion.refs_0_), channel_id=1, source_target_pairs={{0,1},{1,0},{2,3},{3,2},{4,5},{5,4},{6,7},{7,6},{8,9},{9,8},{10,11... | collective-permute-start | bytes 196616 | tf_op jit(solution)/shard_map/ppermute | solution.py:37
  173.1 18.2 %copy-start.1 = (f32[32,128]{1,0:T(8,128)S(1)}, f32[32,128]{1,0:T(8,128)}, u32[]{:S(2)}) copy-start(f32[32,128]{1,0:T(8,128)} %param.15) | copy-start | bytes 49156
  173.8 1.5 collective-permute-start.45
  175.3 7.0 %collective-permute-start.46 = (bf16[24,32,128]{2,1,0:T(8,128)(2,1)S(1)}, bf16[24,32,128]{2,1,0:T(8,128)(2,1)S(1)}, u32[]{:S(2)}, u32[]{:S(2)}) collective-permute-start(bf16[24,32,128]{2,1,0:T(8,128)(2,1)S(1)} %add_convert_fusion.mine), channel_id=1, source_target_pairs={{0,16},{1,17},{2,18},{3,19},{4,20},{5,21},{6,22},{7,23},{8,24},{9,... | collective-permute-start | bytes 589832 | tf_op jit(solution)/shard_map/ppermute | solution.py:37
  184.0 2.4 %collective-permute-start.47 = (bf16[12,32,128]{2,1,0:T(8,128)(2,1)S(1)}, bf16[12,32,128]{2,1,0:T(8,128)(2,1)S(1)}, u32[]{:S(2)}, u32[]{:S(2)}) collective-permute-start(bf16[12,32,128]{2,1,0:T(8,128)(2,1)S(1)} %slice_select_fusion.1), channel_id=1, source_target_pairs={{1,8},{2,9},{3,10},{4,11},{5,12},{6,13},{7,14},{8,1},{9,2},{10,3},... | collective-permute-start | bytes 294920 | tf_op jit(solution)/shard_map/ppermute | solution.py:37
  184.7 2.7 %collective-permute-start.48 = (bf16[12,32,128]{2,1,0:T(8,128)(2,1)S(1)}, bf16[12,32,128]{2,1,0:T(8,128)(2,1)S(1)}, u32[]{:S(2)}, u32[]{:S(2)}) collective-permute-start(bf16[12,32,128]{2,1,0:T(8,128)(2,1)S(1)} %slice_select_fusion), channel_id=1, source_target_pairs={{0,8},{1,9},{2,10},{3,11},{4,12},{5,13},{6,14},{7,15},{8,0},{9,1},... | collective-permute-start | bytes 294920 | tf_op jit(solution)/shard_map/ppermute | solution.py:37
  187.5 3.0 %collective-permute-start.49 = (bf16[24,32,128]{2,1,0:T(8,128)(2,1)S(1)}, bf16[24,32,128]{2,1,0:T(8,128)(2,1)S(1)}, u32[]{:S(2)}, u32[]{:S(2)}) collective-permute-start(bf16[24,32,128]{2,1,0:T(8,128)(2,1)S(1)} %fusion), channel_id=1, source_target_pairs={{0,8},{1,9},{2,10},{3,11},{4,12},{5,13},{6,14},{7,15},{8,0},{9,1},... | collective-permute-start | bytes 589832 | tf_op jit(solution)/shard_map/ppermute | solution.py:37

commit v11 on v10

--- a/solution.py
+++ b/solution.py
@@ -144,7 +144,13 @@
     )
     for plan, (src, dst, use), out in zip(FORWARD_PLANS, uses, built):
         plan_groups(plan, jnp.where(use, src, 0), jnp.where(use, dst, most), 0, most, out)
-    ext = nbr_in[...] - first_tile + reach
+    count = tile_rows * fan
+    entry = lax.broadcasted_iota(i32, (fan, count), 1) - lax.broadcasted_iota(i32, (fan, count), 0)
+    local = nbr_in[...] - first_tile + reach
+    spread = sum(
+        jnp.where(entry == t * fan, local[:, t : t + 1], 0).astype(F32) for t in range(tile_rows)
+    )
+    ext = jnp.sum(spread, axis=0, keepdims=True).astype(i32)
     ext_row[...] = ext
     built[3][:, : ext.shape[1]] = ext
     built[3][:, ext.shape[1] :] = jnp.zeros((1, LANES), i32) + side
@@ -194,13 +200,13 @@
     vmem = pl.BlockSpec(memory_space=pltpu.VMEM)
     hbm = pl.BlockSpec(memory_space=pl.ANY)
     i32 = jnp.int32
-    lengths = plan_lengths(FORWARD_PLANS, obs.shape[1], max(rows[:2])) + [nbr.shape[1] + LANES]
+    lengths = plan_lengths(FORWARD_PLANS, obs.shape[1], max(rows[:2])) + [nbr.size + LANES]
     return pl.pallas_call(
         functools.partial(setup_kernel, rows, chunk),
         in_specs=[smem] + [hbm] * 4,
         out_specs=[vmem] * 4 + [smem] * 4,
         out_shape=[pltpu.VMEM((owned,) + prior.shape[1:], HALF)]
-        + [pltpu.VMEM(v.shape, i32) for v in (obs, flux, nbr)]
+        + [pltpu.VMEM(s, i32) for s in (obs.shape, flux.shape, (1, nbr.size))]
         + [pltpu.SMEM((1, n), i32) for n in lengths],
         scratch_shapes=[pltpu.VMEM(v.shape, i32) for v in (obs, flux, nbr)]
         + [pltpu.VMEM((1, n), i32) for n in lengths]
@@ -431,12 +437,11 @@
     edge = jnp.where(side == 0, probes[:reach], probes[tile_count - reach :])
     beyond = swap_far(edge)
     where = jnp.stack([side, corner, counts[0, 0], flux_at * tile_count + side * half])
-    nbr = neighbours.reshape(1, tile_count * fan)
-
-    where, own_rinv, nbr, prior, blocks = lax.optimization_barrier((where, own_rinv, nbr, prior, blocks))
+
+    where, own_rinv, prior, blocks = lax.optimization_barrier((where, own_rinv, prior, blocks))
     jac_plain = blocks
     prior_plain, *index_rows, own_lists, other_lists, near_lists, nbr = setup(
-        where, jac_obs[0], jac_flux[0], nbr, prior, sizes
+        where, jac_obs[0], jac_flux[0], neighbours.T, prior, sizes
     )
     fields = (probes, beyond)
     for step in range(STEPS):
@@ -455,7 +460,7 @@
         if step == 0:
             pieces, jac_plain = lax.optimization_barrier((pieces, jac_plain))
             jac_turned = turn_blocks(jac_plain, "jac_turn")
-        for bits in range(1, 4):
+        for bits in (3, 2, 1):
             total = total + swap_flux(pieces[bits - 1], bits).astype(F32)
         if step == 0:
             total, jac_turned, index_rows = lax.optimization_barrier((total, jac_turned, index_rows))
@@ -503,7 +508,8 @@
                 mine = (mine.astype(F32) + other.astype(F32)).astype(HALF)
         ext, to_core, to_far = gather_tiles(nbr, prior_lists, mine, other, prior_turned, rows)
         if step < STEPS - 1:
-            fields = (ext, swap_core(to_core), swap_far(to_far))
+            from_far = swap_far(to_far)
+            fields = (ext, swap_core(to_core), from_far)
     lower = side == 0
     from_core = swap_core(jnp.where(lower, to_core[half - reach :], to_core[:reach])).astype(F32)
     from_far = swap_far(jnp.where(lower, to_far[:reach], to_far[half - reach :])).astype(F32)

time: 192 us -> 190 us (0.990)
  starting transfers between devices: 78.1 us -> 75.8 us
    ppermute x50, starting transfers between devices: 78.1 us -> 75.8 us  [exchange(): return lax.ppermute(value, ('obs', 'flux'), route)]
  transfers between devices with their start and end apart: 50 -> 50, of which waited for: 37 -> 30; matrix products, arithmetic and copies ran while one was open for 1% -> 0% of each run, Pallas kernels for 19% -> 20%
where the time goes in v11:
time: 190 us; the launch traced here: 189 us
  starting transfers between devices  75.8 us (40%)
  Pallas kernels  55 us (29%)
  waiting for transfers between devices  53.8 us (28%)
  other arithmetic  2.46 us (1%)
    ppermute x50, starting transfers between devices, exchange(): return lax.ppermute(value, ('obs', 'flux'), route)  75.8 us
    ppermute x50, waiting for transfers between devices, exchange(): return lax.ppermute(value, ('obs', 'flux'), route)  53.8 us
    pallas_call x32, Pallas kernels, jac_pass(): pl.pallas_call(functools.partial(jac_kernel, plan, sizes, len(parts), beg...  30.8 us
    pallas_call x4, Pallas kernels, gather_tiles(): pl.pallas_call(functools.partial(gather_kernel, rows, plan_sizes(PRIOR_PL...  6.69 us
    pallas_call x2, Pallas kernels, turn_blocks(): pl.pallas_call(functools.partial(turn_kernel, chunk_of(plain.shape[0], 48...  5.5 us
    pallas_call x4, Pallas kernels, spread_tiles(): pl.pallas_call(functools.partial(spread_kernel, len(fields) == 2, prior.s...  4.83 us
    pallas_call x1, Pallas kernels, setup(): pl.pallas_call(functools.partial(setup_kernel, rows, chunk), in_specs=[sm...  3.8 us
  transfers between devices with their start and end apart: 50, of which 30 were waited for; matrix products, arithmetic and copies ran while one was open for 0% of the time, Pallas kernels for 20%

profile of v11, /device:TPU:0, one launch (start us, length us, event | category | flops | bytes accessed | tf_op | source)
XLA Modules:
  0.0 188.5 jit_solution(7724089889318041120)
XLA Ops:
  2.5 3.8 %setup.1 = (bf16[192,128,128]{2,1,0:T(8,128)(2,1)S(1)}, s32[1,384]{1,0:T(1,128)S(1)}, s32[1,384]{1,0:T(1,128)S(1)}, s32[1,384]{1,0:T(1,128)S(1)}, s32[1,1280]{1,...) custom-call(s32[4]{0:T(128)S(1)} %pad_add_fusion.where, s32[1,384]{1,0:T(1,128)} %bitcast.32, ...), custom_call_target="tpu_custom_call" | custom-call | tf_op jit(solution)/shard_map/setup/pallas_call | solution.py:204
  6.3 1.1 prior_spread.4.refs_0_
  7.4 4.4 %collective-permute-start.1 = (bf16[24,32,128]{2,1,0:T(8,128)(2,1)S(1)}, bf16[24,32,128]{2,1,0:T(8,128)(2,1)S(1)}, u32[]{:S(2)}, u32[]{:S(2)}) collective-permute-start(bf16[24,32,128]{2,1,0:T(8,128)(2,1)S(1)} %prior_spread.4.refs_0_), channel_id=1, source_target_pairs={{0,8},{1,9},{2,10},{3,11},{4,12},{5,13},{6,14},{7,15},{8,0},{9,1},... | collective-permute-start | bytes 589832 | tf_op jit(solution)/shard_map/ppermute | solution.py:37
  11.8 1.3 forward_own.4.refs_1_
  13.1 1.2 forward_other.4
  14.3 2.0 %collective-permute-start.2 = (bf16[8,32,128]{2,1,0:T(8,128)(2,1)S(1)}, bf16[8,32,128]{2,1,0:T(8,128)(2,1)S(1)}, u32[]{:S(2)}, u32[]{:S(2)}) collective-permute-start(bf16[8,32,128]{2,1,0:T(8,128)(2,1)S(1)} %get-tuple-element.84), channel_id=1, source_target_pairs={{0,3},{1,2},{2,1},{3,0},{4,7},{5,6},{6,5},{7,4},{8,11},{9,10},{10,... | collective-permute-start | bytes 196616 | tf_op jit(solution)/shard_map/ppermute | solution.py:37
  16.5 1.3 collective-permute-start.4
  17.9 3.7 %jac_turn.1.refs_1_.refs_2_ = bf16[384,128,128]{2,1,0:T(8,128)(2,1)S(1)} custom-call(bf16[384,128,128]{2,1,0:T(8,128)(2,1)S(1)} %bitcast.15), custom_call_target="tpu_custom_call" | custom-call | bytes 12582912 | tf_op jit(solution)/shard_map/jac_turn/pallas_call | solution.py:180
  22.6 3.3 %collective-permute-start.5 = (bf16[8,32,128]{2,1,0:T(8,128)(2,1)S(1)}, bf16[8,32,128]{2,1,0:T(8,128)(2,1)S(1)}, u32[]{:S(2)}, u32[]{:S(2)}) collective-permute-start(bf16[8,32,128]{2,1,0:T(8,128)(2,1)S(1)} %convert_add_fusion.1), channel_id=1, source_target_pairs={{0,4},{1,5},{2,6},{3,7},{4,0},{5,1},{6,2},{7,3},{8,12},{9,13},{10,... | collective-permute-start | bytes 196616 | tf_op jit(solution)/shard_map/ppermute | solution.py:37
  25.9 3.4 %late_plans.1 = (s32[1,1408]{1,0:T(1,128)S(4)}, s32[1,1408]{1,0:T(1,128)S(4)}, s32[1,1408]{1,0:T(1,128)S(4)}, s32[1,1280]{1,0:T(1,128)S(4)}, s32[1,1280]{1,0:T(1,128)S(4)}, /*index=5*/s32[1,1664]{1,0:T(1,128)S(4)}) custom-call(s32[1,512]{1,0:T(1,128)S(4)} %get-tuple-element.75.nbr, s32[1,384]{1,0:T(1,128)S(1)} %get-tuple-element.92.obs_row, ...), custom_call_target="tpu_custom_call" | custom-call | bytes 8388608 | tf_op jit(solution)/shard_map/late_plans/pallas_call | solution.py:256
  29.6 1.5 collective-permute-start.8
  31.1 1.3 collective-permute-start.7
  34.2 1.2 collective-permute-done.8.refs_0_
  35.4 1.0 adjoint_quarter3.4.refs_1_
  36.4 1.0 adjoint_quarter2.4
  39.4 1.7 collective-permute-start.10
  41.1 1.8 prior_turn.1.prior
  43.0 3.4 %collective-permute-done.10.other = bf16[24,32,128]{2,1,0:T(8,128)(2,1)S(1)} collective-permute-done((bf16[24,32,128]{2,1,0:T(8,128)(2,1)S(1)}, bf16[24,32,128]{2,1,0:T(8,128)(2,1)S(1)}, u32[]{:S(2)}, u32[]{:S(2)}) %collective-permute-start.10) | collective-permute-done | bytes 196640 | tf_op jit(solution)/shard_map/ppermute | solution.py:37
  46.4 1.8 prior_adjoint.4
  49.7 1.2 prior_spread.5.refs_0_
  51.0 6.4 %collective-permute-start.13 = (bf16[24,32,128]{2,1,0:T(8,128)(2,1)S(1)}, bf16[24,32,128]{2,1,0:T(8,128)(2,1)S(1)}, u32[]{:S(2)}, u32[]{:S(2)}) collective-permute-start(bf16[24,32,128]{2,1,0:T(8,128)(2,1)S(1)} %prior_spread.5.refs_0_), channel_id=1, source_target_pairs={{0,8},{1,9},{2,10},{3,11},{4,12},{5,13},{6,14},{7,15},{8,0},{9,1},... | collective-permute-start | bytes 589832 | tf_op jit(solution)/shard_map/ppermute | solution.py:37
  57.4 1.3 forward_own.5.refs_1_
  58.7 1.2 forward_other.5
  60.0 2.2 %collective-permute-start.14 = (bf16[8,32,128]{2,1,0:T(8,128)(2,1)S(1)}, bf16[8,32,128]{2,1,0:T(8,128)(2,1)S(1)}, u32[]{:S(2)}, u32[]{:S(2)}) collective-permute-start(bf16[8,32,128]{2,1,0:T(8,128)(2,1)S(1)} %get-tuple-element.117), channel_id=1, source_target_pairs={{0,3},{1,2},{2,1},{3,0},{4,7},{5,6},{6,5},{7,4},{8,11},{9,10},{10,... | collective-permute-start | bytes 196616 | tf_op jit(solution)/shard_map/ppermute | solution.py:37
  62.1 1.3 collective-permute-start.15
  65.2 2.5 %collective-permute-done.15 = bf16[8,32,128]{2,1,0:T(8,128)(2,1)S(1)} collective-permute-done((bf16[8,32,128]{2,1,0:T(8,128)(2,1)S(1)}, bf16[8,32,128]{2,1,0:T(8,128)(2,1)S(1)}, u32[]{:S(2)}, u32[]{:S(2)}) %collective-permute-start.15) | collective-permute-done | bytes 65568 | tf_op jit(solution)/shard_map/ppermute | solution.py:37
  67.8 2.4 %collective-permute-start.17 = (bf16[8,32,128]{2,1,0:T(8,128)(2,1)S(1)}, bf16[8,32,128]{2,1,0:T(8,128)(2,1)S(1)}, u32[]{:S(2)}, u32[]{:S(2)}) collective-permute-start(bf16[8,32,128]{2,1,0:T(8,128)(2,1)S(1)} %add_convert_fusion.6), channel_id=1, source_target_pairs={{0,4},{1,5},{2,6},{3,7},{4,0},{5,1},{6,2},{7,3},{8,12},{9,13},{10,... | collective-permute-start | bytes 196616 | tf_op jit(solution)/shard_map/ppermute | solution.py:37
  70.2 4.2 %collective-permute-done.17 = bf16[8,32,128]{2,1,0:T(8,128)(2,1)S(1)} collective-permute-done((bf16[8,32,128]{2,1,0:T(8,128)(2,1)S(1)}, bf16[8,32,128]{2,1,0:T(8,128)(2,1)S(1)}, u32[]{:S(2)}, u32[]{:S(2)}) %collective-permute-start.17) | collective-permute-done | bytes 65568 | tf_op jit(solution)/shard_map/ppermute | solution.py:37
  75.4 1.5 collective-permute-start.19
  80.7 1.0 adjoint_quarter2.5
  83.7 1.6 collective-permute-start.22
  85.2 5.5 %collective-permute-done.22.other = bf16[24,32,128]{2,1,0:T(8,128)(2,1)S(1)} collective-permute-done((bf16[24,32,128]{2,1,0:T(8,128)(2,1)S(1)}, bf16[24,32,128]{2,1,0:T(8,128)(2,1)S(1)}, u32[]{:S(2)}, u32[]{:S(2)}) %collective-permute-start.22) | collective-permute-done | bytes 196640 | tf_op jit(solution)/shard_map/ppermute | solution.py:37
  90.7 1.6 prior_adjoint.5
  93.9 1.2 prior_spread.6.refs_0_
  95.1 6.2 %collective-permute-start.25 = (bf16[24,32,128]{2,1,0:T(8,128)(2,1)S(1)}, bf16[24,32,128]{2,1,0:T(8,128)(2,1)S(1)}, u32[]{:S(2)}, u32[]{:S(2)}) collective-permute-start(bf16[24,32,128]{2,1,0:T(8,128)(2,1)S(1)} %prior_spread.6.refs_0_), channel_id=1, source_target_pairs={{0,8},{1,9},{2,10},{3,11},{4,12},{5,13},{6,14},{7,15},{8,0},{9,1},... | collective-permute-start | bytes 589832 | tf_op jit(solution)/shard_map/ppermute | solution.py:37
  101.3 1.3 forward_own.6.refs_1_
  102.6 1.2 forward_other.6
  103.8 2.4 %collective-permute-start.26 = (bf16[8,32,128]{2,1,0:T(8,128)(2,1)S(1)}, bf16[8,32,128]{2,1,0:T(8,128)(2,1)S(1)}, u32[]{:S(2)}, u32[]{:S(2)}) collective-permute-start(bf16[8,32,128]{2,1,0:T(8,128)(2,1)S(1)} %get-tuple-element.125), channel_id=1, source_target_pairs={{0,3},{1,2},{2,1},{3,0},{4,7},{5,6},{6,5},{7,4},{8,11},{9,10},{10,... | collective-permute-start | bytes 196616 | tf_op jit(solution)/shard_map/ppermute | solution.py:37
  109.1 2.5 %collective-permute-done.27 = bf16[8,32,128]{2,1,0:T(8,128)(2,1)S(1)} collective-permute-done((bf16[8,32,128]{2,1,0:T(8,128)(2,1)S(1)}, bf16[8,32,128]{2,1,0:T(8,128)(2,1)S(1)}, u32[]{:S(2)}, u32[]{:S(2)}) %collective-permute-start.27) | collective-permute-done | bytes 65568 | tf_op jit(solution)/shard_map/ppermute | solution.py:37
  111.7 3.0 %collective-permute-start.29 = (bf16[8,32,128]{2,1,0:T(8,128)(2,1)S(1)}, bf16[8,32,128]{2,1,0:T(8,128)(2,1)S(1)}, u32[]{:S(2)}, u32[]{:S(2)}) collective-permute-start(bf16[8,32,128]{2,1,0:T(8,128)(2,1)S(1)} %add_convert_fusion.5), channel_id=1, source_target_pairs={{0,4},{1,5},{2,6},{3,7},{4,0},{5,1},{6,2},{7,3},{8,12},{9,13},{10,... | collective-permute-start | bytes 196616 | tf_op jit(solution)/shard_map/ppermute | solution.py:37
  114.7 3.6 %collective-permute-done.29 = bf16[8,32,128]{2,1,0:T(8,128)(2,1)S(1)} collective-permute-done((bf16[8,32,128]{2,1,0:T(8,128)(2,1)S(1)}, bf16[8,32,128]{2,1,0:T(8,128)(2,1)S(1)}, u32[]{:S(2)}, u32[]{:S(2)}) %collective-permute-start.29) | collective-permute-done | bytes 65568 | tf_op jit(solution)/shard_map/ppermute | solution.py:37
  118.4 1.2 collective-permute-start.32
  119.6 1.5 collective-permute-start.31
  123.7 1.0 adjoint_quarter3.6.refs_1_
  124.8 1.3 adjoint_quarter2.6
  128.4 6.6 %collective-permute-done.34.other = bf16[24,32,128]{2,1,0:T(8,128)(2,1)S(1)} collective-permute-done((bf16[24,32,128]{2,1,0:T(8,128)(2,1)S(1)}, bf16[24,32,128]{2,1,0:T(8,128)(2,1)S(1)}, u32[]{:S(2)}, u32[]{:S(2)}) %collective-permute-start.34) | collective-permute-done | bytes 196640 | tf_op jit(solution)/shard_map/ppermute | solution.py:37
  135.0 1.6 prior_adjoint.6
  138.1 1.2 prior_spread.7.refs_0_
  139.4 6.3 %collective-permute-start.37 = (bf16[24,32,128]{2,1,0:T(8,128)(2,1)S(1)}, bf16[24,32,128]{2,1,0:T(8,128)(2,1)S(1)}, u32[]{:S(2)}, u32[]{:S(2)}) collective-permute-start(bf16[24,32,128]{2,1,0:T(8,128)(2,1)S(1)} %prior_spread.7.refs_0_), channel_id=1, source_target_pairs={{0,8},{1,9},{2,10},{3,11},{4,12},{5,13},{6,14},{7,15},{8,0},{9,1},... | collective-permute-start | bytes 589832 | tf_op jit(solution)/shard_map/ppermute | solution.py:37
  145.7 1.3 forward_own.7.refs_1_
  147.0 1.2 forward_other.7
  148.2 2.2 %collective-permute-start.38 = (bf16[8,32,128]{2,1,0:T(8,128)(2,1)S(1)}, bf16[8,32,128]{2,1,0:T(8,128)(2,1)S(1)}, u32[]{:S(2)}, u32[]{:S(2)}) collective-permute-start(bf16[8,32,128]{2,1,0:T(8,128)(2,1)S(1)} %get-tuple-element.133), channel_id=1, source_target_pairs={{0,3},{1,2},{2,1},{3,0},{4,7},{5,6},{6,5},{7,4},{8,11},{9,10},{10,... | collective-permute-start | bytes 196616 | tf_op jit(solution)/shard_map/ppermute | solution.py:37
  150.4 1.2 collective-permute-start.39
  153.4 2.5 %collective-permute-done.39 = bf16[8,32,128]{2,1,0:T(8,128)(2,1)S(1)} collective-permute-done((bf16[8,32,128]{2,1,0:T(8,128)(2,1)S(1)}, bf16[8,32,128]{2,1,0:T(8,128)(2,1)S(1)}, u32[]{:S(2)}, u32[]{:S(2)}) %collective-permute-start.39) | collective-permute-done | bytes 65568 | tf_op jit(solution)/shard_map/ppermute | solution.py:37
  156.1 3.3 %collective-permute-start.41 = (bf16[8,32,128]{2,1,0:T(8,128)(2,1)S(1)}, bf16[8,32,128]{2,1,0:T(8,128)(2,1)S(1)}, u32[]{:S(2)}, u32[]{:S(2)}) collective-permute-start(bf16[8,32,128]{2,1,0:T(8,128)(2,1)S(1)} %add_convert_fusion.4), channel_id=1, source_target_pairs={{0,4},{1,5},{2,6},{3,7},{4,0},{5,1},{6,2},{7,3},{8,12},{9,13},{10,... | collective-permute-start | bytes 196616 | tf_op jit(solution)/shard_map/ppermute | solution.py:37
  159.4 3.6 %collective-permute-done.41 = bf16[8,32,128]{2,1,0:T(8,128)(2,1)S(1)} collective-permute-done((bf16[8,32,128]{2,1,0:T(8,128)(2,1)S(1)}, bf16[8,32,128]{2,1,0:T(8,128)(2,1)S(1)}, u32[]{:S(2)}, u32[]{:S(2)}) %collective-permute-start.41) | collective-permute-done | bytes 65568 | tf_op jit(solution)/shard_map/ppermute | solution.py:37
  163.1 1.2 collective-permute-start.44
  164.8 1.9 collective-permute-start.42
  169.4 1.0 adjoint_quarter2.7
  173.1 6.2 %collective-permute-done.46.other = bf16[24,32,128]{2,1,0:T(8,128)(2,1)S(1)} collective-permute-done((bf16[24,32,128]{2,1,0:T(8,128)(2,1)S(1)}, bf16[24,32,128]{2,1,0:T(8,128)(2,1)S(1)}, u32[]{:S(2)}, u32[]{:S(2)}) %collective-permute-start.46) | collective-permute-done | bytes 196640 | tf_op jit(solution)/shard_map/ppermute | solution.py:37
  179.4 1.6 prior_adjoint.7
  181.7 2.2 %collective-permute-start.48 = (bf16[12,32,128]{2,1,0:T(8,128)(2,1)S(1)}, bf16[12,32,128]{2,1,0:T(8,128)(2,1)S(1)}, u32[]{:S(2)}, u32[]{:S(2)}) collective-permute-start(bf16[12,32,128]{2,1,0:T(8,128)(2,1)S(1)} %slice_select_fusion), channel_id=1, source_target_pairs={{0,8},{1,9},{2,10},{3,11},{4,12},{5,13},{6,14},{7,15},{8,0},{9,1},... | collective-permute-start | bytes 294920 | tf_op jit(solution)/shard_map/ppermute | solution.py:37
  185.0 1.6 collective-permute-start.49
  186.6 1.1 collective-permute-done.49
  (110 shorter events, 38.3 us)
Async XLA Ops:
  0.0 2.3 %copy-start = (f32[32,128]{1,0:T(8,128)S(1)}, f32[32,128]{1,0:T(8,128)}, u32[]{:S(2)}) copy-start(f32[32,128]{1,0:T(8,128)} %param.15) | copy-start | bytes 49156
  0.0 6.3 %copy-start.3 = (bf16[48,32,128]{2,1,0:T(8,128)(2,1)S(1)}, bf16[48,32,128]{2,1,0:T(8,128)(2,1)}, u32[]{:S(2)}) copy-start(bf16[48,32,128]{2,1,0:T(8,128)(2,1)} %refs_0_.1) | copy-start | bytes 1179652
  1.0 5.3 %collective-permute-start = (bf16[12,32,128]{2,1,0:T(8,128)(2,1)S(1)}, bf16[12,32,128]{2,1,0:T(8,128)(2,1)S(1)}, u32[]{:S(2)}, u32[]{:S(2)}) collective-permute-start(bf16[12,32,128]{2,1,0:T(8,128)(2,1)S(1)} %slice_select_fusion.2), channel_id=1, source_target_pairs={{1,8},{2,9},{3,10},{4,11},{5,12},{6,13},{7,14},{8,1},{9,2},{10,3},... | collective-permute-start | bytes 294920 | tf_op jit(solution)/shard_map/ppermute | solution.py:37
  2.4 9.4 %copy-start.2 = (bf16[1,1,384,128,128]{4,3,2,1,0:T(8,128)(2,1)S(1)}, bf16[1,1,384,128,128]{4,3,2,1,0:T(8,128)(2,1)}, u32[]{:S(2)}) copy-start(bf16[1,1,384,128,128]{4,3,2,1,0:T(8,128)(2,1)} %param.11) | copy-start | bytes 37748740
  7.4 5.7 %collective-permute-start.1 = (bf16[24,32,128]{2,1,0:T(8,128)(2,1)S(1)}, bf16[24,32,128]{2,1,0:T(8,128)(2,1)S(1)}, u32[]{:S(2)}, u32[]{:S(2)}) collective-permute-start(bf16[24,32,128]{2,1,0:T(8,128)(2,1)S(1)} %prior_spread.4.refs_0_), channel_id=1, source_target_pairs={{0,8},{1,9},{2,10},{3,11},{4,12},{5,13},{6,14},{7,15},{8,0},{9,1},... | collective-permute-start | bytes 589832 | tf_op jit(solution)/shard_map/ppermute | solution.py:37
  14.3 8.2 %collective-permute-start.2 = (bf16[8,32,128]{2,1,0:T(8,128)(2,1)S(1)}, bf16[8,32,128]{2,1,0:T(8,128)(2,1)S(1)}, u32[]{:S(2)}, u32[]{:S(2)}) collective-permute-start(bf16[8,32,128]{2,1,0:T(8,128)(2,1)S(1)} %get-tuple-element.84), channel_id=1, source_target_pairs={{0,3},{1,2},{2,1},{3,0},{4,7},{5,6},{6,5},{7,4},{8,11},{9,10},{10,... | collective-permute-start | bytes 196616 | tf_op jit(solution)/shard_map/ppermute | solution.py:37
  16.3 6.2 %collective-permute-start.3 = (bf16[8,32,128]{2,1,0:T(8,128)(2,1)S(1)}, bf16[8,32,128]{2,1,0:T(8,128)(2,1)S(1)}, u32[]{:S(2)}, u32[]{:S(2)}) collective-permute-start(bf16[8,32,128]{2,1,0:T(8,128)(2,1)S(1)} %get-tuple-element.85), channel_id=1, source_target_pairs={{0,2},{1,3},{2,0},{3,1},{4,6},{5,7},{6,4},{7,5},{8,10},{9,11},{10,... | collective-permute-start | bytes 196616 | tf_op jit(solution)/shard_map/ppermute | solution.py:37
  16.5 6.0 %collective-permute-start.4 = (bf16[8,32,128]{2,1,0:T(8,128)(2,1)S(1)}, bf16[8,32,128]{2,1,0:T(8,128)(2,1)S(1)}, u32[]{:S(2)}, u32[]{:S(2)}) collective-permute-start(bf16[8,32,128]{2,1,0:T(8,128)(2,1)S(1)} %get-tuple-element.86), channel_id=1, source_target_pairs={{0,1},{1,0},{2,3},{3,2},{4,5},{5,4},{6,7},{7,6},{8,9},{9,8},{10,11... | collective-permute-start | bytes 196616 | tf_op jit(solution)/shard_map/ppermute | solution.py:37
  22.6 6.9 %collective-permute-start.5 = (bf16[8,32,128]{2,1,0:T(8,128)(2,1)S(1)}, bf16[8,32,128]{2,1,0:T(8,128)(2,1)S(1)}, u32[]{:S(2)}, u32[]{:S(2)}) collective-permute-start(bf16[8,32,128]{2,1,0:T(8,128)(2,1)S(1)} %convert_add_fusion.1), channel_id=1, source_target_pairs={{0,4},{1,5},{2,6},{3,7},{4,0},{5,1},{6,2},{7,3},{8,12},{9,13},{10,... | collective-permute-start | bytes 196616 | tf_op jit(solution)/shard_map/ppermute | solution.py:37
  29.6 5.8 %collective-permute-start.8 = (bf16[8,32,128]{2,1,0:T(8,128)(2,1)S(1)}, bf16[8,32,128]{2,1,0:T(8,128)(2,1)S(1)}, u32[]{:S(2)}, u32[]{:S(2)}) collective-permute-start(bf16[8,32,128]{2,1,0:T(8,128)(2,1)S(1)} %multiply_convert_fusion.3.refs_0_), channel_id=1, source_target_pairs={{0,3},{1,2},{2,1},{3,0},{4,7},{5,6},{6,5},{7,4},{8,11},{9,10},{10,... | collective-permute-start | bytes 196616 | tf_op jit(solution)/shard_map/ppermute | solution.py:37
  31.1 5.3 %collective-permute-start.7 = (bf16[8,32,128]{2,1,0:T(8,128)(2,1)S(1)}, bf16[8,32,128]{2,1,0:T(8,128)(2,1)S(1)}, u32[]{:S(2)}, u32[]{:S(2)}) collective-permute-start(bf16[8,32,128]{2,1,0:T(8,128)(2,1)S(1)} %multiply_convert_fusion.3.refs_0_), channel_id=1, source_target_pairs={{0,2},{1,3},{2,0},{3,1},{4,6},{5,7},{6,4},{7,5},{8,10},{9,11},{10,... | collective-permute-start | bytes 196616 | tf_op jit(solution)/shard_map/ppermute | solution.py:37
  32.3 5.1 %collective-permute-start.6 = (bf16[8,32,128]{2,1,0:T(8,128)(2,1)S(1)}, bf16[8,32,128]{2,1,0:T(8,128)(2,1)S(1)}, u32[]{:S(2)}, u32[]{:S(2)}) collective-permute-start(bf16[8,32,128]{2,1,0:T(8,128)(2,1)S(1)} %multiply_convert_fusion.3.refs_0_), channel_id=1, source_target_pairs={{0,1},{1,0},{2,3},{3,2},{4,5},{5,4},{6,7},{7,6},{8,9},{9,8},{10,11... | collective-permute-start | bytes 196616 | tf_op jit(solution)/shard_map/ppermute | solution.py:37
  37.9 1.5 collective-permute-start.9
  39.4 7.0 %collective-permute-start.10 = (bf16[24,32,128]{2,1,0:T(8,128)(2,1)S(1)}, bf16[24,32,128]{2,1,0:T(8,128)(2,1)S(1)}, u32[]{:S(2)}, u32[]{:S(2)}) collective-permute-start(bf16[24,32,128]{2,1,0:T(8,128)(2,1)S(1)} %add_convert_fusion.3.mine), channel_id=1, source_target_pairs={{0,16},{1,17},{2,18},{3,19},{4,20},{5,21},{6,22},{7,23},{8,24},{9,... | collective-permute-start | bytes 589832 | tf_op jit(solution)/shard_map/ppermute | solution.py:37
  48.2 1.5 collective-permute-start.11
  48.3 1.4 collective-permute-start.12
  51.0 7.7 %collective-permute-start.13 = (bf16[24,32,128]{2,1,0:T(8,128)(2,1)S(1)}, bf16[24,32,128]{2,1,0:T(8,128)(2,1)S(1)}, u32[]{:S(2)}, u32[]{:S(2)}) collective-permute-start(bf16[24,32,128]{2,1,0:T(8,128)(2,1)S(1)} %prior_spread.5.refs_0_), channel_id=1, source_target_pairs={{0,8},{1,9},{2,10},{3,11},{4,12},{5,13},{6,14},{7,15},{8,0},{9,1},... | collective-permute-start | bytes 589832 | tf_op jit(solution)/shard_map/ppermute | solution.py:37
  60.0 5.2 %collective-permute-start.14 = (bf16[8,32,128]{2,1,0:T(8,128)(2,1)S(1)}, bf16[8,32,128]{2,1,0:T(8,128)(2,1)S(1)}, u32[]{:S(2)}, u32[]{:S(2)}) collective-permute-start(bf16[8,32,128]{2,1,0:T(8,128)(2,1)S(1)} %get-tuple-element.117), channel_id=1, source_target_pairs={{0,3},{1,2},{2,1},{3,0},{4,7},{5,6},{6,5},{7,4},{8,11},{9,10},{10,... | collective-permute-start | bytes 196616 | tf_op jit(solution)/shard_map/ppermute | solution.py:37
  62.1 5.6 %collective-permute-start.15 = (bf16[8,32,128]{2,1,0:T(8,128)(2,1)S(1)}, bf16[8,32,128]{2,1,0:T(8,128)(2,1)S(1)}, u32[]{:S(2)}, u32[]{:S(2)}) collective-permute-start(bf16[8,32,128]{2,1,0:T(8,128)(2,1)S(1)} %get-tuple-element.118), channel_id=1, source_target_pairs={{0,2},{1,3},{2,0},{3,1},{4,6},{5,7},{6,4},{7,5},{8,10},{9,11},{10,... | collective-permute-start | bytes 196616 | tf_op jit(solution)/shard_map/ppermute | solution.py:37
  63.4 4.4 %collective-permute-start.16 = (bf16[8,32,128]{2,1,0:T(8,128)(2,1)S(1)}, bf16[8,32,128]{2,1,0:T(8,128)(2,1)S(1)}, u32[]{:S(2)}, u32[]{:S(2)}) collective-permute-start(bf16[8,32,128]{2,1,0:T(8,128)(2,1)S(1)} %get-tuple-element.119), channel_id=1, source_target_pairs={{0,1},{1,0},{2,3},{3,2},{4,5},{5,4},{6,7},{7,6},{8,9},{9,8},{10,11... | collective-permute-start | bytes 196616 | tf_op jit(solution)/shard_map/ppermute | solution.py:37
  67.8 6.5 %collective-permute-start.17 = (bf16[8,32,128]{2,1,0:T(8,128)(2,1)S(1)}, bf16[8,32,128]{2,1,0:T(8,128)(2,1)S(1)}, u32[]{:S(2)}, u32[]{:S(2)}) collective-permute-start(bf16[8,32,128]{2,1,0:T(8,128)(2,1)S(1)} %add_convert_fusion.6), channel_id=1, source_target_pairs={{0,4},{1,5},{2,6},{3,7},{4,0},{5,1},{6,2},{7,3},{8,12},{9,13},{10,... | collective-permute-start | bytes 196616 | tf_op jit(solution)/shard_map/ppermute | solution.py:37
  74.4 5.2 %collective-permute-start.20 = (bf16[8,32,128]{2,1,0:T(8,128)(2,1)S(1)}, bf16[8,32,128]{2,1,0:T(8,128)(2,1)S(1)}, u32[]{:S(2)}, u32[]{:S(2)}) collective-permute-start(bf16[8,32,128]{2,1,0:T(8,128)(2,1)S(1)} %multiply_convert_fusion.2.refs_0_), channel_id=1, source_target_pairs={{0,3},{1,2},{2,1},{3,0},{4,7},{5,6},{6,5},{7,4},{8,11},{9,10},{10,... | collective-permute-start | bytes 196616 | tf_op jit(solution)/shard_map/ppermute | solution.py:37
  75.4 5.3 %collective-permute-start.19 = (bf16[8,32,128]{2,1,0:T(8,128)(2,1)S(1)}, bf16[8,32,128]{2,1,0:T(8,128)(2,1)S(1)}, u32[]{:S(2)}, u32[]{:S(2)}) collective-permute-start(bf16[8,32,128]{2,1,0:T(8,128)(2,1)S(1)} %multiply_convert_fusion.2.refs_0_), channel_id=1, source_target_pairs={{0,2},{1,3},{2,0},{3,1},{4,6},{5,7},{6,4},{7,5},{8,10},{9,11},{10,... | collective-permute-start | bytes 196616 | tf_op jit(solution)/shard_map/ppermute | solution.py:37
  76.9 4.8 %collective-permute-start.18 = (bf16[8,32,128]{2,1,0:T(8,128)(2,1)S(1)}, bf16[8,32,128]{2,1,0:T(8,128)(2,1)S(1)}, u32[]{:S(2)}, u32[]{:S(2)}) collective-permute-start(bf16[8,32,128]{2,1,0:T(8,128)(2,1)S(1)} %multiply_convert_fusion.2.refs_0_), channel_id=1, source_target_pairs={{0,1},{1,0},{2,3},{3,2},{4,5},{5,4},{6,7},{7,6},{8,9},{9,8},{10,11... | collective-permute-start | bytes 196616 | tf_op jit(solution)/shard_map/ppermute | solution.py:37
  82.1 1.5 collective-permute-start.21
  83.7 7.0 %collective-permute-start.22 = (bf16[24,32,128]{2,1,0:T(8,128)(2,1)S(1)}, bf16[24,32,128]{2,1,0:T(8,128)(2,1)S(1)}, u32[]{:S(2)}, u32[]{:S(2)}) collective-permute-start(bf16[24,32,128]{2,1,0:T(8,128)(2,1)S(1)} %add_convert_fusion.2.mine), channel_id=1, source_target_pairs={{0,16},{1,17},{2,18},{3,19},{4,20},{5,21},{6,22},{7,23},{8,24},{9,... | collective-permute-start | bytes 589832 | tf_op jit(solution)/shard_map/ppermute | solution.py:37
  92.3 1.5 collective-permute-start.23
  92.4 1.4 collective-permute-start.24
  95.1 7.5 %collective-permute-start.25 = (bf16[24,32,128]{2,1,0:T(8,128)(2,1)S(1)}, bf16[24,32,128]{2,1,0:T(8,128)(2,1)S(1)}, u32[]{:S(2)}, u32[]{:S(2)}) collective-permute-start(bf16[24,32,128]{2,1,0:T(8,128)(2,1)S(1)} %prior_spread.6.refs_0_), channel_id=1, source_target_pairs={{0,8},{1,9},{2,10},{3,11},{4,12},{5,13},{6,14},{7,15},{8,0},{9,1},... | collective-permute-start | bytes 589832 | tf_op jit(solution)/shard_map/ppermute | solution.py:37
  103.8 5.2 %collective-permute-start.26 = (bf16[8,32,128]{2,1,0:T(8,128)(2,1)S(1)}, bf16[8,32,128]{2,1,0:T(8,128)(2,1)S(1)}, u32[]{:S(2)}, u32[]{:S(2)}) collective-permute-start(bf16[8,32,128]{2,1,0:T(8,128)(2,1)S(1)} %get-tuple-element.125), channel_id=1, source_target_pairs={{0,3},{1,2},{2,1},{3,0},{4,7},{5,6},{6,5},{7,4},{8,11},{9,10},{10,... | collective-permute-start | bytes 196616 | tf_op jit(solution)/shard_map/ppermute | solution.py:37
  106.3 5.3 %collective-permute-start.27 = (bf16[8,32,128]{2,1,0:T(8,128)(2,1)S(1)}, bf16[8,32,128]{2,1,0:T(8,128)(2,1)S(1)}, u32[]{:S(2)}, u32[]{:S(2)}) collective-permute-start(bf16[8,32,128]{2,1,0:T(8,128)(2,1)S(1)} %get-tuple-element.126), channel_id=1, source_target_pairs={{0,2},{1,3},{2,0},{3,1},{4,6},{5,7},{6,4},{7,5},{8,10},{9,11},{10,... | collective-permute-start | bytes 196616 | tf_op jit(solution)/shard_map/ppermute | solution.py:37
  107.3 4.4 %collective-permute-start.28 = (bf16[8,32,128]{2,1,0:T(8,128)(2,1)S(1)}, bf16[8,32,128]{2,1,0:T(8,128)(2,1)S(1)}, u32[]{:S(2)}, u32[]{:S(2)}) collective-permute-start(bf16[8,32,128]{2,1,0:T(8,128)(2,1)S(1)} %get-tuple-element.127), channel_id=1, source_target_pairs={{0,1},{1,0},{2,3},{3,2},{4,5},{5,4},{6,7},{7,6},{8,9},{9,8},{10,11... | collective-permute-start | bytes 196616 | tf_op jit(solution)/shard_map/ppermute | solution.py:37
  111.7 6.6 %collective-permute-start.29 = (bf16[8,32,128]{2,1,0:T(8,128)(2,1)S(1)}, bf16[8,32,128]{2,1,0:T(8,128)(2,1)S(1)}, u32[]{:S(2)}, u32[]{:S(2)}) collective-permute-start(bf16[8,32,128]{2,1,0:T(8,128)(2,1)S(1)} %add_convert_fusion.5), channel_id=1, source_target_pairs={{0,4},{1,5},{2,6},{3,7},{4,0},{5,1},{6,2},{7,3},{8,12},{9,13},{10,... | collective-permute-start | bytes 196616 | tf_op jit(solution)/shard_map/ppermute | solution.py:37
  118.4 5.3 %collective-permute-start.32 = (bf16[8,32,128]{2,1,0:T(8,128)(2,1)S(1)}, bf16[8,32,128]{2,1,0:T(8,128)(2,1)S(1)}, u32[]{:S(2)}, u32[]{:S(2)}) collective-permute-start(bf16[8,32,128]{2,1,0:T(8,128)(2,1)S(1)} %multiply_convert_fusion.1.refs_0_), channel_id=1, source_target_pairs={{0,3},{1,2},{2,1},{3,0},{4,7},{5,6},{6,5},{7,4},{8,11},{9,10},{10,... | collective-permute-start | bytes 196616 | tf_op jit(solution)/shard_map/ppermute | solution.py:37
  119.6 5.2 %collective-permute-start.31 = (bf16[8,32,128]{2,1,0:T(8,128)(2,1)S(1)}, bf16[8,32,128]{2,1,0:T(8,128)(2,1)S(1)}, u32[]{:S(2)}, u32[]{:S(2)}) collective-permute-start(bf16[8,32,128]{2,1,0:T(8,128)(2,1)S(1)} %multiply_convert_fusion.1.refs_0_), channel_id=1, source_target_pairs={{0,2},{1,3},{2,0},{3,1},{4,6},{5,7},{6,4},{7,5},{8,10},{9,11},{10,... | collective-permute-start | bytes 196616 | tf_op jit(solution)/shard_map/ppermute | solution.py:37
  121.1 5.0 %collective-permute-start.30 = (bf16[8,32,128]{2,1,0:T(8,128)(2,1)S(1)}, bf16[8,32,128]{2,1,0:T(8,128)(2,1)S(1)}, u32[]{:S(2)}, u32[]{:S(2)}) collective-permute-start(bf16[8,32,128]{2,1,0:T(8,128)(2,1)S(1)} %multiply_convert_fusion.1.refs_0_), channel_id=1, source_target_pairs={{0,1},{1,0},{2,3},{3,2},{4,5},{5,4},{6,7},{7,6},{8,9},{9,8},{10,11... | collective-permute-start | bytes 196616 | tf_op jit(solution)/shard_map/ppermute | solution.py:37
  126.4 1.5 collective-permute-start.33
  128.0 7.0 %collective-permute-start.34 = (bf16[24,32,128]{2,1,0:T(8,128)(2,1)S(1)}, bf16[24,32,128]{2,1,0:T(8,128)(2,1)S(1)}, u32[]{:S(2)}, u32[]{:S(2)}) collective-permute-start(bf16[24,32,128]{2,1,0:T(8,128)(2,1)S(1)} %add_convert_fusion.1.mine), channel_id=1, source_target_pairs={{0,16},{1,17},{2,18},{3,19},{4,20},{5,21},{6,22},{7,23},{8,24},{9,... | collective-permute-start | bytes 589832 | tf_op jit(solution)/shard_map/ppermute | solution.py:37
  136.6 1.5 collective-permute-start.35
  136.7 1.4 collective-permute-start.36
  139.4 7.5 %collective-permute-start.37 = (bf16[24,32,128]{2,1,0:T(8,128)(2,1)S(1)}, bf16[24,32,128]{2,1,0:T(8,128)(2,1)S(1)}, u32[]{:S(2)}, u32[]{:S(2)}) collective-permute-start(bf16[24,32,128]{2,1,0:T(8,128)(2,1)S(1)} %prior_spread.7.refs_0_), channel_id=1, source_target_pairs={{0,8},{1,9},{2,10},{3,11},{4,12},{5,13},{6,14},{7,15},{8,0},{9,1},... | collective-permute-start | bytes 589832 | tf_op jit(solution)/shard_map/ppermute | solution.py:37
  148.2 5.2 %collective-permute-start.38 = (bf16[8,32,128]{2,1,0:T(8,128)(2,1)S(1)}, bf16[8,32,128]{2,1,0:T(8,128)(2,1)S(1)}, u32[]{:S(2)}, u32[]{:S(2)}) collective-permute-start(bf16[8,32,128]{2,1,0:T(8,128)(2,1)S(1)} %get-tuple-element.133), channel_id=1, source_target_pairs={{0,3},{1,2},{2,1},{3,0},{4,7},{5,6},{6,5},{7,4},{8,11},{9,10},{10,... | collective-permute-start | bytes 196616 | tf_op jit(solution)/shard_map/ppermute | solution.py:37
  150.4 5.5 %collective-permute-start.39 = (bf16[8,32,128]{2,1,0:T(8,128)(2,1)S(1)}, bf16[8,32,128]{2,1,0:T(8,128)(2,1)S(1)}, u32[]{:S(2)}, u32[]{:S(2)}) collective-permute-start(bf16[8,32,128]{2,1,0:T(8,128)(2,1)S(1)} %get-tuple-element.134), channel_id=1, source_target_pairs={{0,2},{1,3},{2,0},{3,1},{4,6},{5,7},{6,4},{7,5},{8,10},{9,11},{10,... | collective-permute-start | bytes 196616 | tf_op jit(solution)/shard_map/ppermute | solution.py:37
  151.7 4.4 %collective-permute-start.40 = (bf16[8,32,128]{2,1,0:T(8,128)(2,1)S(1)}, bf16[8,32,128]{2,1,0:T(8,128)(2,1)S(1)}, u32[]{:S(2)}, u32[]{:S(2)}) collective-permute-start(bf16[8,32,128]{2,1,0:T(8,128)(2,1)S(1)} %get-tuple-element.135), channel_id=1, source_target_pairs={{0,1},{1,0},{2,3},{3,2},{4,5},{5,4},{6,7},{7,6},{8,9},{9,8},{10,11... | collective-permute-start | bytes 196616 | tf_op jit(solution)/shard_map/ppermute | solution.py:37
  156.1 7.0 %collective-permute-start.41 = (bf16[8,32,128]{2,1,0:T(8,128)(2,1)S(1)}, bf16[8,32,128]{2,1,0:T(8,128)(2,1)S(1)}, u32[]{:S(2)}, u32[]{:S(2)}) collective-permute-start(bf16[8,32,128]{2,1,0:T(8,128)(2,1)S(1)} %add_convert_fusion.4), channel_id=1, source_target_pairs={{0,4},{1,5},{2,6},{3,7},{4,0},{5,1},{6,2},{7,3},{8,12},{9,13},{10,... | collective-permute-start | bytes 196616 | tf_op jit(solution)/shard_map/ppermute | solution.py:37
  163.1 5.2 %collective-permute-start.44 = (bf16[8,32,128]{2,1,0:T(8,128)(2,1)S(1)}, bf16[8,32,128]{2,1,0:T(8,128)(2,1)S(1)}, u32[]{:S(2)}, u32[]{:S(2)}) collective-permute-start(bf16[8,32,128]{2,1,0:T(8,128)(2,1)S(1)} %multiply_convert_fusion.refs_0_), channel_id=1, source_target_pairs={{0,3},{1,2},{2,1},{3,0},{4,7},{5,6},{6,5},{7,4},{8,11},{9,10},{10,... | collective-permute-start | bytes 196616 | tf_op jit(solution)/shard_map/ppermute | solution.py:37
  164.3 5.1 %collective-permute-start.43 = (bf16[8,32,128]{2,1,0:T(8,128)(2,1)S(1)}, bf16[8,32,128]{2,1,0:T(8,128)(2,1)S(1)}, u32[]{:S(2)}, u32[]{:S(2)}) collective-permute-start(bf16[8,32,128]{2,1,0:T(8,128)(2,1)S(1)} %multiply_convert_fusion.refs_0_), channel_id=1, source_target_pairs={{0,2},{1,3},{2,0},{3,1},{4,6},{5,7},{6,4},{7,5},{8,10},{9,11},{10,... | collective-permute-start | bytes 196616 | tf_op jit(solution)/shard_map/ppermute | solution.py:37
  164.8 5.7 %collective-permute-start.42 = (bf16[8,32,128]{2,1,0:T(8,128)(2,1)S(1)}, bf16[8,32,128]{2,1,0:T(8,128)(2,1)S(1)}, u32[]{:S(2)}, u32[]{:S(2)}) collective-permute-start(bf16[8,32,128]{2,1,0:T(8,128)(2,1)S(1)} %multiply_convert_fusion.refs_0_), channel_id=1, source_target_pairs={{0,1},{1,0},{2,3},{3,2},{4,5},{5,4},{6,7},{7,6},{8,9},{9,8},{10,11... | collective-permute-start | bytes 196616 | tf_op jit(solution)/shard_map/ppermute | solution.py:37
  170.4 18.1 %copy-start.1 = (f32[32,128]{1,0:T(8,128)S(1)}, f32[32,128]{1,0:T(8,128)}, u32[]{:S(2)}) copy-start(f32[32,128]{1,0:T(8,128)} %param.15) | copy-start | bytes 49156
  170.8 1.5 collective-permute-start.45
  172.4 7.0 %collective-permute-start.46 = (bf16[24,32,128]{2,1,0:T(8,128)(2,1)S(1)}, bf16[24,32,128]{2,1,0:T(8,128)(2,1)S(1)}, u32[]{:S(2)}, u32[]{:S(2)}) collective-permute-start(bf16[24,32,128]{2,1,0:T(8,128)(2,1)S(1)} %add_convert_fusion.mine), channel_id=1, source_target_pairs={{0,16},{1,17},{2,18},{3,19},{4,20},{5,21},{6,22},{7,23},{8,24},{9,... | collective-permute-start | bytes 589832 | tf_op jit(solution)/shard_map/ppermute | solution.py:37
  181.0 2.9 %collective-permute-start.47 = (bf16[12,32,128]{2,1,0:T(8,128)(2,1)S(1)}, bf16[12,32,128]{2,1,0:T(8,128)(2,1)S(1)}, u32[]{:S(2)}, u32[]{:S(2)}) collective-permute-start(bf16[12,32,128]{2,1,0:T(8,128)(2,1)S(1)} %slice_select_fusion.1), channel_id=1, source_target_pairs={{1,8},{2,9},{3,10},{4,11},{5,12},{6,13},{7,14},{8,1},{9,2},{10,3},... | collective-permute-start | bytes 294920 | tf_op jit(solution)/shard_map/ppermute | solution.py:37
  181.7 3.1 %collective-permute-start.48 = (bf16[12,32,128]{2,1,0:T(8,128)(2,1)S(1)}, bf16[12,32,128]{2,1,0:T(8,128)(2,1)S(1)}, u32[]{:S(2)}, u32[]{:S(2)}) collective-permute-start(bf16[12,32,128]{2,1,0:T(8,128)(2,1)S(1)} %slice_select_fusion), channel_id=1, source_target_pairs={{0,8},{1,9},{2,10},{3,11},{4,12},{5,13},{6,14},{7,15},{8,0},{9,1},... | collective-permute-start | bytes 294920 | tf_op jit(solution)/shard_map/ppermute | solution.py:37
  185.0 2.7 %collective-permute-start.49 = (bf16[24,32,128]{2,1,0:T(8,128)(2,1)S(1)}, bf16[24,32,128]{2,1,0:T(8,128)(2,1)S(1)}, u32[]{:S(2)}, u32[]{:S(2)}) collective-permute-start(bf16[24,32,128]{2,1,0:T(8,128)(2,1)S(1)} %fusion), channel_id=1, source_target_pairs={{0,8},{1,9},{2,10},{3,11},{4,12},{5,13},{6,14},{7,15},{8,0},{9,1},... | collective-permute-start | bytes 589832 | tf_op jit(solution)/shard_map/ppermute | solution.py:37

commit v12 on v11

--- a/solution.py
+++ b/solution.py
@@ -13,8 +13,8 @@
 HALF = jnp.bfloat16
 VMEM_LIMIT = 8 * 2**20
 LANES = 128
-FORWARD_PLANS = ((2, 42), (2, 42), (2, 28))
-ADJOINT_PLANS = ((2, 32), (2, 32), (2, 32), (2, 18), (2, 18))
+FORWARD_PLANS = ((2, 45), (2, 45), (2, 29))
+ADJOINT_PLANS = ((2, 35), (2, 35), (2, 35), (2, 19), (2, 19))
 PRIOR_PLAN = (2, 56)
 
 
@@ -371,7 +371,7 @@
         field[pl.ds(reach * (1 - side), inner)] = probes[pl.ds(reach * side, inner)]
         field[pl.ds(inner * side, reach)] = beyond[...]
     else:
-        ext, from_core, from_far = refs[:3]
+        ext, from_far, from_core = refs[:3]
         for begin, update in ((tiles * (1 - side), from_core), (tiles * side, from_far)):
             at = pl.ds(begin, tiles)
             field[at] = (ext[at] + update[...].astype(F32)).astype(HALF)
@@ -508,8 +508,7 @@
                 mine = (mine.astype(F32) + other.astype(F32)).astype(HALF)
         ext, to_core, to_far = gather_tiles(nbr, prior_lists, mine, other, prior_turned, rows)
         if step < STEPS - 1:
-            from_far = swap_far(to_far)
-            fields = (ext, swap_core(to_core), from_far)
+            fields = (ext, swap_far(to_far), swap_core(to_core))
     lower = side == 0
     from_core = swap_core(jnp.where(lower, to_core[half - reach :], to_core[:reach])).astype(F32)
     from_far = swap_far(jnp.where(lower, to_far[:reach], to_far[half - reach :])).astype(F32)

time: 190 us -> 188 us (0.989)
  waiting for transfers between devices: 53.8 us -> 46.8 us
  starting transfers between devices: 75.8 us -> 79.2 us
  Pallas kernels: 55 us -> 57.3 us
    ppermute x50, waiting for transfers between devices: 53.8 us -> 46.8 us  [exchange(): return lax.ppermute(value, ('obs', 'flux'), route)]
    ppermute x50, starting transfers between devices: 75.8 us -> 79.2 us  [exchange(): return lax.ppermute(value, ('obs', 'flux'), route)]
    pallas_call x32, Pallas kernels: 30.8 us -> 33 us  [jac_pass(): pl.pallas_call(functools.partial(jac_kernel, plan, sizes, len(parts), beg...]
  transfers between devices with their start and end apart: 50 -> 50, of which waited for: 30 -> 32; matrix products, arithmetic and copies ran while one was open for 0% -> 0% of each run, Pallas kernels for 20% -> 20%
where the time goes in v12:
time: 188 us; the launch traced here: 187 us
  starting transfers between devices  79.2 us (42%)
  Pallas kernels  57.3 us (30%)
  waiting for transfers between devices  46.8 us (25%)
  other arithmetic  2.46 us (1%)
    ppermute x50, starting transfers between devices, exchange(): return lax.ppermute(value, ('obs', 'flux'), route)  79.2 us
    ppermute x50, waiting for transfers between devices, exchange(): return lax.ppermute(value, ('obs', 'flux'), route)  46.8 us
    pallas_call x32, Pallas kernels, jac_pass(): pl.pallas_call(functools.partial(jac_kernel, plan, sizes, len(parts), beg...  33 us
    pallas_call x4, Pallas kernels, gather_tiles(): pl.pallas_call(functools.partial(gather_kernel, rows, plan_sizes(PRIOR_PL...  6.68 us
    pallas_call x2, Pallas kernels, turn_blocks(): pl.pallas_call(functools.partial(turn_kernel, chunk_of(plain.shape[0], 48...  5.5 us
    pallas_call x4, Pallas kernels, spread_tiles(): pl.pallas_call(functools.partial(spread_kernel, len(fields) == 2, prior.s...  4.82 us
    pallas_call x1, Pallas kernels, setup(): pl.pallas_call(functools.partial(setup_kernel, rows, chunk), in_specs=[sm...  3.92 us
  transfers between devices with their start and end apart: 50, of which 32 were waited for; matrix products, arithmetic and copies ran while one was open for 0% of the time, Pallas kernels for 20%

profile of v12, /device:TPU:0, one launch (start us, length us, event | category | flops | bytes accessed | tf_op | source)
XLA Modules:
  0.0 187.1 jit_solution(15773864843566947836)
XLA Ops:
  2.5 3.9 %setup.1 = (bf16[192,128,128]{2,1,0:T(8,128)(2,1)S(1)}, s32[1,384]{1,0:T(1,128)S(1)}, s32[1,384]{1,0:T(1,128)S(1)}, s32[1,384]{1,0:T(1,128)S(1)}, s32[1,1664]{1,...) custom-call(s32[4]{0:T(128)S(1)} %pad_add_fusion.where, s32[1,384]{1,0:T(1,128)} %bitcast.32, ...), custom_call_target="tpu_custom_call" | custom-call | tf_op jit(solution)/shard_map/setup/pallas_call | solution.py:204
  6.4 1.1 prior_spread.4.refs_0_
  7.5 4.4 %collective-permute-start.1 = (bf16[24,32,128]{2,1,0:T(8,128)(2,1)S(1)}, bf16[24,32,128]{2,1,0:T(8,128)(2,1)S(1)}, u32[]{:S(2)}, u32[]{:S(2)}) collective-permute-start(bf16[24,32,128]{2,1,0:T(8,128)(2,1)S(1)} %prior_spread.4.refs_0_), channel_id=1, source_target_pairs={{0,8},{1,9},{2,10},{3,11},{4,12},{5,13},{6,14},{7,15},{8,0},{9,1},... | collective-permute-start | bytes 589832 | tf_op jit(solution)/shard_map/ppermute | solution.py:37
  11.9 1.3 forward_own.4.refs_1_
  13.2 1.3 forward_other.4
  14.5 2.6 %collective-permute-start.2 = (bf16[8,32,128]{2,1,0:T(8,128)(2,1)S(1)}, bf16[8,32,128]{2,1,0:T(8,128)(2,1)S(1)}, u32[]{:S(2)}, u32[]{:S(2)}) collective-permute-start(bf16[8,32,128]{2,1,0:T(8,128)(2,1)S(1)} %get-tuple-element.84), channel_id=1, source_target_pairs={{0,3},{1,2},{2,1},{3,0},{4,7},{5,6},{6,5},{7,4},{8,11},{9,10},{10,... | collective-permute-start | bytes 196616 | tf_op jit(solution)/shard_map/ppermute | solution.py:37
  18.1 3.7 %jac_turn.1.refs_1_.refs_2_ = bf16[384,128,128]{2,1,0:T(8,128)(2,1)S(1)} custom-call(bf16[384,128,128]{2,1,0:T(8,128)(2,1)S(1)} %bitcast.15), custom_call_target="tpu_custom_call" | custom-call | bytes 12582912 | tf_op jit(solution)/shard_map/jac_turn/pallas_call | solution.py:180
  22.8 3.2 %collective-permute-start.5 = (bf16[8,32,128]{2,1,0:T(8,128)(2,1)S(1)}, bf16[8,32,128]{2,1,0:T(8,128)(2,1)S(1)}, u32[]{:S(2)}, u32[]{:S(2)}) collective-permute-start(bf16[8,32,128]{2,1,0:T(8,128)(2,1)S(1)} %convert_add_fusion.1), channel_id=1, source_target_pairs={{0,4},{1,5},{2,6},{3,7},{4,0},{5,1},{6,2},{7,3},{8,12},{9,13},{10,... | collective-permute-start | bytes 196616 | tf_op jit(solution)/shard_map/ppermute | solution.py:37
  26.0 3.4 %late_plans.1 = (s32[1,1280]{1,0:T(1,128)S(4)}, s32[1,1280]{1,0:T(1,128)S(4)}, s32[1,1280]{1,0:T(1,128)S(4)}, s32[1,1280]{1,0:T(1,128)S(4)}, s32[1,1280]{1,0:T(1,128)S(4)}, /*index=5*/s32[1,1664]{1,0:T(1,128)S(4)}) custom-call(s32[1,512]{1,0:T(1,128)S(4)} %get-tuple-element.75.nbr, s32[1,384]{1,0:T(1,128)S(1)} %get-tuple-element.92.obs_row, ...), custom_call_target="tpu_custom_call" | custom-call | bytes 8388608 | tf_op jit(solution)/shard_map/late_plans/pallas_call | solution.py:256
  30.7 2.0 %collective-permute-start.7 = (bf16[8,32,128]{2,1,0:T(8,128)(2,1)S(1)}, bf16[8,32,128]{2,1,0:T(8,128)(2,1)S(1)}, u32[]{:S(2)}, u32[]{:S(2)}) collective-permute-start(bf16[8,32,128]{2,1,0:T(8,128)(2,1)S(1)} %multiply_convert_fusion.3.refs_0_), channel_id=1, source_target_pairs={{0,2},{1,3},{2,0},{3,1},{4,6},{5,7},{6,4},{7,5},{8,10},{9,11},{10,... | collective-permute-start | bytes 196616 | tf_op jit(solution)/shard_map/ppermute | solution.py:37
  36.0 1.1 adjoint_quarter2.4
  39.4 2.0 %collective-permute-start.10 = (bf16[24,32,128]{2,1,0:T(8,128)(2,1)S(1)}, bf16[24,32,128]{2,1,0:T(8,128)(2,1)S(1)}, u32[]{:S(2)}, u32[]{:S(2)}) collective-permute-start(bf16[24,32,128]{2,1,0:T(8,128)(2,1)S(1)} %add_convert_fusion.3.mine), channel_id=1, source_target_pairs={{0,16},{1,17},{2,18},{3,19},{4,20},{5,21},{6,22},{7,23},{8,24},{9,... | collective-permute-start | bytes 589832 | tf_op jit(solution)/shard_map/ppermute | solution.py:37
  41.4 1.8 prior_turn.1.prior
  43.3 3.4 %collective-permute-done.10.other = bf16[24,32,128]{2,1,0:T(8,128)(2,1)S(1)} collective-permute-done((bf16[24,32,128]{2,1,0:T(8,128)(2,1)S(1)}, bf16[24,32,128]{2,1,0:T(8,128)(2,1)S(1)}, u32[]{:S(2)}, u32[]{:S(2)}) %collective-permute-start.10) | collective-permute-done | bytes 196640 | tf_op jit(solution)/shard_map/ppermute | solution.py:37
  46.6 1.8 prior_adjoint.4
  49.1 1.7 collective-permute-start.12
  51.9 1.2 prior_spread.5.refs_0_
  53.2 3.6 %collective-permute-start.13 = (bf16[24,32,128]{2,1,0:T(8,128)(2,1)S(1)}, bf16[24,32,128]{2,1,0:T(8,128)(2,1)S(1)}, u32[]{:S(2)}, u32[]{:S(2)}) collective-permute-start(bf16[24,32,128]{2,1,0:T(8,128)(2,1)S(1)} %prior_spread.5.refs_0_), channel_id=1, source_target_pairs={{0,8},{1,9},{2,10},{3,11},{4,12},{5,13},{6,14},{7,15},{8,0},{9,1},... | collective-permute-start | bytes 589832 | tf_op jit(solution)/shard_map/ppermute | solution.py:37
  56.8 1.3 forward_own.5.refs_1_
  58.1 1.3 forward_other.5
  59.4 3.3 %collective-permute-start.14 = (bf16[8,32,128]{2,1,0:T(8,128)(2,1)S(1)}, bf16[8,32,128]{2,1,0:T(8,128)(2,1)S(1)}, u32[]{:S(2)}, u32[]{:S(2)}) collective-permute-start(bf16[8,32,128]{2,1,0:T(8,128)(2,1)S(1)} %get-tuple-element.117), channel_id=1, source_target_pairs={{0,3},{1,2},{2,1},{3,0},{4,7},{5,6},{6,5},{7,4},{8,11},{9,10},{10,... | collective-permute-start | bytes 196616 | tf_op jit(solution)/shard_map/ppermute | solution.py:37
  65.1 2.1 %collective-permute-done.15 = bf16[8,32,128]{2,1,0:T(8,128)(2,1)S(1)} collective-permute-done((bf16[8,32,128]{2,1,0:T(8,128)(2,1)S(1)}, bf16[8,32,128]{2,1,0:T(8,128)(2,1)S(1)}, u32[]{:S(2)}, u32[]{:S(2)}) %collective-permute-start.15) | collective-permute-done | bytes 65568 | tf_op jit(solution)/shard_map/ppermute | solution.py:37
  67.3 3.2 %collective-permute-start.17 = (bf16[8,32,128]{2,1,0:T(8,128)(2,1)S(1)}, bf16[8,32,128]{2,1,0:T(8,128)(2,1)S(1)}, u32[]{:S(2)}, u32[]{:S(2)}) collective-permute-start(bf16[8,32,128]{2,1,0:T(8,128)(2,1)S(1)} %add_convert_fusion.6), channel_id=1, source_target_pairs={{0,4},{1,5},{2,6},{3,7},{4,0},{5,1},{6,2},{7,3},{8,12},{9,13},{10,... | collective-permute-start | bytes 196616 | tf_op jit(solution)/shard_map/ppermute | solution.py:37
  70.5 2.2 %collective-permute-done.17 = bf16[8,32,128]{2,1,0:T(8,128)(2,1)S(1)} collective-permute-done((bf16[8,32,128]{2,1,0:T(8,128)(2,1)S(1)}, bf16[8,32,128]{2,1,0:T(8,128)(2,1)S(1)}, u32[]{:S(2)}, u32[]{:S(2)}) %collective-permute-start.17) | collective-permute-done | bytes 65568 | tf_op jit(solution)/shard_map/ppermute | solution.py:37
  72.8 2.1 %collective-permute-start.20 = (bf16[8,32,128]{2,1,0:T(8,128)(2,1)S(1)}, bf16[8,32,128]{2,1,0:T(8,128)(2,1)S(1)}, u32[]{:S(2)}, u32[]{:S(2)}) collective-permute-start(bf16[8,32,128]{2,1,0:T(8,128)(2,1)S(1)} %multiply_convert_fusion.2.refs_0_), channel_id=1, source_target_pairs={{0,3},{1,2},{2,1},{3,0},{4,7},{5,6},{6,5},{7,4},{8,11},{9,10},{10,... | collective-permute-start | bytes 196616 | tf_op jit(solution)/shard_map/ppermute | solution.py:37
  74.9 1.7 collective-permute-start.19
  76.6 1.1 adjoint_quarter0.5.refs_1_
  79.6 1.1 adjoint_quarter2.5
  83.2 1.7 collective-permute-start.22
  84.9 5.3 %collective-permute-done.22.other = bf16[24,32,128]{2,1,0:T(8,128)(2,1)S(1)} collective-permute-done((bf16[24,32,128]{2,1,0:T(8,128)(2,1)S(1)}, bf16[24,32,128]{2,1,0:T(8,128)(2,1)S(1)}, u32[]{:S(2)}, u32[]{:S(2)}) %collective-permute-start.22) | collective-permute-done | bytes 196640 | tf_op jit(solution)/shard_map/ppermute | solution.py:37
  90.2 1.6 prior_adjoint.5
  92.5 1.8 collective-permute-start.24
  95.3 1.2 prior_spread.6.refs_0_
  96.6 3.6 %collective-permute-start.25 = (bf16[24,32,128]{2,1,0:T(8,128)(2,1)S(1)}, bf16[24,32,128]{2,1,0:T(8,128)(2,1)S(1)}, u32[]{:S(2)}, u32[]{:S(2)}) collective-permute-start(bf16[24,32,128]{2,1,0:T(8,128)(2,1)S(1)} %prior_spread.6.refs_0_), channel_id=1, source_target_pairs={{0,8},{1,9},{2,10},{3,11},{4,12},{5,13},{6,14},{7,15},{8,0},{9,1},... | collective-permute-start | bytes 589832 | tf_op jit(solution)/shard_map/ppermute | solution.py:37
  100.2 1.3 forward_own.6.refs_1_
  101.5 1.3 forward_other.6
  102.8 3.7 %collective-permute-start.26 = (bf16[8,32,128]{2,1,0:T(8,128)(2,1)S(1)}, bf16[8,32,128]{2,1,0:T(8,128)(2,1)S(1)}, u32[]{:S(2)}, u32[]{:S(2)}) collective-permute-start(bf16[8,32,128]{2,1,0:T(8,128)(2,1)S(1)} %get-tuple-element.125), channel_id=1, source_target_pairs={{0,3},{1,2},{2,1},{3,0},{4,7},{5,6},{6,5},{7,4},{8,11},{9,10},{10,... | collective-permute-start | bytes 196616 | tf_op jit(solution)/shard_map/ppermute | solution.py:37
  108.8 2.0 %collective-permute-done.27 = bf16[8,32,128]{2,1,0:T(8,128)(2,1)S(1)} collective-permute-done((bf16[8,32,128]{2,1,0:T(8,128)(2,1)S(1)}, bf16[8,32,128]{2,1,0:T(8,128)(2,1)S(1)}, u32[]{:S(2)}, u32[]{:S(2)}) %collective-permute-start.27) | collective-permute-done | bytes 65568 | tf_op jit(solution)/shard_map/ppermute | solution.py:37
  110.8 3.4 %collective-permute-start.29 = (bf16[8,32,128]{2,1,0:T(8,128)(2,1)S(1)}, bf16[8,32,128]{2,1,0:T(8,128)(2,1)S(1)}, u32[]{:S(2)}, u32[]{:S(2)}) collective-permute-start(bf16[8,32,128]{2,1,0:T(8,128)(2,1)S(1)} %add_convert_fusion.5), channel_id=1, source_target_pairs={{0,4},{1,5},{2,6},{3,7},{4,0},{5,1},{6,2},{7,3},{8,12},{9,13},{10,... | collective-permute-start | bytes 196616 | tf_op jit(solution)/shard_map/ppermute | solution.py:37
  114.2 2.3 %collective-permute-done.29 = bf16[8,32,128]{2,1,0:T(8,128)(2,1)S(1)} collective-permute-done((bf16[8,32,128]{2,1,0:T(8,128)(2,1)S(1)}, bf16[8,32,128]{2,1,0:T(8,128)(2,1)S(1)}, u32[]{:S(2)}, u32[]{:S(2)}) %collective-permute-start.29) | collective-permute-done | bytes 65568 | tf_op jit(solution)/shard_map/ppermute | solution.py:37
  116.5 1.9 collective-permute-start.32
  118.4 1.6 collective-permute-start.31
  121.9 1.3 adjoint_quarter3.6.refs_1_
  123.2 1.1 adjoint_quarter2.6
  126.6 2.4 %collective-permute-start.34 = (bf16[24,32,128]{2,1,0:T(8,128)(2,1)S(1)}, bf16[24,32,128]{2,1,0:T(8,128)(2,1)S(1)}, u32[]{:S(2)}, u32[]{:S(2)}) collective-permute-start(bf16[24,32,128]{2,1,0:T(8,128)(2,1)S(1)} %add_convert_fusion.1.mine), channel_id=1, source_target_pairs={{0,16},{1,17},{2,18},{3,19},{4,20},{5,21},{6,22},{7,23},{8,24},{9,... | collective-permute-start | bytes 589832 | tf_op jit(solution)/shard_map/ppermute | solution.py:37
  128.9 5.2 %collective-permute-done.34.other = bf16[24,32,128]{2,1,0:T(8,128)(2,1)S(1)} collective-permute-done((bf16[24,32,128]{2,1,0:T(8,128)(2,1)S(1)}, bf16[24,32,128]{2,1,0:T(8,128)(2,1)S(1)}, u32[]{:S(2)}, u32[]{:S(2)}) %collective-permute-start.34) | collective-permute-done | bytes 196640 | tf_op jit(solution)/shard_map/ppermute | solution.py:37
  134.1 1.6 prior_adjoint.6
  136.4 2.2 %collective-permute-start.36 = (bf16[24,32,128]{2,1,0:T(8,128)(2,1)S(1)}, bf16[24,32,128]{2,1,0:T(8,128)(2,1)S(1)}, u32[]{:S(2)}, u32[]{:S(2)}) collective-permute-start(bf16[24,32,128]{2,1,0:T(8,128)(2,1)S(1)} %get-tuple-element.132), channel_id=1, source_target_pairs={{0,8},{1,9},{2,10},{3,11},{4,12},{5,13},{6,14},{7,15},{8,0},{9,1},... | collective-permute-start | bytes 589832 | tf_op jit(solution)/shard_map/ppermute | solution.py:37
  139.7 1.2 prior_spread.7.refs_0_
  141.0 3.6 %collective-permute-start.37 = (bf16[24,32,128]{2,1,0:T(8,128)(2,1)S(1)}, bf16[24,32,128]{2,1,0:T(8,128)(2,1)S(1)}, u32[]{:S(2)}, u32[]{:S(2)}) collective-permute-start(bf16[24,32,128]{2,1,0:T(8,128)(2,1)S(1)} %prior_spread.7.refs_0_), channel_id=1, source_target_pairs={{0,8},{1,9},{2,10},{3,11},{4,12},{5,13},{6,14},{7,15},{8,0},{9,1},... | collective-permute-start | bytes 589832 | tf_op jit(solution)/shard_map/ppermute | solution.py:37
  144.6 1.3 forward_own.7.refs_1_
  145.9 1.3 forward_other.7
  147.2 2.9 %collective-permute-start.38 = (bf16[8,32,128]{2,1,0:T(8,128)(2,1)S(1)}, bf16[8,32,128]{2,1,0:T(8,128)(2,1)S(1)}, u32[]{:S(2)}, u32[]{:S(2)}) collective-permute-start(bf16[8,32,128]{2,1,0:T(8,128)(2,1)S(1)} %get-tuple-element.133), channel_id=1, source_target_pairs={{0,3},{1,2},{2,1},{3,0},{4,7},{5,6},{6,5},{7,4},{8,11},{9,10},{10,... | collective-permute-start | bytes 196616 | tf_op jit(solution)/shard_map/ppermute | solution.py:37
  152.4 2.5 %collective-permute-done.39 = bf16[8,32,128]{2,1,0:T(8,128)(2,1)S(1)} collective-permute-done((bf16[8,32,128]{2,1,0:T(8,128)(2,1)S(1)}, bf16[8,32,128]{2,1,0:T(8,128)(2,1)S(1)}, u32[]{:S(2)}, u32[]{:S(2)}) %collective-permute-start.39) | collective-permute-done | bytes 65568 | tf_op jit(solution)/shard_map/ppermute | solution.py:37
  155.1 3.1 %collective-permute-start.41 = (bf16[8,32,128]{2,1,0:T(8,128)(2,1)S(1)}, bf16[8,32,128]{2,1,0:T(8,128)(2,1)S(1)}, u32[]{:S(2)}, u32[]{:S(2)}) collective-permute-start(bf16[8,32,128]{2,1,0:T(8,128)(2,1)S(1)} %add_convert_fusion.4), channel_id=1, source_target_pairs={{0,4},{1,5},{2,6},{3,7},{4,0},{5,1},{6,2},{7,3},{8,12},{9,13},{10,... | collective-permute-start | bytes 196616 | tf_op jit(solution)/shard_map/ppermute | solution.py:37
  158.2 2.3 %collective-permute-done.41 = bf16[8,32,128]{2,1,0:T(8,128)(2,1)S(1)} collective-permute-done((bf16[8,32,128]{2,1,0:T(8,128)(2,1)S(1)}, bf16[8,32,128]{2,1,0:T(8,128)(2,1)S(1)}, u32[]{:S(2)}, u32[]{:S(2)}) %collective-permute-start.41) | collective-permute-done | bytes 65568 | tf_op jit(solution)/shard_map/ppermute | solution.py:37
  160.5 1.7 collective-permute-start.44
  162.2 2.2 %collective-permute-start.43 = (bf16[8,32,128]{2,1,0:T(8,128)(2,1)S(1)}, bf16[8,32,128]{2,1,0:T(8,128)(2,1)S(1)}, u32[]{:S(2)}, u32[]{:S(2)}) collective-permute-start(bf16[8,32,128]{2,1,0:T(8,128)(2,1)S(1)} %multiply_convert_fusion.refs_0_), channel_id=1, source_target_pairs={{0,2},{1,3},{2,0},{3,1},{4,6},{5,7},{6,4},{7,5},{8,10},{9,11},{10,... | collective-permute-start | bytes 196616 | tf_op jit(solution)/shard_map/ppermute | solution.py:37
  167.7 1.1 adjoint_quarter2.7
  171.1 1.6 collective-permute-start.46
  172.7 5.4 %collective-permute-done.46.other = bf16[24,32,128]{2,1,0:T(8,128)(2,1)S(1)} collective-permute-done((bf16[24,32,128]{2,1,0:T(8,128)(2,1)S(1)}, bf16[24,32,128]{2,1,0:T(8,128)(2,1)S(1)}, u32[]{:S(2)}, u32[]{:S(2)}) %collective-permute-start.46) | collective-permute-done | bytes 196640 | tf_op jit(solution)/shard_map/ppermute | solution.py:37
  178.1 1.6 prior_adjoint.7
  180.4 2.0 %collective-permute-start.48 = (bf16[12,32,128]{2,1,0:T(8,128)(2,1)S(1)}, bf16[12,32,128]{2,1,0:T(8,128)(2,1)S(1)}, u32[]{:S(2)}, u32[]{:S(2)}) collective-permute-start(bf16[12,32,128]{2,1,0:T(8,128)(2,1)S(1)} %slice_select_fusion), channel_id=1, source_target_pairs={{0,8},{1,9},{2,10},{3,11},{4,12},{5,13},{6,14},{7,15},{8,0},{9,1},... | collective-permute-start | bytes 294920 | tf_op jit(solution)/shard_map/ppermute | solution.py:37
  183.5 1.6 collective-permute-start.49
  (110 shorter events, 40.6 us)
Async XLA Ops:
  0.0 2.3 %copy-start = (f32[32,128]{1,0:T(8,128)S(1)}, f32[32,128]{1,0:T(8,128)}, u32[]{:S(2)}) copy-start(f32[32,128]{1,0:T(8,128)} %param.15) | copy-start | bytes 49156
  0.0 6.4 %copy-start.3 = (bf16[48,32,128]{2,1,0:T(8,128)(2,1)S(1)}, bf16[48,32,128]{2,1,0:T(8,128)(2,1)}, u32[]{:S(2)}) copy-start(bf16[48,32,128]{2,1,0:T(8,128)(2,1)} %refs_0_.1) | copy-start | bytes 1179652
  1.0 5.4 %collective-permute-start = (bf16[12,32,128]{2,1,0:T(8,128)(2,1)S(1)}, bf16[12,32,128]{2,1,0:T(8,128)(2,1)S(1)}, u32[]{:S(2)}, u32[]{:S(2)}) collective-permute-start(bf16[12,32,128]{2,1,0:T(8,128)(2,1)S(1)} %slice_select_fusion.2), channel_id=1, source_target_pairs={{1,8},{2,9},{3,10},{4,11},{5,12},{6,13},{7,14},{8,1},{9,2},{10,3},... | collective-permute-start | bytes 294920 | tf_op jit(solution)/shard_map/ppermute | solution.py:37
  2.4 9.5 %copy-start.2 = (bf16[1,1,384,128,128]{4,3,2,1,0:T(8,128)(2,1)S(1)}, bf16[1,1,384,128,128]{4,3,2,1,0:T(8,128)(2,1)}, u32[]{:S(2)}) copy-start(bf16[1,1,384,128,128]{4,3,2,1,0:T(8,128)(2,1)} %param.11) | copy-start | bytes 37748740
  7.5 5.7 %collective-permute-start.1 = (bf16[24,32,128]{2,1,0:T(8,128)(2,1)S(1)}, bf16[24,32,128]{2,1,0:T(8,128)(2,1)S(1)}, u32[]{:S(2)}, u32[]{:S(2)}) collective-permute-start(bf16[24,32,128]{2,1,0:T(8,128)(2,1)S(1)} %prior_spread.4.refs_0_), channel_id=1, source_target_pairs={{0,8},{1,9},{2,10},{3,11},{4,12},{5,13},{6,14},{7,15},{8,0},{9,1},... | collective-permute-start | bytes 589832 | tf_op jit(solution)/shard_map/ppermute | solution.py:37
  14.5 8.2 %collective-permute-start.2 = (bf16[8,32,128]{2,1,0:T(8,128)(2,1)S(1)}, bf16[8,32,128]{2,1,0:T(8,128)(2,1)S(1)}, u32[]{:S(2)}, u32[]{:S(2)}) collective-permute-start(bf16[8,32,128]{2,1,0:T(8,128)(2,1)S(1)} %get-tuple-element.84), channel_id=1, source_target_pairs={{0,3},{1,2},{2,1},{3,0},{4,7},{5,6},{6,5},{7,4},{8,11},{9,10},{10,... | collective-permute-start | bytes 196616 | tf_op jit(solution)/shard_map/ppermute | solution.py:37
  17.1 5.6 %collective-permute-start.3 = (bf16[8,32,128]{2,1,0:T(8,128)(2,1)S(1)}, bf16[8,32,128]{2,1,0:T(8,128)(2,1)S(1)}, u32[]{:S(2)}, u32[]{:S(2)}) collective-permute-start(bf16[8,32,128]{2,1,0:T(8,128)(2,1)S(1)} %get-tuple-element.85), channel_id=1, source_target_pairs={{0,2},{1,3},{2,0},{3,1},{4,6},{5,7},{6,4},{7,5},{8,10},{9,11},{10,... | collective-permute-start | bytes 196616 | tf_op jit(solution)/shard_map/ppermute | solution.py:37
  17.1 5.6 %collective-permute-start.4 = (bf16[8,32,128]{2,1,0:T(8,128)(2,1)S(1)}, bf16[8,32,128]{2,1,0:T(8,128)(2,1)S(1)}, u32[]{:S(2)}, u32[]{:S(2)}) collective-permute-start(bf16[8,32,128]{2,1,0:T(8,128)(2,1)S(1)} %get-tuple-element.86), channel_id=1, source_target_pairs={{0,1},{1,0},{2,3},{3,2},{4,5},{5,4},{6,7},{7,6},{8,9},{9,8},{10,11... | collective-permute-start | bytes 196616 | tf_op jit(solution)/shard_map/ppermute | solution.py:37
  22.8 6.8 %collective-permute-start.5 = (bf16[8,32,128]{2,1,0:T(8,128)(2,1)S(1)}, bf16[8,32,128]{2,1,0:T(8,128)(2,1)S(1)}, u32[]{:S(2)}, u32[]{:S(2)}) collective-permute-start(bf16[8,32,128]{2,1,0:T(8,128)(2,1)S(1)} %convert_add_fusion.1), channel_id=1, source_target_pairs={{0,4},{1,5},{2,6},{3,7},{4,0},{5,1},{6,2},{7,3},{8,12},{9,13},{10,... | collective-permute-start | bytes 196616 | tf_op jit(solution)/shard_map/ppermute | solution.py:37
  29.7 5.3 %collective-permute-start.8 = (bf16[8,32,128]{2,1,0:T(8,128)(2,1)S(1)}, bf16[8,32,128]{2,1,0:T(8,128)(2,1)S(1)}, u32[]{:S(2)}, u32[]{:S(2)}) collective-permute-start(bf16[8,32,128]{2,1,0:T(8,128)(2,1)S(1)} %multiply_convert_fusion.3.refs_0_), channel_id=1, source_target_pairs={{0,3},{1,2},{2,1},{3,0},{4,7},{5,6},{6,5},{7,4},{8,11},{9,10},{10,... | collective-permute-start | bytes 196616 | tf_op jit(solution)/shard_map/ppermute | solution.py:37
  30.7 5.3 %collective-permute-start.7 = (bf16[8,32,128]{2,1,0:T(8,128)(2,1)S(1)}, bf16[8,32,128]{2,1,0:T(8,128)(2,1)S(1)}, u32[]{:S(2)}, u32[]{:S(2)}) collective-permute-start(bf16[8,32,128]{2,1,0:T(8,128)(2,1)S(1)} %multiply_convert_fusion.3.refs_0_), channel_id=1, source_target_pairs={{0,2},{1,3},{2,0},{3,1},{4,6},{5,7},{6,4},{7,5},{8,10},{9,11},{10,... | collective-permute-start | bytes 196616 | tf_op jit(solution)/shard_map/ppermute | solution.py:37
  32.7 4.4 %collective-permute-start.6 = (bf16[8,32,128]{2,1,0:T(8,128)(2,1)S(1)}, bf16[8,32,128]{2,1,0:T(8,128)(2,1)S(1)}, u32[]{:S(2)}, u32[]{:S(2)}) collective-permute-start(bf16[8,32,128]{2,1,0:T(8,128)(2,1)S(1)} %multiply_convert_fusion.3.refs_0_), channel_id=1, source_target_pairs={{0,1},{1,0},{2,3},{3,2},{4,5},{5,4},{6,7},{7,6},{8,9},{9,8},{10,11... | collective-permute-start | bytes 196616 | tf_op jit(solution)/shard_map/ppermute | solution.py:37
  37.8 1.5 collective-permute-start.9
  39.4 7.2 %collective-permute-start.10 = (bf16[24,32,128]{2,1,0:T(8,128)(2,1)S(1)}, bf16[24,32,128]{2,1,0:T(8,128)(2,1)S(1)}, u32[]{:S(2)}, u32[]{:S(2)}) collective-permute-start(bf16[24,32,128]{2,1,0:T(8,128)(2,1)S(1)} %add_convert_fusion.3.mine), channel_id=1, source_target_pairs={{0,16},{1,17},{2,18},{3,19},{4,20},{5,21},{6,22},{7,23},{8,24},{9,... | collective-permute-start | bytes 589832 | tf_op jit(solution)/shard_map/ppermute | solution.py:37
  48.4 2.4 %collective-permute-start.11 = (bf16[24,32,128]{2,1,0:T(8,128)(2,1)S(1)}, bf16[24,32,128]{2,1,0:T(8,128)(2,1)S(1)}, u32[]{:S(2)}, u32[]{:S(2)}) collective-permute-start(bf16[24,32,128]{2,1,0:T(8,128)(2,1)S(1)} %get-tuple-element.115), channel_id=1, source_target_pairs={{1,8},{2,9},{3,10},{4,11},{5,12},{6,13},{7,14},{8,1},{9,2},{10,3},... | collective-permute-start | bytes 589832 | tf_op jit(solution)/shard_map/ppermute | solution.py:37
  49.1 2.8 %collective-permute-start.12 = (bf16[24,32,128]{2,1,0:T(8,128)(2,1)S(1)}, bf16[24,32,128]{2,1,0:T(8,128)(2,1)S(1)}, u32[]{:S(2)}, u32[]{:S(2)}) collective-permute-start(bf16[24,32,128]{2,1,0:T(8,128)(2,1)S(1)} %get-tuple-element.116), channel_id=1, source_target_pairs={{0,8},{1,9},{2,10},{3,11},{4,12},{5,13},{6,14},{7,15},{8,0},{9,1},... | collective-permute-start | bytes 589832 | tf_op jit(solution)/shard_map/ppermute | solution.py:37
  53.2 4.9 %collective-permute-start.13 = (bf16[24,32,128]{2,1,0:T(8,128)(2,1)S(1)}, bf16[24,32,128]{2,1,0:T(8,128)(2,1)S(1)}, u32[]{:S(2)}, u32[]{:S(2)}) collective-permute-start(bf16[24,32,128]{2,1,0:T(8,128)(2,1)S(1)} %prior_spread.5.refs_0_), channel_id=1, source_target_pairs={{0,8},{1,9},{2,10},{3,11},{4,12},{5,13},{6,14},{7,15},{8,0},{9,1},... | collective-permute-start | bytes 589832 | tf_op jit(solution)/shard_map/ppermute | solution.py:37
  59.4 5.6 %collective-permute-start.14 = (bf16[8,32,128]{2,1,0:T(8,128)(2,1)S(1)}, bf16[8,32,128]{2,1,0:T(8,128)(2,1)S(1)}, u32[]{:S(2)}, u32[]{:S(2)}) collective-permute-start(bf16[8,32,128]{2,1,0:T(8,128)(2,1)S(1)} %get-tuple-element.117), channel_id=1, source_target_pairs={{0,3},{1,2},{2,1},{3,0},{4,7},{5,6},{6,5},{7,4},{8,11},{9,10},{10,... | collective-permute-start | bytes 196616 | tf_op jit(solution)/shard_map/ppermute | solution.py:37
  62.8 4.4 %collective-permute-start.15 = (bf16[8,32,128]{2,1,0:T(8,128)(2,1)S(1)}, bf16[8,32,128]{2,1,0:T(8,128)(2,1)S(1)}, u32[]{:S(2)}, u32[]{:S(2)}) collective-permute-start(bf16[8,32,128]{2,1,0:T(8,128)(2,1)S(1)} %get-tuple-element.118), channel_id=1, source_target_pairs={{0,2},{1,3},{2,0},{3,1},{4,6},{5,7},{6,4},{7,5},{8,10},{9,11},{10,... | collective-permute-start | bytes 196616 | tf_op jit(solution)/shard_map/ppermute | solution.py:37
  62.8 4.5 %collective-permute-start.16 = (bf16[8,32,128]{2,1,0:T(8,128)(2,1)S(1)}, bf16[8,32,128]{2,1,0:T(8,128)(2,1)S(1)}, u32[]{:S(2)}, u32[]{:S(2)}) collective-permute-start(bf16[8,32,128]{2,1,0:T(8,128)(2,1)S(1)} %get-tuple-element.119), channel_id=1, source_target_pairs={{0,1},{1,0},{2,3},{3,2},{4,5},{5,4},{6,7},{7,6},{8,9},{9,8},{10,11... | collective-permute-start | bytes 196616 | tf_op jit(solution)/shard_map/ppermute | solution.py:37
  67.3 5.5 %collective-permute-start.17 = (bf16[8,32,128]{2,1,0:T(8,128)(2,1)S(1)}, bf16[8,32,128]{2,1,0:T(8,128)(2,1)S(1)}, u32[]{:S(2)}, u32[]{:S(2)}) collective-permute-start(bf16[8,32,128]{2,1,0:T(8,128)(2,1)S(1)} %add_convert_fusion.6), channel_id=1, source_target_pairs={{0,4},{1,5},{2,6},{3,7},{4,0},{5,1},{6,2},{7,3},{8,12},{9,13},{10,... | collective-permute-start | bytes 196616 | tf_op jit(solution)/shard_map/ppermute | solution.py:37
  72.8 5.3 %collective-permute-start.20 = (bf16[8,32,128]{2,1,0:T(8,128)(2,1)S(1)}, bf16[8,32,128]{2,1,0:T(8,128)(2,1)S(1)}, u32[]{:S(2)}, u32[]{:S(2)}) collective-permute-start(bf16[8,32,128]{2,1,0:T(8,128)(2,1)S(1)} %multiply_convert_fusion.2.refs_0_), channel_id=1, source_target_pairs={{0,3},{1,2},{2,1},{3,0},{4,7},{5,6},{6,5},{7,4},{8,11},{9,10},{10,... | collective-permute-start | bytes 196616 | tf_op jit(solution)/shard_map/ppermute | solution.py:37
  74.9 4.6 %collective-permute-start.19 = (bf16[8,32,128]{2,1,0:T(8,128)(2,1)S(1)}, bf16[8,32,128]{2,1,0:T(8,128)(2,1)S(1)}, u32[]{:S(2)}, u32[]{:S(2)}) collective-permute-start(bf16[8,32,128]{2,1,0:T(8,128)(2,1)S(1)} %multiply_convert_fusion.2.refs_0_), channel_id=1, source_target_pairs={{0,2},{1,3},{2,0},{3,1},{4,6},{5,7},{6,4},{7,5},{8,10},{9,11},{10,... | collective-permute-start | bytes 196616 | tf_op jit(solution)/shard_map/ppermute | solution.py:37
  76.6 4.3 %collective-permute-start.18 = (bf16[8,32,128]{2,1,0:T(8,128)(2,1)S(1)}, bf16[8,32,128]{2,1,0:T(8,128)(2,1)S(1)}, u32[]{:S(2)}, u32[]{:S(2)}) collective-permute-start(bf16[8,32,128]{2,1,0:T(8,128)(2,1)S(1)} %multiply_convert_fusion.2.refs_0_), channel_id=1, source_target_pairs={{0,1},{1,0},{2,3},{3,2},{4,5},{5,4},{6,7},{7,6},{8,9},{9,8},{10,11... | collective-permute-start | bytes 196616 | tf_op jit(solution)/shard_map/ppermute | solution.py:37
  81.6 1.5 collective-permute-start.21
  83.2 7.0 %collective-permute-start.22 = (bf16[24,32,128]{2,1,0:T(8,128)(2,1)S(1)}, bf16[24,32,128]{2,1,0:T(8,128)(2,1)S(1)}, u32[]{:S(2)}, u32[]{:S(2)}) collective-permute-start(bf16[24,32,128]{2,1,0:T(8,128)(2,1)S(1)} %add_convert_fusion.2.mine), channel_id=1, source_target_pairs={{0,16},{1,17},{2,18},{3,19},{4,20},{5,21},{6,22},{7,23},{8,24},{9,... | collective-permute-start | bytes 589832 | tf_op jit(solution)/shard_map/ppermute | solution.py:37
  91.8 2.5 %collective-permute-start.23 = (bf16[24,32,128]{2,1,0:T(8,128)(2,1)S(1)}, bf16[24,32,128]{2,1,0:T(8,128)(2,1)S(1)}, u32[]{:S(2)}, u32[]{:S(2)}) collective-permute-start(bf16[24,32,128]{2,1,0:T(8,128)(2,1)S(1)} %get-tuple-element.123), channel_id=1, source_target_pairs={{1,8},{2,9},{3,10},{4,11},{5,12},{6,13},{7,14},{8,1},{9,2},{10,3},... | collective-permute-start | bytes 589832 | tf_op jit(solution)/shard_map/ppermute | solution.py:37
  92.5 2.8 %collective-permute-start.24 = (bf16[24,32,128]{2,1,0:T(8,128)(2,1)S(1)}, bf16[24,32,128]{2,1,0:T(8,128)(2,1)S(1)}, u32[]{:S(2)}, u32[]{:S(2)}) collective-permute-start(bf16[24,32,128]{2,1,0:T(8,128)(2,1)S(1)} %get-tuple-element.124), channel_id=1, source_target_pairs={{0,8},{1,9},{2,10},{3,11},{4,12},{5,13},{6,14},{7,15},{8,0},{9,1},... | collective-permute-start | bytes 589832 | tf_op jit(solution)/shard_map/ppermute | solution.py:37
  96.6 4.9 %collective-permute-start.25 = (bf16[24,32,128]{2,1,0:T(8,128)(2,1)S(1)}, bf16[24,32,128]{2,1,0:T(8,128)(2,1)S(1)}, u32[]{:S(2)}, u32[]{:S(2)}) collective-permute-start(bf16[24,32,128]{2,1,0:T(8,128)(2,1)S(1)} %prior_spread.6.refs_0_), channel_id=1, source_target_pairs={{0,8},{1,9},{2,10},{3,11},{4,12},{5,13},{6,14},{7,15},{8,0},{9,1},... | collective-permute-start | bytes 589832 | tf_op jit(solution)/shard_map/ppermute | solution.py:37
  102.8 5.9 %collective-permute-start.26 = (bf16[8,32,128]{2,1,0:T(8,128)(2,1)S(1)}, bf16[8,32,128]{2,1,0:T(8,128)(2,1)S(1)}, u32[]{:S(2)}, u32[]{:S(2)}) collective-permute-start(bf16[8,32,128]{2,1,0:T(8,128)(2,1)S(1)} %get-tuple-element.125), channel_id=1, source_target_pairs={{0,3},{1,2},{2,1},{3,0},{4,7},{5,6},{6,5},{7,4},{8,11},{9,10},{10,... | collective-permute-start | bytes 196616 | tf_op jit(solution)/shard_map/ppermute | solution.py:37
  106.5 4.3 %collective-permute-start.27 = (bf16[8,32,128]{2,1,0:T(8,128)(2,1)S(1)}, bf16[8,32,128]{2,1,0:T(8,128)(2,1)S(1)}, u32[]{:S(2)}, u32[]{:S(2)}) collective-permute-start(bf16[8,32,128]{2,1,0:T(8,128)(2,1)S(1)} %get-tuple-element.126), channel_id=1, source_target_pairs={{0,2},{1,3},{2,0},{3,1},{4,6},{5,7},{6,4},{7,5},{8,10},{9,11},{10,... | collective-permute-start | bytes 196616 | tf_op jit(solution)/shard_map/ppermute | solution.py:37
  106.5 4.3 %collective-permute-start.28 = (bf16[8,32,128]{2,1,0:T(8,128)(2,1)S(1)}, bf16[8,32,128]{2,1,0:T(8,128)(2,1)S(1)}, u32[]{:S(2)}, u32[]{:S(2)}) collective-permute-start(bf16[8,32,128]{2,1,0:T(8,128)(2,1)S(1)} %get-tuple-element.127), channel_id=1, source_target_pairs={{0,1},{1,0},{2,3},{3,2},{4,5},{5,4},{6,7},{7,6},{8,9},{9,8},{10,11... | collective-permute-start | bytes 196616 | tf_op jit(solution)/shard_map/ppermute | solution.py:37
  110.8 5.7 %collective-permute-start.29 = (bf16[8,32,128]{2,1,0:T(8,128)(2,1)S(1)}, bf16[8,32,128]{2,1,0:T(8,128)(2,1)S(1)}, u32[]{:S(2)}, u32[]{:S(2)}) collective-permute-start(bf16[8,32,128]{2,1,0:T(8,128)(2,1)S(1)} %add_convert_fusion.5), channel_id=1, source_target_pairs={{0,4},{1,5},{2,6},{3,7},{4,0},{5,1},{6,2},{7,3},{8,12},{9,13},{10,... | collective-permute-start | bytes 196616 | tf_op jit(solution)/shard_map/ppermute | solution.py:37
  116.5 5.3 %collective-permute-start.32 = (bf16[8,32,128]{2,1,0:T(8,128)(2,1)S(1)}, bf16[8,32,128]{2,1,0:T(8,128)(2,1)S(1)}, u32[]{:S(2)}, u32[]{:S(2)}) collective-permute-start(bf16[8,32,128]{2,1,0:T(8,128)(2,1)S(1)} %multiply_convert_fusion.1.refs_0_), channel_id=1, source_target_pairs={{0,3},{1,2},{2,1},{3,0},{4,7},{5,6},{6,5},{7,4},{8,11},{9,10},{10,... | collective-permute-start | bytes 196616 | tf_op jit(solution)/shard_map/ppermute | solution.py:37
  118.4 4.8 %collective-permute-start.31 = (bf16[8,32,128]{2,1,0:T(8,128)(2,1)S(1)}, bf16[8,32,128]{2,1,0:T(8,128)(2,1)S(1)}, u32[]{:S(2)}, u32[]{:S(2)}) collective-permute-start(bf16[8,32,128]{2,1,0:T(8,128)(2,1)S(1)} %multiply_convert_fusion.1.refs_0_), channel_id=1, source_target_pairs={{0,2},{1,3},{2,0},{3,1},{4,6},{5,7},{6,4},{7,5},{8,10},{9,11},{10,... | collective-permute-start | bytes 196616 | tf_op jit(solution)/shard_map/ppermute | solution.py:37
  120.0 4.3 %collective-permute-start.30 = (bf16[8,32,128]{2,1,0:T(8,128)(2,1)S(1)}, bf16[8,32,128]{2,1,0:T(8,128)(2,1)S(1)}, u32[]{:S(2)}, u32[]{:S(2)}) collective-permute-start(bf16[8,32,128]{2,1,0:T(8,128)(2,1)S(1)} %multiply_convert_fusion.1.refs_0_), channel_id=1, source_target_pairs={{0,1},{1,0},{2,3},{3,2},{4,5},{5,4},{6,7},{7,6},{8,9},{9,8},{10,11... | collective-permute-start | bytes 196616 | tf_op jit(solution)/shard_map/ppermute | solution.py:37
  125.0 1.5 collective-permute-start.33
  126.6 7.6 %collective-permute-start.34 = (bf16[24,32,128]{2,1,0:T(8,128)(2,1)S(1)}, bf16[24,32,128]{2,1,0:T(8,128)(2,1)S(1)}, u32[]{:S(2)}, u32[]{:S(2)}) collective-permute-start(bf16[24,32,128]{2,1,0:T(8,128)(2,1)S(1)} %add_convert_fusion.1.mine), channel_id=1, source_target_pairs={{0,16},{1,17},{2,18},{3,19},{4,20},{5,21},{6,22},{7,23},{8,24},{9,... | collective-permute-start | bytes 589832 | tf_op jit(solution)/shard_map/ppermute | solution.py:37
  135.8 2.9 %collective-permute-start.35 = (bf16[24,32,128]{2,1,0:T(8,128)(2,1)S(1)}, bf16[24,32,128]{2,1,0:T(8,128)(2,1)S(1)}, u32[]{:S(2)}, u32[]{:S(2)}) collective-permute-start(bf16[24,32,128]{2,1,0:T(8,128)(2,1)S(1)} %get-tuple-element.131), channel_id=1, source_target_pairs={{1,8},{2,9},{3,10},{4,11},{5,12},{6,13},{7,14},{8,1},{9,2},{10,3},... | collective-permute-start | bytes 589832 | tf_op jit(solution)/shard_map/ppermute | solution.py:37
  136.4 3.3 %collective-permute-start.36 = (bf16[24,32,128]{2,1,0:T(8,128)(2,1)S(1)}, bf16[24,32,128]{2,1,0:T(8,128)(2,1)S(1)}, u32[]{:S(2)}, u32[]{:S(2)}) collective-permute-start(bf16[24,32,128]{2,1,0:T(8,128)(2,1)S(1)} %get-tuple-element.132), channel_id=1, source_target_pairs={{0,8},{1,9},{2,10},{3,11},{4,12},{5,13},{6,14},{7,15},{8,0},{9,1},... | collective-permute-start | bytes 589832 | tf_op jit(solution)/shard_map/ppermute | solution.py:37
  141.0 4.9 %collective-permute-start.37 = (bf16[24,32,128]{2,1,0:T(8,128)(2,1)S(1)}, bf16[24,32,128]{2,1,0:T(8,128)(2,1)S(1)}, u32[]{:S(2)}, u32[]{:S(2)}) collective-permute-start(bf16[24,32,128]{2,1,0:T(8,128)(2,1)S(1)} %prior_spread.7.refs_0_), channel_id=1, source_target_pairs={{0,8},{1,9},{2,10},{3,11},{4,12},{5,13},{6,14},{7,15},{8,0},{9,1},... | collective-permute-start | bytes 589832 | tf_op jit(solution)/shard_map/ppermute | solution.py:37
  147.2 5.2 %collective-permute-start.38 = (bf16[8,32,128]{2,1,0:T(8,128)(2,1)S(1)}, bf16[8,32,128]{2,1,0:T(8,128)(2,1)S(1)}, u32[]{:S(2)}, u32[]{:S(2)}) collective-permute-start(bf16[8,32,128]{2,1,0:T(8,128)(2,1)S(1)} %get-tuple-element.133), channel_id=1, source_target_pairs={{0,3},{1,2},{2,1},{3,0},{4,7},{5,6},{6,5},{7,4},{8,11},{9,10},{10,... | collective-permute-start | bytes 196616 | tf_op jit(solution)/shard_map/ppermute | solution.py:37
  150.2 4.8 %collective-permute-start.39 = (bf16[8,32,128]{2,1,0:T(8,128)(2,1)S(1)}, bf16[8,32,128]{2,1,0:T(8,128)(2,1)S(1)}, u32[]{:S(2)}, u32[]{:S(2)}) collective-permute-start(bf16[8,32,128]{2,1,0:T(8,128)(2,1)S(1)} %get-tuple-element.134), channel_id=1, source_target_pairs={{0,2},{1,3},{2,0},{3,1},{4,6},{5,7},{6,4},{7,5},{8,10},{9,11},{10,... | collective-permute-start | bytes 196616 | tf_op jit(solution)/shard_map/ppermute | solution.py:37
  150.6 4.5 %collective-permute-start.40 = (bf16[8,32,128]{2,1,0:T(8,128)(2,1)S(1)}, bf16[8,32,128]{2,1,0:T(8,128)(2,1)S(1)}, u32[]{:S(2)}, u32[]{:S(2)}) collective-permute-start(bf16[8,32,128]{2,1,0:T(8,128)(2,1)S(1)} %get-tuple-element.135), channel_id=1, source_target_pairs={{0,1},{1,0},{2,3},{3,2},{4,5},{5,4},{6,7},{7,6},{8,9},{9,8},{10,11... | collective-permute-start | bytes 196616 | tf_op jit(solution)/shard_map/ppermute | solution.py:37
  155.1 5.4 %collective-permute-start.41 = (bf16[8,32,128]{2,1,0:T(8,128)(2,1)S(1)}, bf16[8,32,128]{2,1,0:T(8,128)(2,1)S(1)}, u32[]{:S(2)}, u32[]{:S(2)}) collective-permute-start(bf16[8,32,128]{2,1,0:T(8,128)(2,1)S(1)} %add_convert_fusion.4), channel_id=1, source_target_pairs={{0,4},{1,5},{2,6},{3,7},{4,0},{5,1},{6,2},{7,3},{8,12},{9,13},{10,... | collective-permute-start | bytes 196616 | tf_op jit(solution)/shard_map/ppermute | solution.py:37
  160.5 5.8 %collective-permute-start.44 = (bf16[8,32,128]{2,1,0:T(8,128)(2,1)S(1)}, bf16[8,32,128]{2,1,0:T(8,128)(2,1)S(1)}, u32[]{:S(2)}, u32[]{:S(2)}) collective-permute-start(bf16[8,32,128]{2,1,0:T(8,128)(2,1)S(1)} %multiply_convert_fusion.refs_0_), channel_id=1, source_target_pairs={{0,3},{1,2},{2,1},{3,0},{4,7},{5,6},{6,5},{7,4},{8,11},{9,10},{10,... | collective-permute-start | bytes 196616 | tf_op jit(solution)/shard_map/ppermute | solution.py:37
  162.2 5.4 %collective-permute-start.43 = (bf16[8,32,128]{2,1,0:T(8,128)(2,1)S(1)}, bf16[8,32,128]{2,1,0:T(8,128)(2,1)S(1)}, u32[]{:S(2)}, u32[]{:S(2)}) collective-permute-start(bf16[8,32,128]{2,1,0:T(8,128)(2,1)S(1)} %multiply_convert_fusion.refs_0_), channel_id=1, source_target_pairs={{0,2},{1,3},{2,0},{3,1},{4,6},{5,7},{6,4},{7,5},{8,10},{9,11},{10,... | collective-permute-start | bytes 196616 | tf_op jit(solution)/shard_map/ppermute | solution.py:37
  164.4 4.3 %collective-permute-start.42 = (bf16[8,32,128]{2,1,0:T(8,128)(2,1)S(1)}, bf16[8,32,128]{2,1,0:T(8,128)(2,1)S(1)}, u32[]{:S(2)}, u32[]{:S(2)}) collective-permute-start(bf16[8,32,128]{2,1,0:T(8,128)(2,1)S(1)} %multiply_convert_fusion.refs_0_), channel_id=1, source_target_pairs={{0,1},{1,0},{2,3},{3,2},{4,5},{5,4},{6,7},{7,6},{8,9},{9,8},{10,11... | collective-permute-start | bytes 196616 | tf_op jit(solution)/shard_map/ppermute | solution.py:37
  168.8 18.3 %copy-start.1 = (f32[32,128]{1,0:T(8,128)S(1)}, f32[32,128]{1,0:T(8,128)}, u32[]{:S(2)}) copy-start(f32[32,128]{1,0:T(8,128)} %param.15) | copy-start | bytes 49156
  169.5 1.5 collective-permute-start.45
  171.1 7.0 %collective-permute-start.46 = (bf16[24,32,128]{2,1,0:T(8,128)(2,1)S(1)}, bf16[24,32,128]{2,1,0:T(8,128)(2,1)S(1)}, u32[]{:S(2)}, u32[]{:S(2)}) collective-permute-start(bf16[24,32,128]{2,1,0:T(8,128)(2,1)S(1)} %add_convert_fusion.mine), channel_id=1, source_target_pairs={{0,16},{1,17},{2,18},{3,19},{4,20},{5,21},{6,22},{7,23},{8,24},{9,... | collective-permute-start | bytes 589832 | tf_op jit(solution)/shard_map/ppermute | solution.py:37
  179.7 2.7 %collective-permute-start.47 = (bf16[12,32,128]{2,1,0:T(8,128)(2,1)S(1)}, bf16[12,32,128]{2,1,0:T(8,128)(2,1)S(1)}, u32[]{:S(2)}, u32[]{:S(2)}) collective-permute-start(bf16[12,32,128]{2,1,0:T(8,128)(2,1)S(1)} %slice_select_fusion.1), channel_id=1, source_target_pairs={{1,8},{2,9},{3,10},{4,11},{5,12},{6,13},{7,14},{8,1},{9,2},{10,3},... | collective-permute-start | bytes 294920 | tf_op jit(solution)/shard_map/ppermute | solution.py:37
  180.4 3.0 %collective-permute-start.48 = (bf16[12,32,128]{2,1,0:T(8,128)(2,1)S(1)}, bf16[12,32,128]{2,1,0:T(8,128)(2,1)S(1)}, u32[]{:S(2)}, u32[]{:S(2)}) collective-permute-start(bf16[12,32,128]{2,1,0:T(8,128)(2,1)S(1)} %slice_select_fusion), channel_id=1, source_target_pairs={{0,8},{1,9},{2,10},{3,11},{4,12},{5,13},{6,14},{7,15},{8,0},{9,1},... | collective-permute-start | bytes 294920 | tf_op jit(solution)/shard_map/ppermute | solution.py:37
  183.5 2.7 %collective-permute-start.49 = (bf16[24,32,128]{2,1,0:T(8,128)(2,1)S(1)}, bf16[24,32,128]{2,1,0:T(8,128)(2,1)S(1)}, u32[]{:S(2)}, u32[]{:S(2)}) collective-permute-start(bf16[24,32,128]{2,1,0:T(8,128)(2,1)S(1)} %fusion), channel_id=1, source_target_pairs={{0,8},{1,9},{2,10},{3,11},{4,12},{5,13},{6,14},{7,15},{8,0},{9,1},... | collective-permute-start | bytes 589832 | tf_op jit(solution)/shard_map/ppermute | solution.py:37
